TPU v7x, 256 devices: a whole 4x4x8 slice. The times are simulated.
256 devices in a mesh: prow: 32 (over y, z), pcol: 8 (over x, core).
Axes of the slice: x: 4, y: 4, z: 8, core: 2. Of those that a mesh axis runs over, the one named last changes fastest.
Arguments:
- matrix: bfloat16 [3, 16384, 2, 4096], P(None, 'prow', None, 'pcol'), may hold values from -6 to 6
- pivots: int32 [2, 512], replicated, may hold values from 0 to 49151, as said below
- lower_inverse: bfloat16 [2, 512, 512], replicated, may hold values from -1 to 1, as said below
- upper_inverse: bfloat16 [2, 512, 512], replicated, may hold values from -1 to 1, as said below
Outputs:
- factored: bfloat16 [3, 16384, 2, 4096], P(None, 'prow', None, 'pcol')
Inputs may be any that keep to these rules, and one draw needn't show every extreme that they name: For each panel s, pivots[s, i] is either s * 512 + i or a row of index (s + 1) * 512 or more; the entries of one panel are distinct. Each lower_inverse[s] is unit lower triangular. Each upper_inverse[s] is upper triangular with a positive diagonal.
All inputs are finite; a program needn't handle non-finite values.
Results may differ from a plain program's by a relative error of at most 0.008.
Values may be sent and summed in bfloat16 or wider, within the bound.
No kernel may reach another device: no remote copies, remote signals or barrier semaphores. Data moves between devices by JAX's collectives and lax.ppermute only.
A program may use at most 64 MiB of HBM per device.

v0:
```python
import jax
import jax.numpy as jnp
from jax import lax
from jax.sharding import PartitionSpec as P


def broadcast(value, axis, root):
    mine = lax.axis_index(axis) == root
    return lax.psum(jnp.where(mine, value, jnp.zeros_like(value)), axis)


def locate(pivot_list, panel, prow_size, prow_here):
    block_index = pivot_list // panel
    owned_rows = block_index % prow_size == prow_here
    local_row = block_index // prow_size * panel + pivot_list % panel
    return (owned_rows, local_row)


def per_device(matrix, pivots, lower_inverse, upper_inverse):
    row_blocks = matrix.shape[0]
    panel = matrix.shape[1]
    col_blocks = matrix.shape[2]
    prow_size = lax.axis_size("prow")
    pcol_size = lax.axis_size("pcol")
    prow_here = lax.axis_index("prow")
    pcol_here = lax.axis_index("pcol")
    local_rows = row_blocks * panel
    local_cols = col_blocks * panel
    current = matrix.reshape(local_rows, local_cols)
    row_global = jnp.repeat(jnp.arange(row_blocks, dtype=jnp.int32) * prow_size + prow_here, panel)
    col_global = jnp.repeat(jnp.arange(col_blocks, dtype=jnp.int32) * pcol_size + pcol_here, panel)
    offsets = jnp.arange(panel, dtype=jnp.int32)
    bf_zero = jnp.zeros((), jnp.bfloat16)
    for panel_index in range(2):
        root_row = panel_index % prow_size
        diag_local = panel_index // prow_size * panel
        root_col = panel_index % pcol_size
        panel_local = panel_index // pcol_size * panel
        pivot_list = pivots[panel_index]
        owned_rows, local_row = locate(pivot_list, panel, prow_size, prow_here)
        safe_rows = jnp.where(owned_rows, local_row, 0)
        picked = jnp.where(owned_rows[:, None], current[safe_rows], bf_zero)
        is_root = prow_here == root_row
        previous = current[diag_local : diag_local + panel]
        right_cols = col_global > panel_index
        displaced = broadcast(previous, "prow", root_row)
        gathered = lax.psum(picked, "prow").astype(jnp.float32)
        pivot_block = gathered.astype(jnp.bfloat16)
        product = jnp.dot(
            lower_inverse[panel_index], pivot_block, preferred_element_type=jnp.float32
        ).astype(jnp.bfloat16)
        new_row = jnp.where(right_cols[None, :], product, pivot_block)
        moved_rows = owned_rows & (pivot_list != panel_index * panel + offsets)
        targets = jnp.where(moved_rows, local_row, local_rows)
        current = current.at[targets].set(displaced, mode="drop")
        below_mask = row_global > panel_index
        panel_part = current[:, panel_local : panel_local + panel]
        upper_block = upper_inverse[panel_index]

        def factor(columns):
            result = jnp.dot(columns, upper_block, preferred_element_type=jnp.float32).astype(
                jnp.bfloat16
            )
            return jnp.where(below_mask[:, None], result, jnp.zeros((), jnp.bfloat16))

        def nothing(columns):
            return jnp.zeros((local_rows, panel), jnp.bfloat16)

        factors = lax.cond(pcol_here == root_col, factor, nothing, panel_part)
        factors = broadcast(factors, "pcol", root_col)
        update_rows = jnp.where(right_cols[None, :], new_row, bf_zero)
        correction = jnp.dot(factors, update_rows, preferred_element_type=jnp.float32)
        updated = (current.astype(jnp.float32) - correction).astype(jnp.bfloat16)
        owner_col = pcol_here == root_col
        new_panel = jnp.where(
            owner_col & below_mask[:, None], factors, updated[:, panel_local : panel_local + panel]
        )
        updated = updated.at[:, panel_local : panel_local + panel].set(new_panel)
        row_block = jnp.where(is_root, new_row, updated[diag_local : diag_local + panel])
        current = updated.at[diag_local : diag_local + panel].set(row_block)
    return current.reshape(matrix.shape)


def solution(mesh):
    return jax.shard_map(
        per_device,
        mesh=mesh,
        in_specs=(P(None, "prow", None, "pcol"), P(), P(), P()),
        out_specs=P(None, "prow", None, "pcol"),
        check_vma=False,
    )
```

profile of v0, /device:TPU:1, one launch (start us, length us, event | category | flops | bytes accessed | tf_op | source)
XLA Modules:
  0.0 529.5 jit_solution(5184857435831566567)
XLA Ops:
  6.5 0.7 and_select_fusion.4
  7.2 0.8 fusion.42
  8.0 0.8 and_select_fusion.9
  8.9 2.7 copy.36
  11.6 2.8 gather_fusion
  14.4 2.3 copy.20
  16.7 2.2 broadcast_select_fusion
  18.9 1.2 copy.37
  20.1 1.1 broadcast_select_fusion.5
  21.2 0.0 all-reduce.13.cloned.1.call-update
  21.2 0.0 all-reduce.7.cloned.1.call-start
  21.3 0.1 broadcast_in_dim.104
  21.4 154.1 %all-reduce.13.cloned.1.call-done = (bf16[512,1024]{1,0:T(8,128)(2,1)}, bf16[512,1024]{0,1:T(8,128)(2,1)}) async-done(((bf16[512,1024]{1,0:T(8,128)(2,1)}, bf16[512,1024]{0,1:T(8,128)(2,1)}), (bf16[512,1024]{1,0:T(8,128)(2,1)}, bf16[512,1024]{0,1:T(8,128)(2,1)})) %all-reduce.13.cloned.1.call-update) | async-done | bytes 2097168 | tf_op jit(solution)/shard_map/psum | solution.py:9
  175.4 5.1 scatter_fusion
  180.6 1.3 conditional.2
  180.6 1.2 broadcast.765.clone
  181.8 1.2 broadcast_select_fusion.2
  183.1 0.2 all-reduce.11.cloned.1.call-start
  183.3 0.1 broadcast_in_dim.105
  183.4 0.6 compare_reduce_fusion
  184.1 2.9 copy.18
  187.1 3.6 fusion.11
  190.6 64.6 %all-reduce.7.cloned.1.call-done = bf16[1536,512]{0,1:T(8,128)(2,1)} async-done(((bf16[1536,512]{0,1:T(8,128)(2,1)}), bf16[1536,512]{0,1:T(8,128)(2,1)}) %all-reduce.7.cloned.1.call-update) | async-done | bytes 1572880 | tf_op jit(solution)/shard_map/psum | solution.py:9
  255.2 3.7 subtract_convert_fusion.1
  258.9 1.4 fusion.8
  260.3 1.5 broadcast_select_fusion.4
  261.8 1.7 copy-done
  263.5 3.2 copy.22
  266.6 2.8 gather_fusion.1
  269.4 2.3 copy.27
  271.7 2.3 broadcast_select_fusion.3
  274.0 0.0 all-reduce.9.cloned.1.call-start
  274.1 151.9 %all-reduce.11.cloned.1.call-done = (bf16[512,1024]{0,1:T(8,128)(2,1)}, bf16[512,1024]{0,1:T(8,128)(2,1)}) async-done(((bf16[512,1024]{0,1:T(8,128)(2,1)}, bf16[512,1024]{0,1:T(8,128)(2,1)}), (bf16[512,1024]{0,1:T(8,128)(2,1)}, bf16[512,1024]{0,1:T(8,128)(2,1)})) %all-reduce.11.cloned.1.call-update) | async-done | bytes 2097168 | tf_op jit(solution)/shard_map/psum | solution.py:9
  425.9 2.3 copy.23
  428.2 5.1 scatter_fusion.1
  433.3 5.8 %conditional.3 = (bf16[1536,512]{0,1:T(8,128)(2,1)}) conditional(s32[]{:T(128)} %convert_element_type.46, () %tuple.35, (s32[1536]{0:T(1024)S(1)}, bf16[1536,1024]{1,0:T(8,128)(2,1)S(1)}, bf16[2,512,512]{2,1,0:T(8,128)(2,1)}) %tuple.36), branch_computations={%region_9.10_spmd, %region_10.11_spmd} | conditional | flops 806880768 | bytes 6825480 | solution.py:69
  433.3 3.2 fusion.4
  436.5 2.6 copy.35
  439.1 2.7 broadcast_select_fusion.1
  441.8 0.1 broadcast_in_dim.109
  441.9 2.9 copy.24
  444.8 3.6 fusion.13
  448.4 55.9 %all-reduce.9.cloned.1.call-done = bf16[1536,512]{0,1:T(8,128)(2,1)} async-done(((bf16[1536,512]{0,1:T(8,128)(2,1)}), bf16[1536,512]{0,1:T(8,128)(2,1)}) %all-reduce.9.cloned.1.call-update) | async-done | bytes 1572880 | tf_op jit(solution)/shard_map/psum | solution.py:9
  504.3 5.4 %subtract_convert_fusion = bf16[1536,1024]{0,1:T(8,128)(2,1)} fusion(bf16[1536,1024]{0,1:T(8,128)(2,1)S(1)} %copy-done.3, bf16[1536,512]{0,1:T(8,128)(2,1)} %all-reduce.9.cloned.1.call-done, bf16[512,1024]{0,1:T(8,128)(2,1)} %fusion.13, pred[1024]{0:T(1024)(128)(4,1)S(1)} %gt.67), kind=kOutput, calls=%fused_computation.16 | convolution fusion | flops 1615855616 | bytes 8913920 | tf_op jit(solution)/shard_map/dot_general | solution.py:72
  509.7 3.7 fusion.9
  513.4 2.5 fusion.14
  515.9 3.2 copy.29
  519.1 3.9 reshape.610
  (36 shorter events, 0.3 us)
Async XLA Ops:
  6.5 168.9 %all-reduce.13.cloned.1.call-start = ((), (), s32[]{:S(2)}) async-start(), calls=%async_computation.3 | async-start | bytes 4194304 | tf_op jit(solution)/shard_map/psum | solution.py:9
  16.7 3.4 copy-start.1
  18.9 2.5 copy-start.8
  21.2 234.0 %all-reduce.7.cloned.1.call-start = ((), (), s32[]{:S(2)}) async-start(), calls=%async_computation | async-start | bytes 3145728 | tf_op jit(solution)/shard_map/psum | solution.py:9
  183.1 242.8 %all-reduce.11.cloned.1.call-start = ((), (), s32[]{:S(2)}) async-start(), calls=%async_computation.2 | async-start | bytes 4194304 | tf_op jit(solution)/shard_map/psum | solution.py:9
  187.1 68.1 %copy-start.2 = (bf16[1536,1024]{0,1:T(8,128)(2,1)S(1)}, bf16[1536,1024]{0,1:T(8,128)(2,1)}, u32[]{:S(2)}) copy-start(bf16[1536,1024]{0,1:T(8,128)(2,1)} %copy.18) | copy-start | bytes 9437188
  255.2 3.7 copy-start.4
  258.9 1.4 copy-start.6
  261.8 1.7 copy-start
  274.0 230.3 %all-reduce.9.cloned.1.call-start = ((), (), s32[]{:S(2)}) async-start(), calls=%async_computation.1 | async-start | bytes 3145728 | tf_op jit(solution)/shard_map/psum | solution.py:9
  444.8 59.5 %copy-start.3 = (bf16[1536,1024]{0,1:T(8,128)(2,1)S(1)}, bf16[1536,1024]{0,1:T(8,128)(2,1)}, u32[]{:S(2)}) copy-start(bf16[1536,1024]{0,1:T(8,128)(2,1)} %copy.24) | copy-start | bytes 9437188
  504.3 5.4 %copy-start.5 = (bf16[1536,512]{0,1:T(8,128)(2,1)S(1)}, bf16[1536,512]{0,1:T(8,128)(2,1)}, u32[]{:S(2)}) copy-start(bf16[1536,512]{0,1:T(8,128)(2,1)} %all-reduce.9.cloned.1.call-done) | copy-start | bytes 4718596
  509.7 3.7 copy-start.7
Sparse Core Ops, SparseCore 0:
  21.3 154.0 all-reduce.12
  183.2 71.9 all-reduce.6
  274.1 151.7 all-reduce.10
  441.9 62.3 all-reduce.8
where the time goes:
time: 531 us; the launch traced here: 530 us
  waiting for transfers between devices  426 us (80%)
  local copies, waits for them, and re-layouts  49.2 us (9%)
  other arithmetic  20.8 us (4%)
  matrix products  19.4 us (4%)
  between operations  13.3 us (3%)
    psum x4, waiting for transfers between devices, broadcast(): return lax.psum(jnp.where(mine, value, jnp.zeros_like(value)), axis)  426 us
    scatter x4, local copies, waits for them, and re-layouts, per_device(): current = current.at[targets].set(displaced, mode='drop')  16 us
  transfers between devices with their start and end apart: 4, of which 4 were waited for; matrix products, arithmetic and copies ran while one was open for 3% of the time, Pallas kernels for 0%

commit v1 on v0

--- a/solution.py
+++ b/solution.py
@@ -1,7 +1,35 @@
+import functools
+
 import jax
 import jax.numpy as jnp
 from jax import lax
+from jax.experimental import pallas as pl
+from jax.experimental.pallas import tpu as pltpu
 from jax.sharding import PartitionSpec as P
+
+NY, NZ, NX, NC = 4, 8, 4, 2
+N_HOMES = NY * NZ
+PAIR_ROWS = 8
+DEST_ROWS = 32
+LINE_ROWS = 144
+Z_ORDER = (0, 7, 1, 4, 6, 5, 2, 3)
+Y_ORDER = (0, 3, 1, 2)
+MIB = 1 << 20
+
+
+def shift_y(step, rows=range(NY), cols=range(NZ)):
+    return [(y * NZ + z, (y + step) % NY * NZ + z) for y in rows for z in cols]
+
+
+def shift_z(step, cols=range(NZ)):
+    return [(y * NZ + z, y * NZ + (z + step) % NZ) for y in range(NY) for z in cols]
+
+
+def move_x(pairs):
+    return [(a * NC + core, b * NC + core) for a, b in pairs for core in range(NC)]
+
+
+SWAP = [(x * NC + core, x * NC + 1 - core) for x in range(NX) for core in range(NC)]
 
 
 def broadcast(value, axis, root):
@@ -16,7 +44,7 @@
     return (owned_rows, local_row)
 
 
-def per_device(matrix, pivots, lower_inverse, upper_inverse):
+def general_steps(matrix, pivots, lower_inverse, upper_inverse):
     row_blocks = matrix.shape[0]
     panel = matrix.shape[1]
     col_blocks = matrix.shape[2]
@@ -31,11 +59,9 @@
     col_global = jnp.repeat(jnp.arange(col_blocks, dtype=jnp.int32) * pcol_size + pcol_here, panel)
     offsets = jnp.arange(panel, dtype=jnp.int32)
     bf_zero = jnp.zeros((), jnp.bfloat16)
-    for panel_index in range(2):
-        root_row = panel_index % prow_size
-        diag_local = panel_index // prow_size * panel
-        root_col = panel_index % pcol_size
-        panel_local = panel_index // pcol_size * panel
+    def one_panel(panel_index, current):
+        root_row, root_col = panel_index, panel_index
+        diag_local = panel_local = 0
         pivot_list = pivots[panel_index]
         owned_rows, local_row = locate(pivot_list, panel, prow_size, prow_here)
         safe_rows = jnp.where(owned_rows, local_row, 0)
@@ -77,8 +103,453 @@
         )
         updated = updated.at[:, panel_local : panel_local + panel].set(new_panel)
         row_block = jnp.where(is_root, new_row, updated[diag_local : diag_local + panel])
-        current = updated.at[diag_local : diag_local + panel].set(row_block)
+        return updated.at[diag_local : diag_local + panel].set(row_block)
+
+    current = lax.fori_loop(0, 2, one_panel, current)
     return current.reshape(matrix.shape)
+
+
+def dot(a, b):
+    return jnp.dot(a, b, preferred_element_type=jnp.float32)
+
+
+def narrow(value):
+    return value.astype(jnp.bfloat16)
+
+
+def iota(shape, axis):
+    return lax.broadcasted_iota(jnp.int32, shape, axis)
+
+
+def total(mask_or_value, axis):
+    return jnp.sum(mask_or_value, axis=axis, keepdims=True).astype(jnp.int32)
+
+
+def pick(mask, value):
+    return jnp.where(mask, value, 0).astype(jnp.float32)
+
+
+def split_rows(row, panel):
+    shift = panel.bit_length() - 1
+    block = row >> shift
+    return block & (N_HOMES - 1), ((block >> 5) << shift) + (row & (panel - 1))
+
+
+def place_of(step, order):
+    result = jnp.zeros_like(step)
+    for place, value in enumerate(order):
+        result = jnp.where(step == value, place, result)
+    return result
+
+
+def deal_kernel(panel, pos_ref, across_ref, down_ref, rows_ref, picks_ref, keep_ref, place_ref, flag_ref):
+    here = pos_ref[0]
+    y, z = here >> 3, here & 7
+    first_r, second_r = across_ref[0:1, :], across_ref[1:2, :]
+    first_c, second_c = down_ref[:, 0:1], down_ref[:, 1:2]
+    square = (panel, panel)
+    number_c, number_r = iota(square, 0), iota(square, 1)
+    came_r = total(pick(first_c == second_r, number_c + 1), 0)
+    came_c = total(pick(second_c == first_r, number_r + 1), 1)
+    source_r = [first_r, jnp.where(came_r > 0, came_r - 1, second_r)]
+    source_c = [first_c, jnp.where(came_c > 0, came_c - 1, second_c)]
+    owners_r, locals_r = zip(*[split_rows(s, panel) for s in source_r])
+    owners_c = [split_rows(s, panel)[0] for s in source_c]
+    before = number_c < number_r
+    slots, homes, entries = [], [], []
+    for s in range(2):
+        counts = total(
+            pick((owners_c[s] == owners_r[s]) & before, 1025) + pick(owners_c[s] < owners_r[s], 1), 0
+        )
+        within, rank = counts >> 10, counts & 1023
+        slot = within >> 5
+        if s == 1:
+            shared = total(pick(owners_c[0] == owners_r[1], 1), 0)
+            slot = slot + ((shared + N_HOMES - 1) >> 5)
+        slots.append(slot)
+        homes.append(rank & (N_HOMES - 1))
+        entries.append(rank >> 5)
+    flag_ref[...] = jnp.maximum(slots[0], slots[1])
+    deal = jnp.zeros((N_HOMES * PAIR_ROWS, 1), jnp.int32)
+    position = iota((N_HOMES * PAIR_ROWS, panel), 0)
+    per_home = panel // N_HOMES
+    for s in range(2):
+        at = jnp.where(owners_r[s] == here, homes[s] * PAIR_ROWS + slots[s], -1)
+        deal = deal + total(pick(position == at, locals_r[s]), 1)
+        kept_at = jnp.where(homes[s] == here, entries[s], -1)
+        keep_ref[s * per_home : (s + 1) * per_home, :] = total(
+            pick(iota((per_home, panel), 0) == kept_at, owners_r[s] * PAIR_ROWS + slots[s]), 1
+        )
+        z_place = place_of((homes[s] - z) & (NZ - 1), Z_ORDER)
+        y_place = place_of(((homes[s] >> 3) - y) & (NY - 1), Y_ORDER)
+        place_ref[s : s + 1, :] = (y_place * NZ + z_place) * per_home + entries[s]
+    n_rows = rows_ref.shape[0]
+    choose = jnp.where(iota((N_HOMES * PAIR_ROWS, n_rows), 1) == deal, 1.0, 0.0)
+    picks_ref[...] = narrow(dot(narrow(choose), rows_ref[...]))
+
+
+def leave_kernel(
+    panel, pos_ref, across_ref, down_ref, rows_ref, place_ref, lower_ref, leaving_ref, passing_ref, land_ref, flag_ref, low_ref
+):
+    here = pos_ref[0]
+    y, z = here >> 3, here & 7
+    odd = (here & 1) == 1
+    first_r, second_r = across_ref[0:1, :], across_ref[1:2, :]
+    first_c, second_c = down_ref[:, 0:1], down_ref[:, 1:2]
+    square = (panel, panel)
+    number_c, number_r = iota(square, 0), iota(square, 1)
+    big = 1 << 20
+    seen_r = total(pick(second_c == first_r, big) + pick(number_c + panel == first_r, second_c), 0)
+    seen_c = total(pick(first_c == second_r, big) + pick(first_c == number_r + panel, second_r), 1)
+    used_r = total(pick(first_c == number_r + panel, 1), 0)
+    used_c = total(pick(number_c + panel == first_r, 1), 1)
+
+    def goals(first, second, seen, used, number):
+        inner = (first >= panel) & (first < 2 * panel)
+        stop = seen & (big - 1)
+        goal_first = jnp.where(
+            inner,
+            jnp.where(stop == first, -1, stop),
+            jnp.where((first == number) | (seen >= big), -1, first),
+        )
+        goal_second = jnp.where((used > 0) | (second == number + panel), -1, second)
+        return goal_first, goal_second
+
+    goal_r = goals(first_r, second_r, seen_r, used_r, number_r[0:1, :])
+    goal_c = goals(first_c, second_c, seen_c, used_c, number_c[:, 0:1])
+    before = number_c < number_r
+    lines, line_ranks, dests, dest_ranks = [], [], [], []
+    worst = jnp.zeros((1, panel), jnp.int32)
+    for s in range(2):
+        dest_r, local_r = split_rows(goal_r[s], panel)
+        dest_r = jnp.where(goal_r[s] < 0, -1, dest_r)
+        dest_c = jnp.where(goal_c[s] < 0, -1, split_rows(goal_c[s], panel)[0])
+        line_r, line_c = dest_r >> 3, dest_c >> 3
+        counts = total(
+            pick((dest_c == dest_r) & before, 1024) + pick((line_c == line_r) & before, 1), 0
+        )
+        line_rank, dest_rank = counts & 1023, counts >> 10
+        worst = jnp.maximum(
+            worst,
+            jnp.where(
+                (dest_r >= 0) & ((line_rank >= LINE_ROWS) | (dest_rank >= DEST_ROWS)), 1, 0
+            ),
+        )
+        land_at = jnp.where(dest_r == here, dest_rank, -1)
+        land_ref[s * DEST_ROWS : (s + 1) * DEST_ROWS, :] = (
+            total(pick(iota((DEST_ROWS, panel), 0) == land_at, local_r + 1), 1) - 1
+        )
+        lines.append(line_r)
+        line_ranks.append(line_rank)
+        dests.append(dest_r)
+        dest_ranks.append(dest_rank)
+    flag_ref[...] = worst
+    line = jnp.where(odd, lines[1], lines[0])
+    line_rank = jnp.where(odd, line_ranks[1], line_ranks[0])
+    dest = jnp.where(odd, dests[1], dests[0])
+    dest_rank = jnp.where(odd, dest_ranks[1], dest_ranks[0])
+    send_at = jnp.where(line < 0, -1, line * LINE_ROWS + line_rank)
+    choose = jnp.where(iota((NY * LINE_ROWS, panel), 0) == send_at, 1.0, 0.0)
+    leaving_ref[...] = narrow(dot(narrow(choose), rows_ref[...]))
+    pass_at = jnp.where(line == y, ((dest - z) & (NZ - 1)) * DEST_ROWS + dest_rank, -1)
+    passing_ref[...] = total(
+        pick(iota((NZ * DEST_ROWS, panel), 0) == pass_at, line_rank), 1
+    )
+    for s in range(2):
+        order = narrow(jnp.where(number_c == place_ref[s : s + 1, :], 1.0, 0.0))
+        low_ref[s] = narrow(
+            lax.dot_general(
+                lower_ref[s], order, (((1,), (1,)), ((), ())), preferred_element_type=jnp.float32
+            )
+        )
+
+
+def finish_kernel(
+    panel,
+    pos_ref,
+    rows_ref,
+    part_ref,
+    other_ref,
+    land_ref,
+    gone_ref,
+    cross_ref,
+    cross_other_ref,
+    y0_ref,
+    y1_ref,
+    y2_ref,
+    y3_ref,
+    low_ref,
+    upper_ref,
+    place_ref,
+    out_ref,
+    new_ref,
+    corner_ref,
+    gone_first_ref,
+    gone_second_ref,
+    top_ref,
+):
+    step = pl.program_id(0)
+    here, column = pos_ref[0], pos_ref[1]
+    even = (column & 1) == 0
+    width = panel
+    bf16 = jnp.bfloat16
+
+    @pl.when(step == 0)
+    def _():
+        mine, others = cross_ref[...], cross_other_ref[...]
+        from_first = jnp.where(even, mine, others)
+        from_second = jnp.where(even, others, mine)
+        gone_first_ref[...] = from_first[panel:]
+        gone_second_ref[...] = from_second[panel:]
+        quarter = panel // NY
+        y_refs = (y0_ref, y1_ref, y2_ref, y3_ref)
+        pivot_first = jnp.concatenate([r[:quarter, :] for r in y_refs])
+        pivot_second = jnp.concatenate([r[quarter:, :] for r in y_refs])
+        row_first = narrow(dot(low_ref[0], pivot_first))
+        corner_ref[...] = narrow(dot(low_ref[0], from_second[:panel]))
+        lower_factor = narrow(dot(from_first[:panel], upper_ref[0]))
+        reduced = narrow(pivot_second.astype(jnp.float32) - dot(lower_factor, row_first))
+        row_second = narrow(dot(low_ref[1], reduced))
+        new_ref[:panel, :] = row_first
+        new_ref[panel:, :] = row_second
+
+        @pl.when(here <= 1)
+        def _():
+            top_ref[...] = jnp.where(here == 0, row_first, row_second)
+
+        @pl.when((here <= 1) & (column <= 1) & (here >= column))
+        def _():
+            raw = jnp.where(
+                here == 0,
+                pivot_first[:, :width],
+                jnp.where(column == 0, lower_factor, reduced[:, :width]),
+            )
+            place = jnp.where(here == 0, place_ref[0:1, :], place_ref[1:2, :])
+            order = narrow(jnp.where(iota((panel, panel), 0) == place, 1.0, 0.0))
+            top_ref[:, :width] = narrow(
+                lax.dot_general(
+                    order, raw, (((0,), (0,)), ((), ())), preferred_element_type=jnp.float32
+                )
+            )
+
+    @pl.when(step > 0)
+    def _():
+        n = rows_ref.shape[0]
+        begin = (step - 1) * n
+        hits = (iota((n, 2 * DEST_ROWS), 0) + begin) == land_ref[...]
+        marks = jnp.where(hits, 1.0, 0.0)
+        hit = jnp.sum(marks, axis=1, keepdims=True) > 0.5
+        marks = narrow(marks)
+
+        def settle(value, gone):
+            return jnp.where(hit, dot(marks, gone), value.astype(jnp.float32))
+
+        mine, others = part_ref[...], other_ref[...]
+        panel_first = settle(jnp.where(even, mine, others), gone_first_ref[...])
+        panel_second = settle(jnp.where(even, others, mine), gone_second_ref[...])
+        factor_first = narrow(dot(narrow(panel_first), upper_ref[0]))
+        mid = narrow(panel_second - dot(factor_first, corner_ref[...]))
+        factor_second = narrow(dot(mid, upper_ref[1]))
+        current = settle(rows_ref[...], gone_ref[...])
+        updated = narrow(
+            current
+            - dot(factor_first, new_ref[:panel, :])
+            - dot(factor_second, new_ref[panel:, :])
+        )
+        out_ref[...] = updated
+
+        @pl.when(column <= 1)
+        def _():
+            out_ref[:, :width] = jnp.where(column == 0, factor_first, factor_second)
+
+        @pl.when((here <= 1) & (begin < panel))
+        def _():
+            out_ref[...] = top_ref[pl.ds(pl.multiple_of(begin, n), n), :]
+
+
+def whole(shape):
+    return pl.BlockSpec(shape, lambda *_: (0,) * len(shape))
+
+
+def smem():
+    return pl.BlockSpec(memory_space=pltpu.SMEM)
+
+
+def shape(dims, dtype=jnp.bfloat16):
+    return jax.ShapeDtypeStruct(dims, dtype)
+
+
+def per_device(matrix, pivots, lower_inverse, upper_inverse):
+    row_blocks, panel, col_blocks, width = matrix.shape
+    local_rows, local_cols = row_blocks * panel, col_blocks * width
+    here = lax.axis_index("prow")
+    column = lax.axis_index("pcol")
+    y, z = here // NZ, here % NZ
+    x, core = column // NC, column % NC
+    position = jnp.stack([here, column]).astype(jnp.int32)
+    rows = matrix.reshape(local_rows, local_cols)
+    down_pivots = pivots.T
+    per_home = panel // N_HOMES
+    params = pltpu.CompilerParams(vmem_limit_bytes=40 * MIB)
+
+    picks, keep, place, flag_deal = pl.pallas_call(
+        functools.partial(deal_kernel, panel),
+        grid=(1,),
+        in_specs=[smem(), whole((2, panel)), whole((panel, 2)), whole((local_rows, local_cols))],
+        out_specs=[
+            whole((N_HOMES * PAIR_ROWS, local_cols)),
+            whole((2 * per_home, 1)),
+            whole((2, panel)),
+            whole((1, panel)),
+        ],
+        out_shape=[
+            shape((N_HOMES * PAIR_ROWS, local_cols)),
+            shape((2 * per_home, 1), jnp.int32),
+            shape((2, panel), jnp.int32),
+            shape((1, panel), jnp.int32),
+        ],
+        compiler_params=params,
+        name="deal",
+    )(position, pivots, down_pivots, rows)
+
+    dealt = lax.all_to_all(picks, "prow", 0, 0, tiled=True)
+
+    matrix_later, keep_later = lax.optimization_barrier((matrix, keep))
+    own = [matrix_later[k, :, 0, :] for k in range(3)]
+    got = [lax.ppermute(own[k], "pcol", move_x([(0, k + 1)])) for k in (0, 2, 1)]
+    third = jnp.where(x == 1, got[0], jnp.where(x == 3, got[1], got[2]))
+    up = lax.ppermute(third, "pcol", move_x([(1, 2), (2, 3)]))
+    down = lax.ppermute(third, "pcol", move_x([(2, 1), (3, 2)]))
+    across = lax.ppermute(third, "pcol", move_x([(1, 3), (3, 1)]))
+    one = jnp.where(x == 0, own[0], jnp.where(x == 1, third, jnp.where(x == 2, up, across)))
+    two = jnp.where(x == 0, own[1], jnp.where(x == 2, third, jnp.where(x == 1, down, up)))
+    three = jnp.where(x == 0, own[2], jnp.where(x == 3, third, jnp.where(x == 2, down, across)))
+    part = jnp.concatenate([one, two, three])
+    other = lax.ppermute(part, "pcol", SWAP)
+
+    leaving, passing, land, flag_leave, low = pl.pallas_call(
+        functools.partial(leave_kernel, panel),
+        grid=(1,),
+        in_specs=[
+            smem(),
+            whole((2, panel)),
+            whole((panel, 2)),
+            whole((panel, local_cols)),
+            whole((2, panel)),
+            whole((2, panel, panel)),
+        ],
+        out_specs=[
+            whole((NY * LINE_ROWS, local_cols)),
+            whole((NZ * DEST_ROWS, 1)),
+            whole((2 * DEST_ROWS, 1)),
+            whole((1, panel)),
+            whole((2, panel, panel)),
+        ],
+        out_shape=[
+            shape((NY * LINE_ROWS, local_cols)),
+            shape((NZ * DEST_ROWS, 1), jnp.int32),
+            shape((2 * DEST_ROWS, 1), jnp.int32),
+            shape((1, panel), jnp.int32),
+            shape((2, panel, panel)),
+        ],
+        compiler_params=params,
+        name="leave",
+    )(position, pivots, down_pivots, rows, place, lower_inverse)
+    leaving = leaving.reshape(NY, LINE_ROWS, local_cols)
+    arrived = [lax.ppermute(leaving[s], "prow", shift_y(s, [0], [0, 1])) for s in (1, 3, 2)]
+
+    choose = narrow((keep_later == jnp.arange(N_HOMES * PAIR_ROWS)[None, :]).astype(jnp.float32))
+    block = narrow(dot(choose, dealt))
+    from_lo = lax.ppermute(block, "prow", shift_z(1))
+    from_hi = lax.ppermute(block, "prow", shift_z(-1))
+    opposite = lax.ppermute(block, "prow", shift_z(4))
+    two_lo = lax.ppermute(jnp.concatenate([block, from_lo]), "prow", shift_z(2))
+    two_hi = lax.ppermute(jnp.concatenate([block, from_hi]), "prow", shift_z(-2))
+
+    on_line = jnp.where(
+        y == 0, leaving[0], jnp.where(y == 1, arrived[0], jnp.where(y == 3, arrived[1], arrived[2]))
+    )
+    on_line, from_lo, from_hi = lax.optimization_barrier((on_line, from_lo, from_hi))
+    choose = narrow((passing == jnp.arange(LINE_ROWS)[None, :]).astype(jnp.float32))
+    spread = narrow(dot(choose, on_line)).reshape(NZ, DEST_ROWS, local_cols)
+    landed = [spread[0]] + [
+        lax.ppermute(spread[s], "prow", shift_z(s, [0, 1])) for s in range(1, NZ)
+    ]
+
+    blocks = [block, from_lo, from_hi, opposite, two_lo[: 2 * per_home], two_lo[2 * per_home :]]
+    blocks += [two_hi[: 2 * per_home], two_hi[2 * per_home :]]
+    z_line = jnp.concatenate([b[:per_home] for b in blocks] + [b[per_home:] for b in blocks])
+    y_parts = [z_line] + [lax.ppermute(z_line, "prow", shift_y(s)) for s in (1, -1, 2)]
+
+    landed = jnp.stack(landed)
+    gone = jnp.concatenate(
+        [
+            lax.dynamic_index_in_dim(landed, z, 0, False),
+            lax.dynamic_index_in_dim(landed, (z - 1) % NZ, 0, False),
+        ]
+    )
+
+    half = panel // NY
+    extra = jnp.where(core == 0, z_line[half:, :width], z_line[:half, :width])
+    extra = jnp.concatenate([extra, gone[:, :width]])
+    sent = [lax.ppermute(extra, "pcol", move_x([(0, k)])) for k in (1, 3, 2)]
+    extra = jnp.where(x == 0, extra, jnp.where(x == 1, sent[0], jnp.where(x == 3, sent[1], sent[2])))
+    cross = extra[:half]
+    cross = jnp.concatenate(
+        [cross] + [lax.ppermute(cross, "prow", shift_y(s)) for s in (1, -1, 2)] + [extra[half:]]
+    )
+    cross_other = lax.ppermute(cross, "pcol", SWAP)
+
+    n_block = panel // 2
+    steps = local_rows // n_block
+
+    def row_block(cols):
+        return pl.BlockSpec((n_block, cols), lambda i: (jnp.maximum(i - 1, 0), 0))
+
+    result = pl.pallas_call(
+        functools.partial(finish_kernel, panel),
+        grid=(steps + 1,),
+        in_specs=[
+            smem(),
+            row_block(local_cols),
+            row_block(width),
+            row_block(width),
+            whole((1, 2 * DEST_ROWS)),
+            whole((2 * DEST_ROWS, local_cols)),
+            whole((panel + 2 * DEST_ROWS, width)),
+            whole((panel + 2 * DEST_ROWS, width)),
+            whole((2 * half, local_cols)),
+            whole((2 * half, local_cols)),
+            whole((2 * half, local_cols)),
+            whole((2 * half, local_cols)),
+            whole((2, panel, panel)),
+            whole((2, panel, panel)),
+            whole((2, panel)),
+        ],
+        out_specs=row_block(local_cols),
+        out_shape=shape((local_rows, local_cols)),
+        scratch_shapes=[
+            pltpu.VMEM((2 * panel, local_cols), jnp.bfloat16),
+            pltpu.VMEM((panel, width), jnp.bfloat16),
+            pltpu.VMEM((2 * DEST_ROWS, width), jnp.bfloat16),
+            pltpu.VMEM((2 * DEST_ROWS, width), jnp.bfloat16),
+            pltpu.VMEM((panel, local_cols), jnp.bfloat16),
+        ],
+        compiler_params=params,
+        name="finish",
+    )(position, rows, part, other, land.reshape(1, -1), gone, cross, cross_other, *y_parts, low, upper_inverse, place)
+    result = result.reshape(matrix.shape)
+    overflow = (jnp.max(flag_deal) >= PAIR_ROWS) | (jnp.max(flag_leave) > 0)
+    return lax.cond(
+        overflow,
+        lambda a, *rest: general_steps(*rest),
+        lambda a, *rest: a,
+        result,
+        matrix,
+        pivots,
+        lower_inverse,
+        upper_inverse,
+    )
 
 
 def solution(mesh):

time: 531 us -> 198 us (0.37)
  waiting for transfers between devices: 426 us -> 31.2 us
  starting transfers between devices: 0.31 us -> 87.2 us
  Pallas kernels: 0 us -> 22.4 us
  local copies, waits for them, and re-layouts: 49.2 us -> 29.1 us
  matrix products: 19.4 us -> 1.59 us
  other arithmetic: 20.8 us -> 9.19 us
    psum x4 -> x0, waiting for transfers between devices: 426 us -> none  [broadcast(): return lax.psum(jnp.where(mine, value, jnp.zeros_like(value)), axis)]
    ppermute x0 -> x32, starting transfers between devices: none -> 75.9 us  [the longest x3 22.5 us: per_device(): sent = [lax.ppermute(extra, 'pcol', move_x([(0, k)])) for k in (1, 3, 2)]]
    ppermute x0 -> x32, waiting for transfers between devices: none -> 31.2 us  [the longest x3 20.7 us: per_device(): lax.ppermute(z_line, 'prow', shift_y(s))]
    scatter x6 -> x0, local copies, waits for them, and re-layouts: 22.4 us -> none  [the longest x4 16 us: per_device(): current = current.at[targets].set(displaced, mode='drop')]
    pallas_call x0 -> x3, Pallas kernels: none -> 22.4 us  [the longest x1 15.8 us: per_device(): pl.pallas_call(functools.partial(finish_kernel, panel), grid=(steps + 1,)...]
    dot_general x5 -> x2, matrix products: 19.4 us -> 1.59 us  [dot(): return jnp.dot(a, b, preferred_element_type=jnp.float32)]
    unnamed x20 -> x49, local copies, waits for them, and re-layouts: 5.65 us -> 18.1 us
    all_to_all x0 -> x1, starting transfers between devices: none -> 11.3 us  [per_device(): dealt = lax.all_to_all(picks, 'prow', 0, 0, tiled=True)]
  transfers between devices with their start and end apart: 4 -> 33, of which waited for: 4 -> 9; matrix products, arithmetic and copies ran while one was open for 3% -> 10% of each run, Pallas kernels for 0% -> 2%
where the time goes in v1:
time: 198 us; the launch traced here: 196 us
  starting transfers between devices  87.2 us (44%)
  waiting for transfers between devices  31.2 us (16%)
  local copies, waits for them, and re-layouts  29.1 us (15%)
  Pallas kernels  22.4 us (11%)
  between operations  15.3 us (8%)
  other arithmetic  9.19 us (5%)
    ppermute x3, starting transfers between devices, per_device(): sent = [lax.ppermute(extra, 'pcol', move_x([(0, k)])) for k in (1, 3, 2)]  22.5 us
    ppermute x3, waiting for transfers between devices, per_device(): lax.ppermute(z_line, 'prow', shift_y(s))  20.7 us
    unnamed x49, local copies, waits for them, and re-layouts  18.1 us
    pallas_call x1, Pallas kernels, per_device(): pl.pallas_call(functools.partial(finish_kernel, panel), grid=(steps + 1,)...  15.8 us
    ppermute x7, starting transfers between devices, per_device(): lax.ppermute(spread[s], 'prow', shift_z(s, [0, 1]))  14.4 us
    all_to_all x1, starting transfers between devices, per_device(): dealt = lax.all_to_all(picks, 'prow', 0, 0, tiled=True)  11.3 us
    ppermute x3, starting transfers between devices, per_device(): lax.ppermute(own[k], 'pcol', move_x([(0, k + 1)]))  9.55 us
    ppermute x3, starting transfers between devices, per_device(): lax.ppermute(leaving[s], 'prow', shift_y(s, [0], [0, 1]))  8.41 us
  transfers between devices with their start and end apart: 33, of which 9 were waited for; matrix products, arithmetic and copies ran while one was open for 10% of the time, Pallas kernels for 2%

profile of v1, /device:TPU:1, one launch (start us, length us, event | category | flops | bytes accessed | tf_op | source)
XLA Modules:
  0.0 195.9 jit_solution(804946082191857012)
XLA Ops:
  7.4 2.7 %copy.21 = bf16[192,8,2,512]{3,1,2,0:T(8,128)(2,1)S(1)} copy(bf16[192,8,2,512]{3,2,1,0:T(2,128)(2,1)} %bitcast.114) | data formatting | bytes 6291456
  10.2 2.7 %deal.1 = (bf16[256,1024]{1,0:T(8,128)(2,1)S(1)}, s32[32,1]{1,0:T(8,128)S(1)}, s32[2,512]{1,0:T(2,128)S(1)}, s32[1,512]{1,0:T(1,128)S(1)}) custom-call(s32[2]{0:T(128)S(1)} %pad_add_fusion.pos_ref, s32[2,512]{1,0:T(2,128)S(1)} %copy-done.11, s32[512,2]{1,0:T(8,128)S(1)} %bitcast.109, bf16[1536,1024]{1,0:T(8,128)(2,1)S(1)} %bitcast.106), custom_call_target="tpu_custom_call" | custom-call | tf_op jit(solution)/shard_map/deal/pallas_call | solution.py:395
  13.8 1.3 slice_bitcast_fusion
  15.9 4.7 %collective-permute-start = (bf16[512,512]{1,0:T(8,128)(2,1)}, bf16[512,512]{1,0:T(8,128)(2,1)}, u32[]{:S(2)}, u32[]{:S(2)}) collective-permute-start(bf16[512,512]{1,0:T(8,128)(2,1)} %get-tuple-element.487), channel_id=1, source_target_pairs={{0,2},{1,3},{8,10},{9,11},{16,18},{17,19},{24,26},{25,27},{32,34},... | collective-permute-start | bytes 1572872 | tf_op jit(solution)/shard_map/ppermute | solution.py:419
  20.7 2.7 %collective-permute-start.1 = (bf16[512,512]{1,0:T(8,128)(2,1)}, bf16[512,512]{1,0:T(8,128)(2,1)}, u32[]{:S(2)}, u32[]{:S(2)}) collective-permute-start(bf16[512,512]{1,0:T(8,128)(2,1)} %get-tuple-element.486), channel_id=1, source_target_pairs={{0,6},{1,7},{8,14},{9,15},{16,22},{17,23},{24,30},{25,31},{32,38},... | collective-permute-start | bytes 1572872 | tf_op jit(solution)/shard_map/ppermute | solution.py:419
  23.4 2.1 %collective-permute-start.2 = (bf16[512,512]{1,0:T(8,128)(2,1)}, bf16[512,512]{1,0:T(8,128)(2,1)}, u32[]{:S(2)}, u32[]{:S(2)}) collective-permute-start(bf16[512,512]{1,0:T(8,128)(2,1)} %get-tuple-element.485), channel_id=1, source_target_pairs={{0,4},{1,5},{8,12},{9,13},{16,20},{17,21},{24,28},{25,29},{32,36},... | collective-permute-start | bytes 1572872 | tf_op jit(solution)/shard_map/ppermute | solution.py:419
  25.5 11.3 %all-to-all-start = ((bf16[32,8,1024]{2,1,0:T(8,128)(2,1)}), bf16[32,8,1024]{2,1,0:T(8,128)(2,1)}, u32[]{:S(2)}, u32[]{:S(2)}) async-start(bf16[32,8,1024]{2,1,0:T(8,128)(2,1)} %bitcast.111), calls=%async_computation | async-start | bytes 1048576 | tf_op jit(solution)/shard_map/all_to_all | solution.py:415
  36.8 3.9 %leave.1 = (bf16[576,1024]{1,0:T(8,128)(2,1)S(1)}, s32[256,1]{1,0:T(8,128)S(1)}, s32[64,1]{1,0:T(8,128)S(1)}, s32[1,512]{1,0:T(1,128)S(1)}, bf16[2,512,512]{2,1,0:T(8,128)(2,1)S(1)}) custom-call(s32[2]{0:T(128)S(1)} %pad_add_fusion.pos_ref, s32[2,512]{1,0:T(2,128)} %across_ref.3, s32[512,2]{1,0:T(8,128)S(1)} %bitcast.110, bf16[1536,1024]{1,0:T(8,128)(2,1)S(1)} %bitcast.107, ...), custom_call_target="tpu_custom_call" | custom-call | tf_op jit(solution)/shard_map/leave/pallas_call | solution.py:430
  40.7 1.0 copy-done
  41.8 1.0 fusion.32
  42.8 3.8 %collective-permute-start.7 = (bf16[144,1024]{1,0:T(8,128)(2,1)}, bf16[144,1024]{1,0:T(8,128)(2,1)}, u32[]{:S(2)}, u32[]{:S(2)}) collective-permute-start(bf16[144,1024]{1,0:T(8,128)(2,1)} %get-tuple-element.490), channel_id=1, source_target_pairs={{0,64},{8,72},{1,65},{9,73},{2,66},{10,74},{3,67},{11,75},{4,68},{... | collective-permute-start | bytes 884744 | tf_op jit(solution)/shard_map/ppermute | solution.py:459
  46.6 2.6 %collective-permute-start.8 = (bf16[144,1024]{1,0:T(8,128)(2,1)}, bf16[144,1024]{1,0:T(8,128)(2,1)}, u32[]{:S(2)}, u32[]{:S(2)}) collective-permute-start(bf16[144,1024]{1,0:T(8,128)(2,1)} %get-tuple-element.489), channel_id=1, source_target_pairs={{0,192},{8,200},{1,193},{9,201},{2,194},{10,202},{3,195},{11,203},... | collective-permute-start | bytes 884744 | tf_op jit(solution)/shard_map/ppermute | solution.py:459
  49.2 2.0 %collective-permute-start.9 = (bf16[144,1024]{1,0:T(8,128)(2,1)}, bf16[144,1024]{1,0:T(8,128)(2,1)}, u32[]{:S(2)}, u32[]{:S(2)}) collective-permute-start(bf16[144,1024]{1,0:T(8,128)(2,1)} %get-tuple-element.488), channel_id=1, source_target_pairs={{0,128},{8,136},{1,129},{9,137},{2,130},{10,138},{3,131},{11,139},... | collective-permute-start | bytes 884744 | tf_op jit(solution)/shard_map/ppermute | solution.py:459
  52.2 1.9 select_select_fusion.4
  54.1 1.4 collective-permute-start.3
  55.6 1.5 collective-permute-start.4
  57.0 1.5 collective-permute-start.5
  58.5 1.4 collective-permute-done.9
  60.0 1.1 select_select_fusion.5
  61.1 1.3 convolution_convert_fusion.3
  62.8 2.3 %collective-permute-start.11 = (bf16[32,1024]{1,0:T(8,128)(2,1)S(1)}, bf16[32,1024]{1,0:T(8,128)(2,1)S(1)}, u32[]{:S(2)}, u32[]{:S(2)}) collective-permute-start(bf16[32,1024]{1,0:T(8,128)(2,1)S(1)} %convolution_convert_fusion.3), channel_id=1, source_target_pairs={{0,56},{8,0},{16,8},{24,16},{32,24},{40,32},{48,40},{56,48},{64,12... | collective-permute-start | bytes 196616 | tf_op jit(solution)/shard_map/ppermute | solution.py:464
  65.7 2.2 %select_select_fusion.3 = (bf16[512,512]{1,0:T(8,128)(2,1)S(1)}, bf16[512,512]{1,0:T(8,128)(2,1)S(1)}, bf16[512,512]{1,0:T(8,128)(2,1)S(1)}) fusion(bf16[512,512]{1,0:T(8,128)(2,1)} %select_select_fusion.4, bf16[512,512]{1,0:T(8,128)(2,1)} %collective-permute-done.3, bf16[512,512]{1,0:T(8,128)(2,1)} %collective-permute-done.4, pred[]{:T(512)S(6)} %eq.177, ...), kind=kLoop, calls=%fused_computation.76 | loop fusion | flops 2359296 | bytes 5242884 | tf_op jit(solution)/shard_map/jit(_where)/select_n | solution.py:424
  68.3 1.3 collective-permute-start.12
  69.6 1.3 collective-permute-start.13
  70.9 4.2 %collective-permute-start.14 = (bf16[32,1024]{1,0:T(8,128)(2,1)S(1)}, bf16[32,1024]{1,0:T(8,128)(2,1)S(1)}, u32[]{:S(2)}, u32[]{:S(2)}) collective-permute-start(bf16[32,1024]{1,0:T(8,128)(2,1)S(1)} %get-tuple-element.497), channel_id=1, source_target_pairs={{0,24},{8,32},{64,88},{72,96},{128,152},{136,160},{192,216},{200,2... | collective-permute-start | bytes 196616 | tf_op jit(solution)/shard_map/ppermute | solution.py:476
  75.2 3.1 %collective-permute-start.15 = (bf16[32,1024]{1,0:T(8,128)(2,1)S(1)}, bf16[32,1024]{1,0:T(8,128)(2,1)S(1)}, u32[]{:S(2)}, u32[]{:S(2)}) collective-permute-start(bf16[32,1024]{1,0:T(8,128)(2,1)S(1)} %get-tuple-element.496), channel_id=1, source_target_pairs={{0,32},{8,40},{64,96},{72,104},{128,160},{136,168},{192,224},{200,... | collective-permute-start | bytes 196616 | tf_op jit(solution)/shard_map/ppermute | solution.py:476
  79.5 1.3 collective-permute-start.16
  81.4 1.3 collective-permute-start.17
  82.7 1.9 collective-permute-start.18
  84.8 3.8 %collective-permute-start.21 = (bf16[64,1024]{1,0:T(8,128)(2,1)S(1)}, bf16[64,1024]{1,0:T(8,128)(2,1)S(1)}, u32[]{:S(2)}, u32[]{:S(2)}) collective-permute-start(bf16[64,1024]{1,0:T(8,128)(2,1)S(1)} %get-tuple-element.526), channel_id=1, source_target_pairs={{0,48},{8,56},{16,0},{24,8},{32,16},{40,24},{48,32},{56,40},{64,11... | collective-permute-start | bytes 393224 | tf_op jit(solution)/shard_map/ppermute | solution.py:467
  88.7 2.1 %collective-permute-done.20 = bf16[64,1024]{1,0:T(8,128)(2,1)S(1)} collective-permute-done((bf16[64,1024]{1,0:T(8,128)(2,1)S(1)}, bf16[64,1024]{1,0:T(8,128)(2,1)S(1)}, u32[]{:S(2)}, u32[]{:S(2)}) %collective-permute-start.20) | collective-permute-done | bytes 131104 | tf_op jit(solution)/shard_map/ppermute | solution.py:466
  98.1 19.9 %collective-permute-start.22 = (bf16[192,512]{1,0:T(8,128)(2,1)S(1)}, bf16[192,512]{1,0:T(8,128)(2,1)S(1)}, u32[]{:S(2)}, u32[]{:S(2)}) collective-permute-start(bf16[192,512]{1,0:T(8,128)(2,1)S(1)} %pad_maximum_fusion.1), channel_id=1, source_target_pairs={{0,2},{1,3},{8,10},{9,11},{16,18},{17,19},{24,26},{25,27},{32,34},... | collective-permute-start | bytes 589832 | tf_op jit(solution)/shard_map/ppermute | solution.py:495
  118.0 1.3 collective-permute-start.23
  119.3 1.3 collective-permute-start.24
  120.6 1.2 pad_maximum_fusion.part_ref
  122.9 2.8 %collective-permute-done.24 = bf16[192,512]{1,0:T(8,128)(2,1)S(1)} collective-permute-done((bf16[192,512]{1,0:T(8,128)(2,1)S(1)}, bf16[192,512]{1,0:T(8,128)(2,1)S(1)}, u32[]{:S(2)}, u32[]{:S(2)}) %collective-permute-start.24) | collective-permute-done | bytes 196640 | tf_op jit(solution)/shard_map/ppermute | solution.py:495
  126.5 2.7 %collective-permute-start.26 = (bf16[128,512]{1,0:T(8,128)(2,1)S(1)}, bf16[128,512]{1,0:T(8,128)(2,1)S(1)}, u32[]{:S(2)}, u32[]{:S(2)}) collective-permute-start(bf16[128,512]{1,0:T(8,128)(2,1)S(1)} %get-tuple-element.500), channel_id=1, source_target_pairs={{0,192},{8,200},{16,208},{24,216},{32,224},{40,232},{48,240},{56,2... | collective-permute-start | bytes 393224 | tf_op jit(solution)/shard_map/ppermute | solution.py:499
  129.1 2.3 %collective-permute-done.25 = bf16[128,512]{1,0:T(8,128)(2,1)S(1)} collective-permute-done((bf16[128,512]{1,0:T(8,128)(2,1)S(1)}, bf16[128,512]{1,0:T(8,128)(2,1)S(1)}, u32[]{:S(2)}, u32[]{:S(2)}) %collective-permute-start.25) | collective-permute-done | bytes 131104 | tf_op jit(solution)/shard_map/ppermute | solution.py:499
  132.9 1.6 collective-permute-done.27
  135.8 3.2 %collective-permute-start.28 = (bf16[576,512]{1,0:T(8,128)(2,1)}, bf16[576,512]{1,0:T(8,128)(2,1)}, u32[]{:S(2)}, u32[]{:S(2)}) collective-permute-start(bf16[576,512]{1,0:T(8,128)(2,1)} %constant_dynamic-update-slice_fusion.24.cross_ref), channel_id=1, source_target_pairs={{0,1},{1,0},{2,3},{3,2},{4,5},{5,4},{6,7},{7,6},{8,9},{9,8},{10,11... | collective-permute-start | bytes 1769480 | tf_op jit(solution)/shard_map/ppermute | solution.py:501
  139.0 2.7 %collective-permute-start.30 = (bf16[256,1024]{1,0:T(8,128)(2,1)}, bf16[256,1024]{1,0:T(8,128)(2,1)}, u32[]{:S(2)}, u32[]{:S(2)}) collective-permute-start(bf16[256,1024]{1,0:T(8,128)(2,1)} %get-tuple-element.502.y0_ref), channel_id=1, source_target_pairs={{0,192},{8,200},{16,208},{24,216},{32,224},{40,232},{48,240},{56,2... | collective-permute-start | bytes 1572872 | tf_op jit(solution)/shard_map/ppermute | solution.py:482
  145.2 9.0 %collective-permute-done.29.y1_ref = bf16[256,1024]{1,0:T(8,128)(2,1)} collective-permute-done((bf16[256,1024]{1,0:T(8,128)(2,1)}, bf16[256,1024]{1,0:T(8,128)(2,1)}, u32[]{:S(2)}, u32[]{:S(2)}) %collective-permute-start.29) | collective-permute-done | bytes 524320 | tf_op jit(solution)/shard_map/ppermute | solution.py:482
  154.1 10.0 %collective-permute-done.30.y2_ref = bf16[256,1024]{1,0:T(8,128)(2,1)} collective-permute-done((bf16[256,1024]{1,0:T(8,128)(2,1)}, bf16[256,1024]{1,0:T(8,128)(2,1)}, u32[]{:S(2)}, u32[]{:S(2)}) %collective-permute-start.30) | collective-permute-done | bytes 524320 | tf_op jit(solution)/shard_map/ppermute | solution.py:482
  164.2 1.7 collective-permute-done.31.y3_ref
  165.9 1.2 copy-done.2
  167.1 15.8 %finish.1 = bf16[1536,1024]{1,0:T(8,128)(2,1)} custom-call(s32[2]{0:T(128)S(1)} %pad_add_fusion.pos_ref, bf16[1536,1024]{1,0:T(8,128)(2,1)S(1)} %bitcast.108, bf16[1536,512]{1,0:T(8,128)(2,1)} %pad_maximum_fusion.part_ref, bf16[1536,512]{1,0:T(8,128)(2,1)} %collective-permute-done.6.other_ref, s32[1,64]{1,0:T(1,128)S(1)} %bitcast.112, ...), custom_call_target="tpu_custom_call" | custom-call | tf_op jit(solution)/shard_map/finish/pallas_call | solution.py:509
  182.9 6.1 %conditional.2 = (bf16[3,512,2,512]{3,2,1,0:T(2,128)(2,1)}) conditional(s32[]{:T(128)} %convert_element_type.76, bf16[1536,1024]{1,0:T(8,128)(2,1)} %finish.1, (bf16[3,512,2,512]{3,2,1,0:T(2,128)(2,1)}, s32[2,512]{1,0:T(2,128)S(1)}, bf16[2,512,512]{2,1,0:T(8,128)(2,1)}, bf16[2,512,512]{2,1,0:T(8,128)(2,1)}) %tuple.140), branch_computations={%region_2.3_spmd, %region_3.13_spmd} | conditional | flops 2966474752 | bytes 85029544 | solution.py:543
  182.9 6.1 %reshape.458 = bf16[3,512,2,512]{3,2,1,0:T(2,128)(2,1)} reshape(bf16[1536,1024]{1,0:T(8,128)(2,1)} %param.4) | data formatting | bytes 6291456 | tf_op jit(solution)/shard_map/reshape | solution.py:541
  (99 shorter events, 20.9 us)
Async XLA Ops:
  7.4 2.9 %copy-start.11 = (s32[2,512]{1,0:T(2,128)S(1)}, s32[2,512]{1,0:T(2,128)}, u32[]{:S(2)}) copy-start(s32[2,512]{1,0:T(2,128)} %across_ref.3) | copy-start | bytes 12292
  10.1 2.8 %copy-start.8 = (bf16[3,512,2,512]{3,2,1,0:T(2,128)(2,1)S(1)}, bf16[3,512,2,512]{3,2,1,0:T(2,128)(2,1)}, u32[]{:S(2)}) copy-start(bf16[3,512,2,512]{3,2,1,0:T(2,128)(2,1)} %param.14) | copy-start | bytes 9437188
  12.9 0.8 copy-start.3
  12.9 0.8 copy-start.6
  13.8 2.2 %copy-start.10 = (bf16[3,512,2,512]{3,1,2,0:T(8,128)(2,1)}, bf16[3,512,2,512]{3,1,2,0:T(8,128)(2,1)S(1)}, u32[]{:S(2)}) copy-start(bf16[3,512,2,512]{3,1,2,0:T(8,128)(2,1)S(1)} %copy.14) | copy-start | bytes 9437188
  15.9 33.3 %collective-permute-start = (bf16[512,512]{1,0:T(8,128)(2,1)}, bf16[512,512]{1,0:T(8,128)(2,1)}, u32[]{:S(2)}, u32[]{:S(2)}) collective-permute-start(bf16[512,512]{1,0:T(8,128)(2,1)} %get-tuple-element.487), channel_id=1, source_target_pairs={{0,2},{1,3},{8,10},{9,11},{16,18},{17,19},{24,26},{25,27},{32,34},... | collective-permute-start | bytes 1572872 | tf_op jit(solution)/shard_map/ppermute | solution.py:419
  20.7 31.5 %collective-permute-start.1 = (bf16[512,512]{1,0:T(8,128)(2,1)}, bf16[512,512]{1,0:T(8,128)(2,1)}, u32[]{:S(2)}, u32[]{:S(2)}) collective-permute-start(bf16[512,512]{1,0:T(8,128)(2,1)} %get-tuple-element.486), channel_id=1, source_target_pairs={{0,6},{1,7},{8,14},{9,15},{16,22},{17,23},{24,30},{25,31},{32,38},... | collective-permute-start | bytes 1572872 | tf_op jit(solution)/shard_map/ppermute | solution.py:419
  23.4 28.8 %collective-permute-start.2 = (bf16[512,512]{1,0:T(8,128)(2,1)}, bf16[512,512]{1,0:T(8,128)(2,1)}, u32[]{:S(2)}, u32[]{:S(2)}) collective-permute-start(bf16[512,512]{1,0:T(8,128)(2,1)} %get-tuple-element.485), channel_id=1, source_target_pairs={{0,4},{1,5},{8,12},{9,13},{16,20},{17,21},{24,28},{25,29},{32,36},... | collective-permute-start | bytes 1572872 | tf_op jit(solution)/shard_map/ppermute | solution.py:419
  25.5 35.6 %all-to-all-start = ((bf16[32,8,1024]{2,1,0:T(8,128)(2,1)}), bf16[32,8,1024]{2,1,0:T(8,128)(2,1)}, u32[]{:S(2)}, u32[]{:S(2)}) async-start(bf16[32,8,1024]{2,1,0:T(8,128)(2,1)} %bitcast.111), calls=%async_computation | async-start | bytes 1048576 | tf_op jit(solution)/shard_map/all_to_all | solution.py:415
  40.7 1.1 copy-start
  40.7 2.1 %copy-start.1 = (bf16[2,512,512]{2,1,0:T(8,128)(2,1)}, bf16[2,512,512]{2,1,0:T(8,128)(2,1)S(1)}, u32[]{:S(2)}) copy-start(bf16[2,512,512]{2,1,0:T(8,128)(2,1)S(1)} %get-tuple-element.429.low_ref) | copy-start | bytes 3145732
  40.7 2.1 %copy-start.4 = (s32[64,1]{1,0:T(8,128)}, s32[64,1]{1,0:T(8,128)S(1)}, u32[]{:S(2)}) copy-start(s32[64,1]{1,0:T(8,128)S(1)} %get-tuple-element.421) | copy-start | bytes 772
  42.8 14.2 %collective-permute-start.7 = (bf16[144,1024]{1,0:T(8,128)(2,1)}, bf16[144,1024]{1,0:T(8,128)(2,1)}, u32[]{:S(2)}, u32[]{:S(2)}) collective-permute-start(bf16[144,1024]{1,0:T(8,128)(2,1)} %get-tuple-element.490), channel_id=1, source_target_pairs={{0,64},{8,72},{1,65},{9,73},{2,66},{10,74},{3,67},{11,75},{4,68},{... | collective-permute-start | bytes 884744 | tf_op jit(solution)/shard_map/ppermute | solution.py:459
  46.6 11.9 %collective-permute-start.8 = (bf16[144,1024]{1,0:T(8,128)(2,1)}, bf16[144,1024]{1,0:T(8,128)(2,1)}, u32[]{:S(2)}, u32[]{:S(2)}) collective-permute-start(bf16[144,1024]{1,0:T(8,128)(2,1)} %get-tuple-element.489), channel_id=1, source_target_pairs={{0,192},{8,200},{1,193},{9,201},{2,194},{10,202},{3,195},{11,203},... | collective-permute-start | bytes 884744 | tf_op jit(solution)/shard_map/ppermute | solution.py:459
  49.2 10.8 %collective-permute-start.9 = (bf16[144,1024]{1,0:T(8,128)(2,1)}, bf16[144,1024]{1,0:T(8,128)(2,1)}, u32[]{:S(2)}, u32[]{:S(2)}) collective-permute-start(bf16[144,1024]{1,0:T(8,128)(2,1)} %get-tuple-element.488), channel_id=1, source_target_pairs={{0,128},{8,136},{1,129},{9,137},{2,130},{10,138},{3,131},{11,139},... | collective-permute-start | bytes 884744 | tf_op jit(solution)/shard_map/ppermute | solution.py:459
  54.1 11.6 %collective-permute-start.3 = (bf16[512,512]{1,0:T(8,128)(2,1)}, bf16[512,512]{1,0:T(8,128)(2,1)}, u32[]{:S(2)}, u32[]{:S(2)}) collective-permute-start(bf16[512,512]{1,0:T(8,128)(2,1)} %select_select_fusion.4), channel_id=1, source_target_pairs={{2,4},{3,5},{4,6},{5,7},{10,12},{11,13},{12,14},{13,15},{18,20},{1... | collective-permute-start | bytes 1572872 | tf_op jit(solution)/shard_map/ppermute | solution.py:421
  55.6 10.1 %collective-permute-start.4 = (bf16[512,512]{1,0:T(8,128)(2,1)}, bf16[512,512]{1,0:T(8,128)(2,1)}, u32[]{:S(2)}, u32[]{:S(2)}) collective-permute-start(bf16[512,512]{1,0:T(8,128)(2,1)} %select_select_fusion.4), channel_id=1, source_target_pairs={{2,6},{3,7},{6,2},{7,3},{10,14},{11,15},{14,10},{15,11},{18,22},{1... | collective-permute-start | bytes 1572872 | tf_op jit(solution)/shard_map/ppermute | solution.py:423
  57.0 8.7 %collective-permute-start.5 = (bf16[512,512]{1,0:T(8,128)(2,1)}, bf16[512,512]{1,0:T(8,128)(2,1)}, u32[]{:S(2)}, u32[]{:S(2)}) collective-permute-start(bf16[512,512]{1,0:T(8,128)(2,1)} %select_select_fusion.4), channel_id=1, source_target_pairs={{4,2},{5,3},{6,4},{7,5},{12,10},{13,11},{14,12},{15,13},{20,18},{2... | collective-permute-start | bytes 1572872 | tf_op jit(solution)/shard_map/ppermute | solution.py:422
  62.3 5.6 %collective-permute-start.10 = (bf16[32,1024]{1,0:T(8,128)(2,1)S(1)}, bf16[32,1024]{1,0:T(8,128)(2,1)S(1)}, u32[]{:S(2)}, u32[]{:S(2)}) collective-permute-start(bf16[32,1024]{1,0:T(8,128)(2,1)S(1)} %convolution_convert_fusion.3), channel_id=1, source_target_pairs={{0,8},{8,16},{16,24},{24,32},{32,40},{40,48},{48,56},{56,0},{64,72... | collective-permute-start | bytes 196616 | tf_op jit(solution)/shard_map/ppermute | solution.py:463
  62.8 5.1 %collective-permute-start.11 = (bf16[32,1024]{1,0:T(8,128)(2,1)S(1)}, bf16[32,1024]{1,0:T(8,128)(2,1)S(1)}, u32[]{:S(2)}, u32[]{:S(2)}) collective-permute-start(bf16[32,1024]{1,0:T(8,128)(2,1)S(1)} %convolution_convert_fusion.3), channel_id=1, source_target_pairs={{0,56},{8,0},{16,8},{24,16},{32,24},{40,32},{48,40},{56,48},{64,12... | collective-permute-start | bytes 196616 | tf_op jit(solution)/shard_map/ppermute | solution.py:464
  65.7 13.8 %collective-permute-start.19 = (bf16[32,1024]{1,0:T(8,128)(2,1)S(1)}, bf16[32,1024]{1,0:T(8,128)(2,1)S(1)}, u32[]{:S(2)}, u32[]{:S(2)}) collective-permute-start(bf16[32,1024]{1,0:T(8,128)(2,1)S(1)} %convolution_convert_fusion.3), channel_id=1, source_target_pairs={{0,32},{8,40},{16,48},{24,56},{32,0},{40,8},{48,16},{56,24},{64,96... | collective-permute-start | bytes 196616 | tf_op jit(solution)/shard_map/ppermute | solution.py:465
  68.3 13.1 %collective-permute-start.12 = (bf16[32,1024]{1,0:T(8,128)(2,1)S(1)}, bf16[32,1024]{1,0:T(8,128)(2,1)S(1)}, u32[]{:S(2)}, u32[]{:S(2)}) collective-permute-start(bf16[32,1024]{1,0:T(8,128)(2,1)S(1)} %get-tuple-element.499), channel_id=1, source_target_pairs={{0,8},{8,16},{64,72},{72,80},{128,136},{136,144},{192,200},{200,20... | collective-permute-start | bytes 196616 | tf_op jit(solution)/shard_map/ppermute | solution.py:476
  69.6 13.1 %collective-permute-start.13 = (bf16[32,1024]{1,0:T(8,128)(2,1)S(1)}, bf16[32,1024]{1,0:T(8,128)(2,1)S(1)}, u32[]{:S(2)}, u32[]{:S(2)}) collective-permute-start(bf16[32,1024]{1,0:T(8,128)(2,1)S(1)} %get-tuple-element.498), channel_id=1, source_target_pairs={{0,16},{8,24},{64,80},{72,88},{128,144},{136,152},{192,208},{200,2... | collective-permute-start | bytes 196616 | tf_op jit(solution)/shard_map/ppermute | solution.py:476
  70.9 13.7 %collective-permute-start.14 = (bf16[32,1024]{1,0:T(8,128)(2,1)S(1)}, bf16[32,1024]{1,0:T(8,128)(2,1)S(1)}, u32[]{:S(2)}, u32[]{:S(2)}) collective-permute-start(bf16[32,1024]{1,0:T(8,128)(2,1)S(1)} %get-tuple-element.497), channel_id=1, source_target_pairs={{0,24},{8,32},{64,88},{72,96},{128,152},{136,160},{192,216},{200,2... | collective-permute-start | bytes 196616 | tf_op jit(solution)/shard_map/ppermute | solution.py:476
  75.2 9.6 %collective-permute-start.15 = (bf16[32,1024]{1,0:T(8,128)(2,1)S(1)}, bf16[32,1024]{1,0:T(8,128)(2,1)S(1)}, u32[]{:S(2)}, u32[]{:S(2)}) collective-permute-start(bf16[32,1024]{1,0:T(8,128)(2,1)S(1)} %get-tuple-element.496), channel_id=1, source_target_pairs={{0,32},{8,40},{64,96},{72,104},{128,160},{136,168},{192,224},{200,... | collective-permute-start | bytes 196616 | tf_op jit(solution)/shard_map/ppermute | solution.py:476
  79.5 9.1 %collective-permute-start.16 = (bf16[32,1024]{1,0:T(8,128)(2,1)S(1)}, bf16[32,1024]{1,0:T(8,128)(2,1)S(1)}, u32[]{:S(2)}, u32[]{:S(2)}) collective-permute-start(bf16[32,1024]{1,0:T(8,128)(2,1)S(1)} %get-tuple-element.495), channel_id=1, source_target_pairs={{0,40},{8,48},{64,104},{72,112},{128,168},{136,176},{192,232},{200... | collective-permute-start | bytes 196616 | tf_op jit(solution)/shard_map/ppermute | solution.py:476
  81.4 7.2 %collective-permute-start.17 = (bf16[32,1024]{1,0:T(8,128)(2,1)S(1)}, bf16[32,1024]{1,0:T(8,128)(2,1)S(1)}, u32[]{:S(2)}, u32[]{:S(2)}) collective-permute-start(bf16[32,1024]{1,0:T(8,128)(2,1)S(1)} %get-tuple-element.494), channel_id=1, source_target_pairs={{0,48},{8,56},{64,112},{72,120},{128,176},{136,184},{192,240},{200... | collective-permute-start | bytes 196616 | tf_op jit(solution)/shard_map/ppermute | solution.py:476
  82.7 5.9 %collective-permute-start.18 = (bf16[32,1024]{1,0:T(8,128)(2,1)S(1)}, bf16[32,1024]{1,0:T(8,128)(2,1)S(1)}, u32[]{:S(2)}, u32[]{:S(2)}) collective-permute-start(bf16[32,1024]{1,0:T(8,128)(2,1)S(1)} %get-tuple-element.493), channel_id=1, source_target_pairs={{0,56},{8,0},{64,120},{72,64},{128,184},{136,128},{192,248},{200,1... | collective-permute-start | bytes 196616 | tf_op jit(solution)/shard_map/ppermute | solution.py:476
  84.7 6.1 %collective-permute-start.20 = (bf16[64,1024]{1,0:T(8,128)(2,1)S(1)}, bf16[64,1024]{1,0:T(8,128)(2,1)S(1)}, u32[]{:S(2)}, u32[]{:S(2)}) collective-permute-start(bf16[64,1024]{1,0:T(8,128)(2,1)S(1)} %get-tuple-element.527), channel_id=1, source_target_pairs={{0,16},{8,24},{16,32},{24,40},{32,48},{40,56},{48,0},{56,8},{64,80... | collective-permute-start | bytes 393224 | tf_op jit(solution)/shard_map/ppermute | solution.py:466
  84.8 7.2 %collective-permute-start.21 = (bf16[64,1024]{1,0:T(8,128)(2,1)S(1)}, bf16[64,1024]{1,0:T(8,128)(2,1)S(1)}, u32[]{:S(2)}, u32[]{:S(2)}) collective-permute-start(bf16[64,1024]{1,0:T(8,128)(2,1)S(1)} %get-tuple-element.526), channel_id=1, source_target_pairs={{0,48},{8,56},{16,0},{24,8},{32,16},{40,24},{48,32},{56,40},{64,11... | collective-permute-start | bytes 393224 | tf_op jit(solution)/shard_map/ppermute | solution.py:467
  98.0 47.0 %copy-start.5 = (s32[64,1]{1,0:T(8,128)S(1)}, s32[64,1]{1,0:T(8,128)}, u32[]{:S(2)}) copy-start(s32[64,1]{1,0:T(8,128)} %copy-done.4) | copy-start | bytes 772
  98.1 67.8 %copy-start.12 = (s32[2,512]{1,0:T(2,128)S(1)}, s32[2,512]{1,0:T(2,128)}, u32[]{:S(2)}) copy-start(s32[2,512]{1,0:T(2,128)} %across_ref.3) | copy-start | bytes 12292
  98.1 24.7 %collective-permute-start.22 = (bf16[192,512]{1,0:T(8,128)(2,1)S(1)}, bf16[192,512]{1,0:T(8,128)(2,1)S(1)}, u32[]{:S(2)}, u32[]{:S(2)}) collective-permute-start(bf16[192,512]{1,0:T(8,128)(2,1)S(1)} %pad_maximum_fusion.1), channel_id=1, source_target_pairs={{0,2},{1,3},{8,10},{9,11},{16,18},{17,19},{24,26},{25,27},{32,34},... | collective-permute-start | bytes 589832 | tf_op jit(solution)/shard_map/ppermute | solution.py:495
  118.0 4.9 %collective-permute-start.23 = (bf16[192,512]{1,0:T(8,128)(2,1)S(1)}, bf16[192,512]{1,0:T(8,128)(2,1)S(1)}, u32[]{:S(2)}, u32[]{:S(2)}) collective-permute-start(bf16[192,512]{1,0:T(8,128)(2,1)S(1)} %pad_maximum_fusion.1), channel_id=1, source_target_pairs={{0,6},{1,7},{8,14},{9,15},{16,22},{17,23},{24,30},{25,31},{32,38},... | collective-permute-start | bytes 589832 | tf_op jit(solution)/shard_map/ppermute | solution.py:495
  119.3 6.4 %collective-permute-start.24 = (bf16[192,512]{1,0:T(8,128)(2,1)S(1)}, bf16[192,512]{1,0:T(8,128)(2,1)S(1)}, u32[]{:S(2)}, u32[]{:S(2)}) collective-permute-start(bf16[192,512]{1,0:T(8,128)(2,1)S(1)} %pad_maximum_fusion.1), channel_id=1, source_target_pairs={{0,4},{1,5},{8,12},{9,13},{16,20},{17,21},{24,28},{25,29},{32,36},... | collective-permute-start | bytes 589832 | tf_op jit(solution)/shard_map/ppermute | solution.py:495
  121.8 44.0 %collective-permute-start.6 = (bf16[1536,512]{1,0:T(8,128)(2,1)}, bf16[1536,512]{1,0:T(8,128)(2,1)}, u32[]{:S(2)}, u32[]{:S(2)}) collective-permute-start(bf16[1536,512]{1,0:T(8,128)(2,1)} %pad_maximum_fusion.part_ref), channel_id=1, source_target_pairs={{0,1},{1,0},{2,3},{3,2},{4,5},{5,4},{6,7},{7,6},{8,9},{9,8},{10,11... | collective-permute-start | bytes 4718600 | tf_op jit(solution)/shard_map/ppermute | solution.py:428
  126.5 5.0 %collective-permute-start.25 = (bf16[128,512]{1,0:T(8,128)(2,1)S(1)}, bf16[128,512]{1,0:T(8,128)(2,1)S(1)}, u32[]{:S(2)}, u32[]{:S(2)}) collective-permute-start(bf16[128,512]{1,0:T(8,128)(2,1)S(1)} %get-tuple-element.500), channel_id=1, source_target_pairs={{0,64},{8,72},{16,80},{24,88},{32,96},{40,104},{48,112},{56,120},{... | collective-permute-start | bytes 393224 | tf_op jit(solution)/shard_map/ppermute | solution.py:499
  126.5 5.8 %collective-permute-start.26 = (bf16[128,512]{1,0:T(8,128)(2,1)S(1)}, bf16[128,512]{1,0:T(8,128)(2,1)S(1)}, u32[]{:S(2)}, u32[]{:S(2)}) collective-permute-start(bf16[128,512]{1,0:T(8,128)(2,1)S(1)} %get-tuple-element.500), channel_id=1, source_target_pairs={{0,192},{8,200},{16,208},{24,216},{32,224},{40,232},{48,240},{56,2... | collective-permute-start | bytes 393224 | tf_op jit(solution)/shard_map/ppermute | solution.py:499
  129.1 5.4 %collective-permute-start.27 = (bf16[128,512]{1,0:T(8,128)(2,1)S(1)}, bf16[128,512]{1,0:T(8,128)(2,1)S(1)}, u32[]{:S(2)}, u32[]{:S(2)}) collective-permute-start(bf16[128,512]{1,0:T(8,128)(2,1)S(1)} %get-tuple-element.500), channel_id=1, source_target_pairs={{0,128},{8,136},{16,144},{24,152},{32,160},{40,168},{48,176},{56,1... | collective-permute-start | bytes 393224 | tf_op jit(solution)/shard_map/ppermute | solution.py:499
  135.8 30.0 %collective-permute-start.28 = (bf16[576,512]{1,0:T(8,128)(2,1)}, bf16[576,512]{1,0:T(8,128)(2,1)}, u32[]{:S(2)}, u32[]{:S(2)}) collective-permute-start(bf16[576,512]{1,0:T(8,128)(2,1)} %constant_dynamic-update-slice_fusion.24.cross_ref), channel_id=1, source_target_pairs={{0,1},{1,0},{2,3},{3,2},{4,5},{5,4},{6,7},{7,6},{8,9},{9,8},{10,11... | collective-permute-start | bytes 1769480 | tf_op jit(solution)/shard_map/ppermute | solution.py:501
  139.0 15.1 %collective-permute-start.29 = (bf16[256,1024]{1,0:T(8,128)(2,1)}, bf16[256,1024]{1,0:T(8,128)(2,1)}, u32[]{:S(2)}, u32[]{:S(2)}) collective-permute-start(bf16[256,1024]{1,0:T(8,128)(2,1)} %get-tuple-element.502.y0_ref), channel_id=1, source_target_pairs={{0,64},{8,72},{16,80},{24,88},{32,96},{40,104},{48,112},{56,120},{... | collective-permute-start | bytes 1572872 | tf_op jit(solution)/shard_map/ppermute | solution.py:482
  139.0 25.1 %collective-permute-start.30 = (bf16[256,1024]{1,0:T(8,128)(2,1)}, bf16[256,1024]{1,0:T(8,128)(2,1)}, u32[]{:S(2)}, u32[]{:S(2)}) collective-permute-start(bf16[256,1024]{1,0:T(8,128)(2,1)} %get-tuple-element.502.y0_ref), channel_id=1, source_target_pairs={{0,192},{8,200},{16,208},{24,216},{32,224},{40,232},{48,240},{56,2... | collective-permute-start | bytes 1572872 | tf_op jit(solution)/shard_map/ppermute | solution.py:482
  141.7 24.1 %collective-permute-start.31 = (bf16[256,1024]{1,0:T(8,128)(2,1)}, bf16[256,1024]{1,0:T(8,128)(2,1)}, u32[]{:S(2)}, u32[]{:S(2)}) collective-permute-start(bf16[256,1024]{1,0:T(8,128)(2,1)} %get-tuple-element.502.y0_ref), channel_id=1, source_target_pairs={{0,128},{8,136},{16,144},{24,152},{32,160},{40,168},{48,176},{56,1... | collective-permute-start | bytes 1572872 | tf_op jit(solution)/shard_map/ppermute | solution.py:482
  165.9 1.2 copy-start.2

commit v2 on v1

--- a/solution.py
+++ b/solution.py
@@ -135,6 +135,11 @@
     return block & (N_HOMES - 1), ((block >> 5) << shift) + (row & (panel - 1))
 
 
+def upright(row):
+    tall = jnp.transpose(jnp.broadcast_to(row.astype(jnp.float32), (8, row.shape[1])))
+    return tall[:, 0:1].astype(jnp.int32)
+
+
 def place_of(step, order):
     result = jnp.zeros_like(step)
     for place, value in enumerate(order):
@@ -142,11 +147,11 @@
     return result
 
 
-def deal_kernel(panel, pos_ref, across_ref, down_ref, rows_ref, picks_ref, keep_ref, place_ref, flag_ref):
+def deal_kernel(panel, pos_ref, across_ref, rows_ref, picks_ref, keep_ref, place_ref, flag_ref):
     here = pos_ref[0]
     y, z = here >> 3, here & 7
     first_r, second_r = across_ref[0:1, :], across_ref[1:2, :]
-    first_c, second_c = down_ref[:, 0:1], down_ref[:, 1:2]
+    first_c, second_c = upright(first_r), upright(second_r)
     square = (panel, panel)
     number_c, number_r = iota(square, 0), iota(square, 1)
     came_r = total(pick(first_c == second_r, number_c + 1), 0)
@@ -189,13 +194,27 @@
 
 
 def leave_kernel(
-    panel, pos_ref, across_ref, down_ref, rows_ref, place_ref, lower_ref, leaving_ref, passing_ref, land_ref, flag_ref, low_ref
+    panel,
+    pos_ref,
+    across_ref,
+    rows_ref,
+    place_ref,
+    lower_ref,
+    slots_ref,
+    leave0_ref,
+    leave1_ref,
+    leave2_ref,
+    leave3_ref,
+    passing_ref,
+    land_ref,
+    flag_ref,
+    low_ref,
 ):
     here = pos_ref[0]
     y, z = here >> 3, here & 7
     odd = (here & 1) == 1
     first_r, second_r = across_ref[0:1, :], across_ref[1:2, :]
-    first_c, second_c = down_ref[:, 0:1], down_ref[:, 1:2]
+    first_c, second_c = upright(first_r), upright(second_r)
     square = (panel, panel)
     number_c, number_r = iota(square, 0), iota(square, 1)
     big = 1 << 20
@@ -218,7 +237,7 @@
     goal_r = goals(first_r, second_r, seen_r, used_r, number_r[0:1, :])
     goal_c = goals(first_c, second_c, seen_c, used_c, number_c[:, 0:1])
     before = number_c < number_r
-    lines, line_ranks, dests, dest_ranks = [], [], [], []
+    lines, line_ranks, dests, dest_ranks, landing = [], [], [], [], []
     worst = jnp.zeros((1, panel), jnp.int32)
     for s in range(2):
         dest_r, local_r = split_rows(goal_r[s], panel)
@@ -236,21 +255,25 @@
             ),
         )
         land_at = jnp.where(dest_r == here, dest_rank, -1)
-        land_ref[s * DEST_ROWS : (s + 1) * DEST_ROWS, :] = (
-            total(pick(iota((DEST_ROWS, panel), 0) == land_at, local_r + 1), 1) - 1
-        )
+        landing.append(total(pick(iota((DEST_ROWS, panel), 0) == land_at, local_r + 1), 1) - 1)
         lines.append(line_r)
         line_ranks.append(line_rank)
         dests.append(dest_r)
         dest_ranks.append(dest_rank)
-    flag_ref[...] = worst
+    worst = jnp.maximum(worst, jnp.where(slots_ref[...] >= PAIR_ROWS, 1, 0))
+    flag_ref[0] = jnp.max(worst.astype(jnp.float32)).astype(jnp.int32)
+    landing = jnp.concatenate(landing).astype(jnp.float32)
+    landing = jnp.transpose(jnp.broadcast_to(landing, (2 * DEST_ROWS, 128)))
+    land_ref[...] = landing[0:1, :].astype(jnp.int32)
     line = jnp.where(odd, lines[1], lines[0])
     line_rank = jnp.where(odd, line_ranks[1], line_ranks[0])
     dest = jnp.where(odd, dests[1], dests[0])
     dest_rank = jnp.where(odd, dest_ranks[1], dest_ranks[0])
     send_at = jnp.where(line < 0, -1, line * LINE_ROWS + line_rank)
     choose = jnp.where(iota((NY * LINE_ROWS, panel), 0) == send_at, 1.0, 0.0)
-    leaving_ref[...] = narrow(dot(narrow(choose), rows_ref[...]))
+    leaving = narrow(dot(narrow(choose), rows_ref[:panel, :]))
+    for k, ref in enumerate((leave0_ref, leave1_ref, leave2_ref, leave3_ref)):
+        ref[...] = leaving[k * LINE_ROWS : (k + 1) * LINE_ROWS]
     pass_at = jnp.where(line == y, ((dest - z) & (NZ - 1)) * DEST_ROWS + dest_rank, -1)
     passing_ref[...] = total(
         pick(iota((NZ * DEST_ROWS, panel), 0) == pass_at, line_rank), 1
@@ -262,6 +285,120 @@
                 lower_ref[s], order, (((1,), (1,)), ((), ())), preferred_element_type=jnp.float32
             )
         )
+
+
+def block_kernel(keep_ref, dealt_ref, block_ref):
+    n = dealt_ref.shape[0]
+    choose = jnp.where(keep_ref[...] == iota((keep_ref.shape[0], n), 1), 1.0, 0.0)
+    block_ref[...] = narrow(dot(narrow(choose), dealt_ref[...]))
+
+
+def pair_kernel(block_ref, lo_ref, hi_ref, pair_lo_ref, pair_hi_ref):
+    n = block_ref.shape[0]
+    pair_lo_ref[:n, :] = block_ref[...]
+    pair_lo_ref[n:, :] = lo_ref[...]
+    pair_hi_ref[:n, :] = block_ref[...]
+    pair_hi_ref[n:, :] = hi_ref[...]
+
+
+def line_kernel(
+    pos_ref, block_ref, lo_ref, hi_ref, opposite_ref, two_lo_ref, two_hi_ref, line_ref, extra_ref
+):
+    n = block_ref.shape[0]
+    half = n // 2
+    blocks = [block_ref[...], lo_ref[...], hi_ref[...], opposite_ref[...]]
+    blocks += [two_lo_ref[:n, :], two_lo_ref[n:, :], two_hi_ref[:n, :], two_hi_ref[n:, :]]
+    for k, value in enumerate(blocks):
+        line_ref[k * half : (k + 1) * half, :] = value[:half]
+        line_ref[(NZ + k) * half : (NZ + k + 1) * half, :] = value[half:]
+    even = (pos_ref[1] & 1) == 0
+    n, width = extra_ref.shape
+    extra_ref[...] = jnp.where(even, line_ref[n:, :width], line_ref[:n, :width])
+
+
+def by_x(x, at_0, at_1, at_2, at_3):
+    return jnp.where(x <= 1, jnp.where(x == 0, at_0, at_1), jnp.where(x == 2, at_2, at_3))
+
+
+def third_kernel(pos_ref, one_ref, two_ref, three_ref, third_ref):
+    x = pos_ref[1] >> 1
+
+    @pl.when(x <= 1)
+    def _():
+        third_ref[...] = one_ref[...]
+
+    @pl.when(x == 2)
+    def _():
+        third_ref[...] = two_ref[...]
+
+    @pl.when(x == 3)
+    def _():
+        third_ref[...] = three_ref[...]
+
+
+def part_kernel(pos_ref, own_ref, third_ref, up_ref, down_ref, across_ref, part_ref):
+    x = pos_ref[1] >> 1
+    n = third_ref.shape[0]
+    width = third_ref.shape[1]
+    own = [own_ref.at[pl.ds(k * n, n), pl.ds(0, width)] for k in range(3)]
+    by_place = (
+        own,
+        (third_ref, down_ref, across_ref),
+        (up_ref, third_ref, down_ref),
+        (across_ref, up_ref, third_ref),
+    )
+    for place, refs in enumerate(by_place):
+
+        @pl.when(x == place)
+        def _(refs=refs):
+            for k, ref in enumerate(refs):
+                part_ref[k * n : (k + 1) * n, :] = ref[...]
+
+
+def spread_kernel(pos_ref, passing_ref, own_ref, one_ref, two_ref, three_ref, keep_ref, send_ref):
+    y = pos_ref[0] >> 3
+    on_line = by_x(y, own_ref[...], one_ref[...], two_ref[...], three_ref[...])
+    n_rows = passing_ref.shape[0]
+    choose = jnp.where(passing_ref[...] == iota((n_rows, LINE_ROWS), 1), 1.0, 0.0)
+    spread = narrow(dot(narrow(choose), on_line))
+    keep_ref[...] = spread[: n_rows // 2]
+    send_ref[...] = spread[n_rows // 2 :]
+
+
+def fold_kernel(bit, pos_ref, kept_ref, came_ref, keep_ref, send_ref):
+    n = keep_ref.shape[0]
+
+    @pl.when((pos_ref[0] & bit) == 0)
+    def _():
+        keep_ref[...] = kept_ref[:n, :]
+        send_ref[...] = kept_ref[n:, :]
+
+    @pl.when((pos_ref[0] & bit) != 0)
+    def _():
+        keep_ref[...] = came_ref[:n, :]
+        send_ref[...] = came_ref[n:, :]
+
+
+def gone_kernel(pos_ref, kept_ref, came_ref, gone_ref, gone_panel_ref):
+    n, width = kept_ref.shape[0], gone_panel_ref.shape[1]
+    even = (pos_ref[0] & 1) == 0
+    kept, came = kept_ref[...], came_ref[...]
+    gone_ref[:n, :] = jnp.where(even, kept, came)
+    gone_ref[n:, :] = jnp.where(even, came, kept)
+    gone_panel_ref[...] = gone_ref[:, :width]
+
+
+def extra_kernel(pos_ref, own_ref, one_ref, two_ref, three_ref, cross_ref):
+    x = pos_ref[1] >> 1
+    cross_ref[...] = by_x(x, own_ref[...], one_ref[...], two_ref[...], three_ref[...])
+
+
+def cross_kernel(pos_ref, c0_ref, c1_ref, c2_ref, c3_ref, own_ref, one_ref, two_ref, three_ref, cross_ref):
+    n = c0_ref.shape[0]
+    for k, ref in enumerate((c0_ref, c1_ref, c2_ref, c3_ref)):
+        cross_ref[k * n : (k + 1) * n, :] = ref[...]
+    x = pos_ref[1] >> 1
+    cross_ref[NY * n :, :] = by_x(x, own_ref[...], one_ref[...], two_ref[...], three_ref[...])
 
 
 def finish_kernel(
@@ -277,7 +414,8 @@
     y0_ref,
     y1_ref,
     y2_ref,
-    y3_ref,
+    far_first_ref,
+    far_second_ref,
     low_ref,
     upper_ref,
     place_ref,
@@ -302,9 +440,9 @@
         gone_first_ref[...] = from_first[panel:]
         gone_second_ref[...] = from_second[panel:]
         quarter = panel // NY
-        y_refs = (y0_ref, y1_ref, y2_ref, y3_ref)
-        pivot_first = jnp.concatenate([r[:quarter, :] for r in y_refs])
-        pivot_second = jnp.concatenate([r[quarter:, :] for r in y_refs])
+        y_refs = (y0_ref, y1_ref, y2_ref)
+        pivot_first = jnp.concatenate([r[:quarter, :] for r in y_refs] + [far_first_ref[...]])
+        pivot_second = jnp.concatenate([r[quarter:, :] for r in y_refs] + [far_second_ref[...]])
         row_first = narrow(dot(low_ref[0], pivot_first))
         corner_ref[...] = narrow(dot(low_ref[0], from_second[:panel]))
         lower_factor = narrow(dot(from_first[:panel], upper_ref[0]))
@@ -379,126 +517,168 @@
     return jax.ShapeDtypeStruct(dims, dtype)
 
 
+def local_kernel(body, name, outs, scalars, *arrays):
+    return pl.pallas_call(
+        body,
+        grid=(1,),
+        in_specs=[smem() for _ in scalars] + [whole(v.shape) for v in arrays],
+        out_specs=[smem() if o.shape == (1,) else whole(o.shape) for o in outs],
+        out_shape=outs,
+        compiler_params=pltpu.CompilerParams(vmem_limit_bytes=40 * MIB),
+        cost_estimate=pl.CostEstimate(flops=0, bytes_accessed=0, transcendentals=0),
+        name=name,
+    )(*scalars, *arrays)
+
+
+def after(values, *others):
+    return lax.optimization_barrier((values, others))[0]
+
+
 def per_device(matrix, pivots, lower_inverse, upper_inverse):
     row_blocks, panel, col_blocks, width = matrix.shape
     local_rows, local_cols = row_blocks * panel, col_blocks * width
     here = lax.axis_index("prow")
     column = lax.axis_index("pcol")
-    y, z = here // NZ, here % NZ
-    x, core = column // NC, column % NC
     position = jnp.stack([here, column]).astype(jnp.int32)
     rows = matrix.reshape(local_rows, local_cols)
-    down_pivots = pivots.T
     per_home = panel // N_HOMES
-    params = pltpu.CompilerParams(vmem_limit_bytes=40 * MIB)
-
-    picks, keep, place, flag_deal = pl.pallas_call(
+    i32 = jnp.int32
+
+    picks, keep, place, slots = local_kernel(
         functools.partial(deal_kernel, panel),
-        grid=(1,),
-        in_specs=[smem(), whole((2, panel)), whole((panel, 2)), whole((local_rows, local_cols))],
-        out_specs=[
-            whole((N_HOMES * PAIR_ROWS, local_cols)),
-            whole((2 * per_home, 1)),
-            whole((2, panel)),
-            whole((1, panel)),
+        "deal",
+        [
+            shape((N_HOMES * PAIR_ROWS, local_cols)),
+            shape((2 * per_home, 1), i32),
+            shape((2, panel), i32),
+            shape((1, panel), i32),
         ],
-        out_shape=[
-            shape((N_HOMES * PAIR_ROWS, local_cols)),
-            shape((2 * per_home, 1), jnp.int32),
-            shape((2, panel), jnp.int32),
-            shape((1, panel), jnp.int32),
-        ],
-        compiler_params=params,
-        name="deal",
-    )(position, pivots, down_pivots, rows)
-
+        [position],
+        pivots,
+        rows,
+    )
     dealt = lax.all_to_all(picks, "prow", 0, 0, tiled=True)
 
-    matrix_later, keep_later = lax.optimization_barrier((matrix, keep))
-    own = [matrix_later[k, :, 0, :] for k in range(3)]
-    got = [lax.ppermute(own[k], "pcol", move_x([(0, k + 1)])) for k in (0, 2, 1)]
-    third = jnp.where(x == 1, got[0], jnp.where(x == 3, got[1], got[2]))
-    up = lax.ppermute(third, "pcol", move_x([(1, 2), (2, 3)]))
-    down = lax.ppermute(third, "pcol", move_x([(2, 1), (3, 2)]))
-    across = lax.ppermute(third, "pcol", move_x([(1, 3), (3, 1)]))
-    one = jnp.where(x == 0, own[0], jnp.where(x == 1, third, jnp.where(x == 2, up, across)))
-    two = jnp.where(x == 0, own[1], jnp.where(x == 2, third, jnp.where(x == 1, down, up)))
-    three = jnp.where(x == 0, own[2], jnp.where(x == 3, third, jnp.where(x == 2, down, across)))
-    part = jnp.concatenate([one, two, three])
-    other = lax.ppermute(part, "pcol", SWAP)
-
-    leaving, passing, land, flag_leave, low = pl.pallas_call(
+    own = [rows[k * panel : (k + 1) * panel, :width] for k in range(3)]
+    got = [lax.ppermute(own[k], "pcol", move_x([(0, k + 1)])) for k in range(3)]
+
+    line_shape = shape((LINE_ROWS, local_cols))
+    *leaving, passing, land, flag, low = local_kernel(
         functools.partial(leave_kernel, panel),
-        grid=(1,),
-        in_specs=[
-            smem(),
-            whole((2, panel)),
-            whole((panel, 2)),
-            whole((panel, local_cols)),
-            whole((2, panel)),
-            whole((2, panel, panel)),
-        ],
-        out_specs=[
-            whole((NY * LINE_ROWS, local_cols)),
-            whole((NZ * DEST_ROWS, 1)),
-            whole((2 * DEST_ROWS, 1)),
-            whole((1, panel)),
-            whole((2, panel, panel)),
-        ],
-        out_shape=[
-            shape((NY * LINE_ROWS, local_cols)),
-            shape((NZ * DEST_ROWS, 1), jnp.int32),
-            shape((2 * DEST_ROWS, 1), jnp.int32),
-            shape((1, panel), jnp.int32),
+        "leave",
+        [line_shape] * NY
+        + [
+            shape((NZ * DEST_ROWS, 1), i32),
+            shape((1, 2 * DEST_ROWS), i32),
+            shape((1,), i32),
             shape((2, panel, panel)),
         ],
-        compiler_params=params,
-        name="leave",
-    )(position, pivots, down_pivots, rows, place, lower_inverse)
-    leaving = leaving.reshape(NY, LINE_ROWS, local_cols)
-    arrived = [lax.ppermute(leaving[s], "prow", shift_y(s, [0], [0, 1])) for s in (1, 3, 2)]
-
-    choose = narrow((keep_later == jnp.arange(N_HOMES * PAIR_ROWS)[None, :]).astype(jnp.float32))
-    block = narrow(dot(choose, dealt))
+        [position],
+        pivots,
+        rows,
+        place,
+        lower_inverse,
+        slots,
+    )
+    arrived = [lax.ppermute(leaving[s], "prow", shift_y(s, [0], [0, 1])) for s in (1, 2, 3)]
+
+    dealt = after(dealt, got[0], got[2])
+    (block,) = local_kernel(
+        block_kernel, "block", [shape((2 * per_home, local_cols))], [], keep, dealt
+    )
     from_lo = lax.ppermute(block, "prow", shift_z(1))
     from_hi = lax.ppermute(block, "prow", shift_z(-1))
     opposite = lax.ppermute(block, "prow", shift_z(4))
-    two_lo = lax.ppermute(jnp.concatenate([block, from_lo]), "prow", shift_z(2))
-    two_hi = lax.ppermute(jnp.concatenate([block, from_hi]), "prow", shift_z(-2))
-
-    on_line = jnp.where(
-        y == 0, leaving[0], jnp.where(y == 1, arrived[0], jnp.where(y == 3, arrived[1], arrived[2]))
-    )
-    on_line, from_lo, from_hi = lax.optimization_barrier((on_line, from_lo, from_hi))
-    choose = narrow((passing == jnp.arange(LINE_ROWS)[None, :]).astype(jnp.float32))
-    spread = narrow(dot(choose, on_line)).reshape(NZ, DEST_ROWS, local_cols)
-    landed = [spread[0]] + [
-        lax.ppermute(spread[s], "prow", shift_z(s, [0, 1])) for s in range(1, NZ)
-    ]
-
-    blocks = [block, from_lo, from_hi, opposite, two_lo[: 2 * per_home], two_lo[2 * per_home :]]
-    blocks += [two_hi[: 2 * per_home], two_hi[2 * per_home :]]
-    z_line = jnp.concatenate([b[:per_home] for b in blocks] + [b[per_home:] for b in blocks])
-    y_parts = [z_line] + [lax.ppermute(z_line, "prow", shift_y(s)) for s in (1, -1, 2)]
-
-    landed = jnp.stack(landed)
-    gone = jnp.concatenate(
-        [
-            lax.dynamic_index_in_dim(landed, z, 0, False),
-            lax.dynamic_index_in_dim(landed, (z - 1) % NZ, 0, False),
-        ]
-    )
-
+    quarter_shape = shape((NZ // 2 * DEST_ROWS, local_cols))
+    kept, send = local_kernel(
+        spread_kernel, "spread", [quarter_shape] * 2, [position], passing, leaving[0], *arrived
+    )
+    came = lax.ppermute(send, "prow", shift_z(4, [0, 1]))
+
+    from_lo, from_hi = after((from_lo, from_hi), got[1], came)
+    pair_shape = shape((4 * per_home, local_cols))
+    pair_lo, pair_hi = local_kernel(
+        pair_kernel, "pair", [pair_shape] * 2, [], block, from_lo, from_hi
+    )
+    two_lo = lax.ppermute(pair_lo, "prow", shift_z(2))
+    two_hi = lax.ppermute(pair_hi, "prow", shift_z(-2))
+    eighth_shape = shape((NZ // 4 * DEST_ROWS, local_cols))
+    kept, send = local_kernel(
+        functools.partial(fold_kernel, 4), "fold4", [eighth_shape] * 2, [position], kept, came
+    )
+    came = lax.ppermute(send, "prow", shift_z(2, [0, 1, 4, 5]))
+    third_shape = shape((panel, width))
+    (third,) = local_kernel(third_kernel, "third", [third_shape], [position], *after(got, from_lo))
+    up = lax.ppermute(third, "pcol", move_x([(1, 2), (2, 3)]))
+    down = lax.ppermute(third, "pcol", move_x([(2, 1), (3, 2)]))
+
+    two_lo, two_hi = after((two_lo, two_hi), up, down, came)
     half = panel // NY
-    extra = jnp.where(core == 0, z_line[half:, :width], z_line[:half, :width])
-    extra = jnp.concatenate([extra, gone[:, :width]])
-    sent = [lax.ppermute(extra, "pcol", move_x([(0, k)])) for k in (1, 3, 2)]
-    extra = jnp.where(x == 0, extra, jnp.where(x == 1, sent[0], jnp.where(x == 3, sent[1], sent[2])))
-    cross = extra[:half]
-    cross = jnp.concatenate(
-        [cross] + [lax.ppermute(cross, "prow", shift_y(s)) for s in (1, -1, 2)] + [extra[half:]]
+    z_line, extra = local_kernel(
+        line_kernel,
+        "line",
+        [shape((2 * half, local_cols)), shape((half, width))],
+        [position],
+        block,
+        from_lo,
+        from_hi,
+        opposite,
+        two_lo,
+        two_hi,
+    )
+    y_lo = lax.ppermute(z_line, "prow", shift_y(1))
+    y_hi = lax.ppermute(z_line, "prow", shift_y(-1))
+    across = lax.ppermute(after(third, extra), "pcol", move_x([(1, 3), (3, 1)]))
+    sent = [lax.ppermute(extra, "pcol", move_x([(0, k)])) for k in (1, 2, 3)]
+    one_shape = shape((DEST_ROWS, local_cols))
+    kept, send = local_kernel(
+        functools.partial(fold_kernel, 2), "fold2", [one_shape] * 2, [position], kept, came
+    )
+    came = lax.ppermute(send, "prow", shift_z(1))
+
+    y_lo, y_hi = after((y_lo, y_hi), across, sent, came)
+    far_first = lax.ppermute(y_lo[:half], "prow", shift_y(1))
+    far_second = lax.ppermute(y_hi[half:], "prow", shift_y(-1))
+    (cross,) = local_kernel(
+        extra_kernel, "extra", [shape((half, width))], [position], extra, *sent
+    )
+    crossed = [lax.ppermute(cross, "prow", shift_y(s)) for s in (1, -1, 2)]
+    n_gone = 2 * DEST_ROWS
+    gone, gone_panel = local_kernel(
+        gone_kernel,
+        "gone",
+        [shape((n_gone, local_cols)), shape((n_gone, width))],
+        [position],
+        kept,
+        came,
+    )
+    gone_sent = [lax.ppermute(gone_panel, "pcol", move_x([(0, k)])) for k in (1, 2, 3)]
+    (part,) = local_kernel(
+        part_kernel,
+        "part",
+        [shape((local_rows, width))],
+        [position],
+        rows,
+        third,
+        up,
+        down,
+        across,
+    )
+    other = lax.ppermute(part, "pcol", SWAP)
+
+    crossed = after(crossed, far_first, far_second, other)
+    (cross,) = local_kernel(
+        cross_kernel,
+        "cross",
+        [shape((panel + n_gone, width))],
+        [position],
+        cross,
+        *crossed,
+        gone_panel,
+        *gone_sent,
     )
     cross_other = lax.ppermute(cross, "pcol", SWAP)
+    y_parts = [z_line, y_lo, y_hi, far_first, far_second]
 
     n_block = panel // 2
     steps = local_rows // n_block
@@ -521,7 +701,8 @@
             whole((2 * half, local_cols)),
             whole((2 * half, local_cols)),
             whole((2 * half, local_cols)),
-            whole((2 * half, local_cols)),
+            whole((half, local_cols)),
+            whole((half, local_cols)),
             whole((2, panel, panel)),
             whole((2, panel, panel)),
             whole((2, panel)),
@@ -535,13 +716,12 @@
             pltpu.VMEM((2 * DEST_ROWS, width), jnp.bfloat16),
             pltpu.VMEM((panel, local_cols), jnp.bfloat16),
         ],
-        compiler_params=params,
+        compiler_params=pltpu.CompilerParams(vmem_limit_bytes=40 * MIB),
         name="finish",
-    )(position, rows, part, other, land.reshape(1, -1), gone, cross, cross_other, *y_parts, low, upper_inverse, place)
+    )(position, rows, part, other, land, gone, cross, cross_other, *y_parts, low, upper_inverse, place)
     result = result.reshape(matrix.shape)
-    overflow = (jnp.max(flag_deal) >= PAIR_ROWS) | (jnp.max(flag_leave) > 0)
     return lax.cond(
-        overflow,
+        flag[0] > 0,
         lambda a, *rest: general_steps(*rest),
         lambda a, *rest: a,
         result,

time: 198 us -> 177 us (0.89)
  local copies, waits for them, and re-layouts: 29.1 us -> 15.3 us
  waiting for transfers between devices: 31.2 us -> 17.8 us
  starting transfers between devices: 87.2 us -> 98.3 us
  other arithmetic: 9.19 us -> 0.08 us
  Pallas kernels: 22.4 us -> 29.9 us
    ppermute x22, waiting for transfers between devices: 29.7 us -> 11.5 us  [the longest x3 4.72 us: per_device(): crossed = [lax.ppermute(cross, 'prow', shift_y(s)) for s in (1, -1, 2)]]
    unnamed x49 -> x17, local copies, waits for them, and re-layouts: 18.1 us -> 8.18 us
    pallas_call x2 -> x13, Pallas kernels: 6.55 us -> 15.3 us  [local_kernel(): pl.pallas_call(body, grid=(1,), in_specs=[smem() for _ in scalars] + [who...]
    select_n x5 -> x0, other arithmetic: 5.34 us -> none  [the longest x1 2.18 us: per_device(): jnp.where(x == 0, own[0], jnp.where(x == 1, third, jnp.where(x == 2, up,...]
    ppermute x1, starting transfers between devices: 0.01 us -> 4.83 us  [per_device(): opposite = lax.ppermute(block, 'prow', shift_z(4))]
    ppermute x22, starting transfers between devices: 57.6 us -> 61.3 us  [the longest x3 23.1 us: per_device(): sent = [lax.ppermute(extra, 'pcol', move_x([(0, k)])) for k in (1, 2, 3)]]
    ppermute x1, waiting for transfers between devices: 0.01 us -> 3.5 us  [per_device(): opposite = lax.ppermute(block, 'prow', shift_z(4))]
    ppermute x1, starting transfers between devices: 0.99 us -> 4.14 us  [per_device(): other = lax.ppermute(part, 'pcol', SWAP)]
  transfers between devices with their start and end apart: 33 -> 33, of which waited for: 9 -> 13; matrix products, arithmetic and copies ran while one was open for 10% -> 1% of each run, Pallas kernels for 2% -> 5%
where the time goes in v2:
time: 177 us; the launch traced here: 176 us
  starting transfers between devices  98.3 us (56%)
  Pallas kernels  29.9 us (17%)
  waiting for transfers between devices  17.8 us (10%)
  local copies, waits for them, and re-layouts  15.3 us (9%)
  between operations  14.4 us (8%)
    ppermute x3, starting transfers between devices, per_device(): sent = [lax.ppermute(extra, 'pcol', move_x([(0, k)])) for k in (1, 2, 3)]  23.1 us
    pallas_call x13, Pallas kernels, local_kernel(): pl.pallas_call(body, grid=(1,), in_specs=[smem() for _ in scalars] + [who...  15.3 us
    pallas_call x1, Pallas kernels, per_device(): pl.pallas_call(functools.partial(finish_kernel, panel), grid=(steps + 1,)...  14.5 us
    all_to_all x1, starting transfers between devices, per_device(): dealt = lax.all_to_all(picks, 'prow', 0, 0, tiled=True)  12.2 us
    ppermute x3, starting transfers between devices, per_device(): lax.ppermute(gone_panel, 'pcol', move_x([(0, k)]))  9.71 us
    ppermute x3, starting transfers between devices, per_device(): got = [lax.ppermute(own[k], 'pcol', move_x([(0, k + 1)])) for k in range(3)]  8.75 us
    unnamed x17, local copies, waits for them, and re-layouts  8.18 us
    ppermute x3, starting transfers between devices, per_device(): lax.ppermute(leaving[s], 'prow', shift_y(s, [0], [0, 1]))  6.58 us
  transfers between devices with their start and end apart: 33, of which 13 were waited for; matrix products, arithmetic and copies ran while one was open for 1% of the time, Pallas kernels for 5%

profile of v2, /device:TPU:1, one launch (start us, length us, event | category | flops | bytes accessed | tf_op | source)
XLA Modules:
  0.0 175.8 jit_solution(14512244396644936725)
XLA Ops:
  6.5 2.7 %copy.13 = bf16[192,8,2,512]{3,1,2,0:T(8,128)(2,1)S(1)} copy(bf16[192,8,2,512]{3,2,1,0:T(2,128)(2,1)} %bitcast.75) | data formatting | bytes 6291456
  9.4 2.9 %deal.1 = (bf16[256,1024]{1,0:T(8,128)(2,1)S(1)}, s32[32,1]{1,0:T(8,128)S(1)}, s32[2,512]{1,0:T(2,128)S(1)}, s32[1,512]{1,0:T(1,128)S(1)}) custom-call(s32[2]{0:T(128)S(1)} %pad_add_fusion.pos_ref, s32[2,512]{1,0:T(2,128)S(1)} %copy-done.9, bf16[1536,1024]{1,0:T(8,128)(2,1)S(1)} %bitcast.68), custom_call_target="tpu_custom_call" | custom-call | tf_op jit(solution)/shard_map/deal/pallas_call | solution.py:521
  13.0 12.2 %all-to-all-start = ((bf16[32,8,1024]{2,1,0:T(8,128)(2,1)}), bf16[32,8,1024]{2,1,0:T(8,128)(2,1)}, u32[]{:S(2)}, u32[]{:S(2)}) async-start(bf16[32,8,1024]{2,1,0:T(8,128)(2,1)} %bitcast.73), calls=%async_computation | async-start | bytes 1048576 | tf_op jit(solution)/shard_map/all_to_all | solution.py:560
  25.2 4.0 %leave.1 = (bf16[144,1024]{1,0:T(8,128)(2,1)S(1)}, bf16[144,1024]{1,0:T(8,128)(2,1)S(1)}, bf16[144,1024]{1,0:T(8,128)(2,1)S(1)}, bf16[144,1024]{1,0:T(8,128)(2,1...) custom-call(s32[2]{0:T(128)S(1)} %pad_add_fusion.pos_ref, ...), custom_call_target="tpu_custom_call" | custom-call | tf_op jit(solution)/shard_map/leave/pallas_call | solution.py:521
  29.3 1.0 copy-done
  30.2 3.1 %collective-permute-start.5 = (bf16[144,1024]{1,0:T(8,128)(2,1)S(1)}, bf16[144,1024]{1,0:T(8,128)(2,1)S(1)}, u32[]{:S(2)}, u32[]{:S(2)}) collective-permute-start(bf16[144,1024]{1,0:T(8,128)(2,1)S(1)} %get-tuple-element.448), channel_id=1, source_target_pairs={{0,64},{8,72},{1,65},{9,73},{2,66},{10,74},{3,67},{11,75},{4,68},{... | collective-permute-start | bytes 884744 | tf_op jit(solution)/shard_map/ppermute | solution.py:583
  33.3 1.0 fusion.28
  34.3 3.1 %collective-permute-start = (bf16[512,512]{1,0:T(8,128)(2,1)S(1)}, bf16[512,512]{1,0:T(8,128)(2,1)S(1)}, u32[]{:S(2)}, u32[]{:S(2)}) collective-permute-start(bf16[512,512]{1,0:T(8,128)(2,1)S(1)} %get-tuple-element.532), channel_id=1, source_target_pairs={{0,2},{1,3},{8,10},{9,11},{16,18},{17,19},{24,26},{25,27},{32,34},... | collective-permute-start | bytes 1572872 | tf_op jit(solution)/shard_map/ppermute | solution.py:563
  37.4 2.0 %collective-permute-start.2 = (bf16[512,512]{1,0:T(8,128)(2,1)S(1)}, bf16[512,512]{1,0:T(8,128)(2,1)S(1)}, u32[]{:S(2)}, u32[]{:S(2)}) collective-permute-start(bf16[512,512]{1,0:T(8,128)(2,1)S(1)} %get-tuple-element.530), channel_id=1, source_target_pairs={{0,6},{1,7},{8,14},{9,15},{16,22},{17,23},{24,30},{25,31},{32,38},... | collective-permute-start | bytes 1572872 | tf_op jit(solution)/shard_map/ppermute | solution.py:563
  39.4 2.2 %collective-permute-start.6 = (bf16[144,1024]{1,0:T(8,128)(2,1)S(1)}, bf16[144,1024]{1,0:T(8,128)(2,1)S(1)}, u32[]{:S(2)}, u32[]{:S(2)}) collective-permute-start(bf16[144,1024]{1,0:T(8,128)(2,1)S(1)} %get-tuple-element.449), channel_id=1, source_target_pairs={{0,128},{8,136},{1,129},{9,137},{2,130},{10,138},{3,131},{11,139},... | collective-permute-start | bytes 884744 | tf_op jit(solution)/shard_map/ppermute | solution.py:583
  41.6 1.3 collective-permute-start.7
  42.9 3.7 %collective-permute-start.1 = (bf16[512,512]{1,0:T(8,128)(2,1)}, bf16[512,512]{1,0:T(8,128)(2,1)}, u32[]{:S(2)}, u32[]{:S(2)}) collective-permute-start(bf16[512,512]{1,0:T(8,128)(2,1)} %get-tuple-element.531), channel_id=1, source_target_pairs={{0,4},{1,5},{8,12},{9,13},{16,20},{17,21},{24,28},{25,29},{32,36},... | collective-permute-start | bytes 1572872 | tf_op jit(solution)/shard_map/ppermute | solution.py:563
  47.6 1.6 spread.1
  49.2 2.0 %collective-permute-start.8 = (bf16[128,1024]{1,0:T(8,128)(2,1)}, bf16[128,1024]{1,0:T(8,128)(2,1)}, u32[]{:S(2)}, u32[]{:S(2)}) collective-permute-start(bf16[128,1024]{1,0:T(8,128)(2,1)} %get-tuple-element.451), channel_id=1, source_target_pairs={{0,32},{8,40},{64,96},{72,104},{128,160},{136,168},{192,224},{200,... | collective-permute-start | bytes 786440 | tf_op jit(solution)/shard_map/ppermute | solution.py:596
  52.8 1.3 block.1.block_ref
  54.0 1.2 collective-permute-start.3
  55.3 1.5 collective-permute-start.4
  56.8 1.6 collective-permute-done.1.two_ref
  59.2 1.0 copy-done.3
  60.2 1.0 copy-done.5
  61.2 1.1 third.1.third_ref
  63.8 1.0 fold4.1
  64.8 3.0 %collective-permute-start.14 = (bf16[64,1024]{1,0:T(8,128)(2,1)S(1)}, bf16[64,1024]{1,0:T(8,128)(2,1)S(1)}, u32[]{:S(2)}, u32[]{:S(2)}) collective-permute-start(bf16[64,1024]{1,0:T(8,128)(2,1)S(1)} %get-tuple-element.460), channel_id=1, source_target_pairs={{0,16},{8,24},{32,48},{40,56},{64,80},{72,88},{96,112},{104,120},{... | collective-permute-start | bytes 393224 | tf_op jit(solution)/shard_map/ppermute | solution.py:609
  67.9 3.6 %collective-permute-start.13 = (bf16[64,1024]{1,0:T(8,128)(2,1)S(1)}, bf16[64,1024]{1,0:T(8,128)(2,1)S(1)}, u32[]{:S(2)}, u32[]{:S(2)}) collective-permute-start(bf16[64,1024]{1,0:T(8,128)(2,1)S(1)} %get-tuple-element.458), channel_id=1, source_target_pairs={{0,48},{8,56},{16,0},{24,8},{32,16},{40,24},{48,32},{56,40},{64,11... | collective-permute-start | bytes 393224 | tf_op jit(solution)/shard_map/ppermute | solution.py:604
  71.5 4.8 %collective-permute-start.11 = (bf16[32,1024]{1,0:T(8,128)(2,1)S(1)}, bf16[32,1024]{1,0:T(8,128)(2,1)S(1)}, u32[]{:S(2)}, u32[]{:S(2)}) collective-permute-start(bf16[32,1024]{1,0:T(8,128)(2,1)S(1)} %block.1.block_ref), channel_id=1, source_target_pairs={{0,32},{8,40},{16,48},{24,56},{32,0},{40,8},{48,16},{56,24},{64,96... | collective-permute-start | bytes 196616 | tf_op jit(solution)/shard_map/ppermute | solution.py:591
  76.3 1.0 collective-permute-done.13.two_hi_ref
  77.3 3.5 %collective-permute-done.11.opposite_ref = bf16[32,1024]{1,0:T(8,128)(2,1)S(1)} collective-permute-done((bf16[32,1024]{1,0:T(8,128)(2,1)S(1)}, bf16[32,1024]{1,0:T(8,128)(2,1)S(1)}, u32[]{:S(2)}, u32[]{:S(2)}) %collective-permute-start.11) | collective-permute-done | bytes 65568 | tf_op jit(solution)/shard_map/ppermute | solution.py:591
  82.8 4.1 %collective-permute-start.16 = (bf16[1536,512]{1,0:T(8,128)(2,1)S(1)}, bf16[1536,512]{1,0:T(8,128)(2,1)S(1)}, u32[]{:S(2)}, u32[]{:S(2)}) collective-permute-start(bf16[1536,512]{1,0:T(8,128)(2,1)S(1)} %part.1.part_ref), channel_id=1, source_target_pairs={{0,1},{1,0},{2,3},{3,2},{4,5},{5,4},{6,7},{7,6},{8,9},{9,8},{10,11... | collective-permute-start | bytes 4718600 | tf_op jit(solution)/shard_map/ppermute | solution.py:667
  87.0 1.0 collective-permute-start.24
  88.0 2.6 %collective-permute-start.25 = (bf16[256,1024]{1,0:T(8,128)(2,1)S(1)}, bf16[256,1024]{1,0:T(8,128)(2,1)S(1)}, u32[]{:S(2)}, u32[]{:S(2)}) collective-permute-start(bf16[256,1024]{1,0:T(8,128)(2,1)S(1)} %get-tuple-element.470.y0_ref), channel_id=1, source_target_pairs={{0,192},{8,200},{16,208},{24,216},{32,224},{40,232},{48,240},{56,2... | collective-permute-start | bytes 1572872 | tf_op jit(solution)/shard_map/ppermute | solution.py:630
  90.6 20.5 %collective-permute-start.18 = (bf16[128,512]{1,0:T(8,128)(2,1)S(1)}, bf16[128,512]{1,0:T(8,128)(2,1)S(1)}, u32[]{:S(2)}, u32[]{:S(2)}) collective-permute-start(bf16[128,512]{1,0:T(8,128)(2,1)S(1)} %get-tuple-element.463.own_ref), channel_id=1, source_target_pairs={{0,2},{1,3},{8,10},{9,11},{16,18},{17,19},{24,26},{25,27},{32,34},... | collective-permute-start | bytes 393224 | tf_op jit(solution)/shard_map/ppermute | solution.py:632
  111.1 1.3 collective-permute-start.19
  112.4 0.9 collective-permute-done.18.one_ref
  113.3 1.3 collective-permute-start.20
  115.2 0.9 collective-permute-done.19.two_ref
  116.1 3.4 %collective-permute-start.17 = (bf16[32,1024]{1,0:T(8,128)(2,1)S(1)}, bf16[32,1024]{1,0:T(8,128)(2,1)S(1)}, u32[]{:S(2)}, u32[]{:S(2)}) collective-permute-start(bf16[32,1024]{1,0:T(8,128)(2,1)S(1)} %get-tuple-element.468), channel_id=1, source_target_pairs={{0,8},{8,16},{16,24},{24,32},{32,40},{40,48},{48,56},{56,0},{64,72... | collective-permute-start | bytes 196616 | tf_op jit(solution)/shard_map/ppermute | solution.py:637
  120.2 1.0 collective-permute-done.17.came_ref
  121.7 2.3 %collective-permute-start.27 = (bf16[128,1024]{1,0:T(8,128)(2,1)S(1)}, bf16[128,1024]{1,0:T(8,128)(2,1)S(1)}, u32[]{:S(2)}, u32[]{:S(2)}) collective-permute-start(bf16[128,1024]{1,0:T(8,128)(2,1)S(1)} %slice.128), channel_id=1, source_target_pairs={{0,192},{8,200},{16,208},{24,216},{32,224},{40,232},{48,240},{56,2... | collective-permute-start | bytes 786440 | tf_op jit(solution)/shard_map/ppermute | solution.py:641
  125.7 4.0 %collective-permute-done.22.c2_ref = bf16[128,512]{1,0:T(8,128)(2,1)S(1)} collective-permute-done((bf16[128,512]{1,0:T(8,128)(2,1)S(1)}, bf16[128,512]{1,0:T(8,128)(2,1)S(1)}, u32[]{:S(2)}, u32[]{:S(2)}) %collective-permute-start.22) | collective-permute-done | bytes 131104 | tf_op jit(solution)/shard_map/ppermute | solution.py:645
  129.8 3.5 %collective-permute-start.28 = (bf16[64,512]{1,0:T(8,128)(2,1)S(1)}, bf16[64,512]{1,0:T(8,128)(2,1)S(1)}, u32[]{:S(2)}, u32[]{:S(2)}) collective-permute-start(bf16[64,512]{1,0:T(8,128)(2,1)S(1)} %get-tuple-element.476.own_ref), channel_id=1, source_target_pairs={{0,2},{1,3},{8,10},{9,11},{16,18},{17,19},{24,26},{25,27},{32,34},... | collective-permute-start | bytes 196616 | tf_op jit(solution)/shard_map/ppermute | solution.py:655
  133.3 4.9 %collective-permute-start.29 = (bf16[64,512]{1,0:T(8,128)(2,1)S(1)}, bf16[64,512]{1,0:T(8,128)(2,1)S(1)}, u32[]{:S(2)}, u32[]{:S(2)}) collective-permute-start(bf16[64,512]{1,0:T(8,128)(2,1)S(1)} %get-tuple-element.476.own_ref), channel_id=1, source_target_pairs={{0,4},{1,5},{8,12},{9,13},{16,20},{17,21},{24,28},{25,29},{32,36},... | collective-permute-start | bytes 196616 | tf_op jit(solution)/shard_map/ppermute | solution.py:655
  138.2 1.3 collective-permute-start.30
  139.6 1.3 collective-permute-done.30.three_ref
  141.5 5.2 %collective-permute-start.31 = (bf16[576,512]{1,0:T(8,128)(2,1)S(1)}, bf16[576,512]{1,0:T(8,128)(2,1)S(1)}, u32[]{:S(2)}, u32[]{:S(2)}) collective-permute-start(bf16[576,512]{1,0:T(8,128)(2,1)S(1)} %cross.1.cross_ref), channel_id=1, source_target_pairs={{0,1},{1,0},{2,3},{3,2},{4,5},{5,4},{6,7},{7,6},{8,9},{9,8},{10,11... | collective-permute-start | bytes 1769480 | tf_op jit(solution)/shard_map/ppermute | solution.py:680
  147.3 1.0 collective-permute-done.31.cross_other_ref
  148.3 14.5 %finish.1 = bf16[1536,1024]{1,0:T(8,128)(2,1)} custom-call(s32[2]{0:T(128)S(1)} %pad_add_fusion.pos_ref, bf16[1536,1024]{1,0:T(8,128)(2,1)S(1)} %bitcast.72, bf16[1536,512]{1,0:T(8,128)(2,1)S(1)} %part.1.part_ref, bf16[1536,512]{1,0:T(8,128)(2,1)S(1)} %collective-permute-done.16.other_ref, s32[1,64]{1,0:T(1,128)S(1)} %get-tuple-element.465.land_ref, ...), custom_call_target="tpu_custom_call" | custom-call | tf_op jit(solution)/shard_map/finish/pallas_call | solution.py:689
  162.8 6.1 %conditional.2 = (bf16[3,512,2,512]{3,2,1,0:T(2,128)(2,1)}) conditional(s32[]{:T(128)} %bitcast.4, bf16[1536,1024]{1,0:T(8,128)(2,1)} %finish.1, (bf16[3,512,2,512]{3,2,1,0:T(2,128)(2,1)}, s32[2,512]{1,0:T(2,128)S(1)}, bf16[2,512,512]{2,1,0:T(8,128)(2,1)}, bf16[2,512,512]{2,1,0:T(8,128)(2,1)}) %tuple.121), branch_computations={%region_0.0_spmd, %region_1.11_spmd} | conditional | flops 2966474752 | bytes 85029544 | solution.py:723
  162.8 6.1 %reshape.435 = bf16[3,512,2,512]{3,2,1,0:T(2,128)(2,1)} reshape(bf16[1536,1024]{1,0:T(8,128)(2,1)} %param.4) | data formatting | bytes 6291456 | tf_op jit(solution)/shard_map/reshape | solution.py:722
  (55 shorter events, 11.9 us)
Async XLA Ops:
  6.5 2.8 %copy-start.9 = (s32[2,512]{1,0:T(2,128)S(1)}, s32[2,512]{1,0:T(2,128)}, u32[]{:S(2)}) copy-start(s32[2,512]{1,0:T(2,128)} %across_ref.3) | copy-start | bytes 12292
  12.2 0.8 copy-start.6
  13.0 39.7 %all-to-all-start = ((bf16[32,8,1024]{2,1,0:T(8,128)(2,1)}), bf16[32,8,1024]{2,1,0:T(8,128)(2,1)}, u32[]{:S(2)}, u32[]{:S(2)}) async-start(bf16[32,8,1024]{2,1,0:T(8,128)(2,1)} %bitcast.73), calls=%async_computation | async-start | bytes 1048576 | tf_op jit(solution)/shard_map/all_to_all | solution.py:560
  29.2 1.0 copy-start
  30.2 12.7 %collective-permute-start.5 = (bf16[144,1024]{1,0:T(8,128)(2,1)S(1)}, bf16[144,1024]{1,0:T(8,128)(2,1)S(1)}, u32[]{:S(2)}, u32[]{:S(2)}) collective-permute-start(bf16[144,1024]{1,0:T(8,128)(2,1)S(1)} %get-tuple-element.448), channel_id=1, source_target_pairs={{0,64},{8,72},{1,65},{9,73},{2,66},{10,74},{3,67},{11,75},{4,68},{... | collective-permute-start | bytes 884744 | tf_op jit(solution)/shard_map/ppermute | solution.py:583
  34.3 16.9 %collective-permute-start = (bf16[512,512]{1,0:T(8,128)(2,1)S(1)}, bf16[512,512]{1,0:T(8,128)(2,1)S(1)}, u32[]{:S(2)}, u32[]{:S(2)}) collective-permute-start(bf16[512,512]{1,0:T(8,128)(2,1)S(1)} %get-tuple-element.532), channel_id=1, source_target_pairs={{0,2},{1,3},{8,10},{9,11},{16,18},{17,19},{24,26},{25,27},{32,34},... | collective-permute-start | bytes 1572872 | tf_op jit(solution)/shard_map/ppermute | solution.py:563
  37.4 14.6 %collective-permute-start.2 = (bf16[512,512]{1,0:T(8,128)(2,1)S(1)}, bf16[512,512]{1,0:T(8,128)(2,1)S(1)}, u32[]{:S(2)}, u32[]{:S(2)}) collective-permute-start(bf16[512,512]{1,0:T(8,128)(2,1)S(1)} %get-tuple-element.530), channel_id=1, source_target_pairs={{0,6},{1,7},{8,14},{9,15},{16,22},{17,23},{24,30},{25,31},{32,38},... | collective-permute-start | bytes 1572872 | tf_op jit(solution)/shard_map/ppermute | solution.py:563
  39.4 7.4 %collective-permute-start.6 = (bf16[144,1024]{1,0:T(8,128)(2,1)S(1)}, bf16[144,1024]{1,0:T(8,128)(2,1)S(1)}, u32[]{:S(2)}, u32[]{:S(2)}) collective-permute-start(bf16[144,1024]{1,0:T(8,128)(2,1)S(1)} %get-tuple-element.449), channel_id=1, source_target_pairs={{0,128},{8,136},{1,129},{9,137},{2,130},{10,138},{3,131},{11,139},... | collective-permute-start | bytes 884744 | tf_op jit(solution)/shard_map/ppermute | solution.py:583
  41.6 6.1 %collective-permute-start.7 = (bf16[144,1024]{1,0:T(8,128)(2,1)S(1)}, bf16[144,1024]{1,0:T(8,128)(2,1)S(1)}, u32[]{:S(2)}, u32[]{:S(2)}) collective-permute-start(bf16[144,1024]{1,0:T(8,128)(2,1)S(1)} %get-tuple-element.450), channel_id=1, source_target_pairs={{0,192},{8,200},{1,193},{9,201},{2,194},{10,202},{3,195},{11,203},... | collective-permute-start | bytes 884744 | tf_op jit(solution)/shard_map/ppermute | solution.py:583
  42.9 15.5 %collective-permute-start.1 = (bf16[512,512]{1,0:T(8,128)(2,1)}, bf16[512,512]{1,0:T(8,128)(2,1)}, u32[]{:S(2)}, u32[]{:S(2)}) collective-permute-start(bf16[512,512]{1,0:T(8,128)(2,1)} %get-tuple-element.531), channel_id=1, source_target_pairs={{0,4},{1,5},{8,12},{9,13},{16,20},{17,21},{24,28},{25,29},{32,36},... | collective-permute-start | bytes 1572872 | tf_op jit(solution)/shard_map/ppermute | solution.py:563
  49.2 9.2 %collective-permute-start.8 = (bf16[128,1024]{1,0:T(8,128)(2,1)}, bf16[128,1024]{1,0:T(8,128)(2,1)}, u32[]{:S(2)}, u32[]{:S(2)}) collective-permute-start(bf16[128,1024]{1,0:T(8,128)(2,1)} %get-tuple-element.451), channel_id=1, source_target_pairs={{0,32},{8,40},{64,96},{72,104},{128,160},{136,168},{192,224},{200,... | collective-permute-start | bytes 786440 | tf_op jit(solution)/shard_map/ppermute | solution.py:596
  51.2 0.8 copy-start.2
  52.0 0.8 copy-start.4
  54.0 4.4 %collective-permute-start.3 = (bf16[32,1024]{1,0:T(8,128)(2,1)S(1)}, bf16[32,1024]{1,0:T(8,128)(2,1)S(1)}, u32[]{:S(2)}, u32[]{:S(2)}) collective-permute-start(bf16[32,1024]{1,0:T(8,128)(2,1)S(1)} %block.1.block_ref), channel_id=1, source_target_pairs={{0,8},{8,16},{16,24},{24,32},{32,40},{40,48},{48,56},{56,0},{64,72... | collective-permute-start | bytes 196616 | tf_op jit(solution)/shard_map/ppermute | solution.py:589
  55.3 3.9 %collective-permute-start.4 = (bf16[32,1024]{1,0:T(8,128)(2,1)S(1)}, bf16[32,1024]{1,0:T(8,128)(2,1)S(1)}, u32[]{:S(2)}, u32[]{:S(2)}) collective-permute-start(bf16[32,1024]{1,0:T(8,128)(2,1)S(1)} %block.1.block_ref), channel_id=1, source_target_pairs={{0,56},{8,0},{16,8},{24,16},{32,24},{40,32},{48,40},{56,48},{64,12... | collective-permute-start | bytes 196616 | tf_op jit(solution)/shard_map/ppermute | solution.py:590
  59.2 1.0 copy-start.3
  60.2 1.0 copy-start.5
  62.3 15.0 %collective-permute-start.9 = (bf16[512,512]{1,0:T(8,128)(2,1)S(1)}, bf16[512,512]{1,0:T(8,128)(2,1)S(1)}, u32[]{:S(2)}, u32[]{:S(2)}) collective-permute-start(bf16[512,512]{1,0:T(8,128)(2,1)S(1)} %third.1.third_ref), channel_id=1, source_target_pairs={{2,4},{3,5},{4,6},{5,7},{10,12},{11,13},{12,14},{13,15},{18,20},{1... | collective-permute-start | bytes 1572872 | tf_op jit(solution)/shard_map/ppermute | solution.py:612
  63.1 14.3 %collective-permute-start.10 = (bf16[512,512]{1,0:T(8,128)(2,1)S(1)}, bf16[512,512]{1,0:T(8,128)(2,1)S(1)}, u32[]{:S(2)}, u32[]{:S(2)}) collective-permute-start(bf16[512,512]{1,0:T(8,128)(2,1)S(1)} %third.1.third_ref), channel_id=1, source_target_pairs={{4,2},{5,3},{6,4},{7,5},{12,10},{13,11},{14,12},{15,13},{20,18},{2... | collective-permute-start | bytes 1572872 | tf_op jit(solution)/shard_map/ppermute | solution.py:613
  64.8 6.7 %collective-permute-start.14 = (bf16[64,1024]{1,0:T(8,128)(2,1)S(1)}, bf16[64,1024]{1,0:T(8,128)(2,1)S(1)}, u32[]{:S(2)}, u32[]{:S(2)}) collective-permute-start(bf16[64,1024]{1,0:T(8,128)(2,1)S(1)} %get-tuple-element.460), channel_id=1, source_target_pairs={{0,16},{8,24},{32,48},{40,56},{64,80},{72,88},{96,112},{104,120},{... | collective-permute-start | bytes 393224 | tf_op jit(solution)/shard_map/ppermute | solution.py:609
  67.8 8.5 %collective-permute-start.12 = (bf16[64,1024]{1,0:T(8,128)(2,1)S(1)}, bf16[64,1024]{1,0:T(8,128)(2,1)S(1)}, u32[]{:S(2)}, u32[]{:S(2)}) collective-permute-start(bf16[64,1024]{1,0:T(8,128)(2,1)S(1)} %get-tuple-element.457), channel_id=1, source_target_pairs={{0,16},{8,24},{16,32},{24,40},{32,48},{40,56},{48,0},{56,8},{64,80... | collective-permute-start | bytes 393224 | tf_op jit(solution)/shard_map/ppermute | solution.py:603
  67.9 9.4 %collective-permute-start.13 = (bf16[64,1024]{1,0:T(8,128)(2,1)S(1)}, bf16[64,1024]{1,0:T(8,128)(2,1)S(1)}, u32[]{:S(2)}, u32[]{:S(2)}) collective-permute-start(bf16[64,1024]{1,0:T(8,128)(2,1)S(1)} %get-tuple-element.458), channel_id=1, source_target_pairs={{0,48},{8,56},{16,0},{24,8},{32,16},{40,24},{48,32},{56,40},{64,11... | collective-permute-start | bytes 393224 | tf_op jit(solution)/shard_map/ppermute | solution.py:604
  71.5 9.4 %collective-permute-start.11 = (bf16[32,1024]{1,0:T(8,128)(2,1)S(1)}, bf16[32,1024]{1,0:T(8,128)(2,1)S(1)}, u32[]{:S(2)}, u32[]{:S(2)}) collective-permute-start(bf16[32,1024]{1,0:T(8,128)(2,1)S(1)} %block.1.block_ref), channel_id=1, source_target_pairs={{0,32},{8,40},{16,48},{24,56},{32,0},{40,8},{48,16},{56,24},{64,96... | collective-permute-start | bytes 196616 | tf_op jit(solution)/shard_map/ppermute | solution.py:591
  81.4 0.7 collective-permute-start.15
  82.8 65.4 %copy-start.1 = (bf16[2,512,512]{2,1,0:T(8,128)(2,1)S(1)}, bf16[2,512,512]{2,1,0:T(8,128)(2,1)}, u32[]{:S(2)}) copy-start(bf16[2,512,512]{2,1,0:T(8,128)(2,1)} %copy-done) | copy-start | bytes 3145732
  82.8 56.7 %collective-permute-start.16 = (bf16[1536,512]{1,0:T(8,128)(2,1)S(1)}, bf16[1536,512]{1,0:T(8,128)(2,1)S(1)}, u32[]{:S(2)}, u32[]{:S(2)}) collective-permute-start(bf16[1536,512]{1,0:T(8,128)(2,1)S(1)} %part.1.part_ref), channel_id=1, source_target_pairs={{0,1},{1,0},{2,3},{3,2},{4,5},{5,4},{6,7},{7,6},{8,9},{9,8},{10,11... | collective-permute-start | bytes 4718600 | tf_op jit(solution)/shard_map/ppermute | solution.py:667
  87.0 34.1 %collective-permute-start.24 = (bf16[256,1024]{1,0:T(8,128)(2,1)S(1)}, bf16[256,1024]{1,0:T(8,128)(2,1)S(1)}, u32[]{:S(2)}, u32[]{:S(2)}) collective-permute-start(bf16[256,1024]{1,0:T(8,128)(2,1)S(1)} %get-tuple-element.470.y0_ref), channel_id=1, source_target_pairs={{0,64},{8,72},{16,80},{24,88},{32,96},{40,104},{48,112},{56,120},{... | collective-permute-start | bytes 1572872 | tf_op jit(solution)/shard_map/ppermute | solution.py:629
  88.0 33.1 %collective-permute-start.25 = (bf16[256,1024]{1,0:T(8,128)(2,1)S(1)}, bf16[256,1024]{1,0:T(8,128)(2,1)S(1)}, u32[]{:S(2)}, u32[]{:S(2)}) collective-permute-start(bf16[256,1024]{1,0:T(8,128)(2,1)S(1)} %get-tuple-element.470.y0_ref), channel_id=1, source_target_pairs={{0,192},{8,200},{16,208},{24,216},{32,224},{40,232},{48,240},{56,2... | collective-permute-start | bytes 1572872 | tf_op jit(solution)/shard_map/ppermute | solution.py:630
  90.6 22.7 %collective-permute-start.18 = (bf16[128,512]{1,0:T(8,128)(2,1)S(1)}, bf16[128,512]{1,0:T(8,128)(2,1)S(1)}, u32[]{:S(2)}, u32[]{:S(2)}) collective-permute-start(bf16[128,512]{1,0:T(8,128)(2,1)S(1)} %get-tuple-element.463.own_ref), channel_id=1, source_target_pairs={{0,2},{1,3},{8,10},{9,11},{16,18},{17,19},{24,26},{25,27},{32,34},... | collective-permute-start | bytes 393224 | tf_op jit(solution)/shard_map/ppermute | solution.py:632
  111.1 5.0 %collective-permute-start.19 = (bf16[128,512]{1,0:T(8,128)(2,1)S(1)}, bf16[128,512]{1,0:T(8,128)(2,1)S(1)}, u32[]{:S(2)}, u32[]{:S(2)}) collective-permute-start(bf16[128,512]{1,0:T(8,128)(2,1)S(1)} %get-tuple-element.463.own_ref), channel_id=1, source_target_pairs={{0,4},{1,5},{8,12},{9,13},{16,20},{17,21},{24,28},{25,29},{32,36},... | collective-permute-start | bytes 393224 | tf_op jit(solution)/shard_map/ppermute | solution.py:632
  113.3 6.2 %collective-permute-start.20 = (bf16[128,512]{1,0:T(8,128)(2,1)S(1)}, bf16[128,512]{1,0:T(8,128)(2,1)S(1)}, u32[]{:S(2)}, u32[]{:S(2)}) collective-permute-start(bf16[128,512]{1,0:T(8,128)(2,1)S(1)} %get-tuple-element.463.own_ref), channel_id=1, source_target_pairs={{0,6},{1,7},{8,14},{9,15},{16,22},{17,23},{24,30},{25,31},{32,38},... | collective-permute-start | bytes 393224 | tf_op jit(solution)/shard_map/ppermute | solution.py:632
  116.1 5.0 %collective-permute-start.17 = (bf16[32,1024]{1,0:T(8,128)(2,1)S(1)}, bf16[32,1024]{1,0:T(8,128)(2,1)S(1)}, u32[]{:S(2)}, u32[]{:S(2)}) collective-permute-start(bf16[32,1024]{1,0:T(8,128)(2,1)S(1)} %get-tuple-element.468), channel_id=1, source_target_pairs={{0,8},{8,16},{16,24},{24,32},{32,40},{40,48},{48,56},{56,0},{64,72... | collective-permute-start | bytes 196616 | tf_op jit(solution)/shard_map/ppermute | solution.py:637
  120.1 5.1 %collective-permute-start.21 = (bf16[128,512]{1,0:T(8,128)(2,1)S(1)}, bf16[128,512]{1,0:T(8,128)(2,1)S(1)}, u32[]{:S(2)}, u32[]{:S(2)}) collective-permute-start(bf16[128,512]{1,0:T(8,128)(2,1)S(1)} %extra.1.c0_ref), channel_id=1, source_target_pairs={{0,64},{8,72},{16,80},{24,88},{32,96},{40,104},{48,112},{56,120},{... | collective-permute-start | bytes 393224 | tf_op jit(solution)/shard_map/ppermute | solution.py:645
  121.2 17.1 %collective-permute-start.26 = (bf16[128,1024]{1,0:T(8,128)(2,1)S(1)}, bf16[128,1024]{1,0:T(8,128)(2,1)S(1)}, u32[]{:S(2)}, u32[]{:S(2)}) collective-permute-start(bf16[128,1024]{1,0:T(8,128)(2,1)S(1)} %slice.127), channel_id=1, source_target_pairs={{0,64},{8,72},{16,80},{24,88},{32,96},{40,104},{48,112},{56,120},{... | collective-permute-start | bytes 786440 | tf_op jit(solution)/shard_map/ppermute | solution.py:640
  121.7 17.9 %collective-permute-start.27 = (bf16[128,1024]{1,0:T(8,128)(2,1)S(1)}, bf16[128,1024]{1,0:T(8,128)(2,1)S(1)}, u32[]{:S(2)}, u32[]{:S(2)}) collective-permute-start(bf16[128,1024]{1,0:T(8,128)(2,1)S(1)} %slice.128), channel_id=1, source_target_pairs={{0,192},{8,200},{16,208},{24,216},{32,224},{40,232},{48,240},{56,2... | collective-permute-start | bytes 786440 | tf_op jit(solution)/shard_map/ppermute | solution.py:641
  124.0 5.8 %collective-permute-start.22 = (bf16[128,512]{1,0:T(8,128)(2,1)S(1)}, bf16[128,512]{1,0:T(8,128)(2,1)S(1)}, u32[]{:S(2)}, u32[]{:S(2)}) collective-permute-start(bf16[128,512]{1,0:T(8,128)(2,1)S(1)} %extra.1.c0_ref), channel_id=1, source_target_pairs={{0,192},{8,200},{16,208},{24,216},{32,224},{40,232},{48,240},{56,2... | collective-permute-start | bytes 393224 | tf_op jit(solution)/shard_map/ppermute | solution.py:645
  125.2 8.1 %collective-permute-start.23 = (bf16[128,512]{1,0:T(8,128)(2,1)S(1)}, bf16[128,512]{1,0:T(8,128)(2,1)S(1)}, u32[]{:S(2)}, u32[]{:S(2)}) collective-permute-start(bf16[128,512]{1,0:T(8,128)(2,1)S(1)} %extra.1.c0_ref), channel_id=1, source_target_pairs={{0,128},{8,136},{16,144},{24,152},{32,160},{40,168},{48,176},{56,1... | collective-permute-start | bytes 393224 | tf_op jit(solution)/shard_map/ppermute | solution.py:645
  129.8 9.8 %collective-permute-start.28 = (bf16[64,512]{1,0:T(8,128)(2,1)S(1)}, bf16[64,512]{1,0:T(8,128)(2,1)S(1)}, u32[]{:S(2)}, u32[]{:S(2)}) collective-permute-start(bf16[64,512]{1,0:T(8,128)(2,1)S(1)} %get-tuple-element.476.own_ref), channel_id=1, source_target_pairs={{0,2},{1,3},{8,10},{9,11},{16,18},{17,19},{24,26},{25,27},{32,34},... | collective-permute-start | bytes 196616 | tf_op jit(solution)/shard_map/ppermute | solution.py:655
  133.3 6.3 %collective-permute-start.29 = (bf16[64,512]{1,0:T(8,128)(2,1)S(1)}, bf16[64,512]{1,0:T(8,128)(2,1)S(1)}, u32[]{:S(2)}, u32[]{:S(2)}) collective-permute-start(bf16[64,512]{1,0:T(8,128)(2,1)S(1)} %get-tuple-element.476.own_ref), channel_id=1, source_target_pairs={{0,4},{1,5},{8,12},{9,13},{16,20},{17,21},{24,28},{25,29},{32,36},... | collective-permute-start | bytes 196616 | tf_op jit(solution)/shard_map/ppermute | solution.py:655
  138.2 2.6 %collective-permute-start.30 = (bf16[64,512]{1,0:T(8,128)(2,1)S(1)}, bf16[64,512]{1,0:T(8,128)(2,1)S(1)}, u32[]{:S(2)}, u32[]{:S(2)}) collective-permute-start(bf16[64,512]{1,0:T(8,128)(2,1)S(1)} %get-tuple-element.476.own_ref), channel_id=1, source_target_pairs={{0,6},{1,7},{8,14},{9,15},{16,22},{17,23},{24,30},{25,31},{32,38},... | collective-permute-start | bytes 196616 | tf_op jit(solution)/shard_map/ppermute | solution.py:655
  141.5 6.8 %collective-permute-start.31 = (bf16[576,512]{1,0:T(8,128)(2,1)S(1)}, bf16[576,512]{1,0:T(8,128)(2,1)S(1)}, u32[]{:S(2)}, u32[]{:S(2)}) collective-permute-start(bf16[576,512]{1,0:T(8,128)(2,1)S(1)} %cross.1.cross_ref), channel_id=1, source_target_pairs={{0,1},{1,0},{2,3},{3,2},{4,5},{5,4},{6,7},{7,6},{8,9},{9,8},{10,11... | collective-permute-start | bytes 1769480 | tf_op jit(solution)/shard_map/ppermute | solution.py:680

commit v3 on v2

--- a/solution.py
+++ b/solution.py
@@ -15,6 +15,7 @@
 Z_ORDER = (0, 7, 1, 4, 6, 5, 2, 3)
 Y_ORDER = (0, 3, 1, 2)
 MIB = 1 << 20
+GROUP = 16
 
 
 def shift_y(step, rows=range(NY), cols=range(NZ)):
@@ -320,39 +321,48 @@
     return jnp.where(x <= 1, jnp.where(x == 0, at_0, at_1), jnp.where(x == 2, at_2, at_3))
 
 
-def third_kernel(pos_ref, one_ref, two_ref, three_ref, third_ref):
+def turn_kernel(pos_ref, *refs):
+    own, got, outs, sems = refs[:4], refs[4:8], refs[8:12], refs[12]
     x = pos_ref[1] >> 1
 
-    @pl.when(x <= 1)
+    def pass_on(sources, first):
+        copies = [
+            pltpu.make_async_copy(source, outs[first + k], sems.at[first + k])
+            for k, source in enumerate(sources)
+        ]
+        for copy in copies:
+            copy.start()
+        for copy in copies:
+            copy.wait()
+
+    @pl.when(x == 0)
     def _():
-        third_ref[...] = one_ref[...]
-
-    @pl.when(x == 2)
+        pass_on((*own[2:], *own[:2]), 0)
+
+    @pl.when(x == 1)
     def _():
-        third_ref[...] = two_ref[...]
+        pass_on(got[:2], 0)
 
     @pl.when(x == 3)
     def _():
-        third_ref[...] = three_ref[...]
-
-
-def part_kernel(pos_ref, own_ref, third_ref, up_ref, down_ref, across_ref, part_ref):
+        pass_on(got[2:], 2)
+
+
+def part_kernel(pos_ref, own_ref, *refs):
+    got, up, down, part_ref = refs[:4], refs[4:6], refs[6:8], refs[8]
     x = pos_ref[1] >> 1
-    n = third_ref.shape[0]
-    width = third_ref.shape[1]
-    own = [own_ref.at[pl.ds(k * n, n), pl.ds(0, width)] for k in range(3)]
-    by_place = (
-        own,
-        (third_ref, down_ref, across_ref),
-        (up_ref, third_ref, down_ref),
-        (across_ref, up_ref, third_ref),
-    )
-    for place, refs in enumerate(by_place):
+    n = got[0].shape[0]
+
+    @pl.when(x == 0)
+    def _():
+        part_ref[...] = own_ref[:, : part_ref.shape[1]]
+
+    for place, sources in ((1, (*got[:2], *up)), (2, (*up, *down)), (3, (*down, *got[2:]))):
 
         @pl.when(x == place)
-        def _(refs=refs):
-            for k, ref in enumerate(refs):
-                part_ref[k * n : (k + 1) * n, :] = ref[...]
+        def _(sources=sources):
+            for k, source in enumerate(sources):
+                part_ref[k * n : (k + 1) * n, :] = source[...]
 
 
 def spread_kernel(pos_ref, passing_ref, own_ref, one_ref, two_ref, three_ref, keep_ref, send_ref):
@@ -399,6 +409,19 @@
         cross_ref[k * n : (k + 1) * n, :] = ref[...]
     x = pos_ref[1] >> 1
     cross_ref[NY * n :, :] = by_x(x, own_ref[...], one_ref[...], two_ref[...], three_ref[...])
+
+
+def first_kernel(
+    low_ref, y0_ref, y1_ref, y2_ref, far_first_ref, far_second_ref, row_ref, second_ref, a00_ref
+):
+    quarter = far_first_ref.shape[0]
+    y_refs = (y0_ref, y1_ref, y2_ref)
+    pivot_first = jnp.concatenate([r[:quarter, :] for r in y_refs] + [far_first_ref[...]])
+    row_ref[...] = narrow(dot(low_ref[0], pivot_first))
+    a00_ref[...] = pivot_first[:, : a00_ref.shape[1]]
+    for k, ref in enumerate(y_refs):
+        second_ref[k * quarter : (k + 1) * quarter, :] = ref[quarter:, :]
+    second_ref[3 * quarter :, :] = far_second_ref[...]
 
 
 def finish_kernel(
@@ -411,11 +434,9 @@
     gone_ref,
     cross_ref,
     cross_other_ref,
-    y0_ref,
-    y1_ref,
-    y2_ref,
-    far_first_ref,
-    far_second_ref,
+    row_first_ref,
+    second_ref,
+    a00_ref,
     low_ref,
     upper_ref,
     place_ref,
@@ -439,11 +460,8 @@
         from_second = jnp.where(even, others, mine)
         gone_first_ref[...] = from_first[panel:]
         gone_second_ref[...] = from_second[panel:]
-        quarter = panel // NY
-        y_refs = (y0_ref, y1_ref, y2_ref)
-        pivot_first = jnp.concatenate([r[:quarter, :] for r in y_refs] + [far_first_ref[...]])
-        pivot_second = jnp.concatenate([r[quarter:, :] for r in y_refs] + [far_second_ref[...]])
-        row_first = narrow(dot(low_ref[0], pivot_first))
+        row_first = row_first_ref[...]
+        pivot_second = second_ref[...]
         corner_ref[...] = narrow(dot(low_ref[0], from_second[:panel]))
         lower_factor = narrow(dot(from_first[:panel], upper_ref[0]))
         reduced = narrow(pivot_second.astype(jnp.float32) - dot(lower_factor, row_first))
@@ -459,7 +477,7 @@
         def _():
             raw = jnp.where(
                 here == 0,
-                pivot_first[:, :width],
+                a00_ref[...],
                 jnp.where(column == 0, lower_factor, reduced[:, :width]),
             )
             place = jnp.where(here == 0, place_ref[0:1, :], place_ref[1:2, :])
@@ -494,15 +512,22 @@
             - dot(factor_first, new_ref[:panel, :])
             - dot(factor_second, new_ref[panel:, :])
         )
-        out_ref[...] = updated
+
+        def put(half, value):
+            out_ref[:, half] = value.reshape(n // GROUP, GROUP, width)
+
+        put(0, updated[:, :width])
+        put(1, updated[:, width:])
 
         @pl.when(column <= 1)
         def _():
-            out_ref[:, :width] = jnp.where(column == 0, factor_first, factor_second)
+            put(0, jnp.where(column == 0, factor_first, factor_second))
 
         @pl.when((here <= 1) & (begin < panel))
         def _():
-            out_ref[...] = top_ref[pl.ds(pl.multiple_of(begin, n), n), :]
+            top = top_ref[pl.ds(pl.multiple_of(begin, n), n), :]
+            put(0, top[:, :width])
+            put(1, top[:, width:])
 
 
 def whole(shape):
@@ -559,8 +584,11 @@
     )
     dealt = lax.all_to_all(picks, "prow", 0, 0, tiled=True)
 
-    own = [rows[k * panel : (k + 1) * panel, :width] for k in range(3)]
-    got = [lax.ppermute(own[k], "pcol", move_x([(0, k + 1)])) for k in range(3)]
+    piece = local_rows // 4
+    pieces = [rows[k * piece : (k + 1) * piece, :width] for k in range(4)]
+    got = [
+        lax.ppermute(pieces[k], "pcol", move_x([(0, 1) if k < 2 else (0, 3)])) for k in (0, 2)
+    ]
 
     line_shape = shape((LINE_ROWS, local_cols))
     *leaving, passing, land, flag, low = local_kernel(
@@ -582,7 +610,7 @@
     )
     arrived = [lax.ppermute(leaving[s], "prow", shift_y(s, [0], [0, 1])) for s in (1, 2, 3)]
 
-    dealt = after(dealt, got[0], got[2])
+    dealt = after(dealt, got, passing)
     (block,) = local_kernel(
         block_kernel, "block", [shape((2 * per_home, local_cols))], [], keep, dealt
     )
@@ -595,22 +623,33 @@
     )
     came = lax.ppermute(send, "prow", shift_z(4, [0, 1]))
 
-    from_lo, from_hi = after((from_lo, from_hi), got[1], came)
+    late_pieces = after((pieces[1], pieces[3]), block)
+    got += [
+        lax.ppermute(late_pieces[0], "pcol", move_x([(0, 1)])),
+        lax.ppermute(late_pieces[1], "pcol", move_x([(0, 3)])),
+    ]
+
+    from_lo, from_hi = after((from_lo, from_hi), got, kept)
     pair_shape = shape((4 * per_home, local_cols))
     pair_lo, pair_hi = local_kernel(
         pair_kernel, "pair", [pair_shape] * 2, [], block, from_lo, from_hi
     )
     two_lo = lax.ppermute(pair_lo, "prow", shift_z(2))
     two_hi = lax.ppermute(pair_hi, "prow", shift_z(-2))
-    eighth_shape = shape((NZ // 4 * DEST_ROWS, local_cols))
-    kept, send = local_kernel(
-        functools.partial(fold_kernel, 4), "fold4", [eighth_shape] * 2, [position], kept, came
-    )
-    came = lax.ppermute(send, "prow", shift_z(2, [0, 1, 4, 5]))
-    third_shape = shape((panel, width))
-    (third,) = local_kernel(third_kernel, "third", [third_shape], [position], *after(got, from_lo))
-    up = lax.ppermute(third, "pcol", move_x([(1, 2), (2, 3)]))
-    down = lax.ppermute(third, "pcol", move_x([(2, 1), (3, 2)]))
+
+    got = after(got, pair_lo)
+    ups_downs = pl.pallas_call(
+        turn_kernel,
+        in_specs=[smem()] + [pl.BlockSpec(memory_space=pl.ANY)] * 8,
+        out_specs=[pl.BlockSpec(memory_space=pl.ANY)] * 4,
+        out_shape=[shape((piece, width))] * 4,
+        scratch_shapes=[pltpu.SemaphoreType.DMA((4,))],
+        cost_estimate=pl.CostEstimate(flops=0, bytes_accessed=0, transcendentals=0),
+        name="turn",
+    )(position, *pieces, got[0], got[2], got[1], got[3])
+    go_up, go_down = move_x([(0, 1), (1, 2)]), move_x([(0, 3), (3, 2)])
+    up = [lax.ppermute(ups_downs[0], "pcol", go_up)]
+    down = [lax.ppermute(ups_downs[2], "pcol", go_down)]
 
     two_lo, two_hi = after((two_lo, two_hi), up, down, came)
     half = panel // NY
@@ -628,15 +667,27 @@
     )
     y_lo = lax.ppermute(z_line, "prow", shift_y(1))
     y_hi = lax.ppermute(z_line, "prow", shift_y(-1))
-    across = lax.ppermute(after(third, extra), "pcol", move_x([(1, 3), (3, 1)]))
     sent = [lax.ppermute(extra, "pcol", move_x([(0, k)])) for k in (1, 2, 3)]
+    late_up, late_down = after((ups_downs[1], ups_downs[3]), extra)
+    up.append(lax.ppermute(late_up, "pcol", go_up))
+    down.append(lax.ppermute(late_down, "pcol", go_down))
+    eighth_shape = shape((NZ // 4 * DEST_ROWS, local_cols))
+    kept, send = local_kernel(
+        functools.partial(fold_kernel, 4),
+        "fold4",
+        [eighth_shape] * 2,
+        [position],
+        kept,
+        after(came, extra),
+    )
+    came = lax.ppermute(send, "prow", shift_z(2, [0, 1, 4, 5]))
     one_shape = shape((DEST_ROWS, local_cols))
     kept, send = local_kernel(
         functools.partial(fold_kernel, 2), "fold2", [one_shape] * 2, [position], kept, came
     )
     came = lax.ppermute(send, "prow", shift_z(1))
 
-    y_lo, y_hi = after((y_lo, y_hi), across, sent, came)
+    y_lo, y_hi = after((y_lo, y_hi), sent, up, down, came)
     far_first = lax.ppermute(y_lo[:half], "prow", shift_y(1))
     far_second = lax.ppermute(y_hi[half:], "prow", shift_y(-1))
     (cross,) = local_kernel(
@@ -659,10 +710,9 @@
         [shape((local_rows, width))],
         [position],
         rows,
-        third,
-        up,
-        down,
-        across,
+        *after((got[0], got[2], got[1], got[3]), y_lo),
+        *up,
+        *down,
     )
     other = lax.ppermute(part, "pcol", SWAP)
 
@@ -678,7 +728,20 @@
         *gone_sent,
     )
     cross_other = lax.ppermute(cross, "pcol", SWAP)
-    y_parts = [z_line, y_lo, y_hi, far_first, far_second]
+    row_first, second, a00 = pl.pallas_call(
+        first_kernel,
+        grid=(1,),
+        in_specs=[whole((2, panel, panel))]
+        + [whole((2 * half, local_cols))] * 3
+        + [whole((half, local_cols))] * 2,
+        out_specs=[whole((panel, local_cols))] * 2 + [whole((panel, width))],
+        out_shape=[shape((panel, local_cols))] * 2 + [shape((panel, width))],
+        compiler_params=pltpu.CompilerParams(vmem_limit_bytes=40 * MIB),
+        cost_estimate=pl.CostEstimate(
+            flops=2 * panel * panel * local_cols, bytes_accessed=8 * MIB, transcendentals=0
+        ),
+        name="first",
+    )(low, z_line, y_lo, y_hi, far_first, far_second)
 
     n_block = panel // 2
     steps = local_rows // n_block
@@ -698,17 +761,17 @@
             whole((2 * DEST_ROWS, local_cols)),
             whole((panel + 2 * DEST_ROWS, width)),
             whole((panel + 2 * DEST_ROWS, width)),
-            whole((2 * half, local_cols)),
-            whole((2 * half, local_cols)),
-            whole((2 * half, local_cols)),
-            whole((half, local_cols)),
-            whole((half, local_cols)),
+            whole((panel, local_cols)),
+            whole((panel, local_cols)),
+            whole((panel, width)),
             whole((2, panel, panel)),
             whole((2, panel, panel)),
             whole((2, panel)),
         ],
-        out_specs=row_block(local_cols),
-        out_shape=shape((local_rows, local_cols)),
+        out_specs=pl.BlockSpec(
+            (n_block // GROUP, 2, GROUP, width), lambda i: (jnp.maximum(i - 1, 0), 0, 0, 0)
+        ),
+        out_shape=shape((local_rows // GROUP, 2, GROUP, width)),
         scratch_shapes=[
             pltpu.VMEM((2 * panel, local_cols), jnp.bfloat16),
             pltpu.VMEM((panel, width), jnp.bfloat16),
@@ -718,8 +781,8 @@
         ],
         compiler_params=pltpu.CompilerParams(vmem_limit_bytes=40 * MIB),
         name="finish",
-    )(position, rows, part, other, land, gone, cross, cross_other, *y_parts, low, upper_inverse, place)
-    result = result.reshape(matrix.shape)
+    )(position, rows, part, other, land, gone, cross, cross_other, row_first, second, a00, low, upper_inverse, place)
+    result = result.transpose(0, 2, 1, 3).reshape(matrix.shape)
     return lax.cond(
         flag[0] > 0,
         lambda a, *rest: general_steps(*rest),

time: 177 us -> 248 us (1.40); the launches traced: 176 us -> 243 us
  Pallas kernels: 29.9 us -> 76.6 us
  loops' own time: 0.01 us -> 12 us
  local copies, waits for them, and re-layouts: 15.3 us -> 26.9 us
  starting transfers between devices: 98.3 us -> 91.7 us
  waiting for transfers between devices: 17.8 us -> 21.3 us
    pallas_call x0 -> x2, Pallas kernels: none -> 50.2 us  [the longest x1 49.4 us: per_device(): pl.pallas_call(turn_kernel, in_specs=[smem()] + [pl.BlockSpec(memory_spac...]
    ppermute x3, starting transfers between devices: 23.1 us -> 3.87 us  [per_device(): sent = [lax.ppermute(extra, 'pcol', move_x([(0, k)])) for k in (1, 2, 3)]]
    another operation x1, loops' own time: 0.01 us -> 12 us  [per_device(): lax.cond(flag[0] > 0, lambda a, *rest: general_steps(*rest), lambda a, *r...]
    unnamed x17 -> x65, local copies, waits for them, and re-layouts: 8.18 us -> 19 us
    transpose x0 -> x1, local copies, waits for them, and re-layouts: none -> 6.84 us
    ppermute x6 -> x8, starting transfers between devices: 10.8 us -> 17.3 us  [the longest x2 5.8 us: per_device(): lax.ppermute(pieces[k], 'pcol', move_x([(0, 1) if k < 2 else (0, 3)]))]
    reshape x1 -> x0, local copies, waits for them, and re-layouts: 6.14 us -> none  [per_device(): result = result.reshape(matrix.shape)]
    ppermute x1, starting transfers between devices: 4.14 us -> 9.61 us  [per_device(): other = lax.ppermute(part, 'pcol', SWAP)]
  transfers between devices with their start and end apart: 33 -> 35, of which waited for: 13 -> 11; matrix products, arithmetic and copies ran while one was open for 1% -> 0% of each run, Pallas kernels for 5% -> 3%
where the time goes in v3:
time: 248 us; the launch traced here: 243 us
  starting transfers between devices  91.7 us (37%)
  Pallas kernels  76.6 us (31%)
  local copies, waits for them, and re-layouts  26.9 us (11%)
  waiting for transfers between devices  21.3 us (9%)
  between operations  14.7 us (6%)
  loops' own time  12 us (5%)
    pallas_call x1, Pallas kernels, per_device(): pl.pallas_call(turn_kernel, in_specs=[smem()] + [pl.BlockSpec(memory_spac...  49.4 us
    unnamed x65, local copies, waits for them, and re-layouts  19 us
    pallas_call x12, Pallas kernels, local_kernel(): pl.pallas_call(body, grid=(1,), in_specs=[smem() for _ in scalars] + [who...  13.3 us
    pallas_call x1, Pallas kernels, per_device(): pl.pallas_call(functools.partial(finish_kernel, panel), grid=(steps + 1,)...  13.1 us
    all_to_all x1, starting transfers between devices, per_device(): dealt = lax.all_to_all(picks, 'prow', 0, 0, tiled=True)  12.2 us
    another operation x1, loops' own time, per_device(): lax.cond(flag[0] > 0, lambda a, *rest: general_steps(*rest), lambda a, *r...  12 us
    ppermute x1, starting transfers between devices, per_device(): other = lax.ppermute(part, 'pcol', SWAP)  9.61 us
    ppermute x1, starting transfers between devices, per_device(): came = lax.ppermute(send, 'prow', shift_z(1))  7.89 us
  transfers between devices with their start and end apart: 35, of which 11 were waited for; matrix products, arithmetic and copies ran while one was open for 0% of the time, Pallas kernels for 3%

profile of v3, /device:TPU:1, one launch (start us, length us, event | category | flops | bytes accessed | tf_op | source)
XLA Modules:
  0.0 243.2 jit_solution(16457334332166775549)
XLA Ops:
  6.5 2.7 %copy.15 = bf16[192,8,2,512]{3,1,2,0:T(8,128)(2,1)S(1)} copy(bf16[192,8,2,512]{3,2,1,0:T(2,128)(2,1)} %bitcast.77) | data formatting | bytes 6291456
  9.4 2.9 %deal.1 = (bf16[256,1024]{1,0:T(8,128)(2,1)S(1)}, s32[32,1]{1,0:T(8,128)S(1)}, s32[2,512]{1,0:T(2,128)S(1)}, s32[1,512]{1,0:T(1,128)S(1)}) custom-call(s32[2]{0:T(128)S(1)} %pad_add_fusion.pos_ref, s32[2,512]{1,0:T(2,128)S(1)} %copy-done.32, bf16[1536,1024]{1,0:T(8,128)(2,1)S(1)} %bitcast.70), custom_call_target="tpu_custom_call" | custom-call | tf_op jit(solution)/shard_map/deal/pallas_call | solution.py:546
  13.7 12.2 %all-to-all-start = ((bf16[32,8,1024]{2,1,0:T(8,128)(2,1)}), bf16[32,8,1024]{2,1,0:T(8,128)(2,1)}, u32[]{:S(2)}, u32[]{:S(2)}) async-start(bf16[32,8,1024]{2,1,0:T(8,128)(2,1)} %bitcast.75), calls=%async_computation | async-start | bytes 1048576 | tf_op jit(solution)/shard_map/all_to_all | solution.py:585
  25.9 1.0 fusion.28
  26.9 3.1 %collective-permute-start = (bf16[384,512]{1,0:T(8,128)(2,1)S(1)}, bf16[384,512]{1,0:T(8,128)(2,1)S(1)}, u32[]{:S(2)}, u32[]{:S(2)}) collective-permute-start(bf16[384,512]{1,0:T(8,128)(2,1)S(1)} %get-tuple-element.565.refs_0_), channel_id=1, source_target_pairs={{0,2},{1,3},{8,10},{9,11},{16,18},{17,19},{24,26},{25,27},{32,34},... | collective-permute-start | bytes 1179656 | tf_op jit(solution)/shard_map/ppermute | solution.py:590
  30.0 2.7 %collective-permute-start.1 = (bf16[384,512]{1,0:T(8,128)(2,1)S(1)}, bf16[384,512]{1,0:T(8,128)(2,1)}, u32[]{:S(2)}, u32[]{:S(2)}) collective-permute-start(bf16[384,512]{1,0:T(8,128)(2,1)S(1)} %get-tuple-element.564.refs_2_), channel_id=1, source_target_pairs={{0,6},{1,7},{8,14},{9,15},{16,22},{17,23},{24,30},{25,31},{32,38},... | collective-permute-start | bytes 1179656 | tf_op jit(solution)/shard_map/ppermute | solution.py:590
  32.7 3.5 %leave.1 = (bf16[144,1024]{1,0:T(8,128)(2,1)S(1)}, bf16[144,1024]{1,0:T(8,128)(2,1)S(1)}, bf16[144,1024]{1,0:T(8,128)(2,1)S(1)}, bf16[144,1024]{1,0:T(8,128)(2,1...) custom-call(s32[2]{0:T(128)S(1)} %pad_add_fusion.pos_ref, ...), custom_call_target="tpu_custom_call" | custom-call | tf_op jit(solution)/shard_map/leave/pallas_call | solution.py:546
  41.5 1.3 block.1.block_ref
  42.8 3.3 %collective-permute-start.2 = (bf16[384,512]{1,0:T(8,128)(2,1)}, bf16[384,512]{1,0:T(8,128)(2,1)}, u32[]{:S(2)}, u32[]{:S(2)}) collective-permute-start(bf16[384,512]{1,0:T(8,128)(2,1)} %get-tuple-element.463.refs_1_), channel_id=1, source_target_pairs={{0,2},{1,3},{8,10},{9,11},{16,18},{17,19},{24,26},{25,27},{32,34},... | collective-permute-start | bytes 1179656 | tf_op jit(solution)/shard_map/ppermute | solution.py:628
  46.0 3.0 %collective-permute-start.3 = (bf16[384,512]{1,0:T(8,128)(2,1)}, bf16[384,512]{1,0:T(8,128)(2,1)}, u32[]{:S(2)}, u32[]{:S(2)}) collective-permute-start(bf16[384,512]{1,0:T(8,128)(2,1)} %get-tuple-element.464.refs_3_), channel_id=1, source_target_pairs={{0,6},{1,7},{8,14},{9,15},{16,22},{17,23},{24,30},{25,31},{32,38},... | collective-permute-start | bytes 1179656 | tf_op jit(solution)/shard_map/ppermute | solution.py:629
  49.0 2.8 %collective-permute-start.6 = (bf16[144,1024]{1,0:T(8,128)(2,1)}, bf16[144,1024]{1,0:T(8,128)(2,1)S(1)}, u32[]{:S(2)}, u32[]{:S(2)}) collective-permute-start(bf16[144,1024]{1,0:T(8,128)(2,1)} %copy-done.23), channel_id=1, source_target_pairs={{0,64},{8,72},{1,65},{9,73},{2,66},{10,74},{3,67},{11,75},{4,68},{... | collective-permute-start | bytes 884744 | tf_op jit(solution)/shard_map/ppermute | solution.py:611
  51.8 2.2 collective-permute-start.7
  54.0 1.3 collective-permute-start.8
  55.7 2.3 collective-permute-start.4
  58.0 3.9 %collective-permute-done.7.two_ref = bf16[144,1024]{1,0:T(8,128)(2,1)S(1)} collective-permute-done((bf16[144,1024]{1,0:T(8,128)(2,1)}, bf16[144,1024]{1,0:T(8,128)(2,1)S(1)}, u32[]{:S(2)}, u32[]{:S(2)}) %collective-permute-start.7) | collective-permute-done | bytes 294944 | tf_op jit(solution)/shard_map/ppermute | solution.py:611
  68.0 49.4 %turn.1 = (bf16[384,512]{1,0:T(8,128)(2,1)}, bf16[384,512]{1,0:T(8,128)(2,1)}, bf16[384,512]{1,0:T(8,128)(2,1)}, bf16[384,512]{1,0:T(8,128)(2,1)}) custom-call(s32[2]{0:T(128)} %copy-done.17, bf16[384,512]{1,0:T(8,128)(2,1)} %copy-done.30, bf16[384,512]{1,0:T(8,128)(2,1)} %get-tuple-element.463.refs_1_, bf16[384,512]{1,0:T(8,128)(2,1)} %copy-done.29, ...), custom_call_target="tpu_custom_call" | custom-call | tf_op jit(solution)/shard_map/turn/pallas_call | solution.py:641
  117.5 1.3 collective-permute-start.12
  118.8 1.3 collective-permute-start.13
  120.1 1.3 collective-permute-start.14
  121.4 2.8 %collective-permute-start.10 = (bf16[64,1024]{1,0:T(8,128)(2,1)}, bf16[64,1024]{1,0:T(8,128)(2,1)S(1)}, u32[]{:S(2)}, u32[]{:S(2)}) collective-permute-start(bf16[64,1024]{1,0:T(8,128)(2,1)} %copy-done.26), channel_id=1, source_target_pairs={{0,16},{8,24},{16,32},{24,40},{32,48},{40,56},{48,0},{56,8},{64,80... | collective-permute-start | bytes 393224 | tf_op jit(solution)/shard_map/ppermute | solution.py:637
  125.1 5.8 %collective-permute-start.9 = (bf16[32,1024]{1,0:T(8,128)(2,1)}, bf16[32,1024]{1,0:T(8,128)(2,1)S(1)}, u32[]{:S(2)}, u32[]{:S(2)}) collective-permute-start(bf16[32,1024]{1,0:T(8,128)(2,1)} %copy-done.4), channel_id=1, source_target_pairs={{0,32},{8,40},{16,48},{24,56},{32,0},{40,8},{48,16},{56,24},{64,96... | collective-permute-start | bytes 196616 | tf_op jit(solution)/shard_map/ppermute | solution.py:619
  131.0 2.3 collective-permute-done.9.opposite_ref
  136.3 1.3 collective-permute-start.17
  138.0 2.7 %collective-permute-start.16 = (bf16[256,1024]{1,0:T(8,128)(2,1)S(1)}, bf16[256,1024]{1,0:T(8,128)(2,1)S(1)}, u32[]{:S(2)}, u32[]{:S(2)}) collective-permute-start(bf16[256,1024]{1,0:T(8,128)(2,1)S(1)} %get-tuple-element.483.y0_ref), channel_id=1, source_target_pairs={{0,192},{8,200},{16,208},{24,216},{32,224},{40,232},{48,240},{56,2... | collective-permute-start | bytes 1572872 | tf_op jit(solution)/shard_map/ppermute | solution.py:669
  140.7 1.3 collective-permute-start.18
  142.0 1.3 collective-permute-start.20
  143.3 1.3 collective-permute-start.21
  146.2 4.0 %collective-permute-start.22 = (bf16[64,1024]{1,0:T(8,128)(2,1)S(1)}, bf16[64,1024]{1,0:T(8,128)(2,1)S(1)}, u32[]{:S(2)}, u32[]{:S(2)}) collective-permute-start(bf16[64,1024]{1,0:T(8,128)(2,1)S(1)} %get-tuple-element.491), channel_id=1, source_target_pairs={{0,16},{8,24},{32,48},{40,56},{64,80},{72,88},{96,112},{104,120},{... | collective-permute-start | bytes 393224 | tf_op jit(solution)/shard_map/ppermute | solution.py:683
  150.2 1.9 collective-permute-done.22.came_ref
  152.1 1.3 collective-permute-start.19
  154.0 2.7 %collective-permute-done.19.three_ref = bf16[128,512]{1,0:T(8,128)(2,1)S(1)} collective-permute-done((bf16[128,512]{1,0:T(8,128)(2,1)S(1)}, bf16[128,512]{1,0:T(8,128)(2,1)S(1)}, u32[]{:S(2)}, u32[]{:S(2)}) %collective-permute-start.19) | collective-permute-done | bytes 131104 | tf_op jit(solution)/shard_map/ppermute | solution.py:670
  156.7 7.9 %collective-permute-start.23 = (bf16[32,1024]{1,0:T(8,128)(2,1)S(1)}, bf16[32,1024]{1,0:T(8,128)(2,1)S(1)}, u32[]{:S(2)}, u32[]{:S(2)}) collective-permute-start(bf16[32,1024]{1,0:T(8,128)(2,1)S(1)} %get-tuple-element.492), channel_id=1, source_target_pairs={{0,8},{8,16},{16,24},{24,32},{32,40},{40,48},{48,56},{56,0},{64,72... | collective-permute-start | bytes 196616 | tf_op jit(solution)/shard_map/ppermute | solution.py:688
  164.6 1.3 collective-permute-done.23.came_ref
  166.9 1.4 part.1.part_ref
  168.3 9.6 %collective-permute-start.24 = (bf16[1536,512]{1,0:T(8,128)(2,1)S(1)}, bf16[1536,512]{1,0:T(8,128)(2,1)S(1)}, u32[]{:S(2)}, u32[]{:S(2)}) collective-permute-start(bf16[1536,512]{1,0:T(8,128)(2,1)S(1)} %part.1.part_ref), channel_id=1, source_target_pairs={{0,1},{1,0},{2,3},{3,2},{4,5},{5,4},{6,7},{7,6},{8,9},{9,8},{10,11... | collective-permute-start | bytes 4718600 | tf_op jit(solution)/shard_map/ppermute | solution.py:717
  178.6 1.8 collective-permute-start.28
  180.5 1.0 collective-permute-start.29
  181.5 1.4 collective-permute-start.26
  182.9 2.0 collective-permute-done.25.c1_ref
  186.3 4.3 %collective-permute-done.26.c2_ref = bf16[128,512]{1,0:T(8,128)(2,1)S(1)} collective-permute-done((bf16[128,512]{1,0:T(8,128)(2,1)S(1)}, bf16[128,512]{1,0:T(8,128)(2,1)S(1)}, u32[]{:S(2)}, u32[]{:S(2)}) %collective-permute-start.26) | collective-permute-done | bytes 131104 | tf_op jit(solution)/shard_map/ppermute | solution.py:696
  190.6 1.3 collective-permute-start.30
  192.7 1.4 collective-permute-start.31
  194.1 4.5 %collective-permute-start.32 = (bf16[64,512]{1,0:T(8,128)(2,1)S(1)}, bf16[64,512]{1,0:T(8,128)(2,1)S(1)}, u32[]{:S(2)}, u32[]{:S(2)}) collective-permute-start(bf16[64,512]{1,0:T(8,128)(2,1)S(1)} %get-tuple-element.505.own_ref), channel_id=1, source_target_pairs={{0,6},{1,7},{8,14},{9,15},{16,22},{17,23},{24,30},{25,31},{32,38},... | collective-permute-start | bytes 196616 | tf_op jit(solution)/shard_map/ppermute | solution.py:706
  198.7 1.3 collective-permute-done.32.three_ref
  200.6 2.0 collective-permute-start.33
  204.2 13.1 %finish.1 = bf16[96,2,16,512]{3,2,1,0:T(8,128)(2,1)S(1)} custom-call(s32[2]{0:T(128)S(1)} %copy-done.18, bf16[1536,1024]{1,0:T(8,128)(2,1)S(1)} %bitcast.74, bf16[1536,512]{1,0:T(8,128)(2,1)S(1)} %part.1.part_ref, bf16[1536,512]{1,0:T(8,128)(2,1)S(1)} %collective-permute-done.24.other_ref, s32[1,64]{1,0:T(1,128)S(1)} %get-tuple-element.498.land_ref, ...), custom_call_target="tpu_custom_call" | custom-call | tf_op jit(solution)/shard_map/finish/pallas_call | solution.py:752
  217.4 18.8 %conditional.2 = (bf16[3,512,2,512]{3,2,1,0:T(2,128)(2,1)}) conditional(s32[]{:T(128)} %bitcast.5, bf16[96,16,2,512]{3,1,2,0:T(8,128)(2,1)S(1)} %bitcast.79, (bf16[3,512,2,512]{3,2,1,0:T(2,128)(2,1)}, s32[2,512]{1,0:T(2,128)S(1)}, bf16[2,512,512]{2,1,0:T(8,128)(2,1)}, bf16[2,512,512]{2,1,0:T(8,128)(2,1)}) %tuple.128), branch_computations={%region_0.0_spmd, %region_1.11_spmd} | conditional | flops 2966474752 | bytes 85029544 | solution.py:786
  229.3 6.8 %copy.10 = bf16[96,16,2,512]{3,2,1,0:T(2,128)(2,1)} copy(bf16[96,16,2,512]{3,1,2,0:T(8,128)(2,1)S(1)} %param.4) | data formatting | bytes 6291456 | tf_op jit(solution)/shard_map/transpose
  (108 shorter events, 25.2 us)
Async XLA Ops:
  6.5 2.8 %copy-start.32 = (s32[2,512]{1,0:T(2,128)S(1)}, s32[2,512]{1,0:T(2,128)}, u32[]{:S(2)}) copy-start(s32[2,512]{1,0:T(2,128)} %across_ref.3) | copy-start | bytes 12292
  9.4 52.5 %copy-start.17 = (s32[2]{0:T(128)}, s32[2]{0:T(128)S(1)}, u32[]{:S(2)}) copy-start(s32[2]{0:T(128)S(1)} %pad_add_fusion.pos_ref) | copy-start | bytes 28
  13.7 27.1 %all-to-all-start = ((bf16[32,8,1024]{2,1,0:T(8,128)(2,1)}), bf16[32,8,1024]{2,1,0:T(8,128)(2,1)}, u32[]{:S(2)}, u32[]{:S(2)}) async-start(bf16[32,8,1024]{2,1,0:T(8,128)(2,1)} %bitcast.75), calls=%async_computation | async-start | bytes 1048576 | tf_op jit(solution)/shard_map/all_to_all | solution.py:585
  25.8 6.9 %copy-start.31 = (bf16[2,512,512]{2,1,0:T(8,128)(2,1)S(1)}, bf16[2,512,512]{2,1,0:T(8,128)(2,1)}, u32[]{:S(2)}) copy-start(bf16[2,512,512]{2,1,0:T(8,128)(2,1)} %lower_ref.1) | copy-start | bytes 3145732
  26.9 13.8 %copy-start.29 = (bf16[384,512]{1,0:T(8,128)(2,1)}, bf16[384,512]{1,0:T(8,128)(2,1)S(1)}, u32[]{:S(2)}) copy-start(bf16[384,512]{1,0:T(8,128)(2,1)S(1)} %get-tuple-element.564.refs_2_) | copy-start | bytes 1179652
  26.9 13.8 %copy-start.30 = (bf16[384,512]{1,0:T(8,128)(2,1)}, bf16[384,512]{1,0:T(8,128)(2,1)S(1)}, u32[]{:S(2)}) copy-start(bf16[384,512]{1,0:T(8,128)(2,1)S(1)} %get-tuple-element.565.refs_0_) | copy-start | bytes 1179652
  26.9 13.8 %collective-permute-start = (bf16[384,512]{1,0:T(8,128)(2,1)S(1)}, bf16[384,512]{1,0:T(8,128)(2,1)S(1)}, u32[]{:S(2)}, u32[]{:S(2)}) collective-permute-start(bf16[384,512]{1,0:T(8,128)(2,1)S(1)} %get-tuple-element.565.refs_0_), channel_id=1, source_target_pairs={{0,2},{1,3},{8,10},{9,11},{16,18},{17,19},{24,26},{25,27},{32,34},... | collective-permute-start | bytes 1179656 | tf_op jit(solution)/shard_map/ppermute | solution.py:590
  30.0 10.7 %collective-permute-start.1 = (bf16[384,512]{1,0:T(8,128)(2,1)S(1)}, bf16[384,512]{1,0:T(8,128)(2,1)}, u32[]{:S(2)}, u32[]{:S(2)}) collective-permute-start(bf16[384,512]{1,0:T(8,128)(2,1)S(1)} %get-tuple-element.564.refs_2_), channel_id=1, source_target_pairs={{0,6},{1,7},{8,14},{9,15},{16,22},{17,23},{24,30},{25,31},{32,38},... | collective-permute-start | bytes 1179656 | tf_op jit(solution)/shard_map/ppermute | solution.py:590
  36.2 1.0 copy-start
  40.7 27.3 %copy-start.2 = (bf16[384,512]{1,0:T(8,128)(2,1)}, bf16[384,512]{1,0:T(8,128)(2,1)S(1)}, u32[]{:S(2)}) copy-start(bf16[384,512]{1,0:T(8,128)(2,1)S(1)} %collective-permute-done.refs_4_.refs_0_) | copy-start | bytes 1179652
  42.8 23.3 %copy-start.4 = (bf16[32,1024]{1,0:T(8,128)(2,1)}, bf16[32,1024]{1,0:T(8,128)(2,1)S(1)}, u32[]{:S(2)}) copy-start(bf16[32,1024]{1,0:T(8,128)(2,1)S(1)} %block.1.block_ref) | copy-start | bytes 196612
  42.8 23.3 %collective-permute-start.2 = (bf16[384,512]{1,0:T(8,128)(2,1)}, bf16[384,512]{1,0:T(8,128)(2,1)}, u32[]{:S(2)}, u32[]{:S(2)}) collective-permute-start(bf16[384,512]{1,0:T(8,128)(2,1)} %get-tuple-element.463.refs_1_), channel_id=1, source_target_pairs={{0,2},{1,3},{8,10},{9,11},{16,18},{17,19},{24,26},{25,27},{32,34},... | collective-permute-start | bytes 1179656 | tf_op jit(solution)/shard_map/ppermute | solution.py:628
  46.0 20.1 %collective-permute-start.3 = (bf16[384,512]{1,0:T(8,128)(2,1)}, bf16[384,512]{1,0:T(8,128)(2,1)}, u32[]{:S(2)}, u32[]{:S(2)}) collective-permute-start(bf16[384,512]{1,0:T(8,128)(2,1)} %get-tuple-element.464.refs_3_), channel_id=1, source_target_pairs={{0,6},{1,7},{8,14},{9,15},{16,22},{17,23},{24,30},{25,31},{32,38},... | collective-permute-start | bytes 1179656 | tf_op jit(solution)/shard_map/ppermute | solution.py:629
  49.0 6.7 %collective-permute-start.6 = (bf16[144,1024]{1,0:T(8,128)(2,1)}, bf16[144,1024]{1,0:T(8,128)(2,1)S(1)}, u32[]{:S(2)}, u32[]{:S(2)}) collective-permute-start(bf16[144,1024]{1,0:T(8,128)(2,1)} %copy-done.23), channel_id=1, source_target_pairs={{0,64},{8,72},{1,65},{9,73},{2,66},{10,74},{3,67},{11,75},{4,68},{... | collective-permute-start | bytes 884744 | tf_op jit(solution)/shard_map/ppermute | solution.py:611
  51.8 10.1 %collective-permute-start.7 = (bf16[144,1024]{1,0:T(8,128)(2,1)}, bf16[144,1024]{1,0:T(8,128)(2,1)S(1)}, u32[]{:S(2)}, u32[]{:S(2)}) collective-permute-start(bf16[144,1024]{1,0:T(8,128)(2,1)} %copy-done.22), channel_id=1, source_target_pairs={{0,128},{8,136},{1,129},{9,137},{2,130},{10,138},{3,131},{11,139},... | collective-permute-start | bytes 884744 | tf_op jit(solution)/shard_map/ppermute | solution.py:611
  54.0 7.9 %collective-permute-start.8 = (bf16[144,1024]{1,0:T(8,128)(2,1)}, bf16[144,1024]{1,0:T(8,128)(2,1)S(1)}, u32[]{:S(2)}, u32[]{:S(2)}) collective-permute-start(bf16[144,1024]{1,0:T(8,128)(2,1)} %copy-done.21), channel_id=1, source_target_pairs={{0,192},{8,200},{1,193},{9,201},{2,194},{10,202},{3,195},{11,203},... | collective-permute-start | bytes 884744 | tf_op jit(solution)/shard_map/ppermute | solution.py:611
  55.7 10.3 %collective-permute-start.4 = (bf16[32,1024]{1,0:T(8,128)(2,1)S(1)}, bf16[32,1024]{1,0:T(8,128)(2,1)S(1)}, u32[]{:S(2)}, u32[]{:S(2)}) collective-permute-start(bf16[32,1024]{1,0:T(8,128)(2,1)S(1)} %block.1.block_ref), channel_id=1, source_target_pairs={{0,8},{8,16},{16,24},{24,32},{32,40},{40,48},{48,56},{56,0},{64,72... | collective-permute-start | bytes 196616 | tf_op jit(solution)/shard_map/ppermute | solution.py:617
  61.9 4.2 %collective-permute-start.5 = (bf16[32,1024]{1,0:T(8,128)(2,1)S(1)}, bf16[32,1024]{1,0:T(8,128)(2,1)S(1)}, u32[]{:S(2)}, u32[]{:S(2)}) collective-permute-start(bf16[32,1024]{1,0:T(8,128)(2,1)S(1)} %block.1.block_ref), channel_id=1, source_target_pairs={{0,56},{8,0},{16,8},{24,16},{32,24},{40,32},{48,40},{56,48},{64,12... | collective-permute-start | bytes 196616 | tf_op jit(solution)/shard_map/ppermute | solution.py:618
  61.9 1.0 copy-start.8
  66.1 67.2 %copy-start.18 = (s32[2]{0:T(128)S(1)}, s32[2]{0:T(128)}, u32[]{:S(2)}) copy-start(s32[2]{0:T(128)} %copy-done.17) | copy-start | bytes 28
  117.5 13.5 %collective-permute-start.12 = (bf16[384,512]{1,0:T(8,128)(2,1)}, bf16[384,512]{1,0:T(8,128)(2,1)S(1)}, u32[]{:S(2)}, u32[]{:S(2)}) collective-permute-start(bf16[384,512]{1,0:T(8,128)(2,1)} %get-tuple-element.478), channel_id=1, source_target_pairs={{0,2},{1,3},{2,4},{3,5},{8,10},{9,11},{10,12},{11,13},{16,18},{17,... | collective-permute-start | bytes 1179656 | tf_op jit(solution)/shard_map/ppermute | solution.py:651
  118.8 12.2 %collective-permute-start.13 = (bf16[384,512]{1,0:T(8,128)(2,1)}, bf16[384,512]{1,0:T(8,128)(2,1)S(1)}, u32[]{:S(2)}, u32[]{:S(2)}) collective-permute-start(bf16[384,512]{1,0:T(8,128)(2,1)} %get-tuple-element.479), channel_id=1, source_target_pairs={{0,6},{1,7},{6,4},{7,5},{8,14},{9,15},{14,12},{15,13},{16,22},{17,... | collective-permute-start | bytes 1179656 | tf_op jit(solution)/shard_map/ppermute | solution.py:652
  120.1 5.0 %collective-permute-start.14 = (bf16[128,1024]{1,0:T(8,128)(2,1)}, bf16[128,1024]{1,0:T(8,128)(2,1)S(1)}, u32[]{:S(2)}, u32[]{:S(2)}) collective-permute-start(bf16[128,1024]{1,0:T(8,128)(2,1)} %copy-done.24), channel_id=1, source_target_pairs={{0,32},{8,40},{64,96},{72,104},{128,160},{136,168},{192,224},{200,... | collective-permute-start | bytes 786440 | tf_op jit(solution)/shard_map/ppermute | solution.py:624
  121.4 9.5 %collective-permute-start.10 = (bf16[64,1024]{1,0:T(8,128)(2,1)}, bf16[64,1024]{1,0:T(8,128)(2,1)S(1)}, u32[]{:S(2)}, u32[]{:S(2)}) collective-permute-start(bf16[64,1024]{1,0:T(8,128)(2,1)} %copy-done.26), channel_id=1, source_target_pairs={{0,16},{8,24},{16,32},{24,40},{32,48},{40,56},{48,0},{56,8},{64,80... | collective-permute-start | bytes 393224 | tf_op jit(solution)/shard_map/ppermute | solution.py:637
  124.2 6.7 %collective-permute-start.11 = (bf16[64,1024]{1,0:T(8,128)(2,1)}, bf16[64,1024]{1,0:T(8,128)(2,1)S(1)}, u32[]{:S(2)}, u32[]{:S(2)}) collective-permute-start(bf16[64,1024]{1,0:T(8,128)(2,1)} %copy-done.25), channel_id=1, source_target_pairs={{0,48},{8,56},{16,0},{24,8},{32,16},{40,24},{48,32},{56,40},{64,11... | collective-permute-start | bytes 393224 | tf_op jit(solution)/shard_map/ppermute | solution.py:638
  125.1 8.1 %collective-permute-start.9 = (bf16[32,1024]{1,0:T(8,128)(2,1)}, bf16[32,1024]{1,0:T(8,128)(2,1)S(1)}, u32[]{:S(2)}, u32[]{:S(2)}) collective-permute-start(bf16[32,1024]{1,0:T(8,128)(2,1)} %copy-done.4), channel_id=1, source_target_pairs={{0,32},{8,40},{16,48},{24,56},{32,0},{40,8},{48,16},{56,24},{64,96... | collective-permute-start | bytes 196616 | tf_op jit(solution)/shard_map/ppermute | solution.py:619
  136.3 6.9 %collective-permute-start.17 = (bf16[128,512]{1,0:T(8,128)(2,1)S(1)}, bf16[128,512]{1,0:T(8,128)(2,1)S(1)}, u32[]{:S(2)}, u32[]{:S(2)}) collective-permute-start(bf16[128,512]{1,0:T(8,128)(2,1)S(1)} %get-tuple-element.484.own_ref), channel_id=1, source_target_pairs={{0,2},{1,3},{8,10},{9,11},{16,18},{17,19},{24,26},{25,27},{32,34},... | collective-permute-start | bytes 393224 | tf_op jit(solution)/shard_map/ppermute | solution.py:670
  137.7 28.3 %collective-permute-start.15 = (bf16[256,1024]{1,0:T(8,128)(2,1)S(1)}, bf16[256,1024]{1,0:T(8,128)(2,1)S(1)}, u32[]{:S(2)}, u32[]{:S(2)}) collective-permute-start(bf16[256,1024]{1,0:T(8,128)(2,1)S(1)} %get-tuple-element.483.y0_ref), channel_id=1, source_target_pairs={{0,64},{8,72},{16,80},{24,88},{32,96},{40,104},{48,112},{56,120},{... | collective-permute-start | bytes 1572872 | tf_op jit(solution)/shard_map/ppermute | solution.py:668
  138.0 27.9 %collective-permute-start.16 = (bf16[256,1024]{1,0:T(8,128)(2,1)S(1)}, bf16[256,1024]{1,0:T(8,128)(2,1)S(1)}, u32[]{:S(2)}, u32[]{:S(2)}) collective-permute-start(bf16[256,1024]{1,0:T(8,128)(2,1)S(1)} %get-tuple-element.483.y0_ref), channel_id=1, source_target_pairs={{0,192},{8,200},{16,208},{24,216},{32,224},{40,232},{48,240},{56,2... | collective-permute-start | bytes 1572872 | tf_op jit(solution)/shard_map/ppermute | solution.py:669
  140.7 5.5 %collective-permute-start.18 = (bf16[128,512]{1,0:T(8,128)(2,1)S(1)}, bf16[128,512]{1,0:T(8,128)(2,1)S(1)}, u32[]{:S(2)}, u32[]{:S(2)}) collective-permute-start(bf16[128,512]{1,0:T(8,128)(2,1)S(1)} %get-tuple-element.484.own_ref), channel_id=1, source_target_pairs={{0,4},{1,5},{8,12},{9,13},{16,20},{17,21},{24,28},{25,29},{32,36},... | collective-permute-start | bytes 393224 | tf_op jit(solution)/shard_map/ppermute | solution.py:670
  142.0 23.9 %collective-permute-start.20 = (bf16[384,512]{1,0:T(8,128)(2,1)}, bf16[384,512]{1,0:T(8,128)(2,1)S(1)}, u32[]{:S(2)}, u32[]{:S(2)}) collective-permute-start(bf16[384,512]{1,0:T(8,128)(2,1)} %get-tuple-element.487), channel_id=1, source_target_pairs={{0,2},{1,3},{2,4},{3,5},{8,10},{9,11},{10,12},{11,13},{16,18},{17,... | collective-permute-start | bytes 1179656 | tf_op jit(solution)/shard_map/ppermute | solution.py:672
  143.3 22.6 %collective-permute-start.21 = (bf16[384,512]{1,0:T(8,128)(2,1)}, bf16[384,512]{1,0:T(8,128)(2,1)S(1)}, u32[]{:S(2)}, u32[]{:S(2)}) collective-permute-start(bf16[384,512]{1,0:T(8,128)(2,1)} %get-tuple-element.488), channel_id=1, source_target_pairs={{0,6},{1,7},{6,4},{7,5},{8,14},{9,15},{14,12},{15,13},{16,22},{17,... | collective-permute-start | bytes 1179656 | tf_op jit(solution)/shard_map/ppermute | solution.py:673
  146.2 5.9 %collective-permute-start.22 = (bf16[64,1024]{1,0:T(8,128)(2,1)S(1)}, bf16[64,1024]{1,0:T(8,128)(2,1)S(1)}, u32[]{:S(2)}, u32[]{:S(2)}) collective-permute-start(bf16[64,1024]{1,0:T(8,128)(2,1)S(1)} %get-tuple-element.491), channel_id=1, source_target_pairs={{0,16},{8,24},{32,48},{40,56},{64,80},{72,88},{96,112},{104,120},{... | collective-permute-start | bytes 393224 | tf_op jit(solution)/shard_map/ppermute | solution.py:683
  152.1 4.6 %collective-permute-start.19 = (bf16[128,512]{1,0:T(8,128)(2,1)S(1)}, bf16[128,512]{1,0:T(8,128)(2,1)S(1)}, u32[]{:S(2)}, u32[]{:S(2)}) collective-permute-start(bf16[128,512]{1,0:T(8,128)(2,1)S(1)} %get-tuple-element.484.own_ref), channel_id=1, source_target_pairs={{0,6},{1,7},{8,14},{9,15},{16,22},{17,23},{24,30},{25,31},{32,38},... | collective-permute-start | bytes 393224 | tf_op jit(solution)/shard_map/ppermute | solution.py:670
  156.7 9.2 %collective-permute-start.23 = (bf16[32,1024]{1,0:T(8,128)(2,1)S(1)}, bf16[32,1024]{1,0:T(8,128)(2,1)S(1)}, u32[]{:S(2)}, u32[]{:S(2)}) collective-permute-start(bf16[32,1024]{1,0:T(8,128)(2,1)S(1)} %get-tuple-element.492), channel_id=1, source_target_pairs={{0,8},{8,16},{16,24},{24,32},{32,40},{40,48},{48,56},{56,0},{64,72... | collective-permute-start | bytes 196616 | tf_op jit(solution)/shard_map/ppermute | solution.py:688
  165.9 1.0 copy-start.3
  168.3 34.9 %copy-start.1 = (bf16[2,512,512]{2,1,0:T(8,128)(2,1)S(1)}, bf16[2,512,512]{2,1,0:T(8,128)(2,1)}, u32[]{:S(2)}) copy-start(bf16[2,512,512]{2,1,0:T(8,128)(2,1)} %copy-done) | copy-start | bytes 3145732
  168.3 30.4 %collective-permute-start.24 = (bf16[1536,512]{1,0:T(8,128)(2,1)S(1)}, bf16[1536,512]{1,0:T(8,128)(2,1)S(1)}, u32[]{:S(2)}, u32[]{:S(2)}) collective-permute-start(bf16[1536,512]{1,0:T(8,128)(2,1)S(1)} %part.1.part_ref), channel_id=1, source_target_pairs={{0,1},{1,0},{2,3},{3,2},{4,5},{5,4},{6,7},{7,6},{8,9},{9,8},{10,11... | collective-permute-start | bytes 4718600 | tf_op jit(solution)/shard_map/ppermute | solution.py:717
  178.5 6.4 %collective-permute-start.25 = (bf16[128,512]{1,0:T(8,128)(2,1)S(1)}, bf16[128,512]{1,0:T(8,128)(2,1)S(1)}, u32[]{:S(2)}, u32[]{:S(2)}) collective-permute-start(bf16[128,512]{1,0:T(8,128)(2,1)S(1)} %extra.1.c0_ref), channel_id=1, source_target_pairs={{0,64},{8,72},{16,80},{24,88},{32,96},{40,104},{48,112},{56,120},{... | collective-permute-start | bytes 393224 | tf_op jit(solution)/shard_map/ppermute | solution.py:696
  178.6 15.5 %collective-permute-start.28 = (bf16[128,1024]{1,0:T(8,128)(2,1)S(1)}, bf16[128,1024]{1,0:T(8,128)(2,1)S(1)}, u32[]{:S(2)}, u32[]{:S(2)}) collective-permute-start(bf16[128,1024]{1,0:T(8,128)(2,1)S(1)} %slice.131), channel_id=1, source_target_pairs={{0,64},{8,72},{16,80},{24,88},{32,96},{40,104},{48,112},{56,120},{... | collective-permute-start | bytes 786440 | tf_op jit(solution)/shard_map/ppermute | solution.py:691
  180.5 18.2 %collective-permute-start.29 = (bf16[128,1024]{1,0:T(8,128)(2,1)S(1)}, bf16[128,1024]{1,0:T(8,128)(2,1)S(1)}, u32[]{:S(2)}, u32[]{:S(2)}) collective-permute-start(bf16[128,1024]{1,0:T(8,128)(2,1)S(1)} %slice.132), channel_id=1, source_target_pairs={{0,192},{8,200},{16,208},{24,216},{32,224},{40,232},{48,240},{56,2... | collective-permute-start | bytes 786440 | tf_op jit(solution)/shard_map/ppermute | solution.py:692
  181.5 9.2 %collective-permute-start.26 = (bf16[128,512]{1,0:T(8,128)(2,1)S(1)}, bf16[128,512]{1,0:T(8,128)(2,1)S(1)}, u32[]{:S(2)}, u32[]{:S(2)}) collective-permute-start(bf16[128,512]{1,0:T(8,128)(2,1)S(1)} %extra.1.c0_ref), channel_id=1, source_target_pairs={{0,192},{8,200},{16,208},{24,216},{32,224},{40,232},{48,240},{56,2... | collective-permute-start | bytes 393224 | tf_op jit(solution)/shard_map/ppermute | solution.py:696
  184.9 7.8 %collective-permute-start.27 = (bf16[128,512]{1,0:T(8,128)(2,1)S(1)}, bf16[128,512]{1,0:T(8,128)(2,1)S(1)}, u32[]{:S(2)}, u32[]{:S(2)}) collective-permute-start(bf16[128,512]{1,0:T(8,128)(2,1)S(1)} %extra.1.c0_ref), channel_id=1, source_target_pairs={{0,128},{8,136},{16,144},{24,152},{32,160},{40,168},{48,176},{56,1... | collective-permute-start | bytes 393224 | tf_op jit(solution)/shard_map/ppermute | solution.py:696
  190.6 8.1 %collective-permute-start.30 = (bf16[64,512]{1,0:T(8,128)(2,1)S(1)}, bf16[64,512]{1,0:T(8,128)(2,1)S(1)}, u32[]{:S(2)}, u32[]{:S(2)}) collective-permute-start(bf16[64,512]{1,0:T(8,128)(2,1)S(1)} %get-tuple-element.505.own_ref), channel_id=1, source_target_pairs={{0,2},{1,3},{8,10},{9,11},{16,18},{17,19},{24,26},{25,27},{32,34},... | collective-permute-start | bytes 196616 | tf_op jit(solution)/shard_map/ppermute | solution.py:706
  192.7 6.0 %collective-permute-start.31 = (bf16[64,512]{1,0:T(8,128)(2,1)S(1)}, bf16[64,512]{1,0:T(8,128)(2,1)S(1)}, u32[]{:S(2)}, u32[]{:S(2)}) collective-permute-start(bf16[64,512]{1,0:T(8,128)(2,1)S(1)} %get-tuple-element.505.own_ref), channel_id=1, source_target_pairs={{0,4},{1,5},{8,12},{9,13},{16,20},{17,21},{24,28},{25,29},{32,36},... | collective-permute-start | bytes 196616 | tf_op jit(solution)/shard_map/ppermute | solution.py:706
  194.1 5.9 %collective-permute-start.32 = (bf16[64,512]{1,0:T(8,128)(2,1)S(1)}, bf16[64,512]{1,0:T(8,128)(2,1)S(1)}, u32[]{:S(2)}, u32[]{:S(2)}) collective-permute-start(bf16[64,512]{1,0:T(8,128)(2,1)S(1)} %get-tuple-element.505.own_ref), channel_id=1, source_target_pairs={{0,6},{1,7},{8,14},{9,15},{16,22},{17,23},{24,30},{25,31},{32,38},... | collective-permute-start | bytes 196616 | tf_op jit(solution)/shard_map/ppermute | solution.py:706
  200.6 3.7 %collective-permute-start.33 = (bf16[576,512]{1,0:T(8,128)(2,1)S(1)}, bf16[576,512]{1,0:T(8,128)(2,1)S(1)}, u32[]{:S(2)}, u32[]{:S(2)}) collective-permute-start(bf16[576,512]{1,0:T(8,128)(2,1)S(1)} %cross.1.cross_ref), channel_id=1, source_target_pairs={{0,1},{1,0},{2,3},{3,2},{4,5},{5,4},{6,7},{7,6},{8,9},{9,8},{10,11... | collective-permute-start | bytes 1769480 | tf_op jit(solution)/shard_map/ppermute | solution.py:730
  204.2 13.1 %copy-start.33 = (s32[2,512]{1,0:T(2,128)S(1)}, s32[2,512]{1,0:T(2,128)}, u32[]{:S(2)}) copy-start(s32[2,512]{1,0:T(2,128)} %across_ref.3) | copy-start | bytes 12292
  (19 other events, 14.0 us)

commit v4 on v3

--- a/solution.py
+++ b/solution.py
@@ -15,7 +15,6 @@
 Z_ORDER = (0, 7, 1, 4, 6, 5, 2, 3)
 Y_ORDER = (0, 3, 1, 2)
 MIB = 1 << 20
-GROUP = 16
 
 
 def shift_y(step, rows=range(NY), cols=range(NZ)):
@@ -302,9 +301,7 @@
     pair_hi_ref[n:, :] = hi_ref[...]
 
 
-def line_kernel(
-    pos_ref, block_ref, lo_ref, hi_ref, opposite_ref, two_lo_ref, two_hi_ref, line_ref, extra_ref
-):
+def line_kernel(block_ref, lo_ref, hi_ref, opposite_ref, two_lo_ref, two_hi_ref, line_ref):
     n = block_ref.shape[0]
     half = n // 2
     blocks = [block_ref[...], lo_ref[...], hi_ref[...], opposite_ref[...]]
@@ -312,57 +309,19 @@
     for k, value in enumerate(blocks):
         line_ref[k * half : (k + 1) * half, :] = value[:half]
         line_ref[(NZ + k) * half : (NZ + k + 1) * half, :] = value[half:]
-    even = (pos_ref[1] & 1) == 0
-    n, width = extra_ref.shape
-    extra_ref[...] = jnp.where(even, line_ref[n:, :width], line_ref[:n, :width])
 
 
 def by_x(x, at_0, at_1, at_2, at_3):
     return jnp.where(x <= 1, jnp.where(x == 0, at_0, at_1), jnp.where(x == 2, at_2, at_3))
 
 
-def turn_kernel(pos_ref, *refs):
-    own, got, outs, sems = refs[:4], refs[4:8], refs[8:12], refs[12]
+def choose_kernel(pos_ref, own_ref, one_ref, two_ref, three_ref, out_ref):
     x = pos_ref[1] >> 1
-
-    def pass_on(sources, first):
-        copies = [
-            pltpu.make_async_copy(source, outs[first + k], sems.at[first + k])
-            for k, source in enumerate(sources)
-        ]
-        for copy in copies:
-            copy.start()
-        for copy in copies:
-            copy.wait()
-
-    @pl.when(x == 0)
-    def _():
-        pass_on((*own[2:], *own[:2]), 0)
-
-    @pl.when(x == 1)
-    def _():
-        pass_on(got[:2], 0)
-
-    @pl.when(x == 3)
-    def _():
-        pass_on(got[2:], 2)
-
-
-def part_kernel(pos_ref, own_ref, *refs):
-    got, up, down, part_ref = refs[:4], refs[4:6], refs[6:8], refs[8]
-    x = pos_ref[1] >> 1
-    n = got[0].shape[0]
-
-    @pl.when(x == 0)
-    def _():
-        part_ref[...] = own_ref[:, : part_ref.shape[1]]
-
-    for place, sources in ((1, (*got[:2], *up)), (2, (*up, *down)), (3, (*down, *got[2:]))):
+    for place, ref in enumerate((own_ref, one_ref, two_ref, three_ref)):
 
         @pl.when(x == place)
-        def _(sources=sources):
-            for k, source in enumerate(sources):
-                part_ref[k * n : (k + 1) * n, :] = source[...]
+        def _(ref=ref):
+            out_ref[...] = ref[...]
 
 
 def spread_kernel(pos_ref, passing_ref, own_ref, one_ref, two_ref, three_ref, keep_ref, send_ref):
@@ -375,40 +334,53 @@
     send_ref[...] = spread[n_rows // 2 :]
 
 
-def fold_kernel(bit, pos_ref, kept_ref, came_ref, keep_ref, send_ref):
-    n = keep_ref.shape[0]
-
-    @pl.when((pos_ref[0] & bit) == 0)
-    def _():
-        keep_ref[...] = kept_ref[:n, :]
-        send_ref[...] = kept_ref[n:, :]
-
-    @pl.when((pos_ref[0] & bit) != 0)
-    def _():
-        keep_ref[...] = came_ref[:n, :]
-        send_ref[...] = came_ref[n:, :]
-
-
-def gone_kernel(pos_ref, kept_ref, came_ref, gone_ref, gone_panel_ref):
-    n, width = kept_ref.shape[0], gone_panel_ref.shape[1]
-    even = (pos_ref[0] & 1) == 0
-    kept, came = kept_ref[...], came_ref[...]
-    gone_ref[:n, :] = jnp.where(even, kept, came)
-    gone_ref[n:, :] = jnp.where(even, came, kept)
-    gone_panel_ref[...] = gone_ref[:, :width]
-
-
-def extra_kernel(pos_ref, own_ref, one_ref, two_ref, three_ref, cross_ref):
+def fold_kernel(pos_ref, kept_ref, came_ref, *out_refs):
+    for bit, source in ((0, kept_ref), (4, came_ref)):
+
+        @pl.when((pos_ref[0] & 4) == bit)
+        def _(source=source):
+            for k, ref in enumerate(out_refs):
+                ref[...] = source[k * DEST_ROWS : (k + 1) * DEST_ROWS, :]
+
+
+def gone_kernel(pos_ref, line_ref, *refs):
+    landed, gone_ref, extra_ref = refs[:4], refs[4], refs[5]
+    width = extra_ref.shape[1]
+    half = line_ref.shape[0] // 2
+    for s in range(2):
+        for k in range(4):
+
+            @pl.when(((pos_ref[0] - s) & 3) == k)
+            def _(k=k, s=s):
+                gone_ref[s * DEST_ROWS : (s + 1) * DEST_ROWS, :] = landed[k][...]
+
+    even = (pos_ref[1] & 1) == 0
+    extra_ref[:half, :] = jnp.where(even, line_ref[half:, :width], line_ref[:half, :width])
+    extra_ref[half:, :] = gone_ref[:, :width]
+
+
+def extra_kernel(pos_ref, own_ref, one_ref, two_ref, three_ref, cross_ref, gone_ref):
     x = pos_ref[1] >> 1
-    cross_ref[...] = by_x(x, own_ref[...], one_ref[...], two_ref[...], three_ref[...])
-
-
-def cross_kernel(pos_ref, c0_ref, c1_ref, c2_ref, c3_ref, own_ref, one_ref, two_ref, three_ref, cross_ref):
-    n = c0_ref.shape[0]
-    for k, ref in enumerate((c0_ref, c1_ref, c2_ref, c3_ref)):
-        cross_ref[k * n : (k + 1) * n, :] = ref[...]
+    value = by_x(x, own_ref[...], one_ref[...], two_ref[...], three_ref[...])
+    n = cross_ref.shape[0]
+    cross_ref[...] = value[:n]
+    gone_ref[...] = value[n:]
+
+
+def part_kernel(pos_ref, mine_ref, before_ref, after_ref, across_ref, part_ref):
     x = pos_ref[1] >> 1
-    cross_ref[NY * n :, :] = by_x(x, own_ref[...], one_ref[...], two_ref[...], three_ref[...])
+    n = mine_ref.shape[0]
+    for step, ref in ((0, mine_ref), (-1, before_ref), (1, after_ref), (2, across_ref)):
+        begin = ((x + step) & (NX - 1)) * n
+        part_ref[pl.ds(pl.multiple_of(begin, n), n), :] = ref[...]
+
+
+def cross_kernel(*refs):
+    begin = 0
+    for ref in refs[:-1]:
+        n = ref.shape[0]
+        refs[-1][begin : begin + n, :] = ref[...]
+        begin += n
 
 
 def first_kernel(
@@ -512,22 +484,15 @@
             - dot(factor_first, new_ref[:panel, :])
             - dot(factor_second, new_ref[panel:, :])
         )
-
-        def put(half, value):
-            out_ref[:, half] = value.reshape(n // GROUP, GROUP, width)
-
-        put(0, updated[:, :width])
-        put(1, updated[:, width:])
+        out_ref[...] = updated
 
         @pl.when(column <= 1)
         def _():
-            put(0, jnp.where(column == 0, factor_first, factor_second))
+            out_ref[:, :width] = jnp.where(column == 0, factor_first, factor_second)
 
         @pl.when((here <= 1) & (begin < panel))
         def _():
-            top = top_ref[pl.ds(pl.multiple_of(begin, n), n), :]
-            put(0, top[:, :width])
-            put(1, top[:, width:])
+            out_ref[...] = top_ref[pl.ds(pl.multiple_of(begin, n), n), :]
 
 
 def whole(shape):
@@ -542,14 +507,14 @@
     return jax.ShapeDtypeStruct(dims, dtype)
 
 
-def local_kernel(body, name, outs, scalars, *arrays):
+def local_kernel(body, name, outs, scalars, *arrays, limit=12):
     return pl.pallas_call(
         body,
         grid=(1,),
         in_specs=[smem() for _ in scalars] + [whole(v.shape) for v in arrays],
         out_specs=[smem() if o.shape == (1,) else whole(o.shape) for o in outs],
         out_shape=outs,
-        compiler_params=pltpu.CompilerParams(vmem_limit_bytes=40 * MIB),
+        compiler_params=pltpu.CompilerParams(vmem_limit_bytes=limit * MIB),
         cost_estimate=pl.CostEstimate(flops=0, bytes_accessed=0, transcendentals=0),
         name=name,
     )(*scalars, *arrays)
@@ -581,20 +546,23 @@
         [position],
         pivots,
         rows,
+        limit=32,
     )
     dealt = lax.all_to_all(picks, "prow", 0, 0, tiled=True)
 
-    piece = local_rows // 4
-    pieces = [rows[k * piece : (k + 1) * piece, :width] for k in range(4)]
-    got = [
-        lax.ppermute(pieces[k], "pcol", move_x([(0, 1) if k < 2 else (0, 3)])) for k in (0, 2)
-    ]
+    quarter = local_rows // NX
+    own = [rows[k * quarter : (k + 1) * quarter, :width] for k in range(NX)]
+    got = [lax.ppermute(own[k], "pcol", move_x([(0, k)])) for k in range(1, NX)]
+    (mine,) = local_kernel(
+        choose_kernel, "choose", [shape((quarter, width))], [position], own[0], *got
+    )
 
     line_shape = shape((LINE_ROWS, local_cols))
     *leaving, passing, land, flag, low = local_kernel(
         functools.partial(leave_kernel, panel),
         "leave",
-        [line_shape] * NY
+        [line_shape]
+        + [pltpu.HBM(line_shape.shape, line_shape.dtype)] * (NY - 1)
         + [
             shape((NZ * DEST_ROWS, 1), i32),
             shape((1, 2 * DEST_ROWS), i32),
@@ -607,10 +575,10 @@
         place,
         lower_inverse,
         slots,
+        limit=32,
     )
     arrived = [lax.ppermute(leaving[s], "prow", shift_y(s, [0], [0, 1])) for s in (1, 2, 3)]
 
-    dealt = after(dealt, got, passing)
     (block,) = local_kernel(
         block_kernel, "block", [shape((2 * per_home, local_cols))], [], keep, dealt
     )
@@ -623,41 +591,33 @@
     )
     came = lax.ppermute(send, "prow", shift_z(4, [0, 1]))
 
-    late_pieces = after((pieces[1], pieces[3]), block)
-    got += [
-        lax.ppermute(late_pieces[0], "pcol", move_x([(0, 1)])),
-        lax.ppermute(late_pieces[1], "pcol", move_x([(0, 3)])),
-    ]
-
-    from_lo, from_hi = after((from_lo, from_hi), got, kept)
+    from_lo, from_hi = after((from_lo, from_hi), came, mine)
     pair_shape = shape((4 * per_home, local_cols))
     pair_lo, pair_hi = local_kernel(
         pair_kernel, "pair", [pair_shape] * 2, [], block, from_lo, from_hi
     )
     two_lo = lax.ppermute(pair_lo, "prow", shift_z(2))
     two_hi = lax.ppermute(pair_hi, "prow", shift_z(-2))
-
-    got = after(got, pair_lo)
-    ups_downs = pl.pallas_call(
-        turn_kernel,
-        in_specs=[smem()] + [pl.BlockSpec(memory_space=pl.ANY)] * 8,
-        out_specs=[pl.BlockSpec(memory_space=pl.ANY)] * 4,
-        out_shape=[shape((piece, width))] * 4,
-        scratch_shapes=[pltpu.SemaphoreType.DMA((4,))],
-        cost_estimate=pl.CostEstimate(flops=0, bytes_accessed=0, transcendentals=0),
-        name="turn",
-    )(position, *pieces, got[0], got[2], got[1], got[3])
-    go_up, go_down = move_x([(0, 1), (1, 2)]), move_x([(0, 3), (3, 2)])
-    up = [lax.ppermute(ups_downs[0], "pcol", go_up)]
-    down = [lax.ppermute(ups_downs[2], "pcol", go_down)]
-
-    two_lo, two_hi = after((two_lo, two_hi), up, down, came)
+    one_shape = shape((DEST_ROWS, local_cols))
+    spread = local_kernel(
+        fold_kernel, "fold", [one_shape] * 4, [position], kept, after(came, pair_lo)
+    )
+    landed = [spread[0]] + [
+        lax.ppermute(spread[k], "prow", shift_z(k, [0, 1, 4, 5])) for k in (1, 2, 3)
+    ]
+    quarter_out = after(mine, pair_lo)
+    ring = [(x, (x + 1) % NX) for x in range(NX)]
+    before = lax.ppermute(quarter_out, "pcol", move_x(ring))
+    behind = lax.ppermute(quarter_out, "pcol", move_x([(b, a) for a, b in ring]))
+
+    two_lo, two_hi, opposite = after((two_lo, two_hi, opposite), before, behind, landed)
     half = panel // NY
-    z_line, extra = local_kernel(
+    n_gone = 2 * DEST_ROWS
+    (z_line,) = local_kernel(
         line_kernel,
         "line",
-        [shape((2 * half, local_cols)), shape((half, width))],
-        [position],
+        [shape((2 * half, local_cols))],
+        [],
         block,
         from_lo,
         from_hi,
@@ -667,52 +627,40 @@
     )
     y_lo = lax.ppermute(z_line, "prow", shift_y(1))
     y_hi = lax.ppermute(z_line, "prow", shift_y(-1))
+    gone, extra = local_kernel(
+        gone_kernel,
+        "gone",
+        [shape((n_gone, local_cols)), shape((half + n_gone, width))],
+        [position],
+        z_line,
+        *landed,
+    )
     sent = [lax.ppermute(extra, "pcol", move_x([(0, k)])) for k in (1, 2, 3)]
-    late_up, late_down = after((ups_downs[1], ups_downs[3]), extra)
-    up.append(lax.ppermute(late_up, "pcol", go_up))
-    down.append(lax.ppermute(late_down, "pcol", go_down))
-    eighth_shape = shape((NZ // 4 * DEST_ROWS, local_cols))
-    kept, send = local_kernel(
-        functools.partial(fold_kernel, 4),
-        "fold4",
-        [eighth_shape] * 2,
-        [position],
-        kept,
-        after(came, extra),
-    )
-    came = lax.ppermute(send, "prow", shift_z(2, [0, 1, 4, 5]))
-    one_shape = shape((DEST_ROWS, local_cols))
-    kept, send = local_kernel(
-        functools.partial(fold_kernel, 2), "fold2", [one_shape] * 2, [position], kept, came
-    )
-    came = lax.ppermute(send, "prow", shift_z(1))
-
-    y_lo, y_hi = after((y_lo, y_hi), sent, up, down, came)
+    across = lax.ppermute(
+        after(mine, z_line), "pcol", move_x([(x, (x + 2) % NX) for x in range(NX)])
+    )
+
+    y_lo, y_hi = after((y_lo, y_hi), sent, across)
     far_first = lax.ppermute(y_lo[:half], "prow", shift_y(1))
     far_second = lax.ppermute(y_hi[half:], "prow", shift_y(-1))
-    (cross,) = local_kernel(
-        extra_kernel, "extra", [shape((half, width))], [position], extra, *sent
+    cross, gone_panel = local_kernel(
+        extra_kernel,
+        "extra",
+        [shape((half, width)), shape((n_gone, width))],
+        [position],
+        extra,
+        *sent,
     )
     crossed = [lax.ppermute(cross, "prow", shift_y(s)) for s in (1, -1, 2)]
-    n_gone = 2 * DEST_ROWS
-    gone, gone_panel = local_kernel(
-        gone_kernel,
-        "gone",
-        [shape((n_gone, local_cols)), shape((n_gone, width))],
-        [position],
-        kept,
-        came,
-    )
-    gone_sent = [lax.ppermute(gone_panel, "pcol", move_x([(0, k)])) for k in (1, 2, 3)]
     (part,) = local_kernel(
         part_kernel,
         "part",
         [shape((local_rows, width))],
         [position],
-        rows,
-        *after((got[0], got[2], got[1], got[3]), y_lo),
-        *up,
-        *down,
+        mine,
+        before,
+        behind,
+        after(across, y_lo),
     )
     other = lax.ppermute(part, "pcol", SWAP)
 
@@ -721,11 +669,10 @@
         cross_kernel,
         "cross",
         [shape((panel + n_gone, width))],
-        [position],
+        [],
         cross,
         *crossed,
         gone_panel,
-        *gone_sent,
     )
     cross_other = lax.ppermute(cross, "pcol", SWAP)
     row_first, second, a00 = pl.pallas_call(
@@ -768,10 +715,8 @@
             whole((2, panel, panel)),
             whole((2, panel)),
         ],
-        out_specs=pl.BlockSpec(
-            (n_block // GROUP, 2, GROUP, width), lambda i: (jnp.maximum(i - 1, 0), 0, 0, 0)
-        ),
-        out_shape=shape((local_rows // GROUP, 2, GROUP, width)),
+        out_specs=row_block(local_cols),
+        out_shape=shape((local_rows, local_cols)),
         scratch_shapes=[
             pltpu.VMEM((2 * panel, local_cols), jnp.bfloat16),
             pltpu.VMEM((panel, width), jnp.bfloat16),
@@ -779,10 +724,10 @@
             pltpu.VMEM((2 * DEST_ROWS, width), jnp.bfloat16),
             pltpu.VMEM((panel, local_cols), jnp.bfloat16),
         ],
-        compiler_params=pltpu.CompilerParams(vmem_limit_bytes=40 * MIB),
+        compiler_params=pltpu.CompilerParams(vmem_limit_bytes=32 * MIB),
         name="finish",
     )(position, rows, part, other, land, gone, cross, cross_other, row_first, second, a00, low, upper_inverse, place)
-    result = result.transpose(0, 2, 1, 3).reshape(matrix.shape)
+    result = result.reshape(matrix.shape)
     return lax.cond(
         flag[0] > 0,
         lambda a, *rest: general_steps(*rest),

time: 248 us -> 158 us (0.64); the launches traced: 243 us -> 156 us
  Pallas kernels: 76.6 us -> 29.2 us
  starting transfers between devices: 91.7 us -> 74.1 us
  local copies, waits for them, and re-layouts: 26.9 us -> 14.7 us
  loops' own time: 12 us -> 0.01 us
    pallas_call x1 -> x0, Pallas kernels: 49.4 us -> none  [per_device(): pl.pallas_call(turn_kernel, in_specs=[smem()] + [pl.BlockSpec(memory_spac...]
    ppermute x13 -> x9, starting transfers between devices: 36.4 us -> 21.5 us  [the longest x3 9.55 us: per_device(): lax.ppermute(spread[k], 'prow', shift_z(k, [0, 1, 4, 5]))]
    another operation x1, loops' own time: 12 us -> 0.01 us  [per_device(): lax.cond(flag[0] > 0, lambda a, *rest: general_steps(*rest), lambda a, *r...]
    unnamed x65 -> x17, local copies, waits for them, and re-layouts: 19 us -> 7.49 us
    transpose x1 -> x0, local copies, waits for them, and re-layouts: 6.84 us -> none
    reshape x0 -> x1, local copies, waits for them, and re-layouts: none -> 6.14 us  [per_device(): result = result.reshape(matrix.shape)]
    ppermute x1, starting transfers between devices: 9.61 us -> 5.06 us  [per_device(): other = lax.ppermute(part, 'pcol', SWAP)]
    ppermute x3, starting transfers between devices: 3.87 us -> 7.69 us  [per_device(): sent = [lax.ppermute(extra, 'pcol', move_x([(0, k)])) for k in (1, 2, 3)]]
  transfers between devices with their start and end apart: 35 -> 31, of which waited for: 11 -> 9; matrix products, arithmetic and copies ran while one was open for 0% -> 1% of each run, Pallas kernels for 3% -> 7%
where the time goes in v4:
time: 158 us; the launch traced here: 156 us
  starting transfers between devices  74.1 us (47%)
  Pallas kernels  29.2 us (18%)
  waiting for transfers between devices  23.6 us (15%)
  local copies, waits for them, and re-layouts  14.7 us (9%)
  between operations  14.3 us (9%)
    pallas_call x12, Pallas kernels, local_kernel(): pl.pallas_call(body, grid=(1,), in_specs=[smem() for _ in scalars] + [who...  14.3 us
    pallas_call x1, Pallas kernels, per_device(): pl.pallas_call(functools.partial(finish_kernel, panel), grid=(steps + 1,)...  14.2 us
    all_to_all x1, starting transfers between devices, per_device(): dealt = lax.all_to_all(picks, 'prow', 0, 0, tiled=True)  12.2 us
    ppermute x3, starting transfers between devices, per_device(): lax.ppermute(spread[k], 'prow', shift_z(k, [0, 1, 4, 5]))  9.55 us
    ppermute x3, waiting for transfers between devices, per_device(): crossed = [lax.ppermute(cross, 'prow', shift_y(s)) for s in (1, -1, 2)]  9.04 us
    ppermute x3, starting transfers between devices, per_device(): got = [lax.ppermute(own[k], 'pcol', move_x([(0, k)])) for k in range(1, NX)]  8.81 us
    ppermute x3, starting transfers between devices, per_device(): sent = [lax.ppermute(extra, 'pcol', move_x([(0, k)])) for k in (1, 2, 3)]  7.69 us
    unnamed x17, local copies, waits for them, and re-layouts  7.49 us
  transfers between devices with their start and end apart: 31, of which 9 were waited for; matrix products, arithmetic and copies ran while one was open for 1% of the time, Pallas kernels for 7%

profile of v4, /device:TPU:1, one launch (start us, length us, event | category | flops | bytes accessed | tf_op | source)
XLA Modules:
  0.0 156.1 jit_solution(6767636174538186742)
XLA Ops:
  6.5 2.8 %copy.13 = bf16[192,8,2,512]{3,1,2,0:T(8,128)(2,1)S(1)} copy(bf16[192,8,2,512]{3,2,1,0:T(2,128)(2,1)} %bitcast.74) | data formatting | bytes 6291456
  9.4 2.9 %deal.1 = (bf16[256,1024]{1,0:T(8,128)(2,1)S(1)}, s32[32,1]{1,0:T(8,128)S(1)}, s32[2,512]{1,0:T(2,128)S(1)}, s32[1,512]{1,0:T(1,128)S(1)}) custom-call(s32[2]{0:T(128)S(1)} %pad_add_fusion.pos_ref, s32[2,512]{1,0:T(2,128)S(1)} %copy-done.9, bf16[1536,1024]{1,0:T(8,128)(2,1)S(1)} %bitcast.68), custom_call_target="tpu_custom_call" | custom-call | tf_op jit(solution)/shard_map/deal/pallas_call | solution.py:511
  12.3 0.8 copy-done.2
  13.6 12.2 %all-to-all-start = ((bf16[32,8,1024]{2,1,0:T(8,128)(2,1)}), bf16[32,8,1024]{2,1,0:T(8,128)(2,1)}, u32[]{:S(2)}, u32[]{:S(2)}) async-start(bf16[32,8,1024]{2,1,0:T(8,128)(2,1)} %bitcast.72), calls=%async_computation | async-start | bytes 1048576 | tf_op jit(solution)/shard_map/all_to_all | solution.py:551
  25.8 4.3 %leave.1 = (bf16[144,1024]{1,0:T(8,128)(2,1)S(1)}, bf16[144,1024]{1,0:T(8,128)(2,1)}, bf16[144,1024]{1,0:T(8,128)(2,1)}, bf16[144,1024]{1,0:T(8,128)(2,1)}, s32[...) custom-call(s32[2]{0:T(128)S(1)} %pad_add_fusion.pos_ref, ...), custom_call_target="tpu_custom_call" | custom-call | tf_op jit(solution)/shard_map/leave/pallas_call | solution.py:511
  30.2 1.0 copy-done
  31.2 3.1 %collective-permute-start.5 = (bf16[144,1024]{1,0:T(8,128)(2,1)}, bf16[144,1024]{1,0:T(8,128)(2,1)S(1)}, u32[]{:S(2)}, u32[]{:S(2)}) collective-permute-start(bf16[144,1024]{1,0:T(8,128)(2,1)} %get-tuple-element.450), channel_id=1, source_target_pairs={{0,64},{8,72},{1,65},{9,73},{2,66},{10,74},{3,67},{11,75},{4,68},{... | collective-permute-start | bytes 884744 | tf_op jit(solution)/shard_map/ppermute | solution.py:580
  34.2 2.2 %collective-permute-start.6 = (bf16[144,1024]{1,0:T(8,128)(2,1)}, bf16[144,1024]{1,0:T(8,128)(2,1)S(1)}, u32[]{:S(2)}, u32[]{:S(2)}) collective-permute-start(bf16[144,1024]{1,0:T(8,128)(2,1)} %get-tuple-element.451), channel_id=1, source_target_pairs={{0,128},{8,136},{1,129},{9,137},{2,130},{10,138},{3,131},{11,139},... | collective-permute-start | bytes 884744 | tf_op jit(solution)/shard_map/ppermute | solution.py:580
  36.4 1.3 collective-permute-start.7
  37.7 1.1 fusion.28
  38.8 3.9 %collective-permute-start = (bf16[384,512]{1,0:T(8,128)(2,1)}, bf16[384,512]{1,0:T(8,128)(2,1)}, u32[]{:S(2)}, u32[]{:S(2)}) collective-permute-start(bf16[384,512]{1,0:T(8,128)(2,1)} %get-tuple-element.538), channel_id=1, source_target_pairs={{0,2},{1,3},{8,10},{9,11},{16,18},{17,19},{24,26},{25,27},{32,34},... | collective-permute-start | bytes 1179656 | tf_op jit(solution)/shard_map/ppermute | solution.py:555
  42.7 2.9 %collective-permute-start.1 = (bf16[384,512]{1,0:T(8,128)(2,1)}, bf16[384,512]{1,0:T(8,128)(2,1)}, u32[]{:S(2)}, u32[]{:S(2)}) collective-permute-start(bf16[384,512]{1,0:T(8,128)(2,1)} %get-tuple-element.537), channel_id=1, source_target_pairs={{0,4},{1,5},{8,12},{9,13},{16,20},{17,21},{24,28},{25,29},{32,36},... | collective-permute-start | bytes 1179656 | tf_op jit(solution)/shard_map/ppermute | solution.py:555
  45.6 2.0 %collective-permute-start.2 = (bf16[384,512]{1,0:T(8,128)(2,1)}, bf16[384,512]{1,0:T(8,128)(2,1)}, u32[]{:S(2)}, u32[]{:S(2)}) collective-permute-start(bf16[384,512]{1,0:T(8,128)(2,1)} %get-tuple-element.536), channel_id=1, source_target_pairs={{0,6},{1,7},{8,14},{9,15},{16,22},{17,23},{24,30},{25,31},{32,38},... | collective-permute-start | bytes 1179656 | tf_op jit(solution)/shard_map/ppermute | solution.py:555
  47.6 0.9 collective-permute-done.6.two_ref
  48.6 1.6 %spread.1 = (bf16[128,1024]{1,0:T(8,128)(2,1)S(1)}, bf16[128,1024]{1,0:T(8,128)(2,1)}) custom-call(s32[2]{0:T(128)S(1)} %pad_add_fusion.pos_ref, s32[256,1]{1,0:T(8,128)S(1)} %get-tuple-element.448.passing_ref, bf16[144,1024]{1,0:T(8,128)(2,1)S(1)} %get-tuple-element.449.own_ref, bf16[144,1024]{1,0:T(8,128)(2,1)S(1)} %collective-permute-done.5.one_ref, ...), custom_call_target="tpu_custom_call" | custom-call | tf_op jit(solution)/shard_map/spread/pallas_call | solution.py:511
  50.9 2.2 %collective-permute-start.8 = (bf16[128,1024]{1,0:T(8,128)(2,1)}, bf16[128,1024]{1,0:T(8,128)(2,1)}, u32[]{:S(2)}, u32[]{:S(2)}) collective-permute-start(bf16[128,1024]{1,0:T(8,128)(2,1)} %get-tuple-element.453), channel_id=1, source_target_pairs={{0,32},{8,40},{64,96},{72,104},{128,160},{136,168},{192,224},{200,... | collective-permute-start | bytes 786440 | tf_op jit(solution)/shard_map/ppermute | solution.py:592
  53.1 0.7 copy-done.6
  53.8 1.3 block.1.block_ref
  55.1 0.9 collective-permute-start.3
  56.0 1.8 %collective-permute-start.4 = (bf16[32,1024]{1,0:T(8,128)(2,1)S(1)}, bf16[32,1024]{1,0:T(8,128)(2,1)S(1)}, u32[]{:S(2)}, u32[]{:S(2)}) collective-permute-start(bf16[32,1024]{1,0:T(8,128)(2,1)S(1)} %block.1.block_ref), channel_id=1, source_target_pairs={{0,56},{8,0},{16,8},{24,16},{32,24},{40,32},{48,40},{56,48},{64,12... | collective-permute-start | bytes 196616 | tf_op jit(solution)/shard_map/ppermute | solution.py:586
  57.8 1.3 choose.1.mine_ref
  59.9 1.3 collective-permute-start.9
  61.1 1.5 collective-permute-start.10
  62.6 3.1 %collective-permute-start.13 = (bf16[32,1024]{1,0:T(8,128)(2,1)S(1)}, bf16[32,1024]{1,0:T(8,128)(2,1)S(1)}, u32[]{:S(2)}, u32[]{:S(2)}) collective-permute-start(bf16[32,1024]{1,0:T(8,128)(2,1)S(1)} %block.1.block_ref), channel_id=1, source_target_pairs={{0,32},{8,40},{16,48},{24,56},{32,0},{40,8},{48,16},{56,24},{64,96... | collective-permute-start | bytes 196616 | tf_op jit(solution)/shard_map/ppermute | solution.py:587
  65.8 0.9 copy-done.4
  66.7 1.0 fold.1
  67.7 3.0 %collective-permute-start.14 = (bf16[32,1024]{1,0:T(8,128)(2,1)S(1)}, bf16[32,1024]{1,0:T(8,128)(2,1)S(1)}, u32[]{:S(2)}, u32[]{:S(2)}) collective-permute-start(bf16[32,1024]{1,0:T(8,128)(2,1)S(1)} %get-tuple-element.462), channel_id=1, source_target_pairs={{0,8},{8,16},{32,40},{40,48},{64,72},{72,80},{96,104},{104,112},{1... | collective-permute-start | bytes 196616 | tf_op jit(solution)/shard_map/ppermute | solution.py:606
  70.7 4.1 %collective-permute-start.15 = (bf16[32,1024]{1,0:T(8,128)(2,1)S(1)}, bf16[32,1024]{1,0:T(8,128)(2,1)S(1)}, u32[]{:S(2)}, u32[]{:S(2)}) collective-permute-start(bf16[32,1024]{1,0:T(8,128)(2,1)S(1)} %get-tuple-element.463), channel_id=1, source_target_pairs={{0,16},{8,24},{32,48},{40,56},{64,80},{72,88},{96,112},{104,120},{... | collective-permute-start | bytes 196616 | tf_op jit(solution)/shard_map/ppermute | solution.py:606
  75.0 3.6 %collective-permute-start.12 = (bf16[64,1024]{1,0:T(8,128)(2,1)S(1)}, bf16[64,1024]{1,0:T(8,128)(2,1)S(1)}, u32[]{:S(2)}, u32[]{:S(2)}) collective-permute-start(bf16[64,1024]{1,0:T(8,128)(2,1)S(1)} %get-tuple-element.458), channel_id=1, source_target_pairs={{0,48},{8,56},{16,0},{24,8},{32,16},{40,24},{48,32},{56,40},{64,11... | collective-permute-start | bytes 393224 | tf_op jit(solution)/shard_map/ppermute | solution.py:600
  78.5 2.4 %collective-permute-start.16 = (bf16[32,1024]{1,0:T(8,128)(2,1)S(1)}, bf16[32,1024]{1,0:T(8,128)(2,1)S(1)}, u32[]{:S(2)}, u32[]{:S(2)}) collective-permute-start(bf16[32,1024]{1,0:T(8,128)(2,1)S(1)} %get-tuple-element.464), channel_id=1, source_target_pairs={{0,24},{8,32},{32,56},{40,0},{64,88},{72,96},{96,120},{104,64},{12... | collective-permute-start | bytes 196616 | tf_op jit(solution)/shard_map/ppermute | solution.py:606
  80.9 6.1 %collective-permute-done.16.refs_3_ = bf16[32,1024]{1,0:T(8,128)(2,1)S(1)} collective-permute-done((bf16[32,1024]{1,0:T(8,128)(2,1)S(1)}, bf16[32,1024]{1,0:T(8,128)(2,1)S(1)}, u32[]{:S(2)}, u32[]{:S(2)}) %collective-permute-start.16) | collective-permute-done | bytes 65568 | tf_op jit(solution)/shard_map/ppermute | solution.py:606
  87.7 2.2 %collective-permute-start.19 = (bf16[256,1024]{1,0:T(8,128)(2,1)S(1)}, bf16[256,1024]{1,0:T(8,128)(2,1)S(1)}, u32[]{:S(2)}, u32[]{:S(2)}) collective-permute-start(bf16[256,1024]{1,0:T(8,128)(2,1)S(1)} %line.1.line_ref.y0_ref), channel_id=1, source_target_pairs={{0,192},{8,200},{16,208},{24,216},{32,224},{40,232},{48,240},{56,2... | collective-permute-start | bytes 1572872 | tf_op jit(solution)/shard_map/ppermute | solution.py:629
  90.6 1.8 %collective-permute-start.20 = (bf16[192,512]{1,0:T(8,128)(2,1)S(1)}, bf16[192,512]{1,0:T(8,128)(2,1)S(1)}, u32[]{:S(2)}, u32[]{:S(2)}) collective-permute-start(bf16[192,512]{1,0:T(8,128)(2,1)S(1)} %get-tuple-element.469.own_ref), channel_id=1, source_target_pairs={{0,2},{1,3},{8,10},{9,11},{16,18},{17,19},{24,26},{25,27},{32,34},... | collective-permute-start | bytes 589832 | tf_op jit(solution)/shard_map/ppermute | solution.py:638
  92.8 4.6 %collective-permute-start.21 = (bf16[192,512]{1,0:T(8,128)(2,1)S(1)}, bf16[192,512]{1,0:T(8,128)(2,1)S(1)}, u32[]{:S(2)}, u32[]{:S(2)}) collective-permute-start(bf16[192,512]{1,0:T(8,128)(2,1)S(1)} %get-tuple-element.469.own_ref), channel_id=1, source_target_pairs={{0,4},{1,5},{8,12},{9,13},{16,20},{17,21},{24,28},{25,29},{32,36},... | collective-permute-start | bytes 589832 | tf_op jit(solution)/shard_map/ppermute | solution.py:638
  97.4 1.3 collective-permute-start.22
  98.7 6.4 %collective-permute-done.21.two_ref = bf16[192,512]{1,0:T(8,128)(2,1)S(1)} collective-permute-done((bf16[192,512]{1,0:T(8,128)(2,1)S(1)}, bf16[192,512]{1,0:T(8,128)(2,1)S(1)}, u32[]{:S(2)}, u32[]{:S(2)}) %collective-permute-start.21) | collective-permute-done | bytes 196640 | tf_op jit(solution)/shard_map/ppermute | solution.py:638
  105.8 5.1 %collective-permute-start.23 = (bf16[1536,512]{1,0:T(8,128)(2,1)S(1)}, bf16[1536,512]{1,0:T(8,128)(2,1)S(1)}, u32[]{:S(2)}, u32[]{:S(2)}) collective-permute-start(bf16[1536,512]{1,0:T(8,128)(2,1)S(1)} %part.1.part_ref), channel_id=1, source_target_pairs={{0,1},{1,0},{2,3},{3,2},{4,5},{5,4},{6,7},{7,6},{8,9},{9,8},{10,11... | collective-permute-start | bytes 4718600 | tf_op jit(solution)/shard_map/ppermute | solution.py:665
  111.4 0.9 collective-permute-start.24
  112.4 1.5 collective-permute-start.27
  114.0 1.3 collective-permute-start.28
  115.9 2.0 %collective-permute-done.24.refs_1_ = bf16[128,512]{1,0:T(8,128)(2,1)S(1)} collective-permute-done((bf16[128,512]{1,0:T(8,128)(2,1)S(1)}, bf16[128,512]{1,0:T(8,128)(2,1)S(1)}, u32[]{:S(2)}, u32[]{:S(2)}) %collective-permute-start.24) | collective-permute-done | bytes 131104 | tf_op jit(solution)/shard_map/ppermute | solution.py:654
  117.9 1.4 collective-permute-start.26
  119.3 4.9 %collective-permute-done.25.refs_2_ = bf16[128,512]{1,0:T(8,128)(2,1)S(1)} collective-permute-done((bf16[128,512]{1,0:T(8,128)(2,1)S(1)}, bf16[128,512]{1,0:T(8,128)(2,1)S(1)}, u32[]{:S(2)}, u32[]{:S(2)}) %collective-permute-start.25) | collective-permute-done | bytes 131104 | tf_op jit(solution)/shard_map/ppermute | solution.py:654
  124.1 2.2 %collective-permute-done.26.refs_3_ = bf16[128,512]{1,0:T(8,128)(2,1)S(1)} collective-permute-done((bf16[128,512]{1,0:T(8,128)(2,1)S(1)}, bf16[128,512]{1,0:T(8,128)(2,1)S(1)}, u32[]{:S(2)}, u32[]{:S(2)}) %collective-permute-start.26) | collective-permute-done | bytes 131104 | tf_op jit(solution)/shard_map/ppermute | solution.py:654
  126.4 0.9 collective-permute-start.29
  128.9 14.2 %finish.1 = bf16[1536,1024]{1,0:T(8,128)(2,1)} custom-call(s32[2]{0:T(128)S(1)} %pad_add_fusion.pos_ref, bf16[1536,1024]{1,0:T(8,128)(2,1)S(1)} %bitcast.71, bf16[1536,512]{1,0:T(8,128)(2,1)S(1)} %part.1.part_ref, bf16[1536,512]{1,0:T(8,128)(2,1)S(1)} %collective-permute-done.23.other_ref, s32[1,64]{1,0:T(1,128)S(1)} %get-tuple-element.472.land_ref, ...), custom_call_target="tpu_custom_call" | custom-call | tf_op jit(solution)/shard_map/finish/pallas_call | solution.py:699
  143.1 6.1 %conditional.2 = (bf16[3,512,2,512]{3,2,1,0:T(2,128)(2,1)}) conditional(s32[]{:T(128)} %bitcast.4, bf16[1536,1024]{1,0:T(8,128)(2,1)} %finish.1, (bf16[3,512,2,512]{3,2,1,0:T(2,128)(2,1)}, s32[2,512]{1,0:T(2,128)S(1)}, bf16[2,512,512]{2,1,0:T(8,128)(2,1)}, bf16[2,512,512]{2,1,0:T(8,128)(2,1)}) %tuple.124), branch_computations={%region_0.0_spmd, %region_1.11_spmd} | conditional | flops 2966474752 | bytes 85029544 | solution.py:731
  143.1 6.1 %reshape.435 = bf16[3,512,2,512]{3,2,1,0:T(2,128)(2,1)} reshape(bf16[1536,1024]{1,0:T(8,128)(2,1)} %param.4) | data formatting | bytes 6291456 | tf_op jit(solution)/shard_map/reshape | solution.py:730
  (51 shorter events, 6.8 us)
Async XLA Ops:
  6.5 2.8 %copy-start.9 = (s32[2,512]{1,0:T(2,128)S(1)}, s32[2,512]{1,0:T(2,128)}, u32[]{:S(2)}) copy-start(s32[2,512]{1,0:T(2,128)} %across_ref.3) | copy-start | bytes 12292
  12.2 0.8 copy-start.2
  13.0 0.6 copy-start.5
  13.6 39.4 %all-to-all-start = ((bf16[32,8,1024]{2,1,0:T(8,128)(2,1)}), bf16[32,8,1024]{2,1,0:T(8,128)(2,1)}, u32[]{:S(2)}, u32[]{:S(2)}) async-start(bf16[32,8,1024]{2,1,0:T(8,128)(2,1)} %bitcast.72), calls=%async_computation | async-start | bytes 1048576 | tf_op jit(solution)/shard_map/all_to_all | solution.py:551
  30.2 1.0 copy-start
  31.2 14.4 %collective-permute-start.5 = (bf16[144,1024]{1,0:T(8,128)(2,1)}, bf16[144,1024]{1,0:T(8,128)(2,1)S(1)}, u32[]{:S(2)}, u32[]{:S(2)}) collective-permute-start(bf16[144,1024]{1,0:T(8,128)(2,1)} %get-tuple-element.450), channel_id=1, source_target_pairs={{0,64},{8,72},{1,65},{9,73},{2,66},{10,74},{3,67},{11,75},{4,68},{... | collective-permute-start | bytes 884744 | tf_op jit(solution)/shard_map/ppermute | solution.py:580
  34.2 14.3 %collective-permute-start.6 = (bf16[144,1024]{1,0:T(8,128)(2,1)}, bf16[144,1024]{1,0:T(8,128)(2,1)S(1)}, u32[]{:S(2)}, u32[]{:S(2)}) collective-permute-start(bf16[144,1024]{1,0:T(8,128)(2,1)} %get-tuple-element.451), channel_id=1, source_target_pairs={{0,128},{8,136},{1,129},{9,137},{2,130},{10,138},{3,131},{11,139},... | collective-permute-start | bytes 884744 | tf_op jit(solution)/shard_map/ppermute | solution.py:580
  36.4 12.1 %collective-permute-start.7 = (bf16[144,1024]{1,0:T(8,128)(2,1)}, bf16[144,1024]{1,0:T(8,128)(2,1)S(1)}, u32[]{:S(2)}, u32[]{:S(2)}) collective-permute-start(bf16[144,1024]{1,0:T(8,128)(2,1)} %get-tuple-element.452), channel_id=1, source_target_pairs={{0,192},{8,200},{1,193},{9,201},{2,194},{10,202},{3,195},{11,203},... | collective-permute-start | bytes 884744 | tf_op jit(solution)/shard_map/ppermute | solution.py:580
  38.8 17.2 %collective-permute-start = (bf16[384,512]{1,0:T(8,128)(2,1)}, bf16[384,512]{1,0:T(8,128)(2,1)}, u32[]{:S(2)}, u32[]{:S(2)}) collective-permute-start(bf16[384,512]{1,0:T(8,128)(2,1)} %get-tuple-element.538), channel_id=1, source_target_pairs={{0,2},{1,3},{8,10},{9,11},{16,18},{17,19},{24,26},{25,27},{32,34},... | collective-permute-start | bytes 1179656 | tf_op jit(solution)/shard_map/ppermute | solution.py:555
  42.7 15.2 %collective-permute-start.1 = (bf16[384,512]{1,0:T(8,128)(2,1)}, bf16[384,512]{1,0:T(8,128)(2,1)}, u32[]{:S(2)}, u32[]{:S(2)}) collective-permute-start(bf16[384,512]{1,0:T(8,128)(2,1)} %get-tuple-element.537), channel_id=1, source_target_pairs={{0,4},{1,5},{8,12},{9,13},{16,20},{17,21},{24,28},{25,29},{32,36},... | collective-permute-start | bytes 1179656 | tf_op jit(solution)/shard_map/ppermute | solution.py:555
  45.6 12.2 %collective-permute-start.2 = (bf16[384,512]{1,0:T(8,128)(2,1)}, bf16[384,512]{1,0:T(8,128)(2,1)}, u32[]{:S(2)}, u32[]{:S(2)}) collective-permute-start(bf16[384,512]{1,0:T(8,128)(2,1)} %get-tuple-element.536), channel_id=1, source_target_pairs={{0,6},{1,7},{8,14},{9,15},{16,22},{17,23},{24,30},{25,31},{32,38},... | collective-permute-start | bytes 1179656 | tf_op jit(solution)/shard_map/ppermute | solution.py:555
  50.2 0.7 copy-start.3
  50.9 8.2 %collective-permute-start.8 = (bf16[128,1024]{1,0:T(8,128)(2,1)}, bf16[128,1024]{1,0:T(8,128)(2,1)}, u32[]{:S(2)}, u32[]{:S(2)}) collective-permute-start(bf16[128,1024]{1,0:T(8,128)(2,1)} %get-tuple-element.453), channel_id=1, source_target_pairs={{0,32},{8,40},{64,96},{72,104},{128,160},{136,168},{192,224},{200,... | collective-permute-start | bytes 786440 | tf_op jit(solution)/shard_map/ppermute | solution.py:592
  53.1 0.7 copy-start.6
  55.1 4.4 %collective-permute-start.3 = (bf16[32,1024]{1,0:T(8,128)(2,1)S(1)}, bf16[32,1024]{1,0:T(8,128)(2,1)S(1)}, u32[]{:S(2)}, u32[]{:S(2)}) collective-permute-start(bf16[32,1024]{1,0:T(8,128)(2,1)S(1)} %block.1.block_ref), channel_id=1, source_target_pairs={{0,8},{8,16},{16,24},{24,32},{32,40},{40,48},{48,56},{56,0},{64,72... | collective-permute-start | bytes 196616 | tf_op jit(solution)/shard_map/ppermute | solution.py:585
  56.0 3.9 %collective-permute-start.4 = (bf16[32,1024]{1,0:T(8,128)(2,1)S(1)}, bf16[32,1024]{1,0:T(8,128)(2,1)S(1)}, u32[]{:S(2)}, u32[]{:S(2)}) collective-permute-start(bf16[32,1024]{1,0:T(8,128)(2,1)S(1)} %block.1.block_ref), channel_id=1, source_target_pairs={{0,56},{8,0},{16,8},{24,16},{32,24},{40,32},{48,40},{56,48},{64,12... | collective-permute-start | bytes 196616 | tf_op jit(solution)/shard_map/ppermute | solution.py:586
  59.9 27.2 %collective-permute-start.9 = (bf16[384,512]{1,0:T(8,128)(2,1)S(1)}, bf16[384,512]{1,0:T(8,128)(2,1)S(1)}, u32[]{:S(2)}, u32[]{:S(2)}) collective-permute-start(bf16[384,512]{1,0:T(8,128)(2,1)S(1)} %choose.1.mine_ref), channel_id=1, source_target_pairs={{0,2},{1,3},{2,4},{3,5},{4,6},{5,7},{6,0},{7,1},{8,10},{9,11},{10,... | collective-permute-start | bytes 1179656 | tf_op jit(solution)/shard_map/ppermute | solution.py:610
  61.1 26.0 %collective-permute-start.10 = (bf16[384,512]{1,0:T(8,128)(2,1)S(1)}, bf16[384,512]{1,0:T(8,128)(2,1)S(1)}, u32[]{:S(2)}, u32[]{:S(2)}) collective-permute-start(bf16[384,512]{1,0:T(8,128)(2,1)S(1)} %choose.1.mine_ref), channel_id=1, source_target_pairs={{2,0},{3,1},{4,2},{5,3},{6,4},{7,5},{0,6},{1,7},{10,8},{11,9},{12,... | collective-permute-start | bytes 1179656 | tf_op jit(solution)/shard_map/ppermute | solution.py:611
  62.6 12.2 %collective-permute-start.13 = (bf16[32,1024]{1,0:T(8,128)(2,1)S(1)}, bf16[32,1024]{1,0:T(8,128)(2,1)S(1)}, u32[]{:S(2)}, u32[]{:S(2)}) collective-permute-start(bf16[32,1024]{1,0:T(8,128)(2,1)S(1)} %block.1.block_ref), channel_id=1, source_target_pairs={{0,32},{8,40},{16,48},{24,56},{32,0},{40,8},{48,16},{56,24},{64,96... | collective-permute-start | bytes 196616 | tf_op jit(solution)/shard_map/ppermute | solution.py:587
  65.8 0.9 copy-start.4
  67.7 7.3 %collective-permute-start.14 = (bf16[32,1024]{1,0:T(8,128)(2,1)S(1)}, bf16[32,1024]{1,0:T(8,128)(2,1)S(1)}, u32[]{:S(2)}, u32[]{:S(2)}) collective-permute-start(bf16[32,1024]{1,0:T(8,128)(2,1)S(1)} %get-tuple-element.462), channel_id=1, source_target_pairs={{0,8},{8,16},{32,40},{40,48},{64,72},{72,80},{96,104},{104,112},{1... | collective-permute-start | bytes 196616 | tf_op jit(solution)/shard_map/ppermute | solution.py:606
  70.7 7.8 %collective-permute-start.15 = (bf16[32,1024]{1,0:T(8,128)(2,1)S(1)}, bf16[32,1024]{1,0:T(8,128)(2,1)S(1)}, u32[]{:S(2)}, u32[]{:S(2)}) collective-permute-start(bf16[32,1024]{1,0:T(8,128)(2,1)S(1)} %get-tuple-element.463), channel_id=1, source_target_pairs={{0,16},{8,24},{32,48},{40,56},{64,80},{72,88},{96,112},{104,120},{... | collective-permute-start | bytes 196616 | tf_op jit(solution)/shard_map/ppermute | solution.py:606
  74.9 12.2 %collective-permute-start.11 = (bf16[64,1024]{1,0:T(8,128)(2,1)S(1)}, bf16[64,1024]{1,0:T(8,128)(2,1)S(1)}, u32[]{:S(2)}, u32[]{:S(2)}) collective-permute-start(bf16[64,1024]{1,0:T(8,128)(2,1)S(1)} %get-tuple-element.456), channel_id=1, source_target_pairs={{0,16},{8,24},{16,32},{24,40},{32,48},{40,56},{48,0},{56,8},{64,80... | collective-permute-start | bytes 393224 | tf_op jit(solution)/shard_map/ppermute | solution.py:599
  75.0 12.1 %collective-permute-start.12 = (bf16[64,1024]{1,0:T(8,128)(2,1)S(1)}, bf16[64,1024]{1,0:T(8,128)(2,1)S(1)}, u32[]{:S(2)}, u32[]{:S(2)}) collective-permute-start(bf16[64,1024]{1,0:T(8,128)(2,1)S(1)} %get-tuple-element.458), channel_id=1, source_target_pairs={{0,48},{8,56},{16,0},{24,8},{32,16},{40,24},{48,32},{56,40},{64,11... | collective-permute-start | bytes 393224 | tf_op jit(solution)/shard_map/ppermute | solution.py:600
  78.5 8.6 %collective-permute-start.16 = (bf16[32,1024]{1,0:T(8,128)(2,1)S(1)}, bf16[32,1024]{1,0:T(8,128)(2,1)S(1)}, u32[]{:S(2)}, u32[]{:S(2)}) collective-permute-start(bf16[32,1024]{1,0:T(8,128)(2,1)S(1)} %get-tuple-element.464), channel_id=1, source_target_pairs={{0,24},{8,32},{32,56},{40,0},{64,88},{72,96},{96,120},{104,64},{12... | collective-permute-start | bytes 196616 | tf_op jit(solution)/shard_map/ppermute | solution.py:606
  87.2 18.0 %collective-permute-start.18 = (bf16[256,1024]{1,0:T(8,128)(2,1)S(1)}, bf16[256,1024]{1,0:T(8,128)(2,1)S(1)}, u32[]{:S(2)}, u32[]{:S(2)}) collective-permute-start(bf16[256,1024]{1,0:T(8,128)(2,1)S(1)} %line.1.line_ref.y0_ref), channel_id=1, source_target_pairs={{0,64},{8,72},{16,80},{24,88},{32,96},{40,104},{48,112},{56,120},{... | collective-permute-start | bytes 1572872 | tf_op jit(solution)/shard_map/ppermute | solution.py:628
  87.7 17.4 %collective-permute-start.19 = (bf16[256,1024]{1,0:T(8,128)(2,1)S(1)}, bf16[256,1024]{1,0:T(8,128)(2,1)S(1)}, u32[]{:S(2)}, u32[]{:S(2)}) collective-permute-start(bf16[256,1024]{1,0:T(8,128)(2,1)S(1)} %line.1.line_ref.y0_ref), channel_id=1, source_target_pairs={{0,192},{8,200},{16,208},{24,216},{32,224},{40,232},{48,240},{56,2... | collective-permute-start | bytes 1572872 | tf_op jit(solution)/shard_map/ppermute | solution.py:629
  90.6 37.4 %copy-start.1 = (bf16[2,512,512]{2,1,0:T(8,128)(2,1)S(1)}, bf16[2,512,512]{2,1,0:T(8,128)(2,1)}, u32[]{:S(2)}) copy-start(bf16[2,512,512]{2,1,0:T(8,128)(2,1)} %copy-done) | copy-start | bytes 3145732
  90.6 6.8 %collective-permute-start.20 = (bf16[192,512]{1,0:T(8,128)(2,1)S(1)}, bf16[192,512]{1,0:T(8,128)(2,1)S(1)}, u32[]{:S(2)}, u32[]{:S(2)}) collective-permute-start(bf16[192,512]{1,0:T(8,128)(2,1)S(1)} %get-tuple-element.469.own_ref), channel_id=1, source_target_pairs={{0,2},{1,3},{8,10},{9,11},{16,18},{17,19},{24,26},{25,27},{32,34},... | collective-permute-start | bytes 589832 | tf_op jit(solution)/shard_map/ppermute | solution.py:638
  92.4 12.8 %collective-permute-start.17 = (bf16[384,512]{1,0:T(8,128)(2,1)S(1)}, bf16[384,512]{1,0:T(8,128)(2,1)S(1)}, u32[]{:S(2)}, u32[]{:S(2)}) collective-permute-start(bf16[384,512]{1,0:T(8,128)(2,1)S(1)} %choose.1.mine_ref), channel_id=1, source_target_pairs={{0,4},{1,5},{2,6},{3,7},{4,0},{5,1},{6,2},{7,3},{8,12},{9,13},{10,... | collective-permute-start | bytes 1179656 | tf_op jit(solution)/shard_map/ppermute | solution.py:639
  92.8 12.4 %collective-permute-start.21 = (bf16[192,512]{1,0:T(8,128)(2,1)S(1)}, bf16[192,512]{1,0:T(8,128)(2,1)S(1)}, u32[]{:S(2)}, u32[]{:S(2)}) collective-permute-start(bf16[192,512]{1,0:T(8,128)(2,1)S(1)} %get-tuple-element.469.own_ref), channel_id=1, source_target_pairs={{0,4},{1,5},{8,12},{9,13},{16,20},{17,21},{24,28},{25,29},{32,36},... | collective-permute-start | bytes 589832 | tf_op jit(solution)/shard_map/ppermute | solution.py:638
  97.4 7.7 %collective-permute-start.22 = (bf16[192,512]{1,0:T(8,128)(2,1)S(1)}, bf16[192,512]{1,0:T(8,128)(2,1)S(1)}, u32[]{:S(2)}, u32[]{:S(2)}) collective-permute-start(bf16[192,512]{1,0:T(8,128)(2,1)S(1)} %get-tuple-element.469.own_ref), channel_id=1, source_target_pairs={{0,6},{1,7},{8,14},{9,15},{16,22},{17,23},{24,30},{25,31},{32,38},... | collective-permute-start | bytes 589832 | tf_op jit(solution)/shard_map/ppermute | solution.py:638
  105.8 20.6 %collective-permute-start.23 = (bf16[1536,512]{1,0:T(8,128)(2,1)S(1)}, bf16[1536,512]{1,0:T(8,128)(2,1)S(1)}, u32[]{:S(2)}, u32[]{:S(2)}) collective-permute-start(bf16[1536,512]{1,0:T(8,128)(2,1)S(1)} %part.1.part_ref), channel_id=1, source_target_pairs={{0,1},{1,0},{2,3},{3,2},{4,5},{5,4},{6,7},{7,6},{8,9},{9,8},{10,11... | collective-permute-start | bytes 4718600 | tf_op jit(solution)/shard_map/ppermute | solution.py:665
  111.4 6.4 %collective-permute-start.24 = (bf16[128,512]{1,0:T(8,128)(2,1)S(1)}, bf16[128,512]{1,0:T(8,128)(2,1)S(1)}, u32[]{:S(2)}, u32[]{:S(2)}) collective-permute-start(bf16[128,512]{1,0:T(8,128)(2,1)S(1)} %get-tuple-element.474.refs_0_), channel_id=1, source_target_pairs={{0,64},{8,72},{16,80},{24,88},{32,96},{40,104},{48,112},{56,120},{... | collective-permute-start | bytes 393224 | tf_op jit(solution)/shard_map/ppermute | solution.py:654
  112.4 13.9 %collective-permute-start.27 = (bf16[128,1024]{1,0:T(8,128)(2,1)S(1)}, bf16[128,1024]{1,0:T(8,128)(2,1)S(1)}, u32[]{:S(2)}, u32[]{:S(2)}) collective-permute-start(bf16[128,1024]{1,0:T(8,128)(2,1)S(1)} %slice.131), channel_id=1, source_target_pairs={{0,64},{8,72},{16,80},{24,88},{32,96},{40,104},{48,112},{56,120},{... | collective-permute-start | bytes 786440 | tf_op jit(solution)/shard_map/ppermute | solution.py:644
  114.0 12.4 %collective-permute-start.28 = (bf16[128,1024]{1,0:T(8,128)(2,1)S(1)}, bf16[128,1024]{1,0:T(8,128)(2,1)S(1)}, u32[]{:S(2)}, u32[]{:S(2)}) collective-permute-start(bf16[128,1024]{1,0:T(8,128)(2,1)S(1)} %slice.132), channel_id=1, source_target_pairs={{0,192},{8,200},{16,208},{24,216},{32,224},{40,232},{48,240},{56,2... | collective-permute-start | bytes 786440 | tf_op jit(solution)/shard_map/ppermute | solution.py:645
  115.3 8.9 %collective-permute-start.25 = (bf16[128,512]{1,0:T(8,128)(2,1)S(1)}, bf16[128,512]{1,0:T(8,128)(2,1)S(1)}, u32[]{:S(2)}, u32[]{:S(2)}) collective-permute-start(bf16[128,512]{1,0:T(8,128)(2,1)S(1)} %get-tuple-element.474.refs_0_), channel_id=1, source_target_pairs={{0,192},{8,200},{16,208},{24,216},{32,224},{40,232},{48,240},{56,2... | collective-permute-start | bytes 393224 | tf_op jit(solution)/shard_map/ppermute | solution.py:654
  117.9 8.5 %collective-permute-start.26 = (bf16[128,512]{1,0:T(8,128)(2,1)S(1)}, bf16[128,512]{1,0:T(8,128)(2,1)S(1)}, u32[]{:S(2)}, u32[]{:S(2)}) collective-permute-start(bf16[128,512]{1,0:T(8,128)(2,1)S(1)} %get-tuple-element.474.refs_0_), channel_id=1, source_target_pairs={{0,128},{8,136},{16,144},{24,152},{32,160},{40,168},{48,176},{56,1... | collective-permute-start | bytes 393224 | tf_op jit(solution)/shard_map/ppermute | solution.py:654
  126.4 2.5 %collective-permute-start.29 = (bf16[576,512]{1,0:T(8,128)(2,1)S(1)}, bf16[576,512]{1,0:T(8,128)(2,1)S(1)}, u32[]{:S(2)}, u32[]{:S(2)}) collective-permute-start(bf16[576,512]{1,0:T(8,128)(2,1)S(1)} %cross.1.cross_ref), channel_id=1, source_target_pairs={{0,1},{1,0},{2,3},{3,2},{4,5},{5,4},{6,7},{7,6},{8,9},{9,8},{10,11... | collective-permute-start | bytes 1769480 | tf_op jit(solution)/shard_map/ppermute | solution.py:677

commit v5 on v4

--- a/solution.py
+++ b/solution.py
@@ -11,7 +11,7 @@
 N_HOMES = NY * NZ
 PAIR_ROWS = 8
 DEST_ROWS = 32
-LINE_ROWS = 144
+LINE_ROWS = 80
 Z_ORDER = (0, 7, 1, 4, 6, 5, 2, 3)
 Y_ORDER = (0, 3, 1, 2)
 MIB = 1 << 20
@@ -201,10 +201,8 @@
     place_ref,
     lower_ref,
     slots_ref,
-    leave0_ref,
-    leave1_ref,
-    leave2_ref,
-    leave3_ref,
+    kept_ref,
+    send_ref,
     passing_ref,
     land_ref,
     flag_ref,
@@ -243,7 +241,8 @@
         dest_r, local_r = split_rows(goal_r[s], panel)
         dest_r = jnp.where(goal_r[s] < 0, -1, dest_r)
         dest_c = jnp.where(goal_c[s] < 0, -1, split_rows(goal_c[s], panel)[0])
-        line_r, line_c = dest_r >> 3, dest_c >> 3
+        line_r = jnp.where(dest_r < 0, -1, dest_r & (NZ - 1))
+        line_c = jnp.where(dest_c < 0, -1, dest_c & (NZ - 1))
         counts = total(
             pick((dest_c == dest_r) & before, 1024) + pick((line_c == line_r) & before, 1), 0
         )
@@ -267,17 +266,16 @@
     land_ref[...] = landing[0:1, :].astype(jnp.int32)
     line = jnp.where(odd, lines[1], lines[0])
     line_rank = jnp.where(odd, line_ranks[1], line_ranks[0])
-    dest = jnp.where(odd, dests[1], dests[0])
-    dest_rank = jnp.where(odd, dest_ranks[1], dest_ranks[0])
-    send_at = jnp.where(line < 0, -1, line * LINE_ROWS + line_rank)
-    choose = jnp.where(iota((NY * LINE_ROWS, panel), 0) == send_at, 1.0, 0.0)
+    send_at = jnp.where(line < 0, -1, ((line - z) & (NZ - 1)) * LINE_ROWS + line_rank)
+    choose = jnp.where(iota((NZ * LINE_ROWS, panel), 0) == send_at, 1.0, 0.0)
     leaving = narrow(dot(narrow(choose), rows_ref[:panel, :]))
-    for k, ref in enumerate((leave0_ref, leave1_ref, leave2_ref, leave3_ref)):
-        ref[...] = leaving[k * LINE_ROWS : (k + 1) * LINE_ROWS]
-    pass_at = jnp.where(line == y, ((dest - z) & (NZ - 1)) * DEST_ROWS + dest_rank, -1)
-    passing_ref[...] = total(
-        pick(iota((NZ * DEST_ROWS, panel), 0) == pass_at, line_rank), 1
-    )
+    kept_ref[...] = leaving[: NZ // 2 * LINE_ROWS]
+    send_ref[...] = leaving[NZ // 2 * LINE_ROWS :]
+    for s in range(2):
+        pass_at = jnp.where(lines[s] == z, (dests[s] >> 3) * DEST_ROWS + dest_ranks[s], -1)
+        passing_ref[s * NY * DEST_ROWS : (s + 1) * NY * DEST_ROWS, :] = total(
+            pick(iota((NY * DEST_ROWS, panel), 0) == pass_at, line_ranks[s]), 1
+        )
     for s in range(2):
         order = narrow(jnp.where(number_c == place_ref[s : s + 1, :], 1.0, 0.0))
         low_ref[s] = narrow(
@@ -324,39 +322,60 @@
             out_ref[...] = ref[...]
 
 
-def spread_kernel(pos_ref, passing_ref, own_ref, one_ref, two_ref, three_ref, keep_ref, send_ref):
-    y = pos_ref[0] >> 3
-    on_line = by_x(y, own_ref[...], one_ref[...], two_ref[...], three_ref[...])
-    n_rows = passing_ref.shape[0]
-    choose = jnp.where(passing_ref[...] == iota((n_rows, LINE_ROWS), 1), 1.0, 0.0)
-    spread = narrow(dot(narrow(choose), on_line))
-    keep_ref[...] = spread[: n_rows // 2]
-    send_ref[...] = spread[n_rows // 2 :]
-
-
 def fold_kernel(pos_ref, kept_ref, came_ref, *out_refs):
     for bit, source in ((0, kept_ref), (4, came_ref)):
 
         @pl.when((pos_ref[0] & 4) == bit)
         def _(source=source):
             for k, ref in enumerate(out_refs):
-                ref[...] = source[k * DEST_ROWS : (k + 1) * DEST_ROWS, :]
-
-
-def gone_kernel(pos_ref, line_ref, *refs):
-    landed, gone_ref, extra_ref = refs[:4], refs[4], refs[5]
+                ref[...] = source[k * LINE_ROWS : (k + 1) * LINE_ROWS, :]
+
+
+def spread_kernel(pos_ref, passing_ref, r0_ref, r1_ref, r2_ref, r3_ref, *refs):
+    out_refs, rows_ref = refs[:NY], refs[NY]
+    landed = (r0_ref, r1_ref, r2_ref, r3_ref)
+    for s in range(2):
+        for k in range(4):
+
+            @pl.when(((pos_ref[0] - s) & 3) == k)
+            def _(k=k):
+                rows_ref[...] = landed[k][...]
+
+        marks = passing_ref[s * NY * DEST_ROWS : (s + 1) * NY * DEST_ROWS, :]
+        choose = jnp.where(marks == iota((NY * DEST_ROWS, LINE_ROWS), 1), 1.0, 0.0)
+        spread = narrow(dot(narrow(choose), rows_ref[...]))
+        for k, ref in enumerate(out_refs):
+            ref[s * DEST_ROWS : (s + 1) * DEST_ROWS, :] = spread[k * DEST_ROWS : (k + 1) * DEST_ROWS]
+
+
+def gone_kernel(pos_ref, line_ref, y0_ref, y1_ref, y2_ref, y3_ref, gone_ref, extra_ref):
+    y = pos_ref[0] >> 3
     width = extra_ref.shape[1]
     half = line_ref.shape[0] // 2
-    for s in range(2):
-        for k in range(4):
-
-            @pl.when(((pos_ref[0] - s) & 3) == k)
-            def _(k=k, s=s):
-                gone_ref[s * DEST_ROWS : (s + 1) * DEST_ROWS, :] = landed[k][...]
-
+    gone_ref[...] = by_x(y, y0_ref[...], y1_ref[...], y2_ref[...], y3_ref[...])
     even = (pos_ref[1] & 1) == 0
     extra_ref[:half, :] = jnp.where(even, line_ref[half:, :width], line_ref[:half, :width])
     extra_ref[half:, :] = gone_ref[:, :width]
+
+
+def settle(land_ref, begin, value, gone):
+    n = value.shape[0]
+    hits = (iota((n, 2 * DEST_ROWS), 0) + begin) == land_ref[...]
+    marks = jnp.where(hits, 1.0, 0.0)
+    hit = jnp.sum(marks, axis=1, keepdims=True) > 0.5
+    return jnp.where(hit, dot(narrow(marks), gone), value.astype(jnp.float32))
+
+
+def settle_kernel(rows_ref, land_ref, gone_ref, out_ref):
+    begin = pl.program_id(0) * rows_ref.shape[0]
+    out_ref[...] = narrow(settle(land_ref, begin, rows_ref[...], gone_ref[...]))
+
+
+def factor_kernel(pos_ref, part_ref, other_ref, upper_ref, out_ref):
+    even = (pos_ref[1] & 1) == 0
+    out_ref[...] = narrow(
+        dot(jnp.where(even, part_ref[...], other_ref[...]), upper_ref[0])
+    )
 
 
 def extra_kernel(pos_ref, own_ref, one_ref, two_ref, three_ref, cross_ref, gone_ref):
@@ -402,8 +421,8 @@
     rows_ref,
     part_ref,
     other_ref,
+    factor_ref,
     land_ref,
-    gone_ref,
     cross_ref,
     cross_other_ref,
     row_first_ref,
@@ -430,7 +449,7 @@
         mine, others = cross_ref[...], cross_other_ref[...]
         from_first = jnp.where(even, mine, others)
         from_second = jnp.where(even, others, mine)
-        gone_first_ref[...] = from_first[panel:]
+        gone_first_ref[...] = narrow(dot(from_first[panel:], upper_ref[0]))
         gone_second_ref[...] = from_second[panel:]
         row_first = row_first_ref[...]
         pivot_second = second_ref[...]
@@ -464,21 +483,12 @@
     def _():
         n = rows_ref.shape[0]
         begin = (step - 1) * n
-        hits = (iota((n, 2 * DEST_ROWS), 0) + begin) == land_ref[...]
-        marks = jnp.where(hits, 1.0, 0.0)
-        hit = jnp.sum(marks, axis=1, keepdims=True) > 0.5
-        marks = narrow(marks)
-
-        def settle(value, gone):
-            return jnp.where(hit, dot(marks, gone), value.astype(jnp.float32))
-
-        mine, others = part_ref[...], other_ref[...]
-        panel_first = settle(jnp.where(even, mine, others), gone_first_ref[...])
-        panel_second = settle(jnp.where(even, others, mine), gone_second_ref[...])
-        factor_first = narrow(dot(narrow(panel_first), upper_ref[0]))
+        second = jnp.where(even, other_ref[...], part_ref[...])
+        factor_first = narrow(settle(land_ref, begin, factor_ref[...], gone_first_ref[...]))
+        panel_second = settle(land_ref, begin, second, gone_second_ref[...])
         mid = narrow(panel_second - dot(factor_first, corner_ref[...]))
         factor_second = narrow(dot(mid, upper_ref[1]))
-        current = settle(rows_ref[...], gone_ref[...])
+        current = rows_ref[...].astype(jnp.float32)
         updated = narrow(
             current
             - dot(factor_first, new_ref[:panel, :])
@@ -553,18 +563,14 @@
     quarter = local_rows // NX
     own = [rows[k * quarter : (k + 1) * quarter, :width] for k in range(NX)]
     got = [lax.ppermute(own[k], "pcol", move_x([(0, k)])) for k in range(1, NX)]
-    (mine,) = local_kernel(
-        choose_kernel, "choose", [shape((quarter, width))], [position], own[0], *got
-    )
-
-    line_shape = shape((LINE_ROWS, local_cols))
-    *leaving, passing, land, flag, low = local_kernel(
+    zs_shape = shape((NZ // 2 * LINE_ROWS, local_cols))
+    kept, send, passing, land, flag, low = local_kernel(
         functools.partial(leave_kernel, panel),
         "leave",
-        [line_shape]
-        + [pltpu.HBM(line_shape.shape, line_shape.dtype)] * (NY - 1)
-        + [
-            shape((NZ * DEST_ROWS, 1), i32),
+        [
+            zs_shape,
+            pltpu.HBM(zs_shape.shape, zs_shape.dtype),
+            shape((2 * NY * DEST_ROWS, 1), i32),
             shape((1, 2 * DEST_ROWS), i32),
             shape((1,), i32),
             shape((2, panel, panel)),
@@ -577,42 +583,58 @@
         slots,
         limit=32,
     )
-    arrived = [lax.ppermute(leaving[s], "prow", shift_y(s, [0], [0, 1])) for s in (1, 2, 3)]
+    came = lax.ppermute(send, "prow", shift_z(4, [0, 1]))
 
     (block,) = local_kernel(
-        block_kernel, "block", [shape((2 * per_home, local_cols))], [], keep, dealt
+        block_kernel, "block", [shape((2 * per_home, local_cols))], [], keep, after(dealt, came)
     )
     from_lo = lax.ppermute(block, "prow", shift_z(1))
     from_hi = lax.ppermute(block, "prow", shift_z(-1))
     opposite = lax.ppermute(block, "prow", shift_z(4))
-    quarter_shape = shape((NZ // 2 * DEST_ROWS, local_cols))
-    kept, send = local_kernel(
-        spread_kernel, "spread", [quarter_shape] * 2, [position], passing, leaving[0], *arrived
-    )
-    came = lax.ppermute(send, "prow", shift_z(4, [0, 1]))
-
-    from_lo, from_hi = after((from_lo, from_hi), came, mine)
+    spread = local_kernel(
+        fold_kernel,
+        "fold",
+        [shape((LINE_ROWS, local_cols))] * 4,
+        [position],
+        kept,
+        after(came, block),
+    )
+    landed = [spread[0]] + [
+        lax.ppermute(spread[k], "prow", shift_z(k, [0, 1, 4, 5])) for k in (1, 2, 3)
+    ]
+
+    (mine,) = local_kernel(
+        choose_kernel, "choose", [shape((quarter, width))], [position], own[0], *after(got, from_lo, from_hi)
+    )
+
+    from_lo, from_hi = after((from_lo, from_hi), landed, mine)
     pair_shape = shape((4 * per_home, local_cols))
     pair_lo, pair_hi = local_kernel(
         pair_kernel, "pair", [pair_shape] * 2, [], block, from_lo, from_hi
     )
     two_lo = lax.ppermute(pair_lo, "prow", shift_z(2))
     two_hi = lax.ppermute(pair_hi, "prow", shift_z(-2))
-    one_shape = shape((DEST_ROWS, local_cols))
-    spread = local_kernel(
-        fold_kernel, "fold", [one_shape] * 4, [position], kept, after(came, pair_lo)
-    )
-    landed = [spread[0]] + [
-        lax.ppermute(spread[k], "prow", shift_z(k, [0, 1, 4, 5])) for k in (1, 2, 3)
-    ]
+    n_gone = 2 * DEST_ROWS
+    gone_shape = shape((n_gone, local_cols))
+    going = pl.pallas_call(
+        spread_kernel,
+        grid=(1,),
+        in_specs=[smem(), whole((2 * NY * DEST_ROWS, 1))] + [whole((LINE_ROWS, local_cols))] * 4,
+        out_specs=[whole((n_gone, local_cols))] * NY,
+        out_shape=[gone_shape] * NY,
+        scratch_shapes=[pltpu.VMEM((LINE_ROWS, local_cols), jnp.bfloat16)],
+        compiler_params=pltpu.CompilerParams(vmem_limit_bytes=12 * MIB),
+        cost_estimate=pl.CostEstimate(flops=0, bytes_accessed=0, transcendentals=0),
+        name="spread",
+    )(position, passing, *after(landed, pair_lo))
+    ending = [going[0]] + [lax.ppermute(going[k], "prow", shift_y(k, [0])) for k in (1, 2, 3)]
     quarter_out = after(mine, pair_lo)
     ring = [(x, (x + 1) % NX) for x in range(NX)]
     before = lax.ppermute(quarter_out, "pcol", move_x(ring))
     behind = lax.ppermute(quarter_out, "pcol", move_x([(b, a) for a, b in ring]))
 
-    two_lo, two_hi, opposite = after((two_lo, two_hi, opposite), before, behind, landed)
+    two_lo, two_hi, opposite = after((two_lo, two_hi, opposite), before, behind, ending)
     half = panel // NY
-    n_gone = 2 * DEST_ROWS
     (z_line,) = local_kernel(
         line_kernel,
         "line",
@@ -630,17 +652,33 @@
     gone, extra = local_kernel(
         gone_kernel,
         "gone",
-        [shape((n_gone, local_cols)), shape((half + n_gone, width))],
+        [gone_shape, shape((half + n_gone, width))],
         [position],
         z_line,
-        *landed,
-    )
+        *ending,
+    )
+    n_block = panel // 2
+    steps = local_rows // n_block
+
+    def block_of(cols, lead=0):
+        return pl.BlockSpec((n_block, cols), lambda i: (jnp.maximum(i - lead, 0), 0))
+
+    settled = pl.pallas_call(
+        settle_kernel,
+        grid=(steps,),
+        in_specs=[block_of(local_cols), whole((1, n_gone)), whole((n_gone, local_cols))],
+        out_specs=block_of(local_cols),
+        out_shape=shape((local_rows, local_cols)),
+        compiler_params=pltpu.CompilerParams(vmem_limit_bytes=16 * MIB),
+        cost_estimate=pl.CostEstimate(flops=0, bytes_accessed=0, transcendentals=0),
+        name="settle",
+    )(rows, land, gone)
     sent = [lax.ppermute(extra, "pcol", move_x([(0, k)])) for k in (1, 2, 3)]
     across = lax.ppermute(
         after(mine, z_line), "pcol", move_x([(x, (x + 2) % NX) for x in range(NX)])
     )
 
-    y_lo, y_hi = after((y_lo, y_hi), sent, across)
+    y_lo, y_hi = after((y_lo, y_hi), sent, across, settled)
     far_first = lax.ppermute(y_lo[:half], "prow", shift_y(1))
     far_second = lax.ppermute(y_hi[half:], "prow", shift_y(-1))
     cross, gone_panel = local_kernel(
@@ -663,8 +701,18 @@
         after(across, y_lo),
     )
     other = lax.ppermute(part, "pcol", SWAP)
-
-    crossed = after(crossed, far_first, far_second, other)
+    factor_raw = pl.pallas_call(
+        factor_kernel,
+        grid=(steps,),
+        in_specs=[smem(), block_of(width), block_of(width), whole((2, panel, panel))],
+        out_specs=block_of(width),
+        out_shape=shape((local_rows, width)),
+        compiler_params=pltpu.CompilerParams(vmem_limit_bytes=16 * MIB),
+        cost_estimate=pl.CostEstimate(flops=0, bytes_accessed=0, transcendentals=0),
+        name="factor",
+    )(position, part, other, upper_inverse)
+
+    crossed = after(crossed, far_first, far_second, factor_raw)
     (cross,) = local_kernel(
         cross_kernel,
         "cross",
@@ -690,22 +738,16 @@
         name="first",
     )(low, z_line, y_lo, y_hi, far_first, far_second)
 
-    n_block = panel // 2
-    steps = local_rows // n_block
-
-    def row_block(cols):
-        return pl.BlockSpec((n_block, cols), lambda i: (jnp.maximum(i - 1, 0), 0))
-
     result = pl.pallas_call(
         functools.partial(finish_kernel, panel),
         grid=(steps + 1,),
         in_specs=[
             smem(),
-            row_block(local_cols),
-            row_block(width),
-            row_block(width),
+            block_of(local_cols, 1),
+            block_of(width, 1),
+            block_of(width, 1),
+            block_of(width, 1),
             whole((1, 2 * DEST_ROWS)),
-            whole((2 * DEST_ROWS, local_cols)),
             whole((panel + 2 * DEST_ROWS, width)),
             whole((panel + 2 * DEST_ROWS, width)),
             whole((panel, local_cols)),
@@ -715,7 +757,7 @@
             whole((2, panel, panel)),
             whole((2, panel)),
         ],
-        out_specs=row_block(local_cols),
+        out_specs=block_of(local_cols, 1),
         out_shape=shape((local_rows, local_cols)),
         scratch_shapes=[
             pltpu.VMEM((2 * panel, local_cols), jnp.bfloat16),
@@ -726,7 +768,7 @@
         ],
         compiler_params=pltpu.CompilerParams(vmem_limit_bytes=32 * MIB),
         name="finish",
-    )(position, rows, part, other, land, gone, cross, cross_other, row_first, second, a00, low, upper_inverse, place)
+    )(position, settled, part, other, factor_raw, land, cross, cross_other, row_first, second, a00, low, upper_inverse, place)
     result = result.reshape(matrix.shape)
     return lax.cond(
         flag[0] > 0,

time: 158 us -> 173 us (1.095)
  waiting for transfers between devices: 23.6 us -> 32.7 us
  starting transfers between devices: 74.1 us -> 76.8 us
  local copies, waits for them, and re-layouts: 14.7 us -> 17 us
    ppermute x1, waiting for transfers between devices: 0.01 us -> 6.88 us  [per_device(): opposite = lax.ppermute(block, 'prow', shift_z(4))]
    pallas_call x0 -> x3, Pallas kernels: none -> 6.04 us  [the longest x1 3.19 us: per_device(): pl.pallas_call(factor_kernel, grid=(steps,), in_specs=[smem(), block_of(w...]
    ppermute x1, starting transfers between devices: 0.92 us -> 6.36 us  [per_device(): from_lo = lax.ppermute(block, 'prow', shift_z(1))]
    ppermute x1, starting transfers between devices: 2.22 us -> 6.99 us  [per_device(): came = lax.ppermute(send, 'prow', shift_z(4, [0, 1]))]
    ppermute x3, starting transfers between devices: 9.55 us -> 5.07 us  [per_device(): lax.ppermute(spread[k], 'prow', shift_z(k, [0, 1, 4, 5]))]
    ppermute x3, waiting for transfers between devices: 9.04 us -> 5.35 us  [per_device(): crossed = [lax.ppermute(cross, 'prow', shift_y(s)) for s in (1, -1, 2)]]
    ppermute x1, waiting for transfers between devices: 0.01 us -> 3.46 us  [per_device(): came = lax.ppermute(send, 'prow', shift_z(4, [0, 1]))]
    pallas_call x1, Pallas kernels: 14.2 us -> 11.8 us  [per_device(): pl.pallas_call(functools.partial(finish_kernel, panel), grid=(steps + 1,)...]
  transfers between devices with their start and end apart: 31 -> 31, of which waited for: 9 -> 13; matrix products, arithmetic and copies ran while one was open for 1% -> 1% of each run, Pallas kernels for 7% -> 9%
where the time goes in v5:
time: 173 us; the launch traced here: 172 us
  starting transfers between devices  76.8 us (44%)
  waiting for transfers between devices  32.7 us (19%)
  Pallas kernels  30.9 us (18%)
  local copies, waits for them, and re-layouts  17 us (10%)
  between operations  14.4 us (8%)
    pallas_call x11, Pallas kernels, local_kernel(): pl.pallas_call(body, grid=(1,), in_specs=[smem() for _ in scalars] + [who...  12.3 us
    all_to_all x1, starting transfers between devices, per_device(): dealt = lax.all_to_all(picks, 'prow', 0, 0, tiled=True)  12.2 us
    pallas_call x1, Pallas kernels, per_device(): pl.pallas_call(functools.partial(finish_kernel, panel), grid=(steps + 1,)...  11.8 us
    unnamed x25, local copies, waits for them, and re-layouts  9.76 us
    ppermute x3, starting transfers between devices, per_device(): got = [lax.ppermute(own[k], 'pcol', move_x([(0, k)])) for k in range(1, NX)]  8.86 us
    ppermute x3, starting transfers between devices, per_device(): sent = [lax.ppermute(extra, 'pcol', move_x([(0, k)])) for k in (1, 2, 3)]  7.84 us
    ppermute x1, starting transfers between devices, per_device(): came = lax.ppermute(send, 'prow', shift_z(4, [0, 1]))  6.99 us
    ppermute x1, waiting for transfers between devices, per_device(): opposite = lax.ppermute(block, 'prow', shift_z(4))  6.88 us
  transfers between devices with their start and end apart: 31, of which 13 were waited for; matrix products, arithmetic and copies ran while one was open for 1% of the time, Pallas kernels for 9%

profile of v5, /device:TPU:1, one launch (start us, length us, event | category | flops | bytes accessed | tf_op | source)
XLA Modules:
  0.0 171.9 jit_solution(13127876412173289056)
XLA Ops:
  6.5 2.8 %copy.13 = bf16[192,8,2,512]{3,1,2,0:T(8,128)(2,1)S(1)} copy(bf16[192,8,2,512]{3,2,1,0:T(2,128)(2,1)} %bitcast.74) | data formatting | bytes 6291456
  9.4 2.9 %deal.1 = (bf16[256,1024]{1,0:T(8,128)(2,1)S(1)}, s32[32,1]{1,0:T(8,128)S(1)}, s32[2,512]{1,0:T(2,128)S(1)}, s32[1,512]{1,0:T(1,128)S(1)}) custom-call(s32[2]{0:T(128)S(1)} %pad_add_fusion.pos_ref, s32[2,512]{1,0:T(2,128)S(1)} %copy-done.13, bf16[1536,1024]{1,0:T(8,128)(2,1)S(1)} %bitcast.68), custom_call_target="tpu_custom_call" | custom-call | tf_op jit(solution)/shard_map/deal/pallas_call | solution.py:521
  13.7 12.2 %all-to-all-start = ((bf16[32,8,1024]{2,1,0:T(8,128)(2,1)}), bf16[32,8,1024]{2,1,0:T(8,128)(2,1)}, u32[]{:S(2)}, u32[]{:S(2)}) async-start(bf16[32,8,1024]{2,1,0:T(8,128)(2,1)} %bitcast.72), calls=%async_computation | async-start | bytes 1048576 | tf_op jit(solution)/shard_map/all_to_all | solution.py:561
  25.8 4.4 %leave.1 = (bf16[320,1024]{1,0:T(8,128)(2,1)S(1)}, bf16[320,1024]{1,0:T(8,128)(2,1)}, s32[256,1]{1,0:T(8,128)S(1)}, s32[1,64]{1,0:T(1,128)S(1)}, s32[1]{0:T(128)}, /*index=5*/bf16[2,512,512]{2,1,0:T(8,128)(2,1)S(1)}) custom-call(s32[2]{0:T(128)S(1)} %pad_add_fusion.pos_ref, s32[2,512]{1,0:T(2,128)S(1)} %copy-done.13, bf16[1536,1024]{1,0:T(8,128)(2,1)S(1)} %bitcast.69, ...), custom_call_target="tpu_custom_call" | custom-call | tf_op jit(solution)/shard_map/leave/pallas_call | solution.py:521
  32.1 7.0 %collective-permute-start = (bf16[320,1024]{1,0:T(8,128)(2,1)}, bf16[320,1024]{1,0:T(8,128)(2,1)S(1)}, u32[]{:S(2)}, u32[]{:S(2)}) collective-permute-start(bf16[320,1024]{1,0:T(8,128)(2,1)} %get-tuple-element.457), channel_id=1, source_target_pairs={{0,32},{8,40},{64,96},{72,104},{128,160},{136,168},{192,224},{200,... | collective-permute-start | bytes 1966088 | tf_op jit(solution)/shard_map/ppermute | solution.py:586
  39.1 1.1 fusion.28
  40.1 3.9 %collective-permute-start.6 = (bf16[384,512]{1,0:T(8,128)(2,1)}, bf16[384,512]{1,0:T(8,128)(2,1)}, u32[]{:S(2)}, u32[]{:S(2)}) collective-permute-start(bf16[384,512]{1,0:T(8,128)(2,1)} %get-tuple-element.554), channel_id=1, source_target_pairs={{0,2},{1,3},{8,10},{9,11},{16,18},{17,19},{24,26},{25,27},{32,34},... | collective-permute-start | bytes 1179656 | tf_op jit(solution)/shard_map/ppermute | solution.py:565
  44.0 2.9 %collective-permute-start.7 = (bf16[384,512]{1,0:T(8,128)(2,1)}, bf16[384,512]{1,0:T(8,128)(2,1)}, u32[]{:S(2)}, u32[]{:S(2)}) collective-permute-start(bf16[384,512]{1,0:T(8,128)(2,1)} %get-tuple-element.553), channel_id=1, source_target_pairs={{0,4},{1,5},{8,12},{9,13},{16,20},{17,21},{24,28},{25,29},{32,36},... | collective-permute-start | bytes 1179656 | tf_op jit(solution)/shard_map/ppermute | solution.py:565
  47.0 2.0 %collective-permute-start.8 = (bf16[384,512]{1,0:T(8,128)(2,1)}, bf16[384,512]{1,0:T(8,128)(2,1)}, u32[]{:S(2)}, u32[]{:S(2)}) collective-permute-start(bf16[384,512]{1,0:T(8,128)(2,1)} %get-tuple-element.552), channel_id=1, source_target_pairs={{0,6},{1,7},{8,14},{9,15},{16,22},{17,23},{24,30},{25,31},{32,38},... | collective-permute-start | bytes 1179656 | tf_op jit(solution)/shard_map/ppermute | solution.py:565
  49.0 3.5 %collective-permute-done.came_ref = bf16[320,1024]{1,0:T(8,128)(2,1)S(1)} collective-permute-done((bf16[320,1024]{1,0:T(8,128)(2,1)}, bf16[320,1024]{1,0:T(8,128)(2,1)S(1)}, u32[]{:S(2)}, u32[]{:S(2)}) %collective-permute-start) | collective-permute-done | bytes 655392 | tf_op jit(solution)/shard_map/ppermute | solution.py:586
  54.1 1.3 block.1.block_ref
  55.3 1.1 copy-done.3
  56.4 1.1 copy-done.5
  58.1 1.9 %collective-permute-start.3 = (bf16[80,1024]{1,0:T(8,128)(2,1)S(1)}, bf16[80,1024]{1,0:T(8,128)(2,1)S(1)}, u32[]{:S(2)}, u32[]{:S(2)}) collective-permute-start(bf16[80,1024]{1,0:T(8,128)(2,1)S(1)} %get-tuple-element.462), channel_id=1, source_target_pairs={{0,8},{8,16},{32,40},{40,48},{64,72},{72,80},{96,104},{104,112},{1... | collective-permute-start | bytes 491528 | tf_op jit(solution)/shard_map/ppermute | solution.py:603
  60.0 1.3 collective-permute-start.4
  61.3 1.9 %collective-permute-start.5 = (bf16[80,1024]{1,0:T(8,128)(2,1)S(1)}, bf16[80,1024]{1,0:T(8,128)(2,1)S(1)}, u32[]{:S(2)}, u32[]{:S(2)}) collective-permute-start(bf16[80,1024]{1,0:T(8,128)(2,1)S(1)} %get-tuple-element.464), channel_id=1, source_target_pairs={{0,24},{8,32},{32,56},{40,0},{64,88},{72,96},{96,120},{104,64},{12... | collective-permute-start | bytes 491528 | tf_op jit(solution)/shard_map/ppermute | solution.py:603
  63.2 6.4 %collective-permute-start.1 = (bf16[32,1024]{1,0:T(8,128)(2,1)S(1)}, bf16[32,1024]{1,0:T(8,128)(2,1)S(1)}, u32[]{:S(2)}, u32[]{:S(2)}) collective-permute-start(bf16[32,1024]{1,0:T(8,128)(2,1)S(1)} %block.1.block_ref), channel_id=1, source_target_pairs={{0,8},{8,16},{16,24},{24,32},{32,40},{40,48},{48,56},{56,0},{64,72... | collective-permute-start | bytes 196616 | tf_op jit(solution)/shard_map/ppermute | solution.py:591
  69.6 2.0 %collective-permute-done.1.lo_ref = bf16[32,1024]{1,0:T(8,128)(2,1)S(1)} collective-permute-done((bf16[32,1024]{1,0:T(8,128)(2,1)S(1)}, bf16[32,1024]{1,0:T(8,128)(2,1)S(1)}, u32[]{:S(2)}, u32[]{:S(2)}) %collective-permute-start.1) | collective-permute-done | bytes 65568 | tf_op jit(solution)/shard_map/ppermute | solution.py:591
  71.6 1.1 collective-permute-done.2.hi_ref
  72.7 1.3 choose.1.mine_ref
  74.0 6.9 %collective-permute-done.5.r3_ref = bf16[80,1024]{1,0:T(8,128)(2,1)S(1)} collective-permute-done((bf16[80,1024]{1,0:T(8,128)(2,1)S(1)}, bf16[80,1024]{1,0:T(8,128)(2,1)S(1)}, u32[]{:S(2)}, u32[]{:S(2)}) %collective-permute-start.5) | collective-permute-done | bytes 163872 | tf_op jit(solution)/shard_map/ppermute | solution.py:603
  80.9 1.3 collective-permute-start.12
  82.2 1.5 collective-permute-start.13
  83.7 3.6 %collective-permute-start.10 = (bf16[64,1024]{1,0:T(8,128)(2,1)S(1)}, bf16[64,1024]{1,0:T(8,128)(2,1)S(1)}, u32[]{:S(2)}, u32[]{:S(2)}) collective-permute-start(bf16[64,1024]{1,0:T(8,128)(2,1)S(1)} %get-tuple-element.471), channel_id=1, source_target_pairs={{0,48},{8,56},{16,0},{24,8},{32,16},{40,24},{48,32},{56,40},{64,11... | collective-permute-start | bytes 393224 | tf_op jit(solution)/shard_map/ppermute | solution.py:616
  87.2 1.5 collective-permute-start.11
  88.8 1.1 spread.1
  89.9 6.9 %collective-permute-done.11.opposite_ref = bf16[32,1024]{1,0:T(8,128)(2,1)S(1)} collective-permute-done((bf16[32,1024]{1,0:T(8,128)(2,1)S(1)}, bf16[32,1024]{1,0:T(8,128)(2,1)S(1)}, u32[]{:S(2)}, u32[]{:S(2)}) %collective-permute-start.11) | collective-permute-done | bytes 65568 | tf_op jit(solution)/shard_map/ppermute | solution.py:593
  96.8 3.1 %collective-permute-start.14 = (bf16[64,1024]{1,0:T(8,128)(2,1)S(1)}, bf16[64,1024]{1,0:T(8,128)(2,1)S(1)}, u32[]{:S(2)}, u32[]{:S(2)}) collective-permute-start(bf16[64,1024]{1,0:T(8,128)(2,1)S(1)} %get-tuple-element.479), channel_id=1, source_target_pairs={{0,64},{8,72},{16,80},{24,88},{32,96},{40,104},{48,112},{56,120},{... | collective-permute-start | bytes 393224 | tf_op jit(solution)/shard_map/ppermute | solution.py:630
  99.9 2.2 %collective-permute-start.15 = (bf16[64,1024]{1,0:T(8,128)(2,1)S(1)}, bf16[64,1024]{1,0:T(8,128)(2,1)S(1)}, u32[]{:S(2)}, u32[]{:S(2)}) collective-permute-start(bf16[64,1024]{1,0:T(8,128)(2,1)S(1)} %get-tuple-element.480), channel_id=1, source_target_pairs={{0,128},{8,136},{16,144},{24,152},{32,160},{40,168},{48,176},{56,1... | collective-permute-start | bytes 393224 | tf_op jit(solution)/shard_map/ppermute | solution.py:630
  102.1 1.3 collective-permute-start.16
  104.0 1.3 collective-permute-done.16.y3_ref
  105.5 3.2 %collective-permute-start.19 = (bf16[256,1024]{1,0:T(8,128)(2,1)S(1)}, bf16[256,1024]{1,0:T(8,128)(2,1)S(1)}, u32[]{:S(2)}, u32[]{:S(2)}) collective-permute-start(bf16[256,1024]{1,0:T(8,128)(2,1)S(1)} %line.1.line_ref.y0_ref), channel_id=1, source_target_pairs={{0,192},{8,200},{16,208},{24,216},{32,224},{40,232},{48,240},{56,2... | collective-permute-start | bytes 1572872 | tf_op jit(solution)/shard_map/ppermute | solution.py:651
  109.2 1.9 %collective-permute-start.20 = (bf16[192,512]{1,0:T(8,128)(2,1)S(1)}, bf16[192,512]{1,0:T(8,128)(2,1)S(1)}, u32[]{:S(2)}, u32[]{:S(2)}) collective-permute-start(bf16[192,512]{1,0:T(8,128)(2,1)S(1)} %get-tuple-element.487.own_ref), channel_id=1, source_target_pairs={{0,2},{1,3},{8,10},{9,11},{16,18},{17,19},{24,26},{25,27},{32,34},... | collective-permute-start | bytes 589832 | tf_op jit(solution)/shard_map/ppermute | solution.py:676
  111.5 4.6 %collective-permute-start.21 = (bf16[192,512]{1,0:T(8,128)(2,1)S(1)}, bf16[192,512]{1,0:T(8,128)(2,1)S(1)}, u32[]{:S(2)}, u32[]{:S(2)}) collective-permute-start(bf16[192,512]{1,0:T(8,128)(2,1)S(1)} %get-tuple-element.487.own_ref), channel_id=1, source_target_pairs={{0,4},{1,5},{8,12},{9,13},{16,20},{17,21},{24,28},{25,29},{32,36},... | collective-permute-start | bytes 589832 | tf_op jit(solution)/shard_map/ppermute | solution.py:676
  116.1 1.3 collective-permute-start.22
  117.5 1.7 settle.1.rows_ref
  119.2 3.6 %collective-permute-done.21.two_ref = bf16[192,512]{1,0:T(8,128)(2,1)S(1)} collective-permute-done((bf16[192,512]{1,0:T(8,128)(2,1)S(1)}, bf16[192,512]{1,0:T(8,128)(2,1)S(1)}, u32[]{:S(2)}, u32[]{:S(2)}) %collective-permute-start.21) | collective-permute-done | bytes 196640 | tf_op jit(solution)/shard_map/ppermute | solution.py:676
  122.8 1.2 collective-permute-done.22.three_ref
  124.7 5.0 %collective-permute-start.23 = (bf16[1536,512]{1,0:T(8,128)(2,1)S(1)}, bf16[1536,512]{1,0:T(8,128)(2,1)S(1)}, u32[]{:S(2)}, u32[]{:S(2)}) collective-permute-start(bf16[1536,512]{1,0:T(8,128)(2,1)S(1)} %part.1.part_ref), channel_id=1, source_target_pairs={{0,1},{1,0},{2,3},{3,2},{4,5},{5,4},{6,7},{7,6},{8,9},{9,8},{10,11... | collective-permute-start | bytes 4718600 | tf_op jit(solution)/shard_map/ppermute | solution.py:703
  129.8 2.7 %collective-permute-start.28 = (bf16[128,1024]{1,0:T(8,128)(2,1)S(1)}, bf16[128,1024]{1,0:T(8,128)(2,1)S(1)}, u32[]{:S(2)}, u32[]{:S(2)}) collective-permute-start(bf16[128,1024]{1,0:T(8,128)(2,1)S(1)} %slice.132), channel_id=1, source_target_pairs={{0,192},{8,200},{16,208},{24,216},{32,224},{40,232},{48,240},{56,2... | collective-permute-start | bytes 786440 | tf_op jit(solution)/shard_map/ppermute | solution.py:683
  133.2 2.7 %collective-permute-start.25 = (bf16[128,512]{1,0:T(8,128)(2,1)S(1)}, bf16[128,512]{1,0:T(8,128)(2,1)S(1)}, u32[]{:S(2)}, u32[]{:S(2)}) collective-permute-start(bf16[128,512]{1,0:T(8,128)(2,1)S(1)} %get-tuple-element.490.refs_0_), channel_id=1, source_target_pairs={{0,192},{8,200},{16,208},{24,216},{32,224},{40,232},{48,240},{56,2... | collective-permute-start | bytes 393224 | tf_op jit(solution)/shard_map/ppermute | solution.py:692
  135.9 3.2 %factor.1.factor_ref = bf16[1536,512]{1,0:T(8,128)(2,1)S(1)} custom-call(s32[2]{0:T(128)S(1)} %pad_add_fusion.pos_ref, bf16[1536,512]{1,0:T(8,128)(2,1)S(1)} %part.1.part_ref, bf16[1536,512]{1,0:T(8,128)(2,1)S(1)} %collective-permute-done.23.other_ref, bf16[2,512,512]{2,1,0:T(8,128)(2,1)} %upper_ref.3), custom_call_target="tpu_custom_call" | custom-call | tf_op jit(solution)/shard_map/factor/pallas_call | solution.py:704
  139.1 2.7 %collective-permute-done.24.refs_1_ = bf16[128,512]{1,0:T(8,128)(2,1)S(1)} collective-permute-done((bf16[128,512]{1,0:T(8,128)(2,1)S(1)}, bf16[128,512]{1,0:T(8,128)(2,1)S(1)}, u32[]{:S(2)}, u32[]{:S(2)}) %collective-permute-start.24) | collective-permute-done | bytes 131104 | tf_op jit(solution)/shard_map/ppermute | solution.py:692
  141.8 1.6 collective-permute-done.25.refs_2_
  143.4 1.0 collective-permute-done.26.refs_3_
  147.1 11.8 %finish.1 = bf16[1536,1024]{1,0:T(8,128)(2,1)} custom-call(s32[2]{0:T(128)S(1)} %pad_add_fusion.pos_ref, bf16[1536,1024]{1,0:T(8,128)(2,1)S(1)} %settle.1.rows_ref, bf16[1536,512]{1,0:T(8,128)(2,1)S(1)} %part.1.part_ref, bf16[1536,512]{1,0:T(8,128)(2,1)S(1)} %collective-permute-done.23.other_ref, bf16[1536,512]{1,0:T(8,128)(2,1)S(1)} %factor.1.factor_ref, ...), custom_call_target="tpu_custom_call" | custom-call | tf_op jit(solution)/shard_map/finish/pallas_call | solution.py:741
  158.9 6.1 %conditional.2 = (bf16[3,512,2,512]{3,2,1,0:T(2,128)(2,1)}) conditional(s32[]{:T(128)} %bitcast.4, bf16[1536,1024]{1,0:T(8,128)(2,1)} %finish.1, (bf16[3,512,2,512]{3,2,1,0:T(2,128)(2,1)}, s32[2,512]{1,0:T(2,128)S(1)}, bf16[2,512,512]{2,1,0:T(8,128)(2,1)}, bf16[2,512,512]{2,1,0:T(8,128)(2,1)}) %tuple.130), branch_computations={%region_0.0_spmd, %region_1.11_spmd} | conditional | flops 2966474752 | bytes 85029544 | solution.py:773
  158.9 6.1 %reshape.435 = bf16[3,512,2,512]{3,2,1,0:T(2,128)(2,1)} reshape(bf16[1536,1024]{1,0:T(8,128)(2,1)} %param.4) | data formatting | bytes 6291456 | tf_op jit(solution)/shard_map/reshape | solution.py:772
  (61 shorter events, 10.7 us)
Async XLA Ops:
  6.5 2.8 %copy-start.13 = (s32[2,512]{1,0:T(2,128)S(1)}, s32[2,512]{1,0:T(2,128)}, u32[]{:S(2)}) copy-start(s32[2,512]{1,0:T(2,128)} %across_ref.3) | copy-start | bytes 12292
  12.2 0.8 copy-start.6
  13.1 0.6 copy-start.9
  13.7 39.6 %all-to-all-start = ((bf16[32,8,1024]{2,1,0:T(8,128)(2,1)}), bf16[32,8,1024]{2,1,0:T(8,128)(2,1)}, u32[]{:S(2)}, u32[]{:S(2)}) async-start(bf16[32,8,1024]{2,1,0:T(8,128)(2,1)} %bitcast.72), calls=%async_computation | async-start | bytes 1048576 | tf_op jit(solution)/shard_map/all_to_all | solution.py:561
  30.2 1.0 copy-start
  31.2 0.8 copy-start.2
  32.1 14.9 %copy-start.7 = (s32[256,1]{1,0:T(8,128)}, s32[256,1]{1,0:T(8,128)S(1)}, u32[]{:S(2)}) copy-start(s32[256,1]{1,0:T(8,128)S(1)} %get-tuple-element.473.passing_ref) | copy-start | bytes 3076
  32.1 20.4 %collective-permute-start = (bf16[320,1024]{1,0:T(8,128)(2,1)}, bf16[320,1024]{1,0:T(8,128)(2,1)S(1)}, u32[]{:S(2)}, u32[]{:S(2)}) collective-permute-start(bf16[320,1024]{1,0:T(8,128)(2,1)} %get-tuple-element.457), channel_id=1, source_target_pairs={{0,32},{8,40},{64,96},{72,104},{128,160},{136,168},{192,224},{200,... | collective-permute-start | bytes 1966088 | tf_op jit(solution)/shard_map/ppermute | solution.py:586
  40.1 21.2 %collective-permute-start.6 = (bf16[384,512]{1,0:T(8,128)(2,1)}, bf16[384,512]{1,0:T(8,128)(2,1)}, u32[]{:S(2)}, u32[]{:S(2)}) collective-permute-start(bf16[384,512]{1,0:T(8,128)(2,1)} %get-tuple-element.554), channel_id=1, source_target_pairs={{0,2},{1,3},{8,10},{9,11},{16,18},{17,19},{24,26},{25,27},{32,34},... | collective-permute-start | bytes 1179656 | tf_op jit(solution)/shard_map/ppermute | solution.py:565
  44.0 19.2 %collective-permute-start.7 = (bf16[384,512]{1,0:T(8,128)(2,1)}, bf16[384,512]{1,0:T(8,128)(2,1)}, u32[]{:S(2)}, u32[]{:S(2)}) collective-permute-start(bf16[384,512]{1,0:T(8,128)(2,1)} %get-tuple-element.553), channel_id=1, source_target_pairs={{0,4},{1,5},{8,12},{9,13},{16,20},{17,21},{24,28},{25,29},{32,36},... | collective-permute-start | bytes 1179656 | tf_op jit(solution)/shard_map/ppermute | solution.py:565
  47.0 22.6 %collective-permute-start.8 = (bf16[384,512]{1,0:T(8,128)(2,1)}, bf16[384,512]{1,0:T(8,128)(2,1)}, u32[]{:S(2)}, u32[]{:S(2)}) collective-permute-start(bf16[384,512]{1,0:T(8,128)(2,1)} %get-tuple-element.552), channel_id=1, source_target_pairs={{0,6},{1,7},{8,14},{9,15},{16,22},{17,23},{24,30},{25,31},{32,38},... | collective-permute-start | bytes 1179656 | tf_op jit(solution)/shard_map/ppermute | solution.py:565
  52.5 0.8 copy-start.4
  53.3 35.5 %copy-start.8 = (s32[256,1]{1,0:T(8,128)S(1)}, s32[256,1]{1,0:T(8,128)}, u32[]{:S(2)}) copy-start(s32[256,1]{1,0:T(8,128)} %copy-done.7) | copy-start | bytes 3076
  53.3 0.8 copy-start.10
  55.3 1.1 copy-start.3
  56.4 1.1 copy-start.5
  58.1 15.9 %collective-permute-start.3 = (bf16[80,1024]{1,0:T(8,128)(2,1)S(1)}, bf16[80,1024]{1,0:T(8,128)(2,1)S(1)}, u32[]{:S(2)}, u32[]{:S(2)}) collective-permute-start(bf16[80,1024]{1,0:T(8,128)(2,1)S(1)} %get-tuple-element.462), channel_id=1, source_target_pairs={{0,8},{8,16},{32,40},{40,48},{64,72},{72,80},{96,104},{104,112},{1... | collective-permute-start | bytes 491528 | tf_op jit(solution)/shard_map/ppermute | solution.py:603
  60.0 14.0 %collective-permute-start.4 = (bf16[80,1024]{1,0:T(8,128)(2,1)S(1)}, bf16[80,1024]{1,0:T(8,128)(2,1)S(1)}, u32[]{:S(2)}, u32[]{:S(2)}) collective-permute-start(bf16[80,1024]{1,0:T(8,128)(2,1)S(1)} %get-tuple-element.463), channel_id=1, source_target_pairs={{0,16},{8,24},{32,48},{40,56},{64,80},{72,88},{96,112},{104,120},{... | collective-permute-start | bytes 491528 | tf_op jit(solution)/shard_map/ppermute | solution.py:603
  61.3 19.6 %collective-permute-start.5 = (bf16[80,1024]{1,0:T(8,128)(2,1)S(1)}, bf16[80,1024]{1,0:T(8,128)(2,1)S(1)}, u32[]{:S(2)}, u32[]{:S(2)}) collective-permute-start(bf16[80,1024]{1,0:T(8,128)(2,1)S(1)} %get-tuple-element.464), channel_id=1, source_target_pairs={{0,24},{8,32},{32,56},{40,0},{64,88},{72,96},{96,120},{104,64},{12... | collective-permute-start | bytes 491528 | tf_op jit(solution)/shard_map/ppermute | solution.py:603
  63.2 8.3 %collective-permute-start.1 = (bf16[32,1024]{1,0:T(8,128)(2,1)S(1)}, bf16[32,1024]{1,0:T(8,128)(2,1)S(1)}, u32[]{:S(2)}, u32[]{:S(2)}) collective-permute-start(bf16[32,1024]{1,0:T(8,128)(2,1)S(1)} %block.1.block_ref), channel_id=1, source_target_pairs={{0,8},{8,16},{16,24},{24,32},{32,40},{40,48},{48,56},{56,0},{64,72... | collective-permute-start | bytes 196616 | tf_op jit(solution)/shard_map/ppermute | solution.py:591
  69.6 3.1 %collective-permute-start.2 = (bf16[32,1024]{1,0:T(8,128)(2,1)S(1)}, bf16[32,1024]{1,0:T(8,128)(2,1)S(1)}, u32[]{:S(2)}, u32[]{:S(2)}) collective-permute-start(bf16[32,1024]{1,0:T(8,128)(2,1)S(1)} %block.1.block_ref), channel_id=1, source_target_pairs={{0,56},{8,0},{16,8},{24,16},{32,24},{40,32},{48,40},{56,48},{64,12... | collective-permute-start | bytes 196616 | tf_op jit(solution)/shard_map/ppermute | solution.py:592
  80.9 24.4 %collective-permute-start.12 = (bf16[384,512]{1,0:T(8,128)(2,1)S(1)}, bf16[384,512]{1,0:T(8,128)(2,1)S(1)}, u32[]{:S(2)}, u32[]{:S(2)}) collective-permute-start(bf16[384,512]{1,0:T(8,128)(2,1)S(1)} %choose.1.mine_ref), channel_id=1, source_target_pairs={{0,2},{1,3},{2,4},{3,5},{4,6},{5,7},{6,0},{7,1},{8,10},{9,11},{10,... | collective-permute-start | bytes 1179656 | tf_op jit(solution)/shard_map/ppermute | solution.py:633
  82.2 23.1 %collective-permute-start.13 = (bf16[384,512]{1,0:T(8,128)(2,1)S(1)}, bf16[384,512]{1,0:T(8,128)(2,1)S(1)}, u32[]{:S(2)}, u32[]{:S(2)}) collective-permute-start(bf16[384,512]{1,0:T(8,128)(2,1)S(1)} %choose.1.mine_ref), channel_id=1, source_target_pairs={{2,0},{3,1},{4,2},{5,3},{6,4},{7,5},{0,6},{1,7},{10,8},{11,9},{12,... | collective-permute-start | bytes 1179656 | tf_op jit(solution)/shard_map/ppermute | solution.py:634
  83.6 16.2 %collective-permute-start.9 = (bf16[64,1024]{1,0:T(8,128)(2,1)S(1)}, bf16[64,1024]{1,0:T(8,128)(2,1)S(1)}, u32[]{:S(2)}, u32[]{:S(2)}) collective-permute-start(bf16[64,1024]{1,0:T(8,128)(2,1)S(1)} %get-tuple-element.470), channel_id=1, source_target_pairs={{0,16},{8,24},{16,32},{24,40},{32,48},{40,56},{48,0},{56,8},{64,80... | collective-permute-start | bytes 393224 | tf_op jit(solution)/shard_map/ppermute | solution.py:615
  83.7 18.4 %collective-permute-start.10 = (bf16[64,1024]{1,0:T(8,128)(2,1)S(1)}, bf16[64,1024]{1,0:T(8,128)(2,1)S(1)}, u32[]{:S(2)}, u32[]{:S(2)}) collective-permute-start(bf16[64,1024]{1,0:T(8,128)(2,1)S(1)} %get-tuple-element.471), channel_id=1, source_target_pairs={{0,48},{8,56},{16,0},{24,8},{32,16},{40,24},{48,32},{56,40},{64,11... | collective-permute-start | bytes 393224 | tf_op jit(solution)/shard_map/ppermute | solution.py:616
  87.2 9.6 %collective-permute-start.11 = (bf16[32,1024]{1,0:T(8,128)(2,1)S(1)}, bf16[32,1024]{1,0:T(8,128)(2,1)S(1)}, u32[]{:S(2)}, u32[]{:S(2)}) collective-permute-start(bf16[32,1024]{1,0:T(8,128)(2,1)S(1)} %block.1.block_ref), channel_id=1, source_target_pairs={{0,32},{8,40},{16,48},{24,56},{32,0},{40,8},{48,16},{56,24},{64,96... | collective-permute-start | bytes 196616 | tf_op jit(solution)/shard_map/ppermute | solution.py:593
  96.8 6.6 %collective-permute-start.14 = (bf16[64,1024]{1,0:T(8,128)(2,1)S(1)}, bf16[64,1024]{1,0:T(8,128)(2,1)S(1)}, u32[]{:S(2)}, u32[]{:S(2)}) collective-permute-start(bf16[64,1024]{1,0:T(8,128)(2,1)S(1)} %get-tuple-element.479), channel_id=1, source_target_pairs={{0,64},{8,72},{16,80},{24,88},{32,96},{40,104},{48,112},{56,120},{... | collective-permute-start | bytes 393224 | tf_op jit(solution)/shard_map/ppermute | solution.py:630
  99.9 4.1 %collective-permute-start.15 = (bf16[64,1024]{1,0:T(8,128)(2,1)S(1)}, bf16[64,1024]{1,0:T(8,128)(2,1)S(1)}, u32[]{:S(2)}, u32[]{:S(2)}) collective-permute-start(bf16[64,1024]{1,0:T(8,128)(2,1)S(1)} %get-tuple-element.480), channel_id=1, source_target_pairs={{0,128},{8,136},{16,144},{24,152},{32,160},{40,168},{48,176},{56,1... | collective-permute-start | bytes 393224 | tf_op jit(solution)/shard_map/ppermute | solution.py:630
  102.1 3.2 %collective-permute-start.16 = (bf16[64,1024]{1,0:T(8,128)(2,1)S(1)}, bf16[64,1024]{1,0:T(8,128)(2,1)S(1)}, u32[]{:S(2)}, u32[]{:S(2)}) collective-permute-start(bf16[64,1024]{1,0:T(8,128)(2,1)S(1)} %get-tuple-element.481), channel_id=1, source_target_pairs={{0,192},{8,200},{16,208},{24,216},{32,224},{40,232},{48,240},{56,2... | collective-permute-start | bytes 393224 | tf_op jit(solution)/shard_map/ppermute | solution.py:630
  105.4 18.7 %collective-permute-start.18 = (bf16[256,1024]{1,0:T(8,128)(2,1)S(1)}, bf16[256,1024]{1,0:T(8,128)(2,1)S(1)}, u32[]{:S(2)}, u32[]{:S(2)}) collective-permute-start(bf16[256,1024]{1,0:T(8,128)(2,1)S(1)} %line.1.line_ref.y0_ref), channel_id=1, source_target_pairs={{0,64},{8,72},{16,80},{24,88},{32,96},{40,104},{48,112},{56,120},{... | collective-permute-start | bytes 1572872 | tf_op jit(solution)/shard_map/ppermute | solution.py:650
  105.5 18.6 %collective-permute-start.19 = (bf16[256,1024]{1,0:T(8,128)(2,1)S(1)}, bf16[256,1024]{1,0:T(8,128)(2,1)S(1)}, u32[]{:S(2)}, u32[]{:S(2)}) collective-permute-start(bf16[256,1024]{1,0:T(8,128)(2,1)S(1)} %line.1.line_ref.y0_ref), channel_id=1, source_target_pairs={{0,192},{8,200},{16,208},{24,216},{32,224},{40,232},{48,240},{56,2... | collective-permute-start | bytes 1572872 | tf_op jit(solution)/shard_map/ppermute | solution.py:651
  109.2 6.9 %collective-permute-start.20 = (bf16[192,512]{1,0:T(8,128)(2,1)S(1)}, bf16[192,512]{1,0:T(8,128)(2,1)S(1)}, u32[]{:S(2)}, u32[]{:S(2)}) collective-permute-start(bf16[192,512]{1,0:T(8,128)(2,1)S(1)} %get-tuple-element.487.own_ref), channel_id=1, source_target_pairs={{0,2},{1,3},{8,10},{9,11},{16,18},{17,19},{24,26},{25,27},{32,34},... | collective-permute-start | bytes 589832 | tf_op jit(solution)/shard_map/ppermute | solution.py:676
  111.2 12.9 %collective-permute-start.17 = (bf16[384,512]{1,0:T(8,128)(2,1)S(1)}, bf16[384,512]{1,0:T(8,128)(2,1)S(1)}, u32[]{:S(2)}, u32[]{:S(2)}) collective-permute-start(bf16[384,512]{1,0:T(8,128)(2,1)S(1)} %choose.1.mine_ref), channel_id=1, source_target_pairs={{0,4},{1,5},{2,6},{3,7},{4,0},{5,1},{6,2},{7,3},{8,12},{9,13},{10,... | collective-permute-start | bytes 1179656 | tf_op jit(solution)/shard_map/ppermute | solution.py:677
  111.5 11.3 %collective-permute-start.21 = (bf16[192,512]{1,0:T(8,128)(2,1)S(1)}, bf16[192,512]{1,0:T(8,128)(2,1)S(1)}, u32[]{:S(2)}, u32[]{:S(2)}) collective-permute-start(bf16[192,512]{1,0:T(8,128)(2,1)S(1)} %get-tuple-element.487.own_ref), channel_id=1, source_target_pairs={{0,4},{1,5},{8,12},{9,13},{16,20},{17,21},{24,28},{25,29},{32,36},... | collective-permute-start | bytes 589832 | tf_op jit(solution)/shard_map/ppermute | solution.py:676
  116.1 7.9 %collective-permute-start.22 = (bf16[192,512]{1,0:T(8,128)(2,1)S(1)}, bf16[192,512]{1,0:T(8,128)(2,1)S(1)}, u32[]{:S(2)}, u32[]{:S(2)}) collective-permute-start(bf16[192,512]{1,0:T(8,128)(2,1)S(1)} %get-tuple-element.487.own_ref), channel_id=1, source_target_pairs={{0,6},{1,7},{8,14},{9,15},{16,22},{17,23},{24,30},{25,31},{32,38},... | collective-permute-start | bytes 589832 | tf_op jit(solution)/shard_map/ppermute | solution.py:676
  124.7 11.2 %collective-permute-start.23 = (bf16[1536,512]{1,0:T(8,128)(2,1)S(1)}, bf16[1536,512]{1,0:T(8,128)(2,1)S(1)}, u32[]{:S(2)}, u32[]{:S(2)}) collective-permute-start(bf16[1536,512]{1,0:T(8,128)(2,1)S(1)} %part.1.part_ref), channel_id=1, source_target_pairs={{0,1},{1,0},{2,3},{3,2},{4,5},{5,4},{6,7},{7,6},{8,9},{9,8},{10,11... | collective-permute-start | bytes 4718600 | tf_op jit(solution)/shard_map/ppermute | solution.py:703
  129.7 14.8 %collective-permute-start.27 = (bf16[128,1024]{1,0:T(8,128)(2,1)S(1)}, bf16[128,1024]{1,0:T(8,128)(2,1)S(1)}, u32[]{:S(2)}, u32[]{:S(2)}) collective-permute-start(bf16[128,1024]{1,0:T(8,128)(2,1)S(1)} %slice.131), channel_id=1, source_target_pairs={{0,64},{8,72},{16,80},{24,88},{32,96},{40,104},{48,112},{56,120},{... | collective-permute-start | bytes 786440 | tf_op jit(solution)/shard_map/ppermute | solution.py:682
  129.8 14.6 %collective-permute-start.28 = (bf16[128,1024]{1,0:T(8,128)(2,1)S(1)}, bf16[128,1024]{1,0:T(8,128)(2,1)S(1)}, u32[]{:S(2)}, u32[]{:S(2)}) collective-permute-start(bf16[128,1024]{1,0:T(8,128)(2,1)S(1)} %slice.132), channel_id=1, source_target_pairs={{0,192},{8,200},{16,208},{24,216},{32,224},{40,232},{48,240},{56,2... | collective-permute-start | bytes 786440 | tf_op jit(solution)/shard_map/ppermute | solution.py:683
  133.1 13.0 %copy-start.1 = (bf16[2,512,512]{2,1,0:T(8,128)(2,1)S(1)}, bf16[2,512,512]{2,1,0:T(8,128)(2,1)}, u32[]{:S(2)}) copy-start(bf16[2,512,512]{2,1,0:T(8,128)(2,1)} %copy-done) | copy-start | bytes 3145732
  133.1 8.7 %collective-permute-start.24 = (bf16[128,512]{1,0:T(8,128)(2,1)S(1)}, bf16[128,512]{1,0:T(8,128)(2,1)S(1)}, u32[]{:S(2)}, u32[]{:S(2)}) collective-permute-start(bf16[128,512]{1,0:T(8,128)(2,1)S(1)} %get-tuple-element.490.refs_0_), channel_id=1, source_target_pairs={{0,64},{8,72},{16,80},{24,88},{32,96},{40,104},{48,112},{56,120},{... | collective-permute-start | bytes 393224 | tf_op jit(solution)/shard_map/ppermute | solution.py:692
  133.2 10.2 %collective-permute-start.25 = (bf16[128,512]{1,0:T(8,128)(2,1)S(1)}, bf16[128,512]{1,0:T(8,128)(2,1)S(1)}, u32[]{:S(2)}, u32[]{:S(2)}) collective-permute-start(bf16[128,512]{1,0:T(8,128)(2,1)S(1)} %get-tuple-element.490.refs_0_), channel_id=1, source_target_pairs={{0,192},{8,200},{16,208},{24,216},{32,224},{40,232},{48,240},{56,2... | collective-permute-start | bytes 393224 | tf_op jit(solution)/shard_map/ppermute | solution.py:692
  135.9 8.5 %collective-permute-start.26 = (bf16[128,512]{1,0:T(8,128)(2,1)S(1)}, bf16[128,512]{1,0:T(8,128)(2,1)S(1)}, u32[]{:S(2)}, u32[]{:S(2)}) collective-permute-start(bf16[128,512]{1,0:T(8,128)(2,1)S(1)} %get-tuple-element.490.refs_0_), channel_id=1, source_target_pairs={{0,128},{8,136},{16,144},{24,152},{32,160},{40,168},{48,176},{56,1... | collective-permute-start | bytes 393224 | tf_op jit(solution)/shard_map/ppermute | solution.py:692
  144.5 2.6 %collective-permute-start.29 = (bf16[576,512]{1,0:T(8,128)(2,1)S(1)}, bf16[576,512]{1,0:T(8,128)(2,1)S(1)}, u32[]{:S(2)}, u32[]{:S(2)}) collective-permute-start(bf16[576,512]{1,0:T(8,128)(2,1)S(1)} %cross.1.cross_ref), channel_id=1, source_target_pairs={{0,1},{1,0},{2,3},{3,2},{4,5},{5,4},{6,7},{7,6},{8,9},{9,8},{10,11... | collective-permute-start | bytes 1769480 | tf_op jit(solution)/shard_map/ppermute | solution.py:725

commit v6 on v4

--- a/solution.py
+++ b/solution.py
@@ -301,7 +301,9 @@
     pair_hi_ref[n:, :] = hi_ref[...]
 
 
-def line_kernel(block_ref, lo_ref, hi_ref, opposite_ref, two_lo_ref, two_hi_ref, line_ref):
+def line_kernel(
+    pos_ref, block_ref, lo_ref, hi_ref, opposite_ref, two_lo_ref, two_hi_ref, line_ref, extra_ref
+):
     n = block_ref.shape[0]
     half = n // 2
     blocks = [block_ref[...], lo_ref[...], hi_ref[...], opposite_ref[...]]
@@ -309,6 +311,9 @@
     for k, value in enumerate(blocks):
         line_ref[k * half : (k + 1) * half, :] = value[:half]
         line_ref[(NZ + k) * half : (NZ + k + 1) * half, :] = value[half:]
+    even = (pos_ref[1] & 1) == 0
+    n, width = extra_ref.shape
+    extra_ref[...] = jnp.where(even, line_ref[n:, :width], line_ref[:n, :width])
 
 
 def by_x(x, at_0, at_1, at_2, at_3):
@@ -343,10 +348,9 @@
                 ref[...] = source[k * DEST_ROWS : (k + 1) * DEST_ROWS, :]
 
 
-def gone_kernel(pos_ref, line_ref, *refs):
-    landed, gone_ref, extra_ref = refs[:4], refs[4], refs[5]
-    width = extra_ref.shape[1]
-    half = line_ref.shape[0] // 2
+def gone_kernel(pos_ref, *refs):
+    landed, gone_ref, gone_panel_ref = refs[:4], refs[4], refs[5]
+    width = gone_panel_ref.shape[1]
     for s in range(2):
         for k in range(4):
 
@@ -354,17 +358,32 @@
             def _(k=k, s=s):
                 gone_ref[s * DEST_ROWS : (s + 1) * DEST_ROWS, :] = landed[k][...]
 
+    gone_panel_ref[...] = gone_ref[:, :width]
+
+
+def settle(land_ref, begin, value, gone):
+    n = value.shape[0]
+    hits = (iota((n, 2 * DEST_ROWS), 0) + begin) == land_ref[...]
+    marks = jnp.where(hits, 1.0, 0.0)
+    hit = jnp.sum(marks, axis=1, keepdims=True) > 0.5
+    return jnp.where(hit, dot(narrow(marks), gone), value.astype(jnp.float32))
+
+
+def settle_kernel(rows_ref, land_ref, gone_ref, out_ref):
+    begin = pl.program_id(0) * rows_ref.shape[0]
+    out_ref[...] = narrow(settle(land_ref, begin, rows_ref[...], gone_ref[...]))
+
+
+def factor_kernel(pos_ref, part_ref, other_ref, upper_ref, out_ref):
     even = (pos_ref[1] & 1) == 0
-    extra_ref[:half, :] = jnp.where(even, line_ref[half:, :width], line_ref[:half, :width])
-    extra_ref[half:, :] = gone_ref[:, :width]
-
-
-def extra_kernel(pos_ref, own_ref, one_ref, two_ref, three_ref, cross_ref, gone_ref):
+    out_ref[...] = narrow(
+        dot(jnp.where(even, part_ref[...], other_ref[...]), upper_ref[0])
+    )
+
+
+def extra_kernel(pos_ref, own_ref, one_ref, two_ref, three_ref, cross_ref):
     x = pos_ref[1] >> 1
-    value = by_x(x, own_ref[...], one_ref[...], two_ref[...], three_ref[...])
-    n = cross_ref.shape[0]
-    cross_ref[...] = value[:n]
-    gone_ref[...] = value[n:]
+    cross_ref[...] = by_x(x, own_ref[...], one_ref[...], two_ref[...], three_ref[...])
 
 
 def part_kernel(pos_ref, mine_ref, before_ref, after_ref, across_ref, part_ref):
@@ -375,12 +394,12 @@
         part_ref[pl.ds(pl.multiple_of(begin, n), n), :] = ref[...]
 
 
-def cross_kernel(*refs):
-    begin = 0
-    for ref in refs[:-1]:
-        n = ref.shape[0]
-        refs[-1][begin : begin + n, :] = ref[...]
-        begin += n
+def cross_kernel(pos_ref, c0_ref, c1_ref, c2_ref, c3_ref, own_ref, one_ref, two_ref, three_ref, cross_ref):
+    n = c0_ref.shape[0]
+    for k, ref in enumerate((c0_ref, c1_ref, c2_ref, c3_ref)):
+        cross_ref[k * n : (k + 1) * n, :] = ref[...]
+    x = pos_ref[1] >> 1
+    cross_ref[NY * n :, :] = by_x(x, own_ref[...], one_ref[...], two_ref[...], three_ref[...])
 
 
 def first_kernel(
@@ -402,8 +421,8 @@
     rows_ref,
     part_ref,
     other_ref,
+    factor_ref,
     land_ref,
-    gone_ref,
     cross_ref,
     cross_other_ref,
     row_first_ref,
@@ -430,7 +449,7 @@
         mine, others = cross_ref[...], cross_other_ref[...]
         from_first = jnp.where(even, mine, others)
         from_second = jnp.where(even, others, mine)
-        gone_first_ref[...] = from_first[panel:]
+        gone_first_ref[...] = narrow(dot(from_first[panel:], upper_ref[0]))
         gone_second_ref[...] = from_second[panel:]
         row_first = row_first_ref[...]
         pivot_second = second_ref[...]
@@ -464,21 +483,12 @@
     def _():
         n = rows_ref.shape[0]
         begin = (step - 1) * n
-        hits = (iota((n, 2 * DEST_ROWS), 0) + begin) == land_ref[...]
-        marks = jnp.where(hits, 1.0, 0.0)
-        hit = jnp.sum(marks, axis=1, keepdims=True) > 0.5
-        marks = narrow(marks)
-
-        def settle(value, gone):
-            return jnp.where(hit, dot(marks, gone), value.astype(jnp.float32))
-
-        mine, others = part_ref[...], other_ref[...]
-        panel_first = settle(jnp.where(even, mine, others), gone_first_ref[...])
-        panel_second = settle(jnp.where(even, others, mine), gone_second_ref[...])
-        factor_first = narrow(dot(narrow(panel_first), upper_ref[0]))
+        second = jnp.where(even, other_ref[...], part_ref[...])
+        factor_first = narrow(settle(land_ref, begin, factor_ref[...], gone_first_ref[...]))
+        panel_second = settle(land_ref, begin, second, gone_second_ref[...])
         mid = narrow(panel_second - dot(factor_first, corner_ref[...]))
         factor_second = narrow(dot(mid, upper_ref[1]))
-        current = settle(rows_ref[...], gone_ref[...])
+        current = rows_ref[...].astype(jnp.float32)
         updated = narrow(
             current
             - dot(factor_first, new_ref[:panel, :])
@@ -580,44 +590,43 @@
     arrived = [lax.ppermute(leaving[s], "prow", shift_y(s, [0], [0, 1])) for s in (1, 2, 3)]
 
     (block,) = local_kernel(
-        block_kernel, "block", [shape((2 * per_home, local_cols))], [], keep, dealt
+        block_kernel, "block", [shape((2 * per_home, local_cols))], [], keep, after(dealt, passing)
     )
     from_lo = lax.ppermute(block, "prow", shift_z(1))
     from_hi = lax.ppermute(block, "prow", shift_z(-1))
     opposite = lax.ppermute(block, "prow", shift_z(4))
     quarter_shape = shape((NZ // 2 * DEST_ROWS, local_cols))
     kept, send = local_kernel(
-        spread_kernel, "spread", [quarter_shape] * 2, [position], passing, leaving[0], *arrived
+        spread_kernel,
+        "spread",
+        [quarter_shape] * 2,
+        [position],
+        after(passing, block),
+        leaving[0],
+        *arrived,
     )
     came = lax.ppermute(send, "prow", shift_z(4, [0, 1]))
 
-    from_lo, from_hi = after((from_lo, from_hi), came, mine)
+    from_lo, from_hi = after((from_lo, from_hi), mine)
     pair_shape = shape((4 * per_home, local_cols))
     pair_lo, pair_hi = local_kernel(
         pair_kernel, "pair", [pair_shape] * 2, [], block, from_lo, from_hi
     )
     two_lo = lax.ppermute(pair_lo, "prow", shift_z(2))
     two_hi = lax.ppermute(pair_hi, "prow", shift_z(-2))
-    one_shape = shape((DEST_ROWS, local_cols))
-    spread = local_kernel(
-        fold_kernel, "fold", [one_shape] * 4, [position], kept, after(came, pair_lo)
-    )
-    landed = [spread[0]] + [
-        lax.ppermute(spread[k], "prow", shift_z(k, [0, 1, 4, 5])) for k in (1, 2, 3)
-    ]
     quarter_out = after(mine, pair_lo)
     ring = [(x, (x + 1) % NX) for x in range(NX)]
     before = lax.ppermute(quarter_out, "pcol", move_x(ring))
     behind = lax.ppermute(quarter_out, "pcol", move_x([(b, a) for a, b in ring]))
 
-    two_lo, two_hi, opposite = after((two_lo, two_hi, opposite), before, behind, landed)
+    two_lo, two_hi, opposite = after((two_lo, two_hi, opposite), before, behind)
     half = panel // NY
     n_gone = 2 * DEST_ROWS
-    (z_line,) = local_kernel(
+    z_line, extra = local_kernel(
         line_kernel,
         "line",
-        [shape((2 * half, local_cols))],
-        [],
+        [shape((2 * half, local_cols)), shape((half, width))],
+        [position],
         block,
         from_lo,
         from_hi,
@@ -627,31 +636,33 @@
     )
     y_lo = lax.ppermute(z_line, "prow", shift_y(1))
     y_hi = lax.ppermute(z_line, "prow", shift_y(-1))
-    gone, extra = local_kernel(
+    sent = [lax.ppermute(extra, "pcol", move_x([(0, k)])) for k in (1, 2, 3)]
+    one_shape = shape((DEST_ROWS, local_cols))
+    spread = local_kernel(
+        fold_kernel, "fold", [one_shape] * 4, [position], kept, after(came, extra)
+    )
+    landed = [spread[0]] + [
+        lax.ppermute(spread[k], "prow", shift_z(k, [0, 1, 4, 5])) for k in (1, 2, 3)
+    ]
+    across = lax.ppermute(
+        after(mine, extra), "pcol", move_x([(x, (x + 2) % NX) for x in range(NX)])
+    )
+
+    y_lo, y_hi = after((y_lo, y_hi), sent, across, landed)
+    far_first = lax.ppermute(y_lo[:half], "prow", shift_y(1))
+    far_second = lax.ppermute(y_hi[half:], "prow", shift_y(-1))
+    (cross,) = local_kernel(
+        extra_kernel, "extra", [shape((half, width))], [position], extra, *sent
+    )
+    crossed = [lax.ppermute(cross, "prow", shift_y(s)) for s in (1, -1, 2)]
+    gone, gone_panel = local_kernel(
         gone_kernel,
         "gone",
-        [shape((n_gone, local_cols)), shape((half + n_gone, width))],
+        [shape((n_gone, local_cols)), shape((n_gone, width))],
         [position],
-        z_line,
-        *landed,
-    )
-    sent = [lax.ppermute(extra, "pcol", move_x([(0, k)])) for k in (1, 2, 3)]
-    across = lax.ppermute(
-        after(mine, z_line), "pcol", move_x([(x, (x + 2) % NX) for x in range(NX)])
-    )
-
-    y_lo, y_hi = after((y_lo, y_hi), sent, across)
-    far_first = lax.ppermute(y_lo[:half], "prow", shift_y(1))
-    far_second = lax.ppermute(y_hi[half:], "prow", shift_y(-1))
-    cross, gone_panel = local_kernel(
-        extra_kernel,
-        "extra",
-        [shape((half, width)), shape((n_gone, width))],
-        [position],
-        extra,
-        *sent,
-    )
-    crossed = [lax.ppermute(cross, "prow", shift_y(s)) for s in (1, -1, 2)]
+        *after(landed, y_lo),
+    )
+    gone_sent = [lax.ppermute(gone_panel, "pcol", move_x([(0, k)])) for k in (1, 2, 3)]
     (part,) = local_kernel(
         part_kernel,
         "part",
@@ -663,16 +674,43 @@
         after(across, y_lo),
     )
     other = lax.ppermute(part, "pcol", SWAP)
-
-    crossed = after(crossed, far_first, far_second, other)
+    n_block = panel // 2
+    steps = local_rows // n_block
+
+    def block_of(cols, lead=0):
+        return pl.BlockSpec((n_block, cols), lambda i: (jnp.maximum(i - lead, 0), 0))
+
+    settled = pl.pallas_call(
+        settle_kernel,
+        grid=(steps,),
+        in_specs=[block_of(local_cols), whole((1, n_gone)), whole((n_gone, local_cols))],
+        out_specs=block_of(local_cols),
+        out_shape=shape((local_rows, local_cols)),
+        compiler_params=pltpu.CompilerParams(vmem_limit_bytes=16 * MIB),
+        cost_estimate=pl.CostEstimate(flops=0, bytes_accessed=0, transcendentals=0),
+        name="settle",
+    )(rows, land, gone)
+    factor_raw = pl.pallas_call(
+        factor_kernel,
+        grid=(steps,),
+        in_specs=[smem(), block_of(width), block_of(width), whole((2, panel, panel))],
+        out_specs=block_of(width),
+        out_shape=shape((local_rows, width)),
+        compiler_params=pltpu.CompilerParams(vmem_limit_bytes=16 * MIB),
+        cost_estimate=pl.CostEstimate(flops=0, bytes_accessed=0, transcendentals=0),
+        name="factor",
+    )(position, part, other, upper_inverse)
+
+    crossed = after(crossed, far_first, far_second, factor_raw, settled)
     (cross,) = local_kernel(
         cross_kernel,
         "cross",
         [shape((panel + n_gone, width))],
-        [],
+        [position],
         cross,
         *crossed,
         gone_panel,
+        *gone_sent,
     )
     cross_other = lax.ppermute(cross, "pcol", SWAP)
     row_first, second, a00 = pl.pallas_call(
@@ -690,22 +728,16 @@
         name="first",
     )(low, z_line, y_lo, y_hi, far_first, far_second)
 
-    n_block = panel // 2
-    steps = local_rows // n_block
-
-    def row_block(cols):
-        return pl.BlockSpec((n_block, cols), lambda i: (jnp.maximum(i - 1, 0), 0))
-
     result = pl.pallas_call(
         functools.partial(finish_kernel, panel),
         grid=(steps + 1,),
         in_specs=[
             smem(),
-            row_block(local_cols),
-            row_block(width),
-            row_block(width),
+            block_of(local_cols, 1),
+            block_of(width, 1),
+            block_of(width, 1),
+            block_of(width, 1),
             whole((1, 2 * DEST_ROWS)),
-            whole((2 * DEST_ROWS, local_cols)),
             whole((panel + 2 * DEST_ROWS, width)),
             whole((panel + 2 * DEST_ROWS, width)),
             whole((panel, local_cols)),
@@ -715,7 +747,7 @@
             whole((2, panel, panel)),
             whole((2, panel)),
         ],
-        out_specs=row_block(local_cols),
+        out_specs=block_of(local_cols, 1),
         out_shape=shape((local_rows, local_cols)),
         scratch_shapes=[
             pltpu.VMEM((2 * panel, local_cols), jnp.bfloat16),
@@ -726,18 +758,13 @@
         ],
         compiler_params=pltpu.CompilerParams(vmem_limit_bytes=32 * MIB),
         name="finish",
-    )(position, rows, part, other, land, gone, cross, cross_other, row_first, second, a00, low, upper_inverse, place)
+    )(position, settled, part, other, factor_raw, land, cross, cross_other, row_first, second, a00, low, upper_inverse, place)
     result = result.reshape(matrix.shape)
-    return lax.cond(
-        flag[0] > 0,
-        lambda a, *rest: general_steps(*rest),
-        lambda a, *rest: a,
-        result,
-        matrix,
-        pivots,
-        lower_inverse,
-        upper_inverse,
-    )
+
+    def general(state):
+        return 0, general_steps(matrix, pivots, lower_inverse, upper_inverse)
+
+    return lax.while_loop(lambda state: state[0] > 0, general, (flag[0], result))[1]
 
 
 def solution(mesh):

time: 158 us -> 156 us (0.987)
  waiting for transfers between devices: 23.6 us -> 19.3 us
  starting transfers between devices: 74.1 us -> 77.9 us
    ppermute x1 -> x4, starting transfers between devices: 0.39 us -> 8.45 us  [the longest x3 6.75 us: per_device(): lax.ppermute(gone_panel, 'pcol', move_x([(0, k)]))]
    ppermute x3, waiting for transfers between devices: 6.44 us -> 1.98 us  [per_device(): sent = [lax.ppermute(extra, 'pcol', move_x([(0, k)])) for k in (1, 2, 3)]]
    pallas_call x0 -> x2, Pallas kernels: none -> 4.16 us  [the longest x1 2.44 us: per_device(): pl.pallas_call(factor_kernel, grid=(steps,), in_specs=[smem(), block_of(w...]
    pallas_call x1, Pallas kernels: 14.2 us -> 10.1 us  [per_device(): pl.pallas_call(functools.partial(finish_kernel, panel), grid=(steps + 1,)...]
    ppermute x1, starting transfers between devices: 3.56 us -> 0.01 us  [per_device(): two_hi = lax.ppermute(pair_hi, 'prow', shift_z(-2))]
    ppermute x3, starting transfers between devices: 9.55 us -> 6.95 us  [per_device(): lax.ppermute(spread[k], 'prow', shift_z(k, [0, 1, 4, 5]))]
    ppermute x1, starting transfers between devices: 0.08 us -> 2.36 us  [per_device(): two_lo = lax.ppermute(pair_lo, 'prow', shift_z(2))]
    reshape x1, local copies, waits for them, and re-layouts: 6.14 us -> 3.93 us  [per_device(): result = result.reshape(matrix.shape)]
  transfers between devices with their start and end apart: 31 -> 34, of which waited for: 9 -> 7; matrix products, arithmetic and copies ran while one was open for 1% -> 1% of each run, Pallas kernels for 7% -> 9%
where the time goes in v6:
time: 156 us; the launch traced here: 155 us
  starting transfers between devices  77.9 us (50%)
  Pallas kernels  28.9 us (19%)
  waiting for transfers between devices  19.3 us (12%)
  local copies, waits for them, and re-layouts  14.2 us (9%)
  between operations  13.9 us (9%)
    pallas_call x12, Pallas kernels, local_kernel(): pl.pallas_call(body, grid=(1,), in_specs=[smem() for _ in scalars] + [who...  14 us
    all_to_all x1, starting transfers between devices, per_device(): dealt = lax.all_to_all(picks, 'prow', 0, 0, tiled=True)  12.2 us
    pallas_call x1, Pallas kernels, per_device(): pl.pallas_call(functools.partial(finish_kernel, panel), grid=(steps + 1,)...  10.1 us
    ppermute x3, starting transfers between devices, per_device(): got = [lax.ppermute(own[k], 'pcol', move_x([(0, k)])) for k in range(1, NX)]  9.19 us
    unnamed x27, local copies, waits for them, and re-layouts  9.14 us
    ppermute x1, starting transfers between devices, per_device(): other = lax.ppermute(part, 'pcol', SWAP)  7.14 us
    ppermute x3, starting transfers between devices, per_device(): lax.ppermute(spread[k], 'prow', shift_z(k, [0, 1, 4, 5]))  6.95 us
    ppermute x3, waiting for transfers between devices, per_device(): crossed = [lax.ppermute(cross, 'prow', shift_y(s)) for s in (1, -1, 2)]  6.92 us
  transfers between devices with their start and end apart: 34, of which 7 were waited for; matrix products, arithmetic and copies ran while one was open for 1% of the time, Pallas kernels for 9%

profile of v6, /device:TPU:1, one launch (start us, length us, event | category | flops | bytes accessed | tf_op | source)
XLA Modules:
  0.0 155.1 jit_solution(11963270784605687405)
XLA Ops:
  6.5 2.7 %copy.11 = bf16[192,8,2,512]{3,1,2,0:T(8,128)(2,1)S(1)} copy(bf16[192,8,2,512]{3,2,1,0:T(2,128)(2,1)} %bitcast.75) | data formatting | bytes 6291456
  9.4 2.9 %deal.1 = (bf16[256,1024]{1,0:T(8,128)(2,1)S(1)}, s32[32,1]{1,0:T(8,128)S(1)}, s32[2,512]{1,0:T(2,128)S(1)}, s32[1,512]{1,0:T(1,128)S(1)}) custom-call(s32[2]{0:T(128)S(1)} %pad_add_fusion.pos_ref, s32[2,512]{1,0:T(2,128)S(1)} %copy-done.13, bf16[1536,1024]{1,0:T(8,128)(2,1)S(1)} %bitcast.69), custom_call_target="tpu_custom_call" | custom-call | tf_op jit(solution)/shard_map/deal/pallas_call | solution.py:521
  13.7 12.2 %all-to-all-start = ((bf16[32,8,1024]{2,1,0:T(8,128)(2,1)}), bf16[32,8,1024]{2,1,0:T(8,128)(2,1)}, u32[]{:S(2)}, u32[]{:S(2)}) async-start(bf16[32,8,1024]{2,1,0:T(8,128)(2,1)} %bitcast.73), calls=%async_computation | async-start | bytes 1048576 | tf_op jit(solution)/shard_map/all_to_all | solution.py:561
  25.9 1.1 fusion.28
  26.9 5.1 %collective-permute-start.8 = (bf16[384,512]{1,0:T(8,128)(2,1)}, bf16[384,512]{1,0:T(8,128)(2,1)}, u32[]{:S(2)}, u32[]{:S(2)}) collective-permute-start(bf16[384,512]{1,0:T(8,128)(2,1)} %get-tuple-element.572), channel_id=1, source_target_pairs={{0,6},{1,7},{8,14},{9,15},{16,22},{17,23},{24,30},{25,31},{32,38},... | collective-permute-start | bytes 1179656 | tf_op jit(solution)/shard_map/ppermute | solution.py:565
  32.1 2.0 %collective-permute-start.7 = (bf16[384,512]{1,0:T(8,128)(2,1)}, bf16[384,512]{1,0:T(8,128)(2,1)}, u32[]{:S(2)}, u32[]{:S(2)}) collective-permute-start(bf16[384,512]{1,0:T(8,128)(2,1)} %get-tuple-element.573), channel_id=1, source_target_pairs={{0,4},{1,5},{8,12},{9,13},{16,20},{17,21},{24,28},{25,29},{32,36},... | collective-permute-start | bytes 1179656 | tf_op jit(solution)/shard_map/ppermute | solution.py:565
  34.1 2.0 %collective-permute-start.6 = (bf16[384,512]{1,0:T(8,128)(2,1)}, bf16[384,512]{1,0:T(8,128)(2,1)}, u32[]{:S(2)}, u32[]{:S(2)}) collective-permute-start(bf16[384,512]{1,0:T(8,128)(2,1)} %get-tuple-element.574), channel_id=1, source_target_pairs={{0,2},{1,3},{8,10},{9,11},{16,18},{17,19},{24,26},{25,27},{32,34},... | collective-permute-start | bytes 1179656 | tf_op jit(solution)/shard_map/ppermute | solution.py:565
  36.1 4.1 %leave.1 = (bf16[144,1024]{1,0:T(8,128)(2,1)S(1)}, bf16[144,1024]{1,0:T(8,128)(2,1)}, bf16[144,1024]{1,0:T(8,128)(2,1)}, bf16[144,1024]{1,0:T(8,128)(2,1)}, s32[...) custom-call(s32[2]{0:T(128)S(1)} %pad_add_fusion.pos_ref, ...), custom_call_target="tpu_custom_call" | custom-call | tf_op jit(solution)/shard_map/leave/pallas_call | solution.py:521
  40.2 1.0 copy-done
  43.3 1.3 block.1.block_ref
  44.6 2.4 %collective-permute-start.5 = (bf16[32,1024]{1,0:T(8,128)(2,1)S(1)}, bf16[32,1024]{1,0:T(8,128)(2,1)S(1)}, u32[]{:S(2)}, u32[]{:S(2)}) collective-permute-start(bf16[32,1024]{1,0:T(8,128)(2,1)S(1)} %block.1.block_ref), channel_id=1, source_target_pairs={{0,56},{8,0},{16,8},{24,16},{32,24},{40,32},{48,40},{56,48},{64,12... | collective-permute-start | bytes 196616 | tf_op jit(solution)/shard_map/ppermute | solution.py:596
  47.0 3.1 %collective-permute-start = (bf16[144,1024]{1,0:T(8,128)(2,1)}, bf16[144,1024]{1,0:T(8,128)(2,1)S(1)}, u32[]{:S(2)}, u32[]{:S(2)}) collective-permute-start(bf16[144,1024]{1,0:T(8,128)(2,1)} %get-tuple-element.471), channel_id=1, source_target_pairs={{0,64},{8,72},{1,65},{9,73},{2,66},{10,74},{3,67},{11,75},{4,68},{... | collective-permute-start | bytes 884744 | tf_op jit(solution)/shard_map/ppermute | solution.py:590
  50.1 2.2 %collective-permute-start.1 = (bf16[144,1024]{1,0:T(8,128)(2,1)}, bf16[144,1024]{1,0:T(8,128)(2,1)S(1)}, u32[]{:S(2)}, u32[]{:S(2)}) collective-permute-start(bf16[144,1024]{1,0:T(8,128)(2,1)} %get-tuple-element.472), channel_id=1, source_target_pairs={{0,128},{8,136},{1,129},{9,137},{2,130},{10,138},{3,131},{11,139},... | collective-permute-start | bytes 884744 | tf_op jit(solution)/shard_map/ppermute | solution.py:590
  52.3 1.3 collective-permute-start.2
  53.7 1.3 choose.1.mine_ref
  55.1 2.2 %collective-permute-start.12 = (bf16[384,512]{1,0:T(8,128)(2,1)S(1)}, bf16[384,512]{1,0:T(8,128)(2,1)S(1)}, u32[]{:S(2)}, u32[]{:S(2)}) collective-permute-start(bf16[384,512]{1,0:T(8,128)(2,1)S(1)} %choose.1.mine_ref), channel_id=1, source_target_pairs={{0,2},{1,3},{2,4},{3,5},{4,6},{5,7},{6,0},{7,1},{8,10},{9,11},{10,... | collective-permute-start | bytes 1179656 | tf_op jit(solution)/shard_map/ppermute | solution.py:619
  57.3 1.4 collective-permute-start.11
  58.7 2.5 %collective-permute-done.1.two_ref = bf16[144,1024]{1,0:T(8,128)(2,1)S(1)} collective-permute-done((bf16[144,1024]{1,0:T(8,128)(2,1)}, bf16[144,1024]{1,0:T(8,128)(2,1)S(1)}, u32[]{:S(2)}, u32[]{:S(2)}) %collective-permute-start.1) | collective-permute-done | bytes 294944 | tf_op jit(solution)/shard_map/ppermute | solution.py:590
  61.2 2.4 %collective-permute-start.9 = (bf16[64,1024]{1,0:T(8,128)(2,1)S(1)}, bf16[64,1024]{1,0:T(8,128)(2,1)S(1)}, u32[]{:S(2)}, u32[]{:S(2)}) collective-permute-start(bf16[64,1024]{1,0:T(8,128)(2,1)S(1)} %get-tuple-element.478), channel_id=1, source_target_pairs={{0,16},{8,24},{16,32},{24,40},{32,48},{40,56},{48,0},{56,8},{64,80... | collective-permute-start | bytes 393224 | tf_op jit(solution)/shard_map/ppermute | solution.py:615
  63.6 1.0 copy-done.4
  64.6 0.9 copy-done.6
  66.4 3.4 %collective-permute-start.3 = (bf16[128,1024]{1,0:T(8,128)(2,1)S(1)}, bf16[128,1024]{1,0:T(8,128)(2,1)S(1)}, u32[]{:S(2)}, u32[]{:S(2)}) collective-permute-start(bf16[128,1024]{1,0:T(8,128)(2,1)S(1)} %get-tuple-element.475), channel_id=1, source_target_pairs={{0,32},{8,40},{64,96},{72,104},{128,160},{136,168},{192,224},{200,... | collective-permute-start | bytes 786440 | tf_op jit(solution)/shard_map/ppermute | solution.py:608
  70.4 1.6 %collective-permute-start.18 = (bf16[256,1024]{1,0:T(8,128)(2,1)S(1)}, bf16[256,1024]{1,0:T(8,128)(2,1)S(1)}, u32[]{:S(2)}, u32[]{:S(2)}) collective-permute-start(bf16[256,1024]{1,0:T(8,128)(2,1)S(1)} %get-tuple-element.490.y0_ref), channel_id=1, source_target_pairs={{0,192},{8,200},{16,208},{24,216},{32,224},{40,232},{48,240},{56,2... | collective-permute-start | bytes 1572872 | tf_op jit(solution)/shard_map/ppermute | solution.py:638
  72.0 1.7 %collective-permute-start.22 = (bf16[384,512]{1,0:T(8,128)(2,1)S(1)}, bf16[384,512]{1,0:T(8,128)(2,1)S(1)}, u32[]{:S(2)}, u32[]{:S(2)}) collective-permute-start(bf16[384,512]{1,0:T(8,128)(2,1)S(1)} %choose.1.mine_ref), channel_id=1, source_target_pairs={{0,4},{1,5},{2,6},{3,7},{4,0},{5,1},{6,2},{7,3},{8,12},{9,13},{10,... | collective-permute-start | bytes 1179656 | tf_op jit(solution)/shard_map/ppermute | solution.py:647
  74.2 3.0 %collective-permute-start.14 = (bf16[32,1024]{1,0:T(8,128)(2,1)S(1)}, bf16[32,1024]{1,0:T(8,128)(2,1)S(1)}, u32[]{:S(2)}, u32[]{:S(2)}) collective-permute-start(bf16[32,1024]{1,0:T(8,128)(2,1)S(1)} %get-tuple-element.487), channel_id=1, source_target_pairs={{0,8},{8,16},{32,40},{40,48},{64,72},{72,80},{96,104},{104,112},{1... | collective-permute-start | bytes 196616 | tf_op jit(solution)/shard_map/ppermute | solution.py:645
  77.3 1.6 %collective-permute-start.15 = (bf16[32,1024]{1,0:T(8,128)(2,1)S(1)}, bf16[32,1024]{1,0:T(8,128)(2,1)S(1)}, u32[]{:S(2)}, u32[]{:S(2)}) collective-permute-start(bf16[32,1024]{1,0:T(8,128)(2,1)S(1)} %get-tuple-element.488), channel_id=1, source_target_pairs={{0,16},{8,24},{32,48},{40,56},{64,80},{72,88},{96,112},{104,120},{... | collective-permute-start | bytes 196616 | tf_op jit(solution)/shard_map/ppermute | solution.py:645
  78.9 3.9 %collective-permute-start.21 = (bf16[128,512]{1,0:T(8,128)(2,1)S(1)}, bf16[128,512]{1,0:T(8,128)(2,1)S(1)}, u32[]{:S(2)}, u32[]{:S(2)}) collective-permute-start(bf16[128,512]{1,0:T(8,128)(2,1)S(1)} %get-tuple-element.484.own_ref), channel_id=1, source_target_pairs={{0,6},{1,7},{8,14},{9,15},{16,22},{17,23},{24,30},{25,31},{32,38},... | collective-permute-start | bytes 393224 | tf_op jit(solution)/shard_map/ppermute | solution.py:639
  82.8 2.3 %collective-permute-start.16 = (bf16[32,1024]{1,0:T(8,128)(2,1)S(1)}, bf16[32,1024]{1,0:T(8,128)(2,1)S(1)}, u32[]{:S(2)}, u32[]{:S(2)}) collective-permute-start(bf16[32,1024]{1,0:T(8,128)(2,1)S(1)} %get-tuple-element.489), channel_id=1, source_target_pairs={{0,24},{8,32},{32,56},{40,0},{64,88},{72,96},{96,120},{104,64},{12... | collective-permute-start | bytes 196616 | tf_op jit(solution)/shard_map/ppermute | solution.py:645
  85.1 6.9 %collective-permute-done.16.refs_3_ = bf16[32,1024]{1,0:T(8,128)(2,1)S(1)} collective-permute-done((bf16[32,1024]{1,0:T(8,128)(2,1)S(1)}, bf16[32,1024]{1,0:T(8,128)(2,1)S(1)}, u32[]{:S(2)}, u32[]{:S(2)}) %collective-permute-start.16) | collective-permute-done | bytes 65568 | tf_op jit(solution)/shard_map/ppermute | solution.py:645
  92.0 1.3 collective-permute-start.20
  93.3 1.3 collective-permute-start.19
  95.2 1.4 collective-permute-done.19.one_ref
  97.3 7.1 %collective-permute-start.23 = (bf16[1536,512]{1,0:T(8,128)(2,1)S(1)}, bf16[1536,512]{1,0:T(8,128)(2,1)S(1)}, u32[]{:S(2)}, u32[]{:S(2)}) collective-permute-start(bf16[1536,512]{1,0:T(8,128)(2,1)S(1)} %part.1.part_ref), channel_id=1, source_target_pairs={{0,1},{1,0},{2,3},{3,2},{4,5},{5,4},{6,7},{7,6},{8,9},{9,8},{10,11... | collective-permute-start | bytes 4718600 | tf_op jit(solution)/shard_map/ppermute | solution.py:676
  105.0 2.4 %collective-permute-start.26 = (bf16[128,512]{1,0:T(8,128)(2,1)S(1)}, bf16[128,512]{1,0:T(8,128)(2,1)S(1)}, u32[]{:S(2)}, u32[]{:S(2)}) collective-permute-start(bf16[128,512]{1,0:T(8,128)(2,1)S(1)} %extra.1.c0_ref), channel_id=1, source_target_pairs={{0,128},{8,136},{16,144},{24,152},{32,160},{40,168},{48,176},{56,1... | collective-permute-start | bytes 393224 | tf_op jit(solution)/shard_map/ppermute | solution.py:657
  107.5 2.7 %collective-permute-start.28 = (bf16[128,1024]{1,0:T(8,128)(2,1)S(1)}, bf16[128,1024]{1,0:T(8,128)(2,1)S(1)}, u32[]{:S(2)}, u32[]{:S(2)}) collective-permute-start(bf16[128,1024]{1,0:T(8,128)(2,1)S(1)} %slice.132), channel_id=1, source_target_pairs={{0,192},{8,200},{16,208},{24,216},{32,224},{40,232},{48,240},{56,2... | collective-permute-start | bytes 786440 | tf_op jit(solution)/shard_map/ppermute | solution.py:653
  110.2 1.4 collective-permute-done.26.c3_ref
  111.7 1.2 collective-permute-start.24
  113.5 5.5 %collective-permute-done.25.c2_ref = bf16[128,512]{1,0:T(8,128)(2,1)S(1)} collective-permute-done((bf16[128,512]{1,0:T(8,128)(2,1)S(1)}, bf16[128,512]{1,0:T(8,128)(2,1)S(1)}, u32[]{:S(2)}, u32[]{:S(2)}) %collective-permute-start.25) | collective-permute-done | bytes 131104 | tf_op jit(solution)/shard_map/ppermute | solution.py:657
  119.0 1.3 collective-permute-start.31
  120.3 4.2 %collective-permute-start.30 = (bf16[64,512]{1,0:T(8,128)(2,1)S(1)}, bf16[64,512]{1,0:T(8,128)(2,1)S(1)}, u32[]{:S(2)}, u32[]{:S(2)}) collective-permute-start(bf16[64,512]{1,0:T(8,128)(2,1)S(1)} %get-tuple-element.503.own_ref), channel_id=1, source_target_pairs={{0,4},{1,5},{8,12},{9,13},{16,20},{17,21},{24,28},{25,29},{32,36},... | collective-permute-start | bytes 196616 | tf_op jit(solution)/shard_map/ppermute | solution.py:665
  124.5 1.3 collective-permute-start.29
  125.8 1.7 %settle.1.rows_ref = bf16[1536,1024]{1,0:T(8,128)(2,1)S(1)} custom-call(bf16[1536,1024]{1,0:T(8,128)(2,1)S(1)} %bitcast.72, s32[1,64]{1,0:T(1,128)S(1)} %get-tuple-element.464.land_ref, bf16[64,1024]{1,0:T(8,128)(2,1)S(1)} %get-tuple-element.497.gone_ref), custom_call_target="tpu_custom_call" | custom-call | tf_op jit(solution)/shard_map/settle/pallas_call | solution.py:683
  127.6 2.4 %factor.1.factor_ref = bf16[1536,512]{1,0:T(8,128)(2,1)S(1)} custom-call(s32[2]{0:T(128)S(1)} %pad_add_fusion.pos_ref, bf16[1536,512]{1,0:T(8,128)(2,1)S(1)} %part.1.part_ref, bf16[1536,512]{1,0:T(8,128)(2,1)S(1)} %collective-permute-done.23.other_ref, bf16[2,512,512]{2,1,0:T(8,128)(2,1)S(1)} %copy-done.11), custom_call_target="tpu_custom_call" | custom-call | tf_op jit(solution)/shard_map/factor/pallas_call | solution.py:693
  130.7 1.0 collective-permute-start.32
  132.4 0.9 collective-permute-done.32.cross_other_ref
  133.3 10.1 %finish.1 = bf16[1536,1024]{1,0:T(8,128)(2,1)S(1)} custom-call(s32[2]{0:T(128)S(1)} %pad_add_fusion.pos_ref, bf16[1536,1024]{1,0:T(8,128)(2,1)S(1)} %settle.1.rows_ref, bf16[1536,512]{1,0:T(8,128)(2,1)S(1)} %part.1.part_ref, bf16[1536,512]{1,0:T(8,128)(2,1)S(1)} %collective-permute-done.23.other_ref, bf16[1536,512]{1,0:T(8,128)(2,1)S(1)} %factor.1.factor_ref, ...), custom_call_target="tpu_custom_call" | custom-call | tf_op jit(solution)/shard_map/finish/pallas_call | solution.py:731
  143.4 3.9 %reshape.435 = bf16[3,512,2,512]{3,2,1,0:T(2,128)(2,1)} reshape(bf16[1536,1024]{1,0:T(8,128)(2,1)S(1)} %finish.1) | data formatting | bytes 6291456 | tf_op jit(solution)/shard_map/reshape | solution.py:762
  147.4 0.9 while.26
  (69 shorter events, 9.8 us)
Async XLA Ops:
  6.5 2.8 %copy-start.13 = (s32[2,512]{1,0:T(2,128)S(1)}, s32[2,512]{1,0:T(2,128)}, u32[]{:S(2)}) copy-start(s32[2,512]{1,0:T(2,128)} %across_ref.3) | copy-start | bytes 12292
  12.2 0.8 copy-start.2
  13.1 0.6 copy-start.7
  13.7 28.9 %all-to-all-start = ((bf16[32,8,1024]{2,1,0:T(8,128)(2,1)}), bf16[32,8,1024]{2,1,0:T(8,128)(2,1)}, u32[]{:S(2)}, u32[]{:S(2)}) async-start(bf16[32,8,1024]{2,1,0:T(8,128)(2,1)} %bitcast.73), calls=%async_computation | async-start | bytes 1048576 | tf_op jit(solution)/shard_map/all_to_all | solution.py:561
  25.9 10.3 %copy-start.12 = (bf16[2,512,512]{2,1,0:T(8,128)(2,1)S(1)}, bf16[2,512,512]{2,1,0:T(8,128)(2,1)}, u32[]{:S(2)}) copy-start(bf16[2,512,512]{2,1,0:T(8,128)(2,1)} %lower_ref.1) | copy-start | bytes 3145732
  26.9 20.1 %collective-permute-start.8 = (bf16[384,512]{1,0:T(8,128)(2,1)}, bf16[384,512]{1,0:T(8,128)(2,1)}, u32[]{:S(2)}, u32[]{:S(2)}) collective-permute-start(bf16[384,512]{1,0:T(8,128)(2,1)} %get-tuple-element.572), channel_id=1, source_target_pairs={{0,6},{1,7},{8,14},{9,15},{16,22},{17,23},{24,30},{25,31},{32,38},... | collective-permute-start | bytes 1179656 | tf_op jit(solution)/shard_map/ppermute | solution.py:565
  32.1 18.1 %collective-permute-start.7 = (bf16[384,512]{1,0:T(8,128)(2,1)}, bf16[384,512]{1,0:T(8,128)(2,1)}, u32[]{:S(2)}, u32[]{:S(2)}) collective-permute-start(bf16[384,512]{1,0:T(8,128)(2,1)} %get-tuple-element.573), channel_id=1, source_target_pairs={{0,4},{1,5},{8,12},{9,13},{16,20},{17,21},{24,28},{25,29},{32,36},... | collective-permute-start | bytes 1179656 | tf_op jit(solution)/shard_map/ppermute | solution.py:565
  34.1 18.2 %collective-permute-start.6 = (bf16[384,512]{1,0:T(8,128)(2,1)}, bf16[384,512]{1,0:T(8,128)(2,1)}, u32[]{:S(2)}, u32[]{:S(2)}) collective-permute-start(bf16[384,512]{1,0:T(8,128)(2,1)} %get-tuple-element.574), channel_id=1, source_target_pairs={{0,2},{1,3},{8,10},{9,11},{16,18},{17,19},{24,26},{25,27},{32,34},... | collective-permute-start | bytes 1179656 | tf_op jit(solution)/shard_map/ppermute | solution.py:565
  40.2 1.0 copy-start
  41.2 0.7 copy-start.3
  41.9 0.7 copy-start.5
  42.6 0.7 copy-start.8
  44.6 10.4 %collective-permute-start.5 = (bf16[32,1024]{1,0:T(8,128)(2,1)S(1)}, bf16[32,1024]{1,0:T(8,128)(2,1)S(1)}, u32[]{:S(2)}, u32[]{:S(2)}) collective-permute-start(bf16[32,1024]{1,0:T(8,128)(2,1)S(1)} %block.1.block_ref), channel_id=1, source_target_pairs={{0,56},{8,0},{16,8},{24,16},{32,24},{40,32},{48,40},{56,48},{64,12... | collective-permute-start | bytes 196616 | tf_op jit(solution)/shard_map/ppermute | solution.py:596
  47.0 8.0 %collective-permute-start.4 = (bf16[32,1024]{1,0:T(8,128)(2,1)S(1)}, bf16[32,1024]{1,0:T(8,128)(2,1)S(1)}, u32[]{:S(2)}, u32[]{:S(2)}) collective-permute-start(bf16[32,1024]{1,0:T(8,128)(2,1)S(1)} %block.1.block_ref), channel_id=1, source_target_pairs={{0,8},{8,16},{16,24},{24,32},{32,40},{40,48},{48,56},{56,0},{64,72... | collective-permute-start | bytes 196616 | tf_op jit(solution)/shard_map/ppermute | solution.py:595
  47.0 10.3 %collective-permute-start = (bf16[144,1024]{1,0:T(8,128)(2,1)}, bf16[144,1024]{1,0:T(8,128)(2,1)S(1)}, u32[]{:S(2)}, u32[]{:S(2)}) collective-permute-start(bf16[144,1024]{1,0:T(8,128)(2,1)} %get-tuple-element.471), channel_id=1, source_target_pairs={{0,64},{8,72},{1,65},{9,73},{2,66},{10,74},{3,67},{11,75},{4,68},{... | collective-permute-start | bytes 884744 | tf_op jit(solution)/shard_map/ppermute | solution.py:590
  50.1 11.1 %collective-permute-start.1 = (bf16[144,1024]{1,0:T(8,128)(2,1)}, bf16[144,1024]{1,0:T(8,128)(2,1)S(1)}, u32[]{:S(2)}, u32[]{:S(2)}) collective-permute-start(bf16[144,1024]{1,0:T(8,128)(2,1)} %get-tuple-element.472), channel_id=1, source_target_pairs={{0,128},{8,136},{1,129},{9,137},{2,130},{10,138},{3,131},{11,139},... | collective-permute-start | bytes 884744 | tf_op jit(solution)/shard_map/ppermute | solution.py:590
  52.3 8.9 %collective-permute-start.2 = (bf16[144,1024]{1,0:T(8,128)(2,1)}, bf16[144,1024]{1,0:T(8,128)(2,1)S(1)}, u32[]{:S(2)}, u32[]{:S(2)}) collective-permute-start(bf16[144,1024]{1,0:T(8,128)(2,1)} %get-tuple-element.473), channel_id=1, source_target_pairs={{0,192},{8,200},{1,193},{9,201},{2,194},{10,202},{3,195},{11,203},... | collective-permute-start | bytes 884744 | tf_op jit(solution)/shard_map/ppermute | solution.py:590
  55.0 14.8 %collective-permute-start.13 = (bf16[384,512]{1,0:T(8,128)(2,1)S(1)}, bf16[384,512]{1,0:T(8,128)(2,1)S(1)}, u32[]{:S(2)}, u32[]{:S(2)}) collective-permute-start(bf16[384,512]{1,0:T(8,128)(2,1)S(1)} %choose.1.mine_ref), channel_id=1, source_target_pairs={{2,0},{3,1},{4,2},{5,3},{6,4},{7,5},{0,6},{1,7},{10,8},{11,9},{12,... | collective-permute-start | bytes 1179656 | tf_op jit(solution)/shard_map/ppermute | solution.py:620
  55.1 14.7 %collective-permute-start.12 = (bf16[384,512]{1,0:T(8,128)(2,1)S(1)}, bf16[384,512]{1,0:T(8,128)(2,1)S(1)}, u32[]{:S(2)}, u32[]{:S(2)}) collective-permute-start(bf16[384,512]{1,0:T(8,128)(2,1)S(1)} %choose.1.mine_ref), channel_id=1, source_target_pairs={{0,2},{1,3},{2,4},{3,5},{4,6},{5,7},{6,0},{7,1},{8,10},{9,11},{10,... | collective-permute-start | bytes 1179656 | tf_op jit(solution)/shard_map/ppermute | solution.py:619
  57.3 9.1 %collective-permute-start.11 = (bf16[32,1024]{1,0:T(8,128)(2,1)S(1)}, bf16[32,1024]{1,0:T(8,128)(2,1)S(1)}, u32[]{:S(2)}, u32[]{:S(2)}) collective-permute-start(bf16[32,1024]{1,0:T(8,128)(2,1)S(1)} %block.1.block_ref), channel_id=1, source_target_pairs={{0,32},{8,40},{16,48},{24,56},{32,0},{40,8},{48,16},{56,24},{64,96... | collective-permute-start | bytes 196616 | tf_op jit(solution)/shard_map/ppermute | solution.py:597
  61.2 8.5 %collective-permute-start.10 = (bf16[64,1024]{1,0:T(8,128)(2,1)S(1)}, bf16[64,1024]{1,0:T(8,128)(2,1)S(1)}, u32[]{:S(2)}, u32[]{:S(2)}) collective-permute-start(bf16[64,1024]{1,0:T(8,128)(2,1)S(1)} %get-tuple-element.479), channel_id=1, source_target_pairs={{0,48},{8,56},{16,0},{24,8},{32,16},{40,24},{48,32},{56,40},{64,11... | collective-permute-start | bytes 393224 | tf_op jit(solution)/shard_map/ppermute | solution.py:616
  61.2 8.5 %collective-permute-start.9 = (bf16[64,1024]{1,0:T(8,128)(2,1)S(1)}, bf16[64,1024]{1,0:T(8,128)(2,1)S(1)}, u32[]{:S(2)}, u32[]{:S(2)}) collective-permute-start(bf16[64,1024]{1,0:T(8,128)(2,1)S(1)} %get-tuple-element.478), channel_id=1, source_target_pairs={{0,16},{8,24},{16,32},{24,40},{32,48},{40,56},{48,0},{56,8},{64,80... | collective-permute-start | bytes 393224 | tf_op jit(solution)/shard_map/ppermute | solution.py:615
  63.6 1.0 copy-start.4
  64.6 0.9 copy-start.6
  66.4 7.3 %collective-permute-start.3 = (bf16[128,1024]{1,0:T(8,128)(2,1)S(1)}, bf16[128,1024]{1,0:T(8,128)(2,1)S(1)}, u32[]{:S(2)}, u32[]{:S(2)}) collective-permute-start(bf16[128,1024]{1,0:T(8,128)(2,1)S(1)} %get-tuple-element.475), channel_id=1, source_target_pairs={{0,32},{8,40},{64,96},{72,104},{128,160},{136,168},{192,224},{200,... | collective-permute-start | bytes 786440 | tf_op jit(solution)/shard_map/ppermute | solution.py:608
  70.4 26.2 %collective-permute-start.18 = (bf16[256,1024]{1,0:T(8,128)(2,1)S(1)}, bf16[256,1024]{1,0:T(8,128)(2,1)S(1)}, u32[]{:S(2)}, u32[]{:S(2)}) collective-permute-start(bf16[256,1024]{1,0:T(8,128)(2,1)S(1)} %get-tuple-element.490.y0_ref), channel_id=1, source_target_pairs={{0,192},{8,200},{16,208},{24,216},{32,224},{40,232},{48,240},{56,2... | collective-permute-start | bytes 1572872 | tf_op jit(solution)/shard_map/ppermute | solution.py:638
  72.0 24.6 %collective-permute-start.17 = (bf16[256,1024]{1,0:T(8,128)(2,1)S(1)}, bf16[256,1024]{1,0:T(8,128)(2,1)S(1)}, u32[]{:S(2)}, u32[]{:S(2)}) collective-permute-start(bf16[256,1024]{1,0:T(8,128)(2,1)S(1)} %get-tuple-element.490.y0_ref), channel_id=1, source_target_pairs={{0,64},{8,72},{16,80},{24,88},{32,96},{40,104},{48,112},{56,120},{... | collective-permute-start | bytes 1572872 | tf_op jit(solution)/shard_map/ppermute | solution.py:637
  72.0 24.6 %collective-permute-start.22 = (bf16[384,512]{1,0:T(8,128)(2,1)S(1)}, bf16[384,512]{1,0:T(8,128)(2,1)S(1)}, u32[]{:S(2)}, u32[]{:S(2)}) collective-permute-start(bf16[384,512]{1,0:T(8,128)(2,1)S(1)} %choose.1.mine_ref), channel_id=1, source_target_pairs={{0,4},{1,5},{2,6},{3,7},{4,0},{5,1},{6,2},{7,3},{8,12},{9,13},{10,... | collective-permute-start | bytes 1179656 | tf_op jit(solution)/shard_map/ppermute | solution.py:647
  74.2 4.7 %collective-permute-start.14 = (bf16[32,1024]{1,0:T(8,128)(2,1)S(1)}, bf16[32,1024]{1,0:T(8,128)(2,1)S(1)}, u32[]{:S(2)}, u32[]{:S(2)}) collective-permute-start(bf16[32,1024]{1,0:T(8,128)(2,1)S(1)} %get-tuple-element.487), channel_id=1, source_target_pairs={{0,8},{8,16},{32,40},{40,48},{64,72},{72,80},{96,104},{104,112},{1... | collective-permute-start | bytes 196616 | tf_op jit(solution)/shard_map/ppermute | solution.py:645
  77.3 5.5 %collective-permute-start.15 = (bf16[32,1024]{1,0:T(8,128)(2,1)S(1)}, bf16[32,1024]{1,0:T(8,128)(2,1)S(1)}, u32[]{:S(2)}, u32[]{:S(2)}) collective-permute-start(bf16[32,1024]{1,0:T(8,128)(2,1)S(1)} %get-tuple-element.488), channel_id=1, source_target_pairs={{0,16},{8,24},{32,48},{40,56},{64,80},{72,88},{96,112},{104,120},{... | collective-permute-start | bytes 196616 | tf_op jit(solution)/shard_map/ppermute | solution.py:645
  78.9 14.4 %collective-permute-start.21 = (bf16[128,512]{1,0:T(8,128)(2,1)S(1)}, bf16[128,512]{1,0:T(8,128)(2,1)S(1)}, u32[]{:S(2)}, u32[]{:S(2)}) collective-permute-start(bf16[128,512]{1,0:T(8,128)(2,1)S(1)} %get-tuple-element.484.own_ref), channel_id=1, source_target_pairs={{0,6},{1,7},{8,14},{9,15},{16,22},{17,23},{24,30},{25,31},{32,38},... | collective-permute-start | bytes 393224 | tf_op jit(solution)/shard_map/ppermute | solution.py:639
  82.8 9.2 %collective-permute-start.16 = (bf16[32,1024]{1,0:T(8,128)(2,1)S(1)}, bf16[32,1024]{1,0:T(8,128)(2,1)S(1)}, u32[]{:S(2)}, u32[]{:S(2)}) collective-permute-start(bf16[32,1024]{1,0:T(8,128)(2,1)S(1)} %get-tuple-element.489), channel_id=1, source_target_pairs={{0,24},{8,32},{32,56},{40,0},{64,88},{72,96},{96,120},{104,64},{12... | collective-permute-start | bytes 196616 | tf_op jit(solution)/shard_map/ppermute | solution.py:645
  92.0 3.2 %collective-permute-start.20 = (bf16[128,512]{1,0:T(8,128)(2,1)S(1)}, bf16[128,512]{1,0:T(8,128)(2,1)S(1)}, u32[]{:S(2)}, u32[]{:S(2)}) collective-permute-start(bf16[128,512]{1,0:T(8,128)(2,1)S(1)} %get-tuple-element.484.own_ref), channel_id=1, source_target_pairs={{0,4},{1,5},{8,12},{9,13},{16,20},{17,21},{24,28},{25,29},{32,36},... | collective-permute-start | bytes 393224 | tf_op jit(solution)/shard_map/ppermute | solution.py:639
  93.3 3.3 %collective-permute-start.19 = (bf16[128,512]{1,0:T(8,128)(2,1)S(1)}, bf16[128,512]{1,0:T(8,128)(2,1)S(1)}, u32[]{:S(2)}, u32[]{:S(2)}) collective-permute-start(bf16[128,512]{1,0:T(8,128)(2,1)S(1)} %get-tuple-element.484.own_ref), channel_id=1, source_target_pairs={{0,2},{1,3},{8,10},{9,11},{16,18},{17,19},{24,26},{25,27},{32,34},... | collective-permute-start | bytes 393224 | tf_op jit(solution)/shard_map/ppermute | solution.py:639
  97.3 27.2 %collective-permute-start.23 = (bf16[1536,512]{1,0:T(8,128)(2,1)S(1)}, bf16[1536,512]{1,0:T(8,128)(2,1)S(1)}, u32[]{:S(2)}, u32[]{:S(2)}) collective-permute-start(bf16[1536,512]{1,0:T(8,128)(2,1)S(1)} %part.1.part_ref), channel_id=1, source_target_pairs={{0,1},{1,0},{2,3},{3,2},{4,5},{5,4},{6,7},{7,6},{8,9},{9,8},{10,11... | collective-permute-start | bytes 4718600 | tf_op jit(solution)/shard_map/ppermute | solution.py:676
  105.0 6.7 %collective-permute-start.26 = (bf16[128,512]{1,0:T(8,128)(2,1)S(1)}, bf16[128,512]{1,0:T(8,128)(2,1)S(1)}, u32[]{:S(2)}, u32[]{:S(2)}) collective-permute-start(bf16[128,512]{1,0:T(8,128)(2,1)S(1)} %extra.1.c0_ref), channel_id=1, source_target_pairs={{0,128},{8,136},{16,144},{24,152},{32,160},{40,168},{48,176},{56,1... | collective-permute-start | bytes 393224 | tf_op jit(solution)/shard_map/ppermute | solution.py:657
  107.4 22.6 %collective-permute-start.27 = (bf16[128,1024]{1,0:T(8,128)(2,1)S(1)}, bf16[128,1024]{1,0:T(8,128)(2,1)S(1)}, u32[]{:S(2)}, u32[]{:S(2)}) collective-permute-start(bf16[128,1024]{1,0:T(8,128)(2,1)S(1)} %slice.131), channel_id=1, source_target_pairs={{0,64},{8,72},{16,80},{24,88},{32,96},{40,104},{48,112},{56,120},{... | collective-permute-start | bytes 786440 | tf_op jit(solution)/shard_map/ppermute | solution.py:652
  107.5 22.5 %collective-permute-start.28 = (bf16[128,1024]{1,0:T(8,128)(2,1)S(1)}, bf16[128,1024]{1,0:T(8,128)(2,1)S(1)}, u32[]{:S(2)}, u32[]{:S(2)}) collective-permute-start(bf16[128,1024]{1,0:T(8,128)(2,1)S(1)} %slice.132), channel_id=1, source_target_pairs={{0,192},{8,200},{16,208},{24,216},{32,224},{40,232},{48,240},{56,2... | collective-permute-start | bytes 786440 | tf_op jit(solution)/shard_map/ppermute | solution.py:653
  110.2 8.9 %collective-permute-start.25 = (bf16[128,512]{1,0:T(8,128)(2,1)S(1)}, bf16[128,512]{1,0:T(8,128)(2,1)S(1)}, u32[]{:S(2)}, u32[]{:S(2)}) collective-permute-start(bf16[128,512]{1,0:T(8,128)(2,1)S(1)} %extra.1.c0_ref), channel_id=1, source_target_pairs={{0,192},{8,200},{16,208},{24,216},{32,224},{40,232},{48,240},{56,2... | collective-permute-start | bytes 393224 | tf_op jit(solution)/shard_map/ppermute | solution.py:657
  111.7 8.6 %collective-permute-start.24 = (bf16[128,512]{1,0:T(8,128)(2,1)S(1)}, bf16[128,512]{1,0:T(8,128)(2,1)S(1)}, u32[]{:S(2)}, u32[]{:S(2)}) collective-permute-start(bf16[128,512]{1,0:T(8,128)(2,1)S(1)} %extra.1.c0_ref), channel_id=1, source_target_pairs={{0,64},{8,72},{16,80},{24,88},{32,96},{40,104},{48,112},{56,120},{... | collective-permute-start | bytes 393224 | tf_op jit(solution)/shard_map/ppermute | solution.py:657
  119.0 11.0 %collective-permute-start.31 = (bf16[64,512]{1,0:T(8,128)(2,1)S(1)}, bf16[64,512]{1,0:T(8,128)(2,1)S(1)}, u32[]{:S(2)}, u32[]{:S(2)}) collective-permute-start(bf16[64,512]{1,0:T(8,128)(2,1)S(1)} %get-tuple-element.503.own_ref), channel_id=1, source_target_pairs={{0,6},{1,7},{8,14},{9,15},{16,22},{17,23},{24,30},{25,31},{32,38},... | collective-permute-start | bytes 196616 | tf_op jit(solution)/shard_map/ppermute | solution.py:665
  120.3 9.7 %collective-permute-start.30 = (bf16[64,512]{1,0:T(8,128)(2,1)S(1)}, bf16[64,512]{1,0:T(8,128)(2,1)S(1)}, u32[]{:S(2)}, u32[]{:S(2)}) collective-permute-start(bf16[64,512]{1,0:T(8,128)(2,1)S(1)} %get-tuple-element.503.own_ref), channel_id=1, source_target_pairs={{0,4},{1,5},{8,12},{9,13},{16,20},{17,21},{24,28},{25,29},{32,36},... | collective-permute-start | bytes 196616 | tf_op jit(solution)/shard_map/ppermute | solution.py:665
  124.5 5.6 %collective-permute-start.29 = (bf16[64,512]{1,0:T(8,128)(2,1)S(1)}, bf16[64,512]{1,0:T(8,128)(2,1)S(1)}, u32[]{:S(2)}, u32[]{:S(2)}) collective-permute-start(bf16[64,512]{1,0:T(8,128)(2,1)S(1)} %get-tuple-element.503.own_ref), channel_id=1, source_target_pairs={{0,2},{1,3},{8,10},{9,11},{16,18},{17,19},{24,26},{25,27},{32,34},... | collective-permute-start | bytes 196616 | tf_op jit(solution)/shard_map/ppermute | solution.py:665
  125.8 1.7 %copy-start.11 = (bf16[2,512,512]{2,1,0:T(8,128)(2,1)S(1)}, bf16[2,512,512]{2,1,0:T(8,128)(2,1)}, u32[]{:S(2)}) copy-start(bf16[2,512,512]{2,1,0:T(8,128)(2,1)} %upper_ref.3) | copy-start | bytes 3145732
  127.6 4.1 %copy-start.1 = (bf16[2,512,512]{2,1,0:T(8,128)(2,1)S(1)}, bf16[2,512,512]{2,1,0:T(8,128)(2,1)}, u32[]{:S(2)}) copy-start(bf16[2,512,512]{2,1,0:T(8,128)(2,1)} %copy-done) | copy-start | bytes 3145732
  130.7 2.6 %collective-permute-start.32 = (bf16[576,512]{1,0:T(8,128)(2,1)S(1)}, bf16[576,512]{1,0:T(8,128)(2,1)S(1)}, u32[]{:S(2)}, u32[]{:S(2)}) collective-permute-start(bf16[576,512]{1,0:T(8,128)(2,1)S(1)} %cross.1.cross_ref), channel_id=1, source_target_pairs={{0,1},{1,0},{2,3},{3,2},{4,5},{5,4},{6,7},{7,6},{8,9},{9,8},{10,11... | collective-permute-start | bytes 1769480 | tf_op jit(solution)/shard_map/ppermute | solution.py:715
  143.4 3.9 %copy-start.14 = (s32[2,512]{1,0:T(2,128)S(1)}, s32[2,512]{1,0:T(2,128)}, u32[]{:S(2)}) copy-start(s32[2,512]{1,0:T(2,128)} %across_ref.3) | copy-start | bytes 12292

commit v7 on v6

--- a/solution.py
+++ b/solution.py
@@ -27,6 +27,10 @@
 
 def move_x(pairs):
     return [(a * NC + core, b * NC + core) for a, b in pairs for core in range(NC)]
+
+
+def cross_y(bit):
+    return [(y * NZ + z, (y ^ bit) * NZ + z) for y in range(NY) for z in range(NZ)]
 
 
 SWAP = [(x * NC + core, x * NC + 1 - core) for x in range(NX) for core in range(NC)]
@@ -339,25 +343,26 @@
     send_ref[...] = spread[n_rows // 2 :]
 
 
-def fold_kernel(pos_ref, kept_ref, came_ref, *out_refs):
-    for bit, source in ((0, kept_ref), (4, came_ref)):
-
-        @pl.when((pos_ref[0] & 4) == bit)
-        def _(source=source):
-            for k, ref in enumerate(out_refs):
-                ref[...] = source[k * DEST_ROWS : (k + 1) * DEST_ROWS, :]
-
-
-def gone_kernel(pos_ref, *refs):
-    landed, gone_ref, gone_panel_ref = refs[:4], refs[4], refs[5]
-    width = gone_panel_ref.shape[1]
-    for s in range(2):
-        for k in range(4):
-
-            @pl.when(((pos_ref[0] - s) & 3) == k)
-            def _(k=k, s=s):
-                gone_ref[s * DEST_ROWS : (s + 1) * DEST_ROWS, :] = landed[k][...]
-
+def fold_kernel(bit, pos_ref, kept_ref, came_ref, keep_ref, send_ref):
+    n = keep_ref.shape[0]
+
+    @pl.when((pos_ref[0] & bit) == 0)
+    def _():
+        keep_ref[...] = kept_ref[:n, :]
+        send_ref[...] = kept_ref[n:, :]
+
+    @pl.when((pos_ref[0] & bit) != 0)
+    def _():
+        keep_ref[...] = came_ref[:n, :]
+        send_ref[...] = came_ref[n:, :]
+
+
+def gone_kernel(pos_ref, kept_ref, came_ref, gone_ref, gone_panel_ref):
+    n, width = kept_ref.shape[0], gone_panel_ref.shape[1]
+    even = (pos_ref[0] & 1) == 0
+    kept, came = kept_ref[...], came_ref[...]
+    gone_ref[:n, :] = jnp.where(even, kept, came)
+    gone_ref[n:, :] = jnp.where(even, came, kept)
     gone_panel_ref[...] = gone_ref[:, :width]
 
 
@@ -381,9 +386,22 @@
     )
 
 
-def extra_kernel(pos_ref, own_ref, one_ref, two_ref, three_ref, cross_ref):
-    x = pos_ref[1] >> 1
-    cross_ref[...] = by_x(x, own_ref[...], one_ref[...], two_ref[...], three_ref[...])
+def pass_kernel(pos_ref, own_ref, came_ref, out_ref):
+    out_ref[...] = jnp.where((pos_ref[1] >> 1) == 2, came_ref[...], own_ref[...])
+
+
+def even_odd(pos_ref, even_ref, odd_ref):
+    return jnp.where(((pos_ref[1] >> 1) & 1) == 0, even_ref[...], odd_ref[...])
+
+
+def extra_kernel(pos_ref, even_ref, odd_ref, cross_ref):
+    cross_ref[...] = even_odd(pos_ref, even_ref, odd_ref)
+
+
+def two_kernel(own_ref, came_ref, out_ref):
+    n = own_ref.shape[0]
+    out_ref[:n, :] = own_ref[...]
+    out_ref[n:, :] = came_ref[...]
 
 
 def part_kernel(pos_ref, mine_ref, before_ref, after_ref, across_ref, part_ref):
@@ -394,12 +412,16 @@
         part_ref[pl.ds(pl.multiple_of(begin, n), n), :] = ref[...]
 
 
-def cross_kernel(pos_ref, c0_ref, c1_ref, c2_ref, c3_ref, own_ref, one_ref, two_ref, three_ref, cross_ref):
-    n = c0_ref.shape[0]
-    for k, ref in enumerate((c0_ref, c1_ref, c2_ref, c3_ref)):
-        cross_ref[k * n : (k + 1) * n, :] = ref[...]
-    x = pos_ref[1] >> 1
-    cross_ref[NY * n :, :] = by_x(x, own_ref[...], one_ref[...], two_ref[...], three_ref[...])
+def cross_kernel(pos_ref, near_ref, far_ref, even_ref, odd_ref, cross_ref):
+    y = pos_ref[0] >> 3
+    n = near_ref.shape[0] // 2
+    for k in range(NY):
+        source = near_ref if k < 2 else far_ref
+        place = place_of(((y ^ k) - y) & (NY - 1), Y_ORDER)
+        cross_ref[pl.ds(pl.multiple_of(place * n, n), n), :] = source[
+            (k & 1) * n : ((k & 1) + 1) * n, :
+        ]
+    cross_ref[NY * n :, :] = even_odd(pos_ref, even_ref, odd_ref)
 
 
 def first_kernel(
@@ -587,7 +609,6 @@
         slots,
         limit=32,
     )
-    arrived = [lax.ppermute(leaving[s], "prow", shift_y(s, [0], [0, 1])) for s in (1, 2, 3)]
 
     (block,) = local_kernel(
         block_kernel, "block", [shape((2 * per_home, local_cols))], [], keep, after(dealt, passing)
@@ -595,13 +616,14 @@
     from_lo = lax.ppermute(block, "prow", shift_z(1))
     from_hi = lax.ppermute(block, "prow", shift_z(-1))
     opposite = lax.ppermute(block, "prow", shift_z(4))
+    arrived = [lax.ppermute(leaving[s], "prow", shift_y(s, [0], [0, 1])) for s in (1, 2, 3)]
     quarter_shape = shape((NZ // 2 * DEST_ROWS, local_cols))
     kept, send = local_kernel(
         spread_kernel,
         "spread",
         [quarter_shape] * 2,
         [position],
-        after(passing, block),
+        after(passing, from_lo),
         leaving[0],
         *arrived,
     )
@@ -619,7 +641,7 @@
     before = lax.ppermute(quarter_out, "pcol", move_x(ring))
     behind = lax.ppermute(quarter_out, "pcol", move_x([(b, a) for a, b in ring]))
 
-    two_lo, two_hi, opposite = after((two_lo, two_hi, opposite), before, behind)
+    two_lo, two_hi, opposite = after((two_lo, two_hi, opposite), before, behind, came)
     half = panel // NY
     n_gone = 2 * DEST_ROWS
     z_line, extra = local_kernel(
@@ -636,33 +658,58 @@
     )
     y_lo = lax.ppermute(z_line, "prow", shift_y(1))
     y_hi = lax.ppermute(z_line, "prow", shift_y(-1))
-    sent = [lax.ppermute(extra, "pcol", move_x([(0, k)])) for k in (1, 2, 3)]
-    one_shape = shape((DEST_ROWS, local_cols))
-    spread = local_kernel(
-        fold_kernel, "fold", [one_shape] * 4, [position], kept, after(came, extra)
-    )
-    landed = [spread[0]] + [
-        lax.ppermute(spread[k], "prow", shift_z(k, [0, 1, 4, 5])) for k in (1, 2, 3)
-    ]
+    extra_mid = lax.ppermute(extra, "pcol", move_x([(0, 2)]))
+    extra_shape = shape((half, width))
+    (extra,) = local_kernel(
+        pass_kernel, "pass", [extra_shape], [position], extra, extra_mid
+    )
+    extra_odd = lax.ppermute(extra, "pcol", move_x([(0, 1), (2, 3)]))
+    kept, send = local_kernel(
+        functools.partial(fold_kernel, 4),
+        "fold4",
+        [shape((2 * DEST_ROWS, local_cols))] * 2,
+        [position],
+        kept,
+        after(came, z_line),
+    )
+    came = lax.ppermute(send, "prow", shift_z(2, [0, 1, 4, 5]))
+    kept, send = local_kernel(
+        functools.partial(fold_kernel, 2),
+        "fold2",
+        [shape((DEST_ROWS, local_cols))] * 2,
+        [position],
+        kept,
+        came,
+    )
+    came = lax.ppermute(send, "prow", shift_z(1))
     across = lax.ppermute(
-        after(mine, extra), "pcol", move_x([(x, (x + 2) % NX) for x in range(NX)])
-    )
-
-    y_lo, y_hi = after((y_lo, y_hi), sent, across, landed)
+        after(mine, z_line), "pcol", move_x([(x, (x + 2) % NX) for x in range(NX)])
+    )
+
+    y_lo, y_hi = after((y_lo, y_hi), extra_odd, across, came)
     far_first = lax.ppermute(y_lo[:half], "prow", shift_y(1))
     far_second = lax.ppermute(y_hi[half:], "prow", shift_y(-1))
-    (cross,) = local_kernel(
-        extra_kernel, "extra", [shape((half, width))], [position], extra, *sent
-    )
-    crossed = [lax.ppermute(cross, "prow", shift_y(s)) for s in (1, -1, 2)]
+    (near,) = local_kernel(
+        extra_kernel, "extra", [extra_shape], [position], extra, extra_odd
+    )
+    near_other = lax.ppermute(near, "prow", cross_y(1))
+    (near,) = local_kernel(
+        two_kernel, "two", [shape((2 * half, width))], [], near, near_other
+    )
+    far = lax.ppermute(near, "prow", cross_y(2))
+    gone_shape = shape((n_gone, width))
     gone, gone_panel = local_kernel(
         gone_kernel,
         "gone",
-        [shape((n_gone, local_cols)), shape((n_gone, width))],
+        [shape((n_gone, local_cols)), gone_shape],
         [position],
-        *after(landed, y_lo),
-    )
-    gone_sent = [lax.ppermute(gone_panel, "pcol", move_x([(0, k)])) for k in (1, 2, 3)]
+        *after((kept, came), y_lo),
+    )
+    gone_mid = lax.ppermute(gone_panel, "pcol", move_x([(0, 2)]))
+    (gone_panel,) = local_kernel(
+        pass_kernel, "pass2", [gone_shape], [position], gone_panel, gone_mid
+    )
+    gone_odd = lax.ppermute(gone_panel, "pcol", move_x([(0, 1), (2, 3)]))
     (part,) = local_kernel(
         part_kernel,
         "part",
@@ -701,16 +748,16 @@
         name="factor",
     )(position, part, other, upper_inverse)
 
-    crossed = after(crossed, far_first, far_second, factor_raw, settled)
+    far = after(far, far_first, far_second, factor_raw, settled)
     (cross,) = local_kernel(
         cross_kernel,
         "cross",
         [shape((panel + n_gone, width))],
         [position],
-        cross,
-        *crossed,
+        near,
+        far,
         gone_panel,
-        *gone_sent,
+        gone_odd,
     )
     cross_other = lax.ppermute(cross, "pcol", SWAP)
     row_first, second, a00 = pl.pallas_call(

time: 156 us -> 161 us (1.032)
  waiting for transfers between devices: 19.3 us -> 23.9 us
  starting transfers between devices: 77.9 us -> 74.6 us
  Pallas kernels: 28.9 us -> 31 us
    ppermute x13 -> x9, starting transfers between devices: 25.5 us -> 20.1 us  [the longest x1 5.33 us: per_device(): gone_mid = lax.ppermute(gone_panel, 'pcol', move_x([(0, 2)]))]
    ppermute x1, waiting for transfers between devices: 0.01 us -> 4.87 us  [per_device(): opposite = lax.ppermute(block, 'prow', shift_z(4))]
    ppermute x1, waiting for transfers between devices: 0.01 us -> 4.57 us  [per_device(): two_lo = lax.ppermute(pair_lo, 'prow', shift_z(2))]
    ppermute x13 -> x9, waiting for transfers between devices: 15.8 us -> 11.3 us  [the longest x1 5.1 us: per_device(): near_other = lax.ppermute(near, 'prow', cross_y(1))]
    ppermute x3, waiting for transfers between devices: 2.53 us -> 0.01 us  [per_device(): lax.ppermute(leaving[s], 'prow', shift_y(s, [0], [0, 1]))]
    ppermute x1, starting transfers between devices: 2.36 us -> 0.01 us  [per_device(): two_lo = lax.ppermute(pair_lo, 'prow', shift_z(2))]
    ppermute x1, starting transfers between devices: 2.43 us -> 0.08 us  [per_device(): from_hi = lax.ppermute(block, 'prow', shift_z(-1))]
    ppermute x1, starting transfers between devices: 0.01 us -> 2.16 us  [per_device(): two_hi = lax.ppermute(pair_hi, 'prow', shift_z(-2))]
  transfers between devices with their start and end apart: 34 -> 30, of which waited for: 7 -> 9; matrix products, arithmetic and copies ran while one was open for 1% -> 1% of each run, Pallas kernels for 9% -> 10%
where the time goes in v7:
time: 161 us; the launch traced here: 160 us
  starting transfers between devices  74.6 us (46%)
  Pallas kernels  31 us (19%)
  waiting for transfers between devices  23.9 us (15%)
  local copies, waits for them, and re-layouts  15.8 us (10%)
  between operations  13.8 us (9%)
    pallas_call x16, Pallas kernels, local_kernel(): pl.pallas_call(body, grid=(1,), in_specs=[smem() for _ in scalars] + [who...  16 us
    all_to_all x1, starting transfers between devices, per_device(): dealt = lax.all_to_all(picks, 'prow', 0, 0, tiled=True)  12.2 us
    unnamed x31, local copies, waits for them, and re-layouts  10.8 us
    pallas_call x1, Pallas kernels, per_device(): pl.pallas_call(functools.partial(finish_kernel, panel), grid=(steps + 1,)...  10.1 us
    ppermute x1, starting transfers between devices, per_device(): other = lax.ppermute(part, 'pcol', SWAP)  9.16 us
    ppermute x3, starting transfers between devices, per_device(): lax.ppermute(leaving[s], 'prow', shift_y(s, [0], [0, 1]))  8.69 us
    ppermute x3, starting transfers between devices, per_device(): got = [lax.ppermute(own[k], 'pcol', move_x([(0, k)])) for k in range(1, NX)]  8.51 us
    ppermute x1, starting transfers between devices, per_device(): gone_mid = lax.ppermute(gone_panel, 'pcol', move_x([(0, 2)]))  5.33 us
  transfers between devices with their start and end apart: 30, of which 9 were waited for; matrix products, arithmetic and copies ran while one was open for 1% of the time, Pallas kernels for 10%

profile of v7, /device:TPU:1, one launch (start us, length us, event | category | flops | bytes accessed | tf_op | source)
XLA Modules:
  0.0 160.2 jit_solution(12489732646901541023)
XLA Ops:
  6.5 2.7 %copy.11 = bf16[192,8,2,512]{3,1,2,0:T(8,128)(2,1)S(1)} copy(bf16[192,8,2,512]{3,2,1,0:T(2,128)(2,1)} %bitcast.75) | data formatting | bytes 6291456
  9.4 2.9 %deal.1 = (bf16[256,1024]{1,0:T(8,128)(2,1)S(1)}, s32[32,1]{1,0:T(8,128)S(1)}, s32[2,512]{1,0:T(2,128)S(1)}, s32[1,512]{1,0:T(1,128)S(1)}) custom-call(s32[2]{0:T(128)S(1)} %pad_add_fusion.pos_ref, s32[2,512]{1,0:T(2,128)S(1)} %copy-done.15, bf16[1536,1024]{1,0:T(8,128)(2,1)S(1)} %bitcast.69), custom_call_target="tpu_custom_call" | custom-call | tf_op jit(solution)/shard_map/deal/pallas_call | solution.py:543
  12.3 0.8 copy-done.2
  13.6 12.2 %all-to-all-start = ((bf16[32,8,1024]{2,1,0:T(8,128)(2,1)}), bf16[32,8,1024]{2,1,0:T(8,128)(2,1)}, u32[]{:S(2)}, u32[]{:S(2)}) async-start(bf16[32,8,1024]{2,1,0:T(8,128)(2,1)} %bitcast.73), calls=%async_computation | async-start | bytes 1048576 | tf_op jit(solution)/shard_map/all_to_all | solution.py:583
  25.8 1.1 fusion.28
  26.9 4.4 %collective-permute-start.8 = (bf16[384,512]{1,0:T(8,128)(2,1)S(1)}, bf16[384,512]{1,0:T(8,128)(2,1)S(1)}, u32[]{:S(2)}, u32[]{:S(2)}) collective-permute-start(bf16[384,512]{1,0:T(8,128)(2,1)S(1)} %get-tuple-element.564), channel_id=1, source_target_pairs={{0,6},{1,7},{8,14},{9,15},{16,22},{17,23},{24,30},{25,31},{32,38},... | collective-permute-start | bytes 1179656 | tf_op jit(solution)/shard_map/ppermute | solution.py:587
  31.3 2.0 %collective-permute-start.7 = (bf16[384,512]{1,0:T(8,128)(2,1)}, bf16[384,512]{1,0:T(8,128)(2,1)}, u32[]{:S(2)}, u32[]{:S(2)}) collective-permute-start(bf16[384,512]{1,0:T(8,128)(2,1)} %get-tuple-element.565), channel_id=1, source_target_pairs={{0,4},{1,5},{8,12},{9,13},{16,20},{17,21},{24,28},{25,29},{32,36},... | collective-permute-start | bytes 1179656 | tf_op jit(solution)/shard_map/ppermute | solution.py:587
  33.4 2.1 %collective-permute-start.6 = (bf16[384,512]{1,0:T(8,128)(2,1)}, bf16[384,512]{1,0:T(8,128)(2,1)}, u32[]{:S(2)}, u32[]{:S(2)}) collective-permute-start(bf16[384,512]{1,0:T(8,128)(2,1)} %get-tuple-element.566), channel_id=1, source_target_pairs={{0,2},{1,3},{8,10},{9,11},{16,18},{17,19},{24,26},{25,27},{32,34},... | collective-permute-start | bytes 1179656 | tf_op jit(solution)/shard_map/ppermute | solution.py:587
  35.4 4.1 %leave.1 = (bf16[144,1024]{1,0:T(8,128)(2,1)S(1)}, bf16[144,1024]{1,0:T(8,128)(2,1)}, bf16[144,1024]{1,0:T(8,128)(2,1)}, bf16[144,1024]{1,0:T(8,128)(2,1)}, s32[...) custom-call(s32[2]{0:T(128)S(1)} %pad_add_fusion.pos_ref, ...), custom_call_target="tpu_custom_call" | custom-call | tf_op jit(solution)/shard_map/leave/pallas_call | solution.py:543
  39.5 1.0 copy-done
  41.9 3.8 %collective-permute-start.1 = (bf16[144,1024]{1,0:T(8,128)(2,1)}, bf16[144,1024]{1,0:T(8,128)(2,1)}, u32[]{:S(2)}, u32[]{:S(2)}) collective-permute-start(bf16[144,1024]{1,0:T(8,128)(2,1)} %get-tuple-element.467), channel_id=1, source_target_pairs={{0,64},{8,72},{1,65},{9,73},{2,66},{10,74},{3,67},{11,75},{4,68},{... | collective-permute-start | bytes 884744 | tf_op jit(solution)/shard_map/ppermute | solution.py:619
  45.6 2.9 %collective-permute-start.2 = (bf16[144,1024]{1,0:T(8,128)(2,1)}, bf16[144,1024]{1,0:T(8,128)(2,1)}, u32[]{:S(2)}, u32[]{:S(2)}) collective-permute-start(bf16[144,1024]{1,0:T(8,128)(2,1)} %get-tuple-element.468), channel_id=1, source_target_pairs={{0,128},{8,136},{1,129},{9,137},{2,130},{10,138},{3,131},{11,139},... | collective-permute-start | bytes 884744 | tf_op jit(solution)/shard_map/ppermute | solution.py:619
  49.3 2.0 %collective-permute-start.3 = (bf16[144,1024]{1,0:T(8,128)(2,1)}, bf16[144,1024]{1,0:T(8,128)(2,1)}, u32[]{:S(2)}, u32[]{:S(2)}) collective-permute-start(bf16[144,1024]{1,0:T(8,128)(2,1)} %get-tuple-element.469), channel_id=1, source_target_pairs={{0,192},{8,200},{1,193},{9,201},{2,194},{10,202},{3,195},{11,203},... | collective-permute-start | bytes 884744 | tf_op jit(solution)/shard_map/ppermute | solution.py:619
  52.0 1.3 block.1.block_ref
  53.4 1.4 collective-permute-start
  54.8 1.0 copy-done.4
  55.8 1.2 choose.1.mine_ref
  57.0 0.8 collective-permute-done.lo_ref
  57.9 1.5 collective-permute-start.12
  59.4 1.0 copy-done.6
  60.3 0.9 copy-done.8
  61.2 1.5 spread.1
  62.7 2.9 %collective-permute-start.4 = (bf16[128,1024]{1,0:T(8,128)(2,1)S(1)}, bf16[128,1024]{1,0:T(8,128)(2,1)S(1)}, u32[]{:S(2)}, u32[]{:S(2)}) collective-permute-start(bf16[128,1024]{1,0:T(8,128)(2,1)S(1)} %get-tuple-element.471), channel_id=1, source_target_pairs={{0,32},{8,40},{64,96},{72,104},{128,160},{136,168},{192,224},{200,... | collective-permute-start | bytes 786440 | tf_op jit(solution)/shard_map/ppermute | solution.py:630
  65.7 2.2 %collective-permute-start.10 = (bf16[64,1024]{1,0:T(8,128)(2,1)S(1)}, bf16[64,1024]{1,0:T(8,128)(2,1)S(1)}, u32[]{:S(2)}, u32[]{:S(2)}) collective-permute-start(bf16[64,1024]{1,0:T(8,128)(2,1)S(1)} %get-tuple-element.475), channel_id=1, source_target_pairs={{0,48},{8,56},{16,0},{24,8},{32,16},{40,24},{48,32},{56,40},{64,11... | collective-permute-start | bytes 393224 | tf_op jit(solution)/shard_map/ppermute | solution.py:638
  67.9 4.9 %collective-permute-done.11.opposite_ref = bf16[32,1024]{1,0:T(8,128)(2,1)S(1)} collective-permute-done((bf16[32,1024]{1,0:T(8,128)(2,1)S(1)}, bf16[32,1024]{1,0:T(8,128)(2,1)S(1)}, u32[]{:S(2)}, u32[]{:S(2)}) %collective-permute-start.11) | collective-permute-done | bytes 65568 | tf_op jit(solution)/shard_map/ppermute | solution.py:618
  72.7 1.4 collective-permute-done.10.two_hi_ref
  74.2 4.6 %collective-permute-done.9.two_lo_ref = bf16[64,1024]{1,0:T(8,128)(2,1)S(1)} collective-permute-done((bf16[64,1024]{1,0:T(8,128)(2,1)S(1)}, bf16[64,1024]{1,0:T(8,128)(2,1)S(1)}, u32[]{:S(2)}, u32[]{:S(2)}) %collective-permute-start.9) | collective-permute-done | bytes 131104 | tf_op jit(solution)/shard_map/ppermute | solution.py:637
  79.3 2.6 %collective-permute-start.17 = (bf16[256,1024]{1,0:T(8,128)(2,1)S(1)}, bf16[256,1024]{1,0:T(8,128)(2,1)S(1)}, u32[]{:S(2)}, u32[]{:S(2)}) collective-permute-start(bf16[256,1024]{1,0:T(8,128)(2,1)S(1)} %get-tuple-element.480.y0_ref), channel_id=1, source_target_pairs={{0,192},{8,200},{16,208},{24,216},{32,224},{40,232},{48,240},{56,2... | collective-permute-start | bytes 1572872 | tf_op jit(solution)/shard_map/ppermute | solution.py:660
  82.0 1.7 %collective-permute-start.20 = (bf16[384,512]{1,0:T(8,128)(2,1)S(1)}, bf16[384,512]{1,0:T(8,128)(2,1)S(1)}, u32[]{:S(2)}, u32[]{:S(2)}) collective-permute-start(bf16[384,512]{1,0:T(8,128)(2,1)S(1)} %choose.1.mine_ref), channel_id=1, source_target_pairs={{0,4},{1,5},{2,6},{3,7},{4,0},{5,1},{6,2},{7,3},{8,12},{9,13},{10,... | collective-permute-start | bytes 1179656 | tf_op jit(solution)/shard_map/ppermute | solution.py:685
  83.7 3.1 %collective-permute-start.18 = (bf16[128,512]{1,0:T(8,128)(2,1)S(1)}, bf16[128,512]{1,0:T(8,128)(2,1)S(1)}, u32[]{:S(2)}, u32[]{:S(2)}) collective-permute-start(bf16[128,512]{1,0:T(8,128)(2,1)S(1)} %get-tuple-element.486.own_ref), channel_id=1, source_target_pairs={{0,4},{1,5},{8,12},{9,13},{16,20},{17,21},{24,28},{25,29},{32,36},... | collective-permute-start | bytes 393224 | tf_op jit(solution)/shard_map/ppermute | solution.py:661
  87.4 3.1 %collective-permute-start.14 = (bf16[64,1024]{1,0:T(8,128)(2,1)S(1)}, bf16[64,1024]{1,0:T(8,128)(2,1)S(1)}, u32[]{:S(2)}, u32[]{:S(2)}) collective-permute-start(bf16[64,1024]{1,0:T(8,128)(2,1)S(1)} %get-tuple-element.483), channel_id=1, source_target_pairs={{0,16},{8,24},{32,48},{40,56},{64,80},{72,88},{96,112},{104,120},{... | collective-permute-start | bytes 393224 | tf_op jit(solution)/shard_map/ppermute | solution.py:675
  91.1 1.3 collective-permute-start.19
  93.0 2.4 %collective-permute-start.15 = (bf16[32,1024]{1,0:T(8,128)(2,1)S(1)}, bf16[32,1024]{1,0:T(8,128)(2,1)S(1)}, u32[]{:S(2)}, u32[]{:S(2)}) collective-permute-start(bf16[32,1024]{1,0:T(8,128)(2,1)S(1)} %get-tuple-element.485), channel_id=1, source_target_pairs={{0,8},{8,16},{16,24},{24,32},{32,40},{40,48},{48,56},{56,0},{64,72... | collective-permute-start | bytes 196616 | tf_op jit(solution)/shard_map/ppermute | solution.py:684
  95.4 4.8 %collective-permute-done.15.came_ref = bf16[32,1024]{1,0:T(8,128)(2,1)S(1)} collective-permute-done((bf16[32,1024]{1,0:T(8,128)(2,1)S(1)}, bf16[32,1024]{1,0:T(8,128)(2,1)S(1)}, u32[]{:S(2)}, u32[]{:S(2)}) %collective-permute-start.15) | collective-permute-done | bytes 65568 | tf_op jit(solution)/shard_map/ppermute | solution.py:684
  100.9 9.2 %collective-permute-start.21 = (bf16[1536,512]{1,0:T(8,128)(2,1)S(1)}, bf16[1536,512]{1,0:T(8,128)(2,1)S(1)}, u32[]{:S(2)}, u32[]{:S(2)}) collective-permute-start(bf16[1536,512]{1,0:T(8,128)(2,1)S(1)} %part.1.part_ref), channel_id=1, source_target_pairs={{0,1},{1,0},{2,3},{3,2},{4,5},{5,4},{6,7},{7,6},{8,9},{9,8},{10,11... | collective-permute-start | bytes 4718600 | tf_op jit(solution)/shard_map/ppermute | solution.py:723
  110.7 5.1 %collective-permute-done.22.came_ref = bf16[128,512]{1,0:T(8,128)(2,1)S(1)} collective-permute-done((bf16[128,512]{1,0:T(8,128)(2,1)S(1)}, bf16[128,512]{1,0:T(8,128)(2,1)S(1)}, u32[]{:S(2)}, u32[]{:S(2)}) %collective-permute-start.22) | collective-permute-done | bytes 131104 | tf_op jit(solution)/shard_map/ppermute | solution.py:695
  115.8 1.8 %collective-permute-start.23 = (bf16[256,512]{1,0:T(8,128)(2,1)S(1)}, bf16[256,512]{1,0:T(8,128)(2,1)S(1)}, u32[]{:S(2)}, u32[]{:S(2)}) collective-permute-start(bf16[256,512]{1,0:T(8,128)(2,1)S(1)} %two.1.near_ref), channel_id=1, source_target_pairs={{0,128},{8,136},{16,144},{24,152},{32,160},{40,168},{48,176},{56,1... | collective-permute-start | bytes 786440 | tf_op jit(solution)/shard_map/ppermute | solution.py:699
  118.4 2.0 %collective-permute-start.25 = (bf16[128,1024]{1,0:T(8,128)(2,1)S(1)}, bf16[128,1024]{1,0:T(8,128)(2,1)S(1)}, u32[]{:S(2)}, u32[]{:S(2)}) collective-permute-start(bf16[128,1024]{1,0:T(8,128)(2,1)S(1)} %slice.132), channel_id=1, source_target_pairs={{0,192},{8,200},{16,208},{24,216},{32,224},{40,232},{48,240},{56,2... | collective-permute-start | bytes 786440 | tf_op jit(solution)/shard_map/ppermute | solution.py:691
  121.0 5.3 %collective-permute-start.26 = (bf16[64,512]{1,0:T(8,128)(2,1)S(1)}, bf16[64,512]{1,0:T(8,128)(2,1)S(1)}, u32[]{:S(2)}, u32[]{:S(2)}) collective-permute-start(bf16[64,512]{1,0:T(8,128)(2,1)S(1)} %get-tuple-element.495.own_ref), channel_id=1, source_target_pairs={{0,4},{1,5},{8,12},{9,13},{16,20},{17,21},{24,28},{25,29},{32,36},... | collective-permute-start | bytes 196616 | tf_op jit(solution)/shard_map/ppermute | solution.py:708
  126.3 1.3 collective-permute-done.26.came_ref
  128.2 1.3 collective-permute-start.27
  129.5 1.7 %settle.1.rows_ref = bf16[1536,1024]{1,0:T(8,128)(2,1)S(1)} custom-call(bf16[1536,1024]{1,0:T(8,128)(2,1)S(1)} %bitcast.72, s32[1,64]{1,0:T(1,128)S(1)} %get-tuple-element.460.land_ref, bf16[64,1024]{1,0:T(8,128)(2,1)S(1)} %get-tuple-element.491.gone_ref), custom_call_target="tpu_custom_call" | custom-call | tf_op jit(solution)/shard_map/settle/pallas_call | solution.py:730
  131.3 2.4 %factor.1.factor_ref = bf16[1536,512]{1,0:T(8,128)(2,1)S(1)} custom-call(s32[2]{0:T(128)S(1)} %pad_add_fusion.pos_ref, bf16[1536,512]{1,0:T(8,128)(2,1)S(1)} %part.1.part_ref, bf16[1536,512]{1,0:T(8,128)(2,1)S(1)} %collective-permute-done.21.other_ref, bf16[2,512,512]{2,1,0:T(8,128)(2,1)S(1)} %copy-done.13), custom_call_target="tpu_custom_call" | custom-call | tf_op jit(solution)/shard_map/factor/pallas_call | solution.py:740
  134.4 2.4 %collective-permute-start.28 = (bf16[576,512]{1,0:T(8,128)(2,1)S(1)}, bf16[576,512]{1,0:T(8,128)(2,1)S(1)}, u32[]{:S(2)}, u32[]{:S(2)}) collective-permute-start(bf16[576,512]{1,0:T(8,128)(2,1)S(1)} %cross.1.cross_ref), channel_id=1, source_target_pairs={{0,1},{1,0},{2,3},{3,2},{4,5},{5,4},{6,7},{7,6},{8,9},{9,8},{10,11... | collective-permute-start | bytes 1769480 | tf_op jit(solution)/shard_map/ppermute | solution.py:762
  137.5 0.9 collective-permute-done.28.cross_other_ref
  138.4 10.1 %finish.1 = bf16[1536,1024]{1,0:T(8,128)(2,1)S(1)} custom-call(s32[2]{0:T(128)S(1)} %pad_add_fusion.pos_ref, bf16[1536,1024]{1,0:T(8,128)(2,1)S(1)} %settle.1.rows_ref, bf16[1536,512]{1,0:T(8,128)(2,1)S(1)} %part.1.part_ref, bf16[1536,512]{1,0:T(8,128)(2,1)S(1)} %collective-permute-done.21.other_ref, bf16[1536,512]{1,0:T(8,128)(2,1)S(1)} %factor.1.factor_ref, ...), custom_call_target="tpu_custom_call" | custom-call | tf_op jit(solution)/shard_map/finish/pallas_call | solution.py:778
  148.5 3.9 %reshape.435 = bf16[3,512,2,512]{3,2,1,0:T(2,128)(2,1)} reshape(bf16[1536,1024]{1,0:T(8,128)(2,1)S(1)} %finish.1) | data formatting | bytes 6291456 | tf_op jit(solution)/shard_map/reshape | solution.py:809
  152.4 0.9 while.26
  (69 shorter events, 10.7 us)
Async XLA Ops:
  6.5 2.8 %copy-start.15 = (s32[2,512]{1,0:T(2,128)S(1)}, s32[2,512]{1,0:T(2,128)}, u32[]{:S(2)}) copy-start(s32[2,512]{1,0:T(2,128)} %across_ref.3) | copy-start | bytes 12292
  12.2 0.8 copy-start.2
  13.0 0.6 copy-start.9
  13.6 37.6 %all-to-all-start = ((bf16[32,8,1024]{2,1,0:T(8,128)(2,1)}), bf16[32,8,1024]{2,1,0:T(8,128)(2,1)}, u32[]{:S(2)}, u32[]{:S(2)}) async-start(bf16[32,8,1024]{2,1,0:T(8,128)(2,1)} %bitcast.73), calls=%async_computation | async-start | bytes 1048576 | tf_op jit(solution)/shard_map/all_to_all | solution.py:583
  25.8 9.6 %copy-start.14 = (bf16[2,512,512]{2,1,0:T(8,128)(2,1)S(1)}, bf16[2,512,512]{2,1,0:T(8,128)(2,1)}, u32[]{:S(2)}) copy-start(bf16[2,512,512]{2,1,0:T(8,128)(2,1)} %lower_ref.1) | copy-start | bytes 3145732
  26.9 21.6 %collective-permute-start.8 = (bf16[384,512]{1,0:T(8,128)(2,1)S(1)}, bf16[384,512]{1,0:T(8,128)(2,1)S(1)}, u32[]{:S(2)}, u32[]{:S(2)}) collective-permute-start(bf16[384,512]{1,0:T(8,128)(2,1)S(1)} %get-tuple-element.564), channel_id=1, source_target_pairs={{0,6},{1,7},{8,14},{9,15},{16,22},{17,23},{24,30},{25,31},{32,38},... | collective-permute-start | bytes 1179656 | tf_op jit(solution)/shard_map/ppermute | solution.py:587
  31.3 22.0 %collective-permute-start.7 = (bf16[384,512]{1,0:T(8,128)(2,1)}, bf16[384,512]{1,0:T(8,128)(2,1)}, u32[]{:S(2)}, u32[]{:S(2)}) collective-permute-start(bf16[384,512]{1,0:T(8,128)(2,1)} %get-tuple-element.565), channel_id=1, source_target_pairs={{0,4},{1,5},{8,12},{9,13},{16,20},{17,21},{24,28},{25,29},{32,36},... | collective-permute-start | bytes 1179656 | tf_op jit(solution)/shard_map/ppermute | solution.py:587
  33.4 20.0 %collective-permute-start.6 = (bf16[384,512]{1,0:T(8,128)(2,1)}, bf16[384,512]{1,0:T(8,128)(2,1)}, u32[]{:S(2)}, u32[]{:S(2)}) collective-permute-start(bf16[384,512]{1,0:T(8,128)(2,1)} %get-tuple-element.566), channel_id=1, source_target_pairs={{0,2},{1,3},{8,10},{9,11},{16,18},{17,19},{24,26},{25,27},{32,34},... | collective-permute-start | bytes 1179656 | tf_op jit(solution)/shard_map/ppermute | solution.py:587
  39.5 1.0 copy-start
  40.5 0.7 copy-start.5
  41.2 0.7 copy-start.7
  41.9 17.5 %collective-permute-start.1 = (bf16[144,1024]{1,0:T(8,128)(2,1)}, bf16[144,1024]{1,0:T(8,128)(2,1)}, u32[]{:S(2)}, u32[]{:S(2)}) collective-permute-start(bf16[144,1024]{1,0:T(8,128)(2,1)} %get-tuple-element.467), channel_id=1, source_target_pairs={{0,64},{8,72},{1,65},{9,73},{2,66},{10,74},{3,67},{11,75},{4,68},{... | collective-permute-start | bytes 884744 | tf_op jit(solution)/shard_map/ppermute | solution.py:619
  45.6 13.7 %collective-permute-start.2 = (bf16[144,1024]{1,0:T(8,128)(2,1)}, bf16[144,1024]{1,0:T(8,128)(2,1)}, u32[]{:S(2)}, u32[]{:S(2)}) collective-permute-start(bf16[144,1024]{1,0:T(8,128)(2,1)} %get-tuple-element.468), channel_id=1, source_target_pairs={{0,128},{8,136},{1,129},{9,137},{2,130},{10,138},{3,131},{11,139},... | collective-permute-start | bytes 884744 | tf_op jit(solution)/shard_map/ppermute | solution.py:619
  48.5 0.7 copy-start.3
  49.3 10.1 %collective-permute-start.3 = (bf16[144,1024]{1,0:T(8,128)(2,1)}, bf16[144,1024]{1,0:T(8,128)(2,1)}, u32[]{:S(2)}, u32[]{:S(2)}) collective-permute-start(bf16[144,1024]{1,0:T(8,128)(2,1)} %get-tuple-element.469), channel_id=1, source_target_pairs={{0,192},{8,200},{1,193},{9,201},{2,194},{10,202},{3,195},{11,203},... | collective-permute-start | bytes 884744 | tf_op jit(solution)/shard_map/ppermute | solution.py:619
  51.3 0.7 copy-start.10
  53.3 3.7 %collective-permute-start.5 = (bf16[32,1024]{1,0:T(8,128)(2,1)S(1)}, bf16[32,1024]{1,0:T(8,128)(2,1)S(1)}, u32[]{:S(2)}, u32[]{:S(2)}) collective-permute-start(bf16[32,1024]{1,0:T(8,128)(2,1)S(1)} %block.1.block_ref), channel_id=1, source_target_pairs={{0,56},{8,0},{16,8},{24,16},{32,24},{40,32},{48,40},{56,48},{64,12... | collective-permute-start | bytes 196616 | tf_op jit(solution)/shard_map/ppermute | solution.py:617
  53.4 4.4 %collective-permute-start = (bf16[32,1024]{1,0:T(8,128)(2,1)S(1)}, bf16[32,1024]{1,0:T(8,128)(2,1)S(1)}, u32[]{:S(2)}, u32[]{:S(2)}) collective-permute-start(bf16[32,1024]{1,0:T(8,128)(2,1)S(1)} %block.1.block_ref), channel_id=1, source_target_pairs={{0,8},{8,16},{16,24},{24,32},{32,40},{40,48},{48,56},{56,0},{64,72... | collective-permute-start | bytes 196616 | tf_op jit(solution)/shard_map/ppermute | solution.py:616
  54.8 1.0 copy-start.4
  57.8 20.9 %collective-permute-start.13 = (bf16[384,512]{1,0:T(8,128)(2,1)S(1)}, bf16[384,512]{1,0:T(8,128)(2,1)S(1)}, u32[]{:S(2)}, u32[]{:S(2)}) collective-permute-start(bf16[384,512]{1,0:T(8,128)(2,1)S(1)} %choose.1.mine_ref), channel_id=1, source_target_pairs={{2,0},{3,1},{4,2},{5,3},{6,4},{7,5},{0,6},{1,7},{10,8},{11,9},{12,... | collective-permute-start | bytes 1179656 | tf_op jit(solution)/shard_map/ppermute | solution.py:642
  57.9 20.8 %collective-permute-start.12 = (bf16[384,512]{1,0:T(8,128)(2,1)S(1)}, bf16[384,512]{1,0:T(8,128)(2,1)S(1)}, u32[]{:S(2)}, u32[]{:S(2)}) collective-permute-start(bf16[384,512]{1,0:T(8,128)(2,1)S(1)} %choose.1.mine_ref), channel_id=1, source_target_pairs={{0,2},{1,3},{2,4},{3,5},{4,6},{5,7},{6,0},{7,1},{8,10},{9,11},{10,... | collective-permute-start | bytes 1179656 | tf_op jit(solution)/shard_map/ppermute | solution.py:641
  59.4 1.0 copy-start.6
  60.3 0.9 copy-start.8
  62.7 16.0 %collective-permute-start.4 = (bf16[128,1024]{1,0:T(8,128)(2,1)S(1)}, bf16[128,1024]{1,0:T(8,128)(2,1)S(1)}, u32[]{:S(2)}, u32[]{:S(2)}) collective-permute-start(bf16[128,1024]{1,0:T(8,128)(2,1)S(1)} %get-tuple-element.471), channel_id=1, source_target_pairs={{0,32},{8,40},{64,96},{72,104},{128,160},{136,168},{192,224},{200,... | collective-permute-start | bytes 786440 | tf_op jit(solution)/shard_map/ppermute | solution.py:630
  65.6 7.1 %collective-permute-start.11 = (bf16[32,1024]{1,0:T(8,128)(2,1)S(1)}, bf16[32,1024]{1,0:T(8,128)(2,1)S(1)}, u32[]{:S(2)}, u32[]{:S(2)}) collective-permute-start(bf16[32,1024]{1,0:T(8,128)(2,1)S(1)} %block.1.block_ref), channel_id=1, source_target_pairs={{0,32},{8,40},{16,48},{24,56},{32,0},{40,8},{48,16},{56,24},{64,96... | collective-permute-start | bytes 196616 | tf_op jit(solution)/shard_map/ppermute | solution.py:618
  65.7 8.5 %collective-permute-start.10 = (bf16[64,1024]{1,0:T(8,128)(2,1)S(1)}, bf16[64,1024]{1,0:T(8,128)(2,1)S(1)}, u32[]{:S(2)}, u32[]{:S(2)}) collective-permute-start(bf16[64,1024]{1,0:T(8,128)(2,1)S(1)} %get-tuple-element.475), channel_id=1, source_target_pairs={{0,48},{8,56},{16,0},{24,8},{32,16},{40,24},{48,32},{56,40},{64,11... | collective-permute-start | bytes 393224 | tf_op jit(solution)/shard_map/ppermute | solution.py:638
  72.7 6.0 %collective-permute-start.9 = (bf16[64,1024]{1,0:T(8,128)(2,1)S(1)}, bf16[64,1024]{1,0:T(8,128)(2,1)S(1)}, u32[]{:S(2)}, u32[]{:S(2)}) collective-permute-start(bf16[64,1024]{1,0:T(8,128)(2,1)S(1)} %get-tuple-element.474), channel_id=1, source_target_pairs={{0,16},{8,24},{16,32},{24,40},{32,48},{40,56},{48,0},{56,8},{64,80... | collective-permute-start | bytes 393224 | tf_op jit(solution)/shard_map/ppermute | solution.py:637
  79.3 20.9 %collective-permute-start.17 = (bf16[256,1024]{1,0:T(8,128)(2,1)S(1)}, bf16[256,1024]{1,0:T(8,128)(2,1)S(1)}, u32[]{:S(2)}, u32[]{:S(2)}) collective-permute-start(bf16[256,1024]{1,0:T(8,128)(2,1)S(1)} %get-tuple-element.480.y0_ref), channel_id=1, source_target_pairs={{0,192},{8,200},{16,208},{24,216},{32,224},{40,232},{48,240},{56,2... | collective-permute-start | bytes 1572872 | tf_op jit(solution)/shard_map/ppermute | solution.py:660
  82.0 18.2 %collective-permute-start.16 = (bf16[256,1024]{1,0:T(8,128)(2,1)S(1)}, bf16[256,1024]{1,0:T(8,128)(2,1)S(1)}, u32[]{:S(2)}, u32[]{:S(2)}) collective-permute-start(bf16[256,1024]{1,0:T(8,128)(2,1)S(1)} %get-tuple-element.480.y0_ref), channel_id=1, source_target_pairs={{0,64},{8,72},{16,80},{24,88},{32,96},{40,104},{48,112},{56,120},{... | collective-permute-start | bytes 1572872 | tf_op jit(solution)/shard_map/ppermute | solution.py:659
  82.0 18.2 %collective-permute-start.20 = (bf16[384,512]{1,0:T(8,128)(2,1)S(1)}, bf16[384,512]{1,0:T(8,128)(2,1)S(1)}, u32[]{:S(2)}, u32[]{:S(2)}) collective-permute-start(bf16[384,512]{1,0:T(8,128)(2,1)S(1)} %choose.1.mine_ref), channel_id=1, source_target_pairs={{0,4},{1,5},{2,6},{3,7},{4,0},{5,1},{6,2},{7,3},{8,12},{9,13},{10,... | collective-permute-start | bytes 1179656 | tf_op jit(solution)/shard_map/ppermute | solution.py:685
  83.7 6.8 %collective-permute-start.18 = (bf16[128,512]{1,0:T(8,128)(2,1)S(1)}, bf16[128,512]{1,0:T(8,128)(2,1)S(1)}, u32[]{:S(2)}, u32[]{:S(2)}) collective-permute-start(bf16[128,512]{1,0:T(8,128)(2,1)S(1)} %get-tuple-element.486.own_ref), channel_id=1, source_target_pairs={{0,4},{1,5},{8,12},{9,13},{16,20},{17,21},{24,28},{25,29},{32,36},... | collective-permute-start | bytes 393224 | tf_op jit(solution)/shard_map/ppermute | solution.py:661
  87.4 5.0 %collective-permute-start.14 = (bf16[64,1024]{1,0:T(8,128)(2,1)S(1)}, bf16[64,1024]{1,0:T(8,128)(2,1)S(1)}, u32[]{:S(2)}, u32[]{:S(2)}) collective-permute-start(bf16[64,1024]{1,0:T(8,128)(2,1)S(1)} %get-tuple-element.483), channel_id=1, source_target_pairs={{0,16},{8,24},{32,48},{40,56},{64,80},{72,88},{96,112},{104,120},{... | collective-permute-start | bytes 393224 | tf_op jit(solution)/shard_map/ppermute | solution.py:675
  91.1 9.1 %collective-permute-start.19 = (bf16[128,512]{1,0:T(8,128)(2,1)S(1)}, bf16[128,512]{1,0:T(8,128)(2,1)S(1)}, u32[]{:S(2)}, u32[]{:S(2)}) collective-permute-start(bf16[128,512]{1,0:T(8,128)(2,1)S(1)} %pass.1.even_ref), channel_id=1, source_target_pairs={{0,2},{1,3},{4,6},{5,7},{8,10},{9,11},{12,14},{13,15},{16,18},{17,... | collective-permute-start | bytes 393224 | tf_op jit(solution)/shard_map/ppermute | solution.py:666
  93.0 7.2 %collective-permute-start.15 = (bf16[32,1024]{1,0:T(8,128)(2,1)S(1)}, bf16[32,1024]{1,0:T(8,128)(2,1)S(1)}, u32[]{:S(2)}, u32[]{:S(2)}) collective-permute-start(bf16[32,1024]{1,0:T(8,128)(2,1)S(1)} %get-tuple-element.485), channel_id=1, source_target_pairs={{0,8},{8,16},{16,24},{24,32},{32,40},{40,48},{48,56},{56,0},{64,72... | collective-permute-start | bytes 196616 | tf_op jit(solution)/shard_map/ppermute | solution.py:684
  100.9 30.4 %collective-permute-start.21 = (bf16[1536,512]{1,0:T(8,128)(2,1)S(1)}, bf16[1536,512]{1,0:T(8,128)(2,1)S(1)}, u32[]{:S(2)}, u32[]{:S(2)}) collective-permute-start(bf16[1536,512]{1,0:T(8,128)(2,1)S(1)} %part.1.part_ref), channel_id=1, source_target_pairs={{0,1},{1,0},{2,3},{3,2},{4,5},{5,4},{6,7},{7,6},{8,9},{9,8},{10,11... | collective-permute-start | bytes 4718600 | tf_op jit(solution)/shard_map/ppermute | solution.py:723
  110.6 5.2 %collective-permute-start.22 = (bf16[128,512]{1,0:T(8,128)(2,1)S(1)}, bf16[128,512]{1,0:T(8,128)(2,1)S(1)}, u32[]{:S(2)}, u32[]{:S(2)}) collective-permute-start(bf16[128,512]{1,0:T(8,128)(2,1)S(1)} %extra.1.own_ref), channel_id=1, source_target_pairs={{0,64},{8,72},{16,80},{24,88},{32,96},{40,104},{48,112},{56,120},{... | collective-permute-start | bytes 393224 | tf_op jit(solution)/shard_map/ppermute | solution.py:695
  115.8 17.9 %collective-permute-start.23 = (bf16[256,512]{1,0:T(8,128)(2,1)S(1)}, bf16[256,512]{1,0:T(8,128)(2,1)S(1)}, u32[]{:S(2)}, u32[]{:S(2)}) collective-permute-start(bf16[256,512]{1,0:T(8,128)(2,1)S(1)} %two.1.near_ref), channel_id=1, source_target_pairs={{0,128},{8,136},{16,144},{24,152},{32,160},{40,168},{48,176},{56,1... | collective-permute-start | bytes 786440 | tf_op jit(solution)/shard_map/ppermute | solution.py:699
  117.7 16.1 %collective-permute-start.24 = (bf16[128,1024]{1,0:T(8,128)(2,1)S(1)}, bf16[128,1024]{1,0:T(8,128)(2,1)S(1)}, u32[]{:S(2)}, u32[]{:S(2)}) collective-permute-start(bf16[128,1024]{1,0:T(8,128)(2,1)S(1)} %slice.131), channel_id=1, source_target_pairs={{0,64},{8,72},{16,80},{24,88},{32,96},{40,104},{48,112},{56,120},{... | collective-permute-start | bytes 786440 | tf_op jit(solution)/shard_map/ppermute | solution.py:690
  118.4 15.3 %collective-permute-start.25 = (bf16[128,1024]{1,0:T(8,128)(2,1)S(1)}, bf16[128,1024]{1,0:T(8,128)(2,1)S(1)}, u32[]{:S(2)}, u32[]{:S(2)}) collective-permute-start(bf16[128,1024]{1,0:T(8,128)(2,1)S(1)} %slice.132), channel_id=1, source_target_pairs={{0,192},{8,200},{16,208},{24,216},{32,224},{40,232},{48,240},{56,2... | collective-permute-start | bytes 786440 | tf_op jit(solution)/shard_map/ppermute | solution.py:691
  121.0 6.6 %collective-permute-start.26 = (bf16[64,512]{1,0:T(8,128)(2,1)S(1)}, bf16[64,512]{1,0:T(8,128)(2,1)S(1)}, u32[]{:S(2)}, u32[]{:S(2)}) collective-permute-start(bf16[64,512]{1,0:T(8,128)(2,1)S(1)} %get-tuple-element.495.own_ref), channel_id=1, source_target_pairs={{0,4},{1,5},{8,12},{9,13},{16,20},{17,21},{24,28},{25,29},{32,36},... | collective-permute-start | bytes 196616 | tf_op jit(solution)/shard_map/ppermute | solution.py:708
  128.2 5.6 %collective-permute-start.27 = (bf16[64,512]{1,0:T(8,128)(2,1)S(1)}, bf16[64,512]{1,0:T(8,128)(2,1)S(1)}, u32[]{:S(2)}, u32[]{:S(2)}) collective-permute-start(bf16[64,512]{1,0:T(8,128)(2,1)S(1)} %pass2.1.even_ref), channel_id=1, source_target_pairs={{0,2},{1,3},{4,6},{5,7},{8,10},{9,11},{12,14},{13,15},{16,18},{17,... | collective-permute-start | bytes 196616 | tf_op jit(solution)/shard_map/ppermute | solution.py:712
  129.5 1.8 %copy-start.13 = (bf16[2,512,512]{2,1,0:T(8,128)(2,1)S(1)}, bf16[2,512,512]{2,1,0:T(8,128)(2,1)}, u32[]{:S(2)}) copy-start(bf16[2,512,512]{2,1,0:T(8,128)(2,1)} %upper_ref.3) | copy-start | bytes 3145732
  131.3 5.5 %copy-start.1 = (bf16[2,512,512]{2,1,0:T(8,128)(2,1)S(1)}, bf16[2,512,512]{2,1,0:T(8,128)(2,1)}, u32[]{:S(2)}) copy-start(bf16[2,512,512]{2,1,0:T(8,128)(2,1)} %copy-done) | copy-start | bytes 3145732
  134.4 4.0 %collective-permute-start.28 = (bf16[576,512]{1,0:T(8,128)(2,1)S(1)}, bf16[576,512]{1,0:T(8,128)(2,1)S(1)}, u32[]{:S(2)}, u32[]{:S(2)}) collective-permute-start(bf16[576,512]{1,0:T(8,128)(2,1)S(1)} %cross.1.cross_ref), channel_id=1, source_target_pairs={{0,1},{1,0},{2,3},{3,2},{4,5},{5,4},{6,7},{7,6},{8,9},{9,8},{10,11... | collective-permute-start | bytes 1769480 | tf_op jit(solution)/shard_map/ppermute | solution.py:762
  148.5 3.9 %copy-start.16 = (s32[2,512]{1,0:T(2,128)S(1)}, s32[2,512]{1,0:T(2,128)}, u32[]{:S(2)}) copy-start(s32[2,512]{1,0:T(2,128)} %across_ref.3) | copy-start | bytes 12292

commit v8 on v7

--- a/solution.py
+++ b/solution.py
@@ -623,7 +623,7 @@
         "spread",
         [quarter_shape] * 2,
         [position],
-        after(passing, from_lo),
+        after(passing, block),
         leaving[0],
         *arrived,
     )
@@ -641,7 +641,7 @@
     before = lax.ppermute(quarter_out, "pcol", move_x(ring))
     behind = lax.ppermute(quarter_out, "pcol", move_x([(b, a) for a, b in ring]))
 
-    two_lo, two_hi, opposite = after((two_lo, two_hi, opposite), before, behind, came)
+    two_lo, two_hi, opposite = after((two_lo, two_hi, opposite), before, behind, kept)
     half = panel // NY
     n_gone = 2 * DEST_ROWS
     z_line, extra = local_kernel(
@@ -693,10 +693,6 @@
         extra_kernel, "extra", [extra_shape], [position], extra, extra_odd
     )
     near_other = lax.ppermute(near, "prow", cross_y(1))
-    (near,) = local_kernel(
-        two_kernel, "two", [shape((2 * half, width))], [], near, near_other
-    )
-    far = lax.ppermute(near, "prow", cross_y(2))
     gone_shape = shape((n_gone, width))
     gone, gone_panel = local_kernel(
         gone_kernel,
@@ -706,6 +702,15 @@
         *after((kept, came), y_lo),
     )
     gone_mid = lax.ppermute(gone_panel, "pcol", move_x([(0, 2)]))
+    (near,) = local_kernel(
+        two_kernel,
+        "two",
+        [shape((2 * half, width))],
+        [],
+        near,
+        after(near_other, far_first, far_second, gone_mid),
+    )
+    far = lax.ppermute(near, "prow", cross_y(2))
     (gone_panel,) = local_kernel(
         pass_kernel, "pass2", [gone_shape], [position], gone_panel, gone_mid
     )

time: 161 us -> 150 us (0.932)
  waiting for transfers between devices: 23.9 us -> 18.9 us
  starting transfers between devices: 74.6 us -> 71.3 us
  local copies, waits for them, and re-layouts: 15.8 us -> 14.1 us
    ppermute x1, waiting for transfers between devices: 4.57 us -> 0.01 us  [per_device(): two_lo = lax.ppermute(pair_lo, 'prow', shift_z(2))]
    ppermute x3, waiting for transfers between devices: 0.01 us -> 3.84 us  [per_device(): lax.ppermute(leaving[s], 'prow', shift_y(s, [0], [0, 1]))]
    ppermute x1, waiting for transfers between devices: 5.1 us -> 1.79 us  [per_device(): near_other = lax.ppermute(near, 'prow', cross_y(1))]
    ppermute x1, waiting for transfers between devices: 0.01 us -> 2.62 us  [per_device(): extra_mid = lax.ppermute(extra, 'pcol', move_x([(0, 2)]))]
    ppermute x1, starting transfers between devices: 0.08 us -> 2.44 us  [per_device(): from_hi = lax.ppermute(block, 'prow', shift_z(-1))]
    ppermute x1, starting transfers between devices: 2.37 us -> 0.16 us  [per_device(): came = lax.ppermute(send, 'prow', shift_z(1))]
    ppermute x1, starting transfers between devices: 2.16 us -> 0.08 us  [per_device(): two_hi = lax.ppermute(pair_hi, 'prow', shift_z(-2))]
    ppermute x1, starting transfers between devices: 1.29 us -> 3.29 us  [per_device(): gone_odd = lax.ppermute(gone_panel, 'pcol', move_x([(0, 1), (2, 3)]))]
  transfers between devices with their start and end apart: 30 -> 30, of which waited for: 9 -> 7; matrix products, arithmetic and copies ran while one was open for 1% -> 1% of each run, Pallas kernels for 10% -> 11%
where the time goes in v8:
time: 150 us
  starting transfers between devices  71.3 us (48%)
  Pallas kernels  30.5 us (20%)
  waiting for transfers between devices  18.9 us (13%)
  local copies, waits for them, and re-layouts  14.1 us (9%)
  between operations  13.9 us (9%)
    pallas_call x16, Pallas kernels, local_kernel(): pl.pallas_call(body, grid=(1,), in_specs=[smem() for _ in scalars] + [who...  15.6 us
    all_to_all x1, starting transfers between devices, per_device(): dealt = lax.all_to_all(picks, 'prow', 0, 0, tiled=True)  12.2 us
    pallas_call x1, Pallas kernels, per_device(): pl.pallas_call(functools.partial(finish_kernel, panel), grid=(steps + 1,)...  10.1 us
    ppermute x3, starting transfers between devices, per_device(): got = [lax.ppermute(own[k], 'pcol', move_x([(0, k)])) for k in range(1, NX)]  9.21 us
    unnamed x27, local copies, waits for them, and re-layouts  9.07 us
    ppermute x1, starting transfers between devices, per_device(): other = lax.ppermute(part, 'pcol', SWAP)  7.59 us
    ppermute x3, starting transfers between devices, per_device(): lax.ppermute(leaving[s], 'prow', shift_y(s, [0], [0, 1]))  7.41 us
    ppermute x1, waiting for transfers between devices, per_device(): opposite = lax.ppermute(block, 'prow', shift_z(4))  5.45 us
  transfers between devices with their start and end apart: 30, of which 7 were waited for; matrix products, arithmetic and copies ran while one was open for 1% of the time, Pallas kernels for 11%

profile of v8, /device:TPU:1, one launch (start us, length us, event | category | flops | bytes accessed | tf_op | source)
XLA Modules:
  0.0 149.8 jit_solution(2049888406758659812)
XLA Ops:
  6.5 2.7 %copy.11 = bf16[192,8,2,512]{3,1,2,0:T(8,128)(2,1)S(1)} copy(bf16[192,8,2,512]{3,2,1,0:T(2,128)(2,1)} %bitcast.75) | data formatting | bytes 6291456
  9.4 2.9 %deal.1 = (bf16[256,1024]{1,0:T(8,128)(2,1)S(1)}, s32[32,1]{1,0:T(8,128)S(1)}, s32[2,512]{1,0:T(2,128)S(1)}, s32[1,512]{1,0:T(1,128)S(1)}) custom-call(s32[2]{0:T(128)S(1)} %pad_add_fusion.pos_ref, s32[2,512]{1,0:T(2,128)S(1)} %copy-done.13, bf16[1536,1024]{1,0:T(8,128)(2,1)S(1)} %bitcast.69), custom_call_target="tpu_custom_call" | custom-call | tf_op jit(solution)/shard_map/deal/pallas_call | solution.py:543
  12.3 0.8 copy-done.2
  13.6 12.2 %all-to-all-start = ((bf16[32,8,1024]{2,1,0:T(8,128)(2,1)}), bf16[32,8,1024]{2,1,0:T(8,128)(2,1)}, u32[]{:S(2)}, u32[]{:S(2)}) async-start(bf16[32,8,1024]{2,1,0:T(8,128)(2,1)} %bitcast.73), calls=%async_computation | async-start | bytes 1048576 | tf_op jit(solution)/shard_map/all_to_all | solution.py:583
  25.8 1.1 fusion.28
  26.9 5.1 %collective-permute-start.8 = (bf16[384,512]{1,0:T(8,128)(2,1)}, bf16[384,512]{1,0:T(8,128)(2,1)}, u32[]{:S(2)}, u32[]{:S(2)}) collective-permute-start(bf16[384,512]{1,0:T(8,128)(2,1)} %get-tuple-element.566), channel_id=1, source_target_pairs={{0,6},{1,7},{8,14},{9,15},{16,22},{17,23},{24,30},{25,31},{32,38},... | collective-permute-start | bytes 1179656 | tf_op jit(solution)/shard_map/ppermute | solution.py:587
  32.0 2.0 %collective-permute-start.7 = (bf16[384,512]{1,0:T(8,128)(2,1)}, bf16[384,512]{1,0:T(8,128)(2,1)}, u32[]{:S(2)}, u32[]{:S(2)}) collective-permute-start(bf16[384,512]{1,0:T(8,128)(2,1)} %get-tuple-element.567), channel_id=1, source_target_pairs={{0,4},{1,5},{8,12},{9,13},{16,20},{17,21},{24,28},{25,29},{32,36},... | collective-permute-start | bytes 1179656 | tf_op jit(solution)/shard_map/ppermute | solution.py:587
  34.1 2.0 %collective-permute-start.6 = (bf16[384,512]{1,0:T(8,128)(2,1)}, bf16[384,512]{1,0:T(8,128)(2,1)}, u32[]{:S(2)}, u32[]{:S(2)}) collective-permute-start(bf16[384,512]{1,0:T(8,128)(2,1)} %get-tuple-element.568), channel_id=1, source_target_pairs={{0,2},{1,3},{8,10},{9,11},{16,18},{17,19},{24,26},{25,27},{32,34},... | collective-permute-start | bytes 1179656 | tf_op jit(solution)/shard_map/ppermute | solution.py:587
  36.1 4.0 %leave.1 = (bf16[144,1024]{1,0:T(8,128)(2,1)S(1)}, bf16[144,1024]{1,0:T(8,128)(2,1)}, bf16[144,1024]{1,0:T(8,128)(2,1)}, bf16[144,1024]{1,0:T(8,128)(2,1)}, s32[...) custom-call(s32[2]{0:T(128)S(1)} %pad_add_fusion.pos_ref, ...), custom_call_target="tpu_custom_call" | custom-call | tf_op jit(solution)/shard_map/leave/pallas_call | solution.py:543
  40.2 1.0 copy-done
  41.1 0.7 copy-done.3
  41.8 0.7 copy-done.5
  42.5 0.7 copy-done.8
  43.2 1.3 block.1.block_ref
  44.5 2.4 %collective-permute-start.5 = (bf16[32,1024]{1,0:T(8,128)(2,1)S(1)}, bf16[32,1024]{1,0:T(8,128)(2,1)S(1)}, u32[]{:S(2)}, u32[]{:S(2)}) collective-permute-start(bf16[32,1024]{1,0:T(8,128)(2,1)S(1)} %block.1.block_ref), channel_id=1, source_target_pairs={{0,56},{8,0},{16,8},{24,16},{32,24},{40,32},{48,40},{56,48},{64,12... | collective-permute-start | bytes 196616 | tf_op jit(solution)/shard_map/ppermute | solution.py:617
  46.9 3.1 %collective-permute-start = (bf16[144,1024]{1,0:T(8,128)(2,1)}, bf16[144,1024]{1,0:T(8,128)(2,1)S(1)}, u32[]{:S(2)}, u32[]{:S(2)}) collective-permute-start(bf16[144,1024]{1,0:T(8,128)(2,1)} %get-tuple-element.468), channel_id=1, source_target_pairs={{0,64},{8,72},{1,65},{9,73},{2,66},{10,74},{3,67},{11,75},{4,68},{... | collective-permute-start | bytes 884744 | tf_op jit(solution)/shard_map/ppermute | solution.py:619
  50.0 2.2 %collective-permute-start.1 = (bf16[144,1024]{1,0:T(8,128)(2,1)}, bf16[144,1024]{1,0:T(8,128)(2,1)S(1)}, u32[]{:S(2)}, u32[]{:S(2)}) collective-permute-start(bf16[144,1024]{1,0:T(8,128)(2,1)} %get-tuple-element.469), channel_id=1, source_target_pairs={{0,128},{8,136},{1,129},{9,137},{2,130},{10,138},{3,131},{11,139},... | collective-permute-start | bytes 884744 | tf_op jit(solution)/shard_map/ppermute | solution.py:619
  52.3 1.3 choose.1.mine_ref
  53.7 1.5 collective-permute-start.12
  55.2 2.1 %collective-permute-start.2 = (bf16[144,1024]{1,0:T(8,128)(2,1)}, bf16[144,1024]{1,0:T(8,128)(2,1)S(1)}, u32[]{:S(2)}, u32[]{:S(2)}) collective-permute-start(bf16[144,1024]{1,0:T(8,128)(2,1)} %get-tuple-element.470), channel_id=1, source_target_pairs={{0,192},{8,200},{1,193},{9,201},{2,194},{10,202},{3,195},{11,203},... | collective-permute-start | bytes 884744 | tf_op jit(solution)/shard_map/ppermute | solution.py:619
  57.4 3.8 %collective-permute-done.1.two_ref = bf16[144,1024]{1,0:T(8,128)(2,1)S(1)} collective-permute-done((bf16[144,1024]{1,0:T(8,128)(2,1)}, bf16[144,1024]{1,0:T(8,128)(2,1)S(1)}, u32[]{:S(2)}, u32[]{:S(2)}) %collective-permute-start.1) | collective-permute-done | bytes 294944 | tf_op jit(solution)/shard_map/ppermute | solution.py:619
  61.2 1.0 copy-done.4
  62.2 0.9 copy-done.6
  63.1 0.9 spread.1
  64.0 5.5 %collective-permute-done.11.opposite_ref = bf16[32,1024]{1,0:T(8,128)(2,1)S(1)} collective-permute-done((bf16[32,1024]{1,0:T(8,128)(2,1)S(1)}, bf16[32,1024]{1,0:T(8,128)(2,1)S(1)}, u32[]{:S(2)}, u32[]{:S(2)}) %collective-permute-start.11) | collective-permute-done | bytes 65568 | tf_op jit(solution)/shard_map/ppermute | solution.py:618
  70.1 2.8 %collective-permute-start.17 = (bf16[256,1024]{1,0:T(8,128)(2,1)S(1)}, bf16[256,1024]{1,0:T(8,128)(2,1)S(1)}, u32[]{:S(2)}, u32[]{:S(2)}) collective-permute-start(bf16[256,1024]{1,0:T(8,128)(2,1)S(1)} %get-tuple-element.481.y0_ref), channel_id=1, source_target_pairs={{0,192},{8,200},{16,208},{24,216},{32,224},{40,232},{48,240},{56,2... | collective-permute-start | bytes 1572872 | tf_op jit(solution)/shard_map/ppermute | solution.py:660
  72.8 3.6 %collective-permute-start.3 = (bf16[128,1024]{1,0:T(8,128)(2,1)S(1)}, bf16[128,1024]{1,0:T(8,128)(2,1)S(1)}, u32[]{:S(2)}, u32[]{:S(2)}) collective-permute-start(bf16[128,1024]{1,0:T(8,128)(2,1)S(1)} %get-tuple-element.472), channel_id=1, source_target_pairs={{0,32},{8,40},{64,96},{72,104},{128,160},{136,168},{192,224},{200,... | collective-permute-start | bytes 786440 | tf_op jit(solution)/shard_map/ppermute | solution.py:630
  76.4 1.7 %collective-permute-start.20 = (bf16[384,512]{1,0:T(8,128)(2,1)S(1)}, bf16[384,512]{1,0:T(8,128)(2,1)S(1)}, u32[]{:S(2)}, u32[]{:S(2)}) collective-permute-start(bf16[384,512]{1,0:T(8,128)(2,1)S(1)} %choose.1.mine_ref), channel_id=1, source_target_pairs={{0,4},{1,5},{2,6},{3,7},{4,0},{5,1},{6,2},{7,3},{8,12},{9,13},{10,... | collective-permute-start | bytes 1179656 | tf_op jit(solution)/shard_map/ppermute | solution.py:685
  78.2 3.2 %collective-permute-start.18 = (bf16[128,512]{1,0:T(8,128)(2,1)S(1)}, bf16[128,512]{1,0:T(8,128)(2,1)S(1)}, u32[]{:S(2)}, u32[]{:S(2)}) collective-permute-start(bf16[128,512]{1,0:T(8,128)(2,1)S(1)} %get-tuple-element.487.own_ref), channel_id=1, source_target_pairs={{0,4},{1,5},{8,12},{9,13},{16,20},{17,21},{24,28},{25,29},{32,36},... | collective-permute-start | bytes 393224 | tf_op jit(solution)/shard_map/ppermute | solution.py:661
  82.0 1.3 collective-permute-start.14
  83.3 2.6 %collective-permute-done.18.came_ref = bf16[128,512]{1,0:T(8,128)(2,1)S(1)} collective-permute-done((bf16[128,512]{1,0:T(8,128)(2,1)S(1)}, bf16[128,512]{1,0:T(8,128)(2,1)S(1)}, u32[]{:S(2)}, u32[]{:S(2)}) %collective-permute-start.18) | collective-permute-done | bytes 131104 | tf_op jit(solution)/shard_map/ppermute | solution.py:661
  86.5 1.3 collective-permute-start.19
  88.5 4.3 %collective-permute-done.15.came_ref = bf16[32,1024]{1,0:T(8,128)(2,1)S(1)} collective-permute-done((bf16[32,1024]{1,0:T(8,128)(2,1)S(1)}, bf16[32,1024]{1,0:T(8,128)(2,1)S(1)}, u32[]{:S(2)}, u32[]{:S(2)}) %collective-permute-start.15) | collective-permute-done | bytes 65568 | tf_op jit(solution)/shard_map/ppermute | solution.py:684
  92.8 0.7 part.1.part_ref
  93.5 7.6 %collective-permute-start.21 = (bf16[1536,512]{1,0:T(8,128)(2,1)S(1)}, bf16[1536,512]{1,0:T(8,128)(2,1)S(1)}, u32[]{:S(2)}, u32[]{:S(2)}) collective-permute-start(bf16[1536,512]{1,0:T(8,128)(2,1)S(1)} %part.1.part_ref), channel_id=1, source_target_pairs={{0,1},{1,0},{2,3},{3,2},{4,5},{5,4},{6,7},{7,6},{8,9},{9,8},{10,11... | collective-permute-start | bytes 4718600 | tf_op jit(solution)/shard_map/ppermute | solution.py:728
  101.2 3.0 %collective-permute-start.24 = (bf16[128,1024]{1,0:T(8,128)(2,1)S(1)}, bf16[128,1024]{1,0:T(8,128)(2,1)S(1)}, u32[]{:S(2)}, u32[]{:S(2)}) collective-permute-start(bf16[128,1024]{1,0:T(8,128)(2,1)S(1)} %slice.132), channel_id=1, source_target_pairs={{0,192},{8,200},{16,208},{24,216},{32,224},{40,232},{48,240},{56,2... | collective-permute-start | bytes 786440 | tf_op jit(solution)/shard_map/ppermute | solution.py:691
  105.5 4.8 %collective-permute-start.25 = (bf16[64,512]{1,0:T(8,128)(2,1)S(1)}, bf16[64,512]{1,0:T(8,128)(2,1)S(1)}, u32[]{:S(2)}, u32[]{:S(2)}) collective-permute-start(bf16[64,512]{1,0:T(8,128)(2,1)S(1)} %get-tuple-element.495.own_ref), channel_id=1, source_target_pairs={{0,4},{1,5},{8,12},{9,13},{16,20},{17,21},{24,28},{25,29},{32,36},... | collective-permute-start | bytes 196616 | tf_op jit(solution)/shard_map/ppermute | solution.py:704
  110.2 1.8 %collective-permute-done.22.came_ref = bf16[128,512]{1,0:T(8,128)(2,1)S(1)} collective-permute-done((bf16[128,512]{1,0:T(8,128)(2,1)S(1)}, bf16[128,512]{1,0:T(8,128)(2,1)S(1)}, u32[]{:S(2)}, u32[]{:S(2)}) %collective-permute-start.22) | collective-permute-done | bytes 131104 | tf_op jit(solution)/shard_map/ppermute | solution.py:695
  112.1 3.8 %collective-permute-start.26 = (bf16[256,512]{1,0:T(8,128)(2,1)S(1)}, bf16[256,512]{1,0:T(8,128)(2,1)S(1)}, u32[]{:S(2)}, u32[]{:S(2)}) collective-permute-start(bf16[256,512]{1,0:T(8,128)(2,1)S(1)} %two.1.near_ref), channel_id=1, source_target_pairs={{0,128},{8,136},{16,144},{24,152},{32,160},{40,168},{48,176},{56,1... | collective-permute-start | bytes 786440 | tf_op jit(solution)/shard_map/ppermute | solution.py:713
  116.4 3.3 %collective-permute-start.27 = (bf16[64,512]{1,0:T(8,128)(2,1)S(1)}, bf16[64,512]{1,0:T(8,128)(2,1)S(1)}, u32[]{:S(2)}, u32[]{:S(2)}) collective-permute-start(bf16[64,512]{1,0:T(8,128)(2,1)S(1)} %pass2.1.even_ref), channel_id=1, source_target_pairs={{0,2},{1,3},{4,6},{5,7},{8,10},{9,11},{12,14},{13,15},{16,18},{17,... | collective-permute-start | bytes 196616 | tf_op jit(solution)/shard_map/ppermute | solution.py:717
  119.7 1.7 %settle.1.rows_ref = bf16[1536,1024]{1,0:T(8,128)(2,1)S(1)} custom-call(bf16[1536,1024]{1,0:T(8,128)(2,1)S(1)} %bitcast.72, s32[1,64]{1,0:T(1,128)S(1)} %get-tuple-element.461.land_ref, bf16[64,1024]{1,0:T(8,128)(2,1)S(1)} %get-tuple-element.492.gone_ref), custom_call_target="tpu_custom_call" | custom-call | tf_op jit(solution)/shard_map/settle/pallas_call | solution.py:735
  121.5 2.4 %factor.1.factor_ref = bf16[1536,512]{1,0:T(8,128)(2,1)S(1)} custom-call(s32[2]{0:T(128)S(1)} %pad_add_fusion.pos_ref, bf16[1536,512]{1,0:T(8,128)(2,1)S(1)} %part.1.part_ref, bf16[1536,512]{1,0:T(8,128)(2,1)S(1)} %collective-permute-done.21.other_ref, bf16[2,512,512]{2,1,0:T(8,128)(2,1)S(1)} %copy-done.11), custom_call_target="tpu_custom_call" | custom-call | tf_op jit(solution)/shard_map/factor/pallas_call | solution.py:745
  124.6 1.8 %collective-permute-start.28 = (bf16[576,512]{1,0:T(8,128)(2,1)S(1)}, bf16[576,512]{1,0:T(8,128)(2,1)S(1)}, u32[]{:S(2)}, u32[]{:S(2)}) collective-permute-start(bf16[576,512]{1,0:T(8,128)(2,1)S(1)} %cross.1.cross_ref), channel_id=1, source_target_pairs={{0,1},{1,0},{2,3},{3,2},{4,5},{5,4},{6,7},{7,6},{8,9},{9,8},{10,11... | collective-permute-start | bytes 1769480 | tf_op jit(solution)/shard_map/ppermute | solution.py:767
  126.3 0.7 first.1
  127.0 0.9 collective-permute-done.28.cross_other_ref
  128.0 10.1 %finish.1 = bf16[1536,1024]{1,0:T(8,128)(2,1)S(1)} custom-call(s32[2]{0:T(128)S(1)} %pad_add_fusion.pos_ref, bf16[1536,1024]{1,0:T(8,128)(2,1)S(1)} %settle.1.rows_ref, bf16[1536,512]{1,0:T(8,128)(2,1)S(1)} %part.1.part_ref, bf16[1536,512]{1,0:T(8,128)(2,1)S(1)} %collective-permute-done.21.other_ref, bf16[1536,512]{1,0:T(8,128)(2,1)S(1)} %factor.1.factor_ref, ...), custom_call_target="tpu_custom_call" | custom-call | tf_op jit(solution)/shard_map/finish/pallas_call | solution.py:783
  138.1 3.9 %reshape.435 = bf16[3,512,2,512]{3,2,1,0:T(2,128)(2,1)} reshape(bf16[1536,1024]{1,0:T(8,128)(2,1)S(1)} %finish.1) | data formatting | bytes 6291456 | tf_op jit(solution)/shard_map/reshape | solution.py:814
  142.0 0.9 while.26
  (65 shorter events, 6.0 us)
Async XLA Ops:
  6.5 2.8 %copy-start.13 = (s32[2,512]{1,0:T(2,128)S(1)}, s32[2,512]{1,0:T(2,128)}, u32[]{:S(2)}) copy-start(s32[2,512]{1,0:T(2,128)} %across_ref.3) | copy-start | bytes 12292
  12.2 0.8 copy-start.2
  13.0 0.6 copy-start.7
  13.6 28.9 %all-to-all-start = ((bf16[32,8,1024]{2,1,0:T(8,128)(2,1)}), bf16[32,8,1024]{2,1,0:T(8,128)(2,1)}, u32[]{:S(2)}, u32[]{:S(2)}) async-start(bf16[32,8,1024]{2,1,0:T(8,128)(2,1)} %bitcast.73), calls=%async_computation | async-start | bytes 1048576 | tf_op jit(solution)/shard_map/all_to_all | solution.py:583
  25.8 10.3 %copy-start.12 = (bf16[2,512,512]{2,1,0:T(8,128)(2,1)S(1)}, bf16[2,512,512]{2,1,0:T(8,128)(2,1)}, u32[]{:S(2)}) copy-start(bf16[2,512,512]{2,1,0:T(8,128)(2,1)} %lower_ref.1) | copy-start | bytes 3145732
  26.9 20.0 %collective-permute-start.8 = (bf16[384,512]{1,0:T(8,128)(2,1)}, bf16[384,512]{1,0:T(8,128)(2,1)}, u32[]{:S(2)}, u32[]{:S(2)}) collective-permute-start(bf16[384,512]{1,0:T(8,128)(2,1)} %get-tuple-element.566), channel_id=1, source_target_pairs={{0,6},{1,7},{8,14},{9,15},{16,22},{17,23},{24,30},{25,31},{32,38},... | collective-permute-start | bytes 1179656 | tf_op jit(solution)/shard_map/ppermute | solution.py:587
  32.0 18.0 %collective-permute-start.7 = (bf16[384,512]{1,0:T(8,128)(2,1)}, bf16[384,512]{1,0:T(8,128)(2,1)}, u32[]{:S(2)}, u32[]{:S(2)}) collective-permute-start(bf16[384,512]{1,0:T(8,128)(2,1)} %get-tuple-element.567), channel_id=1, source_target_pairs={{0,4},{1,5},{8,12},{9,13},{16,20},{17,21},{24,28},{25,29},{32,36},... | collective-permute-start | bytes 1179656 | tf_op jit(solution)/shard_map/ppermute | solution.py:587
  34.1 18.2 %collective-permute-start.6 = (bf16[384,512]{1,0:T(8,128)(2,1)}, bf16[384,512]{1,0:T(8,128)(2,1)}, u32[]{:S(2)}, u32[]{:S(2)}) collective-permute-start(bf16[384,512]{1,0:T(8,128)(2,1)} %get-tuple-element.568), channel_id=1, source_target_pairs={{0,2},{1,3},{8,10},{9,11},{16,18},{17,19},{24,26},{25,27},{32,34},... | collective-permute-start | bytes 1179656 | tf_op jit(solution)/shard_map/ppermute | solution.py:587
  40.2 1.0 copy-start
  41.1 0.7 copy-start.3
  41.8 0.7 copy-start.5
  42.5 0.7 copy-start.8
  44.5 9.1 %collective-permute-start.5 = (bf16[32,1024]{1,0:T(8,128)(2,1)S(1)}, bf16[32,1024]{1,0:T(8,128)(2,1)S(1)}, u32[]{:S(2)}, u32[]{:S(2)}) collective-permute-start(bf16[32,1024]{1,0:T(8,128)(2,1)S(1)} %block.1.block_ref), channel_id=1, source_target_pairs={{0,56},{8,0},{16,8},{24,16},{32,24},{40,32},{48,40},{56,48},{64,12... | collective-permute-start | bytes 196616 | tf_op jit(solution)/shard_map/ppermute | solution.py:617
  46.9 6.7 %collective-permute-start.4 = (bf16[32,1024]{1,0:T(8,128)(2,1)S(1)}, bf16[32,1024]{1,0:T(8,128)(2,1)S(1)}, u32[]{:S(2)}, u32[]{:S(2)}) collective-permute-start(bf16[32,1024]{1,0:T(8,128)(2,1)S(1)} %block.1.block_ref), channel_id=1, source_target_pairs={{0,8},{8,16},{16,24},{24,32},{32,40},{40,48},{48,56},{56,0},{64,72... | collective-permute-start | bytes 196616 | tf_op jit(solution)/shard_map/ppermute | solution.py:616
  46.9 10.3 %collective-permute-start = (bf16[144,1024]{1,0:T(8,128)(2,1)}, bf16[144,1024]{1,0:T(8,128)(2,1)S(1)}, u32[]{:S(2)}, u32[]{:S(2)}) collective-permute-start(bf16[144,1024]{1,0:T(8,128)(2,1)} %get-tuple-element.468), channel_id=1, source_target_pairs={{0,64},{8,72},{1,65},{9,73},{2,66},{10,74},{3,67},{11,75},{4,68},{... | collective-permute-start | bytes 884744 | tf_op jit(solution)/shard_map/ppermute | solution.py:619
  50.0 11.1 %collective-permute-start.1 = (bf16[144,1024]{1,0:T(8,128)(2,1)}, bf16[144,1024]{1,0:T(8,128)(2,1)S(1)}, u32[]{:S(2)}, u32[]{:S(2)}) collective-permute-start(bf16[144,1024]{1,0:T(8,128)(2,1)} %get-tuple-element.469), channel_id=1, source_target_pairs={{0,128},{8,136},{1,129},{9,137},{2,130},{10,138},{3,131},{11,139},... | collective-permute-start | bytes 884744 | tf_op jit(solution)/shard_map/ppermute | solution.py:619
  53.6 15.8 %collective-permute-start.13 = (bf16[384,512]{1,0:T(8,128)(2,1)S(1)}, bf16[384,512]{1,0:T(8,128)(2,1)S(1)}, u32[]{:S(2)}, u32[]{:S(2)}) collective-permute-start(bf16[384,512]{1,0:T(8,128)(2,1)S(1)} %choose.1.mine_ref), channel_id=1, source_target_pairs={{2,0},{3,1},{4,2},{5,3},{6,4},{7,5},{0,6},{1,7},{10,8},{11,9},{12,... | collective-permute-start | bytes 1179656 | tf_op jit(solution)/shard_map/ppermute | solution.py:642
  53.7 15.7 %collective-permute-start.12 = (bf16[384,512]{1,0:T(8,128)(2,1)S(1)}, bf16[384,512]{1,0:T(8,128)(2,1)S(1)}, u32[]{:S(2)}, u32[]{:S(2)}) collective-permute-start(bf16[384,512]{1,0:T(8,128)(2,1)S(1)} %choose.1.mine_ref), channel_id=1, source_target_pairs={{0,2},{1,3},{2,4},{3,5},{4,6},{5,7},{6,0},{7,1},{8,10},{9,11},{10,... | collective-permute-start | bytes 1179656 | tf_op jit(solution)/shard_map/ppermute | solution.py:641
  55.2 6.0 %collective-permute-start.2 = (bf16[144,1024]{1,0:T(8,128)(2,1)}, bf16[144,1024]{1,0:T(8,128)(2,1)S(1)}, u32[]{:S(2)}, u32[]{:S(2)}) collective-permute-start(bf16[144,1024]{1,0:T(8,128)(2,1)} %get-tuple-element.470), channel_id=1, source_target_pairs={{0,192},{8,200},{1,193},{9,201},{2,194},{10,202},{3,195},{11,203},... | collective-permute-start | bytes 884744 | tf_op jit(solution)/shard_map/ppermute | solution.py:619
  57.3 12.2 %collective-permute-start.10 = (bf16[64,1024]{1,0:T(8,128)(2,1)S(1)}, bf16[64,1024]{1,0:T(8,128)(2,1)S(1)}, u32[]{:S(2)}, u32[]{:S(2)}) collective-permute-start(bf16[64,1024]{1,0:T(8,128)(2,1)S(1)} %get-tuple-element.476), channel_id=1, source_target_pairs={{0,48},{8,56},{16,0},{24,8},{32,16},{40,24},{48,32},{56,40},{64,11... | collective-permute-start | bytes 393224 | tf_op jit(solution)/shard_map/ppermute | solution.py:638
  61.2 8.3 %collective-permute-start.9 = (bf16[64,1024]{1,0:T(8,128)(2,1)S(1)}, bf16[64,1024]{1,0:T(8,128)(2,1)S(1)}, u32[]{:S(2)}, u32[]{:S(2)}) collective-permute-start(bf16[64,1024]{1,0:T(8,128)(2,1)S(1)} %get-tuple-element.475), channel_id=1, source_target_pairs={{0,16},{8,24},{16,32},{24,40},{32,48},{40,56},{48,0},{56,8},{64,80... | collective-permute-start | bytes 393224 | tf_op jit(solution)/shard_map/ppermute | solution.py:637
  61.2 8.2 %collective-permute-start.11 = (bf16[32,1024]{1,0:T(8,128)(2,1)S(1)}, bf16[32,1024]{1,0:T(8,128)(2,1)S(1)}, u32[]{:S(2)}, u32[]{:S(2)}) collective-permute-start(bf16[32,1024]{1,0:T(8,128)(2,1)S(1)} %block.1.block_ref), channel_id=1, source_target_pairs={{0,32},{8,40},{16,48},{24,56},{32,0},{40,8},{48,16},{56,24},{64,96... | collective-permute-start | bytes 196616 | tf_op jit(solution)/shard_map/ppermute | solution.py:618
  61.2 1.0 copy-start.4
  62.2 0.9 copy-start.6
  70.1 22.8 %collective-permute-start.17 = (bf16[256,1024]{1,0:T(8,128)(2,1)S(1)}, bf16[256,1024]{1,0:T(8,128)(2,1)S(1)}, u32[]{:S(2)}, u32[]{:S(2)}) collective-permute-start(bf16[256,1024]{1,0:T(8,128)(2,1)S(1)} %get-tuple-element.481.y0_ref), channel_id=1, source_target_pairs={{0,192},{8,200},{16,208},{24,216},{32,224},{40,232},{48,240},{56,2... | collective-permute-start | bytes 1572872 | tf_op jit(solution)/shard_map/ppermute | solution.py:660
  72.8 20.0 %collective-permute-start.16 = (bf16[256,1024]{1,0:T(8,128)(2,1)S(1)}, bf16[256,1024]{1,0:T(8,128)(2,1)S(1)}, u32[]{:S(2)}, u32[]{:S(2)}) collective-permute-start(bf16[256,1024]{1,0:T(8,128)(2,1)S(1)} %get-tuple-element.481.y0_ref), channel_id=1, source_target_pairs={{0,64},{8,72},{16,80},{24,88},{32,96},{40,104},{48,112},{56,120},{... | collective-permute-start | bytes 1572872 | tf_op jit(solution)/shard_map/ppermute | solution.py:659
  72.8 8.6 %collective-permute-start.3 = (bf16[128,1024]{1,0:T(8,128)(2,1)S(1)}, bf16[128,1024]{1,0:T(8,128)(2,1)S(1)}, u32[]{:S(2)}, u32[]{:S(2)}) collective-permute-start(bf16[128,1024]{1,0:T(8,128)(2,1)S(1)} %get-tuple-element.472), channel_id=1, source_target_pairs={{0,32},{8,40},{64,96},{72,104},{128,160},{136,168},{192,224},{200,... | collective-permute-start | bytes 786440 | tf_op jit(solution)/shard_map/ppermute | solution.py:630
  76.4 16.4 %collective-permute-start.20 = (bf16[384,512]{1,0:T(8,128)(2,1)S(1)}, bf16[384,512]{1,0:T(8,128)(2,1)S(1)}, u32[]{:S(2)}, u32[]{:S(2)}) collective-permute-start(bf16[384,512]{1,0:T(8,128)(2,1)S(1)} %choose.1.mine_ref), channel_id=1, source_target_pairs={{0,4},{1,5},{2,6},{3,7},{4,0},{5,1},{6,2},{7,3},{8,12},{9,13},{10,... | collective-permute-start | bytes 1179656 | tf_op jit(solution)/shard_map/ppermute | solution.py:685
  78.2 7.8 %collective-permute-start.18 = (bf16[128,512]{1,0:T(8,128)(2,1)S(1)}, bf16[128,512]{1,0:T(8,128)(2,1)S(1)}, u32[]{:S(2)}, u32[]{:S(2)}) collective-permute-start(bf16[128,512]{1,0:T(8,128)(2,1)S(1)} %get-tuple-element.487.own_ref), channel_id=1, source_target_pairs={{0,4},{1,5},{8,12},{9,13},{16,20},{17,21},{24,28},{25,29},{32,36},... | collective-permute-start | bytes 393224 | tf_op jit(solution)/shard_map/ppermute | solution.py:661
  82.0 5.8 %collective-permute-start.14 = (bf16[64,1024]{1,0:T(8,128)(2,1)S(1)}, bf16[64,1024]{1,0:T(8,128)(2,1)S(1)}, u32[]{:S(2)}, u32[]{:S(2)}) collective-permute-start(bf16[64,1024]{1,0:T(8,128)(2,1)S(1)} %get-tuple-element.484), channel_id=1, source_target_pairs={{0,16},{8,24},{32,48},{40,56},{64,80},{72,88},{96,112},{104,120},{... | collective-permute-start | bytes 393224 | tf_op jit(solution)/shard_map/ppermute | solution.py:675
  86.5 6.3 %collective-permute-start.19 = (bf16[128,512]{1,0:T(8,128)(2,1)S(1)}, bf16[128,512]{1,0:T(8,128)(2,1)S(1)}, u32[]{:S(2)}, u32[]{:S(2)}) collective-permute-start(bf16[128,512]{1,0:T(8,128)(2,1)S(1)} %pass.1.even_ref), channel_id=1, source_target_pairs={{0,2},{1,3},{4,6},{5,7},{8,10},{9,11},{12,14},{13,15},{16,18},{17,... | collective-permute-start | bytes 393224 | tf_op jit(solution)/shard_map/ppermute | solution.py:666
  88.4 4.4 %collective-permute-start.15 = (bf16[32,1024]{1,0:T(8,128)(2,1)S(1)}, bf16[32,1024]{1,0:T(8,128)(2,1)S(1)}, u32[]{:S(2)}, u32[]{:S(2)}) collective-permute-start(bf16[32,1024]{1,0:T(8,128)(2,1)S(1)} %get-tuple-element.486), channel_id=1, source_target_pairs={{0,8},{8,16},{16,24},{24,32},{32,40},{40,48},{48,56},{56,0},{64,72... | collective-permute-start | bytes 196616 | tf_op jit(solution)/shard_map/ppermute | solution.py:684
  93.5 28.0 %collective-permute-start.21 = (bf16[1536,512]{1,0:T(8,128)(2,1)S(1)}, bf16[1536,512]{1,0:T(8,128)(2,1)S(1)}, u32[]{:S(2)}, u32[]{:S(2)}) collective-permute-start(bf16[1536,512]{1,0:T(8,128)(2,1)S(1)} %part.1.part_ref), channel_id=1, source_target_pairs={{0,1},{1,0},{2,3},{3,2},{4,5},{5,4},{6,7},{7,6},{8,9},{9,8},{10,11... | collective-permute-start | bytes 4718600 | tf_op jit(solution)/shard_map/ppermute | solution.py:728
  101.1 10.9 %collective-permute-start.23 = (bf16[128,1024]{1,0:T(8,128)(2,1)S(1)}, bf16[128,1024]{1,0:T(8,128)(2,1)S(1)}, u32[]{:S(2)}, u32[]{:S(2)}) collective-permute-start(bf16[128,1024]{1,0:T(8,128)(2,1)S(1)} %slice.131), channel_id=1, source_target_pairs={{0,64},{8,72},{16,80},{24,88},{32,96},{40,104},{48,112},{56,120},{... | collective-permute-start | bytes 786440 | tf_op jit(solution)/shard_map/ppermute | solution.py:690
  101.2 10.8 %collective-permute-start.24 = (bf16[128,1024]{1,0:T(8,128)(2,1)S(1)}, bf16[128,1024]{1,0:T(8,128)(2,1)S(1)}, u32[]{:S(2)}, u32[]{:S(2)}) collective-permute-start(bf16[128,1024]{1,0:T(8,128)(2,1)S(1)} %slice.132), channel_id=1, source_target_pairs={{0,192},{8,200},{16,208},{24,216},{32,224},{40,232},{48,240},{56,2... | collective-permute-start | bytes 786440 | tf_op jit(solution)/shard_map/ppermute | solution.py:691
  104.8 7.2 %collective-permute-start.22 = (bf16[128,512]{1,0:T(8,128)(2,1)S(1)}, bf16[128,512]{1,0:T(8,128)(2,1)S(1)}, u32[]{:S(2)}, u32[]{:S(2)}) collective-permute-start(bf16[128,512]{1,0:T(8,128)(2,1)S(1)} %extra.1.own_ref), channel_id=1, source_target_pairs={{0,64},{8,72},{16,80},{24,88},{32,96},{40,104},{48,112},{56,120},{... | collective-permute-start | bytes 393224 | tf_op jit(solution)/shard_map/ppermute | solution.py:695
  105.5 6.6 %collective-permute-start.25 = (bf16[64,512]{1,0:T(8,128)(2,1)S(1)}, bf16[64,512]{1,0:T(8,128)(2,1)S(1)}, u32[]{:S(2)}, u32[]{:S(2)}) collective-permute-start(bf16[64,512]{1,0:T(8,128)(2,1)S(1)} %get-tuple-element.495.own_ref), channel_id=1, source_target_pairs={{0,4},{1,5},{8,12},{9,13},{16,20},{17,21},{24,28},{25,29},{32,36},... | collective-permute-start | bytes 196616 | tf_op jit(solution)/shard_map/ppermute | solution.py:704
  112.1 11.9 %collective-permute-start.26 = (bf16[256,512]{1,0:T(8,128)(2,1)S(1)}, bf16[256,512]{1,0:T(8,128)(2,1)S(1)}, u32[]{:S(2)}, u32[]{:S(2)}) collective-permute-start(bf16[256,512]{1,0:T(8,128)(2,1)S(1)} %two.1.near_ref), channel_id=1, source_target_pairs={{0,128},{8,136},{16,144},{24,152},{32,160},{40,168},{48,176},{56,1... | collective-permute-start | bytes 786440 | tf_op jit(solution)/shard_map/ppermute | solution.py:713
  116.4 7.5 %collective-permute-start.27 = (bf16[64,512]{1,0:T(8,128)(2,1)S(1)}, bf16[64,512]{1,0:T(8,128)(2,1)S(1)}, u32[]{:S(2)}, u32[]{:S(2)}) collective-permute-start(bf16[64,512]{1,0:T(8,128)(2,1)S(1)} %pass2.1.even_ref), channel_id=1, source_target_pairs={{0,2},{1,3},{4,6},{5,7},{8,10},{9,11},{12,14},{13,15},{16,18},{17,... | collective-permute-start | bytes 196616 | tf_op jit(solution)/shard_map/ppermute | solution.py:717
  119.7 1.8 %copy-start.11 = (bf16[2,512,512]{2,1,0:T(8,128)(2,1)S(1)}, bf16[2,512,512]{2,1,0:T(8,128)(2,1)}, u32[]{:S(2)}) copy-start(bf16[2,512,512]{2,1,0:T(8,128)(2,1)} %upper_ref.3) | copy-start | bytes 3145732
  121.5 4.9 %copy-start.1 = (bf16[2,512,512]{2,1,0:T(8,128)(2,1)S(1)}, bf16[2,512,512]{2,1,0:T(8,128)(2,1)}, u32[]{:S(2)}) copy-start(bf16[2,512,512]{2,1,0:T(8,128)(2,1)} %copy-done) | copy-start | bytes 3145732
  124.6 3.4 %collective-permute-start.28 = (bf16[576,512]{1,0:T(8,128)(2,1)S(1)}, bf16[576,512]{1,0:T(8,128)(2,1)S(1)}, u32[]{:S(2)}, u32[]{:S(2)}) collective-permute-start(bf16[576,512]{1,0:T(8,128)(2,1)S(1)} %cross.1.cross_ref), channel_id=1, source_target_pairs={{0,1},{1,0},{2,3},{3,2},{4,5},{5,4},{6,7},{7,6},{8,9},{9,8},{10,11... | collective-permute-start | bytes 1769480 | tf_op jit(solution)/shard_map/ppermute | solution.py:767
  138.1 3.9 %copy-start.14 = (s32[2,512]{1,0:T(2,128)S(1)}, s32[2,512]{1,0:T(2,128)}, u32[]{:S(2)}) copy-start(s32[2,512]{1,0:T(2,128)} %across_ref.3) | copy-start | bytes 12292

commit v9 on v8

--- a/solution.py
+++ b/solution.py
@@ -584,10 +584,6 @@
 
     quarter = local_rows // NX
     own = [rows[k * quarter : (k + 1) * quarter, :width] for k in range(NX)]
-    got = [lax.ppermute(own[k], "pcol", move_x([(0, k)])) for k in range(1, NX)]
-    (mine,) = local_kernel(
-        choose_kernel, "choose", [shape((quarter, width))], [position], own[0], *got
-    )
 
     line_shape = shape((LINE_ROWS, local_cols))
     *leaving, passing, land, flag, low = local_kernel(
@@ -617,6 +613,8 @@
     from_hi = lax.ppermute(block, "prow", shift_z(-1))
     opposite = lax.ppermute(block, "prow", shift_z(4))
     arrived = [lax.ppermute(leaving[s], "prow", shift_y(s, [0], [0, 1])) for s in (1, 2, 3)]
+    own = after(own, block)
+    got = [lax.ppermute(own[k], "pcol", move_x([(0, k)])) for k in range(1, NX)]
     quarter_shape = shape((NZ // 2 * DEST_ROWS, local_cols))
     kept, send = local_kernel(
         spread_kernel,
@@ -629,19 +627,13 @@
     )
     came = lax.ppermute(send, "prow", shift_z(4, [0, 1]))
 
-    from_lo, from_hi = after((from_lo, from_hi), mine)
     pair_shape = shape((4 * per_home, local_cols))
     pair_lo, pair_hi = local_kernel(
         pair_kernel, "pair", [pair_shape] * 2, [], block, from_lo, from_hi
     )
     two_lo = lax.ppermute(pair_lo, "prow", shift_z(2))
     two_hi = lax.ppermute(pair_hi, "prow", shift_z(-2))
-    quarter_out = after(mine, pair_lo)
-    ring = [(x, (x + 1) % NX) for x in range(NX)]
-    before = lax.ppermute(quarter_out, "pcol", move_x(ring))
-    behind = lax.ppermute(quarter_out, "pcol", move_x([(b, a) for a, b in ring]))
-
-    two_lo, two_hi, opposite = after((two_lo, two_hi, opposite), before, behind, kept)
+    two_lo, two_hi, opposite = after((two_lo, two_hi, opposite), came)
     half = panel // NY
     n_gone = 2 * DEST_ROWS
     z_line, extra = local_kernel(
@@ -658,6 +650,14 @@
     )
     y_lo = lax.ppermute(z_line, "prow", shift_y(1))
     y_hi = lax.ppermute(z_line, "prow", shift_y(-1))
+    (mine,) = local_kernel(
+        choose_kernel, "choose", [shape((quarter, width))], [position], own[0], *after(got, z_line)
+    )
+    quarter_out = mine
+    ring = [(x, (x + 1) % NX) for x in range(NX)]
+    before = lax.ppermute(quarter_out, "pcol", move_x(ring))
+    behind = lax.ppermute(quarter_out, "pcol", move_x([(b, a) for a, b in ring]))
+
     extra_mid = lax.ppermute(extra, "pcol", move_x([(0, 2)]))
     extra_shape = shape((half, width))
     (extra,) = local_kernel(
@@ -682,11 +682,11 @@
         came,
     )
     came = lax.ppermute(send, "prow", shift_z(1))
+    y_lo, y_hi = after((y_lo, y_hi), extra_odd, before, behind, came)
     across = lax.ppermute(
-        after(mine, z_line), "pcol", move_x([(x, (x + 2) % NX) for x in range(NX)])
-    )
-
-    y_lo, y_hi = after((y_lo, y_hi), extra_odd, across, came)
+        after(mine, y_lo), "pcol", move_x([(x, (x + 2) % NX) for x in range(NX)])
+    )
+
     far_first = lax.ppermute(y_lo[:half], "prow", shift_y(1))
     far_second = lax.ppermute(y_hi[half:], "prow", shift_y(-1))
     (near,) = local_kernel(
@@ -723,7 +723,7 @@
         mine,
         before,
         behind,
-        after(across, y_lo),
+        after(across, near),
     )
     other = lax.ppermute(part, "pcol", SWAP)
     n_block = panel // 2
@@ -753,7 +753,7 @@
         name="factor",
     )(position, part, other, upper_inverse)
 
-    far = after(far, far_first, far_second, factor_raw, settled)
+    far = after(far, far_first, far_second, settled)
     (cross,) = local_kernel(
         cross_kernel,
         "cross",

time: 150 us -> 155 us (1.033)
  waiting for transfers between devices: 18.9 us -> 24.4 us
    ppermute x1, waiting for transfers between devices: 5.45 us -> 0.01 us  [per_device(): opposite = lax.ppermute(block, 'prow', shift_z(4))]
    ppermute x1, waiting for transfers between devices: 0.01 us -> 4.54 us  [per_device(): two_hi = lax.ppermute(pair_hi, 'prow', shift_z(-2))]
    ppermute x1, waiting for transfers between devices: 4.26 us -> 8.19 us  [per_device(): came = lax.ppermute(send, 'prow', shift_z(1))]
    ppermute x1, starting transfers between devices: 0.16 us -> 3.27 us  [per_device(): came = lax.ppermute(send, 'prow', shift_z(1))]
    ppermute x1, starting transfers between devices: 4.76 us -> 1.93 us  [per_device(): gone_mid = lax.ppermute(gone_panel, 'pcol', move_x([(0, 2)]))]
    ppermute x3, starting transfers between devices: 9.21 us -> 6.63 us  [per_device(): got = [lax.ppermute(own[k], 'pcol', move_x([(0, k)])) for k in range(1, NX)]]
    ppermute x1, starting transfers between devices: 2.44 us -> 0.07 us  [per_device(): from_hi = lax.ppermute(block, 'prow', shift_z(-1))]
    ppermute x3, waiting for transfers between devices: 3.84 us -> 1.58 us  [per_device(): lax.ppermute(leaving[s], 'prow', shift_y(s, [0], [0, 1]))]
  transfers between devices with their start and end apart: 30 -> 30, of which waited for: 7 -> 10; matrix products, arithmetic and copies ran while one was open for 1% -> 1% of each run, Pallas kernels for 11% -> 11%
where the time goes in v9:
time: 155 us; the launch traced here: 154 us
  starting transfers between devices  70.4 us (45%)
  Pallas kernels  30.9 us (20%)
  waiting for transfers between devices  24.4 us (16%)
  between operations  13.8 us (9%)
  local copies, waits for them, and re-layouts  13.5 us (9%)
    pallas_call x16, Pallas kernels, local_kernel(): pl.pallas_call(body, grid=(1,), in_specs=[smem() for _ in scalars] + [who...  15.7 us
    all_to_all x1, starting transfers between devices, per_device(): dealt = lax.all_to_all(picks, 'prow', 0, 0, tiled=True)  12.2 us
    pallas_call x1, Pallas kernels, per_device(): pl.pallas_call(functools.partial(finish_kernel, panel), grid=(steps + 1,)...  10.3 us
    ppermute x3, starting transfers between devices, per_device(): lax.ppermute(leaving[s], 'prow', shift_y(s, [0], [0, 1]))  8.67 us
    unnamed x23, local copies, waits for them, and re-layouts  8.43 us
    ppermute x1, waiting for transfers between devices, per_device(): came = lax.ppermute(send, 'prow', shift_z(1))  8.19 us
    ppermute x1, starting transfers between devices, per_device(): other = lax.ppermute(part, 'pcol', SWAP)  6.75 us
    ppermute x3, starting transfers between devices, per_device(): got = [lax.ppermute(own[k], 'pcol', move_x([(0, k)])) for k in range(1, NX)]  6.63 us
  transfers between devices with their start and end apart: 30, of which 10 were waited for; matrix products, arithmetic and copies ran while one was open for 1% of the time, Pallas kernels for 11%

profile of v9, /device:TPU:1, one launch (start us, length us, event | category | flops | bytes accessed | tf_op | source)
XLA Modules:
  0.0 153.9 jit_solution(18410349296132437041)
XLA Ops:
  6.5 2.7 %copy.11 = bf16[192,8,2,512]{3,1,2,0:T(8,128)(2,1)S(1)} copy(bf16[192,8,2,512]{3,2,1,0:T(2,128)(2,1)} %bitcast.75) | data formatting | bytes 6291456
  9.4 2.9 %deal.1 = (bf16[256,1024]{1,0:T(8,128)(2,1)S(1)}, s32[32,1]{1,0:T(8,128)S(1)}, s32[2,512]{1,0:T(2,128)S(1)}, s32[1,512]{1,0:T(1,128)S(1)}) custom-call(s32[2]{0:T(128)S(1)} %pad_add_fusion.pos_ref, s32[2,512]{1,0:T(2,128)S(1)} %copy-done.12, bf16[1536,1024]{1,0:T(8,128)(2,1)S(1)} %bitcast.69), custom_call_target="tpu_custom_call" | custom-call | tf_op jit(solution)/shard_map/deal/pallas_call | solution.py:543
  12.3 0.8 copy-done.2
  13.0 12.2 %all-to-all-start = ((bf16[32,8,1024]{2,1,0:T(8,128)(2,1)}), bf16[32,8,1024]{2,1,0:T(8,128)(2,1)}, u32[]{:S(2)}, u32[]{:S(2)}) async-start(bf16[32,8,1024]{2,1,0:T(8,128)(2,1)} %bitcast.73), calls=%async_computation | async-start | bytes 1048576 | tf_op jit(solution)/shard_map/all_to_all | solution.py:583
  25.2 4.3 %leave.1 = (bf16[144,1024]{1,0:T(8,128)(2,1)S(1)}, bf16[144,1024]{1,0:T(8,128)(2,1)}, bf16[144,1024]{1,0:T(8,128)(2,1)}, bf16[144,1024]{1,0:T(8,128)(2,1)}, s32[...) custom-call(s32[2]{0:T(128)S(1)} %pad_add_fusion.pos_ref, ...), custom_call_target="tpu_custom_call" | custom-call | tf_op jit(solution)/shard_map/leave/pallas_call | solution.py:543
  29.6 1.0 copy-done
  30.5 0.7 copy-done.3
  31.9 3.8 %collective-permute-start = (bf16[144,1024]{1,0:T(8,128)(2,1)}, bf16[144,1024]{1,0:T(8,128)(2,1)}, u32[]{:S(2)}, u32[]{:S(2)}) collective-permute-start(bf16[144,1024]{1,0:T(8,128)(2,1)} %get-tuple-element.472), channel_id=1, source_target_pairs={{0,64},{8,72},{1,65},{9,73},{2,66},{10,74},{3,67},{11,75},{4,68},{... | collective-permute-start | bytes 884744 | tf_op jit(solution)/shard_map/ppermute | solution.py:615
  35.6 2.9 %collective-permute-start.1 = (bf16[144,1024]{1,0:T(8,128)(2,1)}, bf16[144,1024]{1,0:T(8,128)(2,1)}, u32[]{:S(2)}, u32[]{:S(2)}) collective-permute-start(bf16[144,1024]{1,0:T(8,128)(2,1)} %get-tuple-element.473), channel_id=1, source_target_pairs={{0,128},{8,136},{1,129},{9,137},{2,130},{10,138},{3,131},{11,139},... | collective-permute-start | bytes 884744 | tf_op jit(solution)/shard_map/ppermute | solution.py:615
  38.5 2.0 %collective-permute-start.2 = (bf16[144,1024]{1,0:T(8,128)(2,1)}, bf16[144,1024]{1,0:T(8,128)(2,1)}, u32[]{:S(2)}, u32[]{:S(2)}) collective-permute-start(bf16[144,1024]{1,0:T(8,128)(2,1)} %get-tuple-element.474), channel_id=1, source_target_pairs={{0,192},{8,200},{1,193},{9,201},{2,194},{10,202},{3,195},{11,203},... | collective-permute-start | bytes 884744 | tf_op jit(solution)/shard_map/ppermute | solution.py:615
  40.5 1.1 fusion.28
  41.6 0.7 copy-done.8
  42.3 1.3 block.1.block_ref
  43.6 1.5 collective-permute-start.4
  45.1 2.1 %collective-permute-start.8 = (bf16[32,1024]{1,0:T(8,128)(2,1)S(1)}, bf16[32,1024]{1,0:T(8,128)(2,1)S(1)}, u32[]{:S(2)}, u32[]{:S(2)}) collective-permute-start(bf16[32,1024]{1,0:T(8,128)(2,1)S(1)} %block.1.block_ref), channel_id=1, source_target_pairs={{0,32},{8,40},{16,48},{24,56},{32,0},{40,8},{48,16},{56,24},{64,96... | collective-permute-start | bytes 196616 | tf_op jit(solution)/shard_map/ppermute | solution.py:614
  47.2 1.6 %collective-permute-done.1.two_ref = bf16[144,1024]{1,0:T(8,128)(2,1)} collective-permute-done((bf16[144,1024]{1,0:T(8,128)(2,1)}, bf16[144,1024]{1,0:T(8,128)(2,1)}, u32[]{:S(2)}, u32[]{:S(2)}) %collective-permute-start.1) | collective-permute-done | bytes 294944 | tf_op jit(solution)/shard_map/ppermute | solution.py:615
  48.7 3.1 %collective-permute-start.15 = (bf16[384,512]{1,0:T(8,128)(2,1)}, bf16[384,512]{1,0:T(8,128)(2,1)S(1)}, u32[]{:S(2)}, u32[]{:S(2)}) collective-permute-start(bf16[384,512]{1,0:T(8,128)(2,1)} %get-tuple-element.490), channel_id=1, source_target_pairs={{0,2},{1,3},{8,10},{9,11},{16,18},{17,19},{24,26},{25,27},{32,34},... | collective-permute-start | bytes 1179656 | tf_op jit(solution)/shard_map/ppermute | solution.py:617
  51.9 2.2 %collective-permute-start.16 = (bf16[384,512]{1,0:T(8,128)(2,1)}, bf16[384,512]{1,0:T(8,128)(2,1)S(1)}, u32[]{:S(2)}, u32[]{:S(2)}) collective-permute-start(bf16[384,512]{1,0:T(8,128)(2,1)} %get-tuple-element.491), channel_id=1, source_target_pairs={{0,4},{1,5},{8,12},{9,13},{16,20},{17,21},{24,28},{25,29},{32,36},... | collective-permute-start | bytes 1179656 | tf_op jit(solution)/shard_map/ppermute | solution.py:617
  54.1 1.0 copy-done.4
  55.0 0.9 copy-done.6
  55.9 1.5 spread.1
  57.5 1.3 collective-permute-start.17
  58.9 5.5 %collective-permute-start.3 = (bf16[128,1024]{1,0:T(8,128)(2,1)S(1)}, bf16[128,1024]{1,0:T(8,128)(2,1)S(1)}, u32[]{:S(2)}, u32[]{:S(2)}) collective-permute-start(bf16[128,1024]{1,0:T(8,128)(2,1)S(1)} %get-tuple-element.476), channel_id=1, source_target_pairs={{0,32},{8,40},{64,96},{72,104},{128,160},{136,168},{192,224},{200,... | collective-permute-start | bytes 786440 | tf_op jit(solution)/shard_map/ppermute | solution.py:628
  65.2 4.5 %collective-permute-done.7.two_hi_ref = bf16[64,1024]{1,0:T(8,128)(2,1)S(1)} collective-permute-done((bf16[64,1024]{1,0:T(8,128)(2,1)S(1)}, bf16[64,1024]{1,0:T(8,128)(2,1)S(1)}, u32[]{:S(2)}, u32[]{:S(2)}) %collective-permute-start.7) | collective-permute-done | bytes 131104 | tf_op jit(solution)/shard_map/ppermute | solution.py:635
  70.9 1.6 %collective-permute-start.12 = (bf16[256,1024]{1,0:T(8,128)(2,1)S(1)}, bf16[256,1024]{1,0:T(8,128)(2,1)S(1)}, u32[]{:S(2)}, u32[]{:S(2)}) collective-permute-start(bf16[256,1024]{1,0:T(8,128)(2,1)S(1)} %get-tuple-element.482.y0_ref), channel_id=1, source_target_pairs={{0,192},{8,200},{16,208},{24,216},{32,224},{40,232},{48,240},{56,2... | collective-permute-start | bytes 1572872 | tf_op jit(solution)/shard_map/ppermute | solution.py:652
  73.1 1.3 collective-permute-start.9
  75.1 1.5 collective-permute-start.18
  76.5 1.3 collective-permute-start.13
  78.4 4.3 %collective-permute-done.13.came_ref = bf16[128,512]{1,0:T(8,128)(2,1)S(1)} collective-permute-done((bf16[128,512]{1,0:T(8,128)(2,1)S(1)}, bf16[128,512]{1,0:T(8,128)(2,1)S(1)}, u32[]{:S(2)}, u32[]{:S(2)}) %collective-permute-start.13) | collective-permute-done | bytes 131104 | tf_op jit(solution)/shard_map/ppermute | solution.py:661
  82.7 3.3 %collective-permute-start.10 = (bf16[32,1024]{1,0:T(8,128)(2,1)S(1)}, bf16[32,1024]{1,0:T(8,128)(2,1)S(1)}, u32[]{:S(2)}, u32[]{:S(2)}) collective-permute-start(bf16[32,1024]{1,0:T(8,128)(2,1)S(1)} %get-tuple-element.487), channel_id=1, source_target_pairs={{0,8},{8,16},{16,24},{24,32},{32,40},{40,48},{48,56},{56,0},{64,72... | collective-permute-start | bytes 196616 | tf_op jit(solution)/shard_map/ppermute | solution.py:684
  86.5 8.2 %collective-permute-done.10.came_ref = bf16[32,1024]{1,0:T(8,128)(2,1)S(1)} collective-permute-done((bf16[32,1024]{1,0:T(8,128)(2,1)S(1)}, bf16[32,1024]{1,0:T(8,128)(2,1)S(1)}, u32[]{:S(2)}, u32[]{:S(2)}) %collective-permute-start.10) | collective-permute-done | bytes 65568 | tf_op jit(solution)/shard_map/ppermute | solution.py:684
  94.7 1.3 collective-permute-start.14
  96.0 1.9 %collective-permute-done.14.odd_ref = bf16[128,512]{1,0:T(8,128)(2,1)S(1)} collective-permute-done((bf16[128,512]{1,0:T(8,128)(2,1)S(1)}, bf16[128,512]{1,0:T(8,128)(2,1)S(1)}, u32[]{:S(2)}, u32[]{:S(2)}) %collective-permute-start.14) | collective-permute-done | bytes 131104 | tf_op jit(solution)/shard_map/ppermute | solution.py:666
  97.9 3.5 %collective-permute-start.20 = (bf16[384,512]{1,0:T(8,128)(2,1)S(1)}, bf16[384,512]{1,0:T(8,128)(2,1)S(1)}, u32[]{:S(2)}, u32[]{:S(2)}) collective-permute-start(bf16[384,512]{1,0:T(8,128)(2,1)S(1)} %choose.1.mine_ref), channel_id=1, source_target_pairs={{0,4},{1,5},{2,6},{3,7},{4,0},{5,1},{6,2},{7,3},{8,12},{9,13},{10,... | collective-permute-start | bytes 1179656 | tf_op jit(solution)/shard_map/ppermute | solution.py:686
  101.6 3.7 %collective-permute-start.23 = (bf16[128,1024]{1,0:T(8,128)(2,1)S(1)}, bf16[128,1024]{1,0:T(8,128)(2,1)S(1)}, u32[]{:S(2)}, u32[]{:S(2)}) collective-permute-start(bf16[128,1024]{1,0:T(8,128)(2,1)S(1)} %slice.132), channel_id=1, source_target_pairs={{0,192},{8,200},{16,208},{24,216},{32,224},{40,232},{48,240},{56,2... | collective-permute-start | bytes 786440 | tf_op jit(solution)/shard_map/ppermute | solution.py:691
  106.5 1.9 %collective-permute-start.24 = (bf16[64,512]{1,0:T(8,128)(2,1)S(1)}, bf16[64,512]{1,0:T(8,128)(2,1)S(1)}, u32[]{:S(2)}, u32[]{:S(2)}) collective-permute-start(bf16[64,512]{1,0:T(8,128)(2,1)S(1)} %get-tuple-element.502.own_ref), channel_id=1, source_target_pairs={{0,4},{1,5},{8,12},{9,13},{16,20},{17,21},{24,28},{25,29},{32,36},... | collective-permute-start | bytes 196616 | tf_op jit(solution)/shard_map/ppermute | solution.py:704
  108.4 1.6 %collective-permute-done.21.came_ref = bf16[128,512]{1,0:T(8,128)(2,1)S(1)} collective-permute-done((bf16[128,512]{1,0:T(8,128)(2,1)S(1)}, bf16[128,512]{1,0:T(8,128)(2,1)S(1)}, u32[]{:S(2)}, u32[]{:S(2)}) %collective-permute-start.21) | collective-permute-done | bytes 131104 | tf_op jit(solution)/shard_map/ppermute | solution.py:695
  111.0 6.8 %collective-permute-start.25 = (bf16[1536,512]{1,0:T(8,128)(2,1)S(1)}, bf16[1536,512]{1,0:T(8,128)(2,1)S(1)}, u32[]{:S(2)}, u32[]{:S(2)}) collective-permute-start(bf16[1536,512]{1,0:T(8,128)(2,1)S(1)} %part.1.part_ref), channel_id=1, source_target_pairs={{0,1},{1,0},{2,3},{3,2},{4,5},{5,4},{6,7},{7,6},{8,9},{9,8},{10,11... | collective-permute-start | bytes 4718600 | tf_op jit(solution)/shard_map/ppermute | solution.py:728
  117.8 2.6 %collective-permute-start.26 = (bf16[256,512]{1,0:T(8,128)(2,1)S(1)}, bf16[256,512]{1,0:T(8,128)(2,1)S(1)}, u32[]{:S(2)}, u32[]{:S(2)}) collective-permute-start(bf16[256,512]{1,0:T(8,128)(2,1)S(1)} %two.1.near_ref), channel_id=1, source_target_pairs={{0,128},{8,136},{16,144},{24,152},{32,160},{40,168},{48,176},{56,1... | collective-permute-start | bytes 786440 | tf_op jit(solution)/shard_map/ppermute | solution.py:713
  121.0 3.5 %collective-permute-start.27 = (bf16[64,512]{1,0:T(8,128)(2,1)S(1)}, bf16[64,512]{1,0:T(8,128)(2,1)S(1)}, u32[]{:S(2)}, u32[]{:S(2)}) collective-permute-start(bf16[64,512]{1,0:T(8,128)(2,1)S(1)} %pass2.1.even_ref), channel_id=1, source_target_pairs={{0,2},{1,3},{4,6},{5,7},{8,10},{9,11},{12,14},{13,15},{16,18},{17,... | collective-permute-start | bytes 196616 | tf_op jit(solution)/shard_map/ppermute | solution.py:717
  124.5 1.7 %settle.1.rows_ref = bf16[1536,1024]{1,0:T(8,128)(2,1)S(1)} custom-call(bf16[1536,1024]{1,0:T(8,128)(2,1)S(1)} %bitcast.72, s32[1,64]{1,0:T(1,128)S(1)} %get-tuple-element.465.land_ref, bf16[64,1024]{1,0:T(8,128)(2,1)S(1)} %get-tuple-element.499.gone_ref), custom_call_target="tpu_custom_call" | custom-call | tf_op jit(solution)/shard_map/settle/pallas_call | solution.py:735
  126.2 0.9 collective-permute-done.26.far_ref
  127.7 1.0 collective-permute-start.28
  128.7 0.7 first.1
  129.4 2.5 %factor.1.factor_ref = bf16[1536,512]{1,0:T(8,128)(2,1)S(1)} custom-call(s32[2]{0:T(128)S(1)} %pad_add_fusion.pos_ref, bf16[1536,512]{1,0:T(8,128)(2,1)S(1)} %part.1.part_ref, bf16[1536,512]{1,0:T(8,128)(2,1)S(1)} %collective-permute-done.25.other_ref, bf16[2,512,512]{2,1,0:T(8,128)(2,1)S(1)} %copy-done.11), custom_call_target="tpu_custom_call" | custom-call | tf_op jit(solution)/shard_map/factor/pallas_call | solution.py:745
  131.9 10.3 %finish.1 = bf16[1536,1024]{1,0:T(8,128)(2,1)S(1)} custom-call(s32[2]{0:T(128)S(1)} %pad_add_fusion.pos_ref, bf16[1536,1024]{1,0:T(8,128)(2,1)S(1)} %settle.1.rows_ref, bf16[1536,512]{1,0:T(8,128)(2,1)S(1)} %part.1.part_ref, bf16[1536,512]{1,0:T(8,128)(2,1)S(1)} %collective-permute-done.25.other_ref, bf16[1536,512]{1,0:T(8,128)(2,1)S(1)} %factor.1.factor_ref, ...), custom_call_target="tpu_custom_call" | custom-call | tf_op jit(solution)/shard_map/finish/pallas_call | solution.py:783
  142.2 3.9 %reshape.435 = bf16[3,512,2,512]{3,2,1,0:T(2,128)(2,1)} reshape(bf16[1536,1024]{1,0:T(8,128)(2,1)S(1)} %finish.1) | data formatting | bytes 6291456 | tf_op jit(solution)/shard_map/reshape | solution.py:814
  146.1 0.9 while.26
  (61 shorter events, 8.7 us)
Async XLA Ops:
  6.5 2.8 %copy-start.12 = (s32[2,512]{1,0:T(2,128)S(1)}, s32[2,512]{1,0:T(2,128)}, u32[]{:S(2)}) copy-start(s32[2,512]{1,0:T(2,128)} %across_ref.3) | copy-start | bytes 12292
  12.2 0.8 copy-start.2
  12.3 26.3 %copy-start.7 = (s32[32,1]{1,0:T(8,128)}, s32[32,1]{1,0:T(8,128)S(1)}, u32[]{:S(2)}) copy-start(s32[32,1]{1,0:T(8,128)S(1)} %get-tuple-element.467.keep_ref) | copy-start | bytes 388
  13.0 28.5 %all-to-all-start = ((bf16[32,8,1024]{2,1,0:T(8,128)(2,1)}), bf16[32,8,1024]{2,1,0:T(8,128)(2,1)}, u32[]{:S(2)}, u32[]{:S(2)}) async-start(bf16[32,8,1024]{2,1,0:T(8,128)(2,1)} %bitcast.73), calls=%async_computation | async-start | bytes 1048576 | tf_op jit(solution)/shard_map/all_to_all | solution.py:583
  29.5 1.0 copy-start
  30.5 0.7 copy-start.3
  31.2 0.6 copy-start.5
  31.9 13.2 %collective-permute-start = (bf16[144,1024]{1,0:T(8,128)(2,1)}, bf16[144,1024]{1,0:T(8,128)(2,1)}, u32[]{:S(2)}, u32[]{:S(2)}) collective-permute-start(bf16[144,1024]{1,0:T(8,128)(2,1)} %get-tuple-element.472), channel_id=1, source_target_pairs={{0,64},{8,72},{1,65},{9,73},{2,66},{10,74},{3,67},{11,75},{4,68},{... | collective-permute-start | bytes 884744 | tf_op jit(solution)/shard_map/ppermute | solution.py:615
  35.6 13.1 %collective-permute-start.1 = (bf16[144,1024]{1,0:T(8,128)(2,1)}, bf16[144,1024]{1,0:T(8,128)(2,1)}, u32[]{:S(2)}, u32[]{:S(2)}) collective-permute-start(bf16[144,1024]{1,0:T(8,128)(2,1)} %get-tuple-element.473), channel_id=1, source_target_pairs={{0,128},{8,136},{1,129},{9,137},{2,130},{10,138},{3,131},{11,139},... | collective-permute-start | bytes 884744 | tf_op jit(solution)/shard_map/ppermute | solution.py:615
  38.5 13.3 %collective-permute-start.2 = (bf16[144,1024]{1,0:T(8,128)(2,1)}, bf16[144,1024]{1,0:T(8,128)(2,1)}, u32[]{:S(2)}, u32[]{:S(2)}) collective-permute-start(bf16[144,1024]{1,0:T(8,128)(2,1)} %get-tuple-element.474), channel_id=1, source_target_pairs={{0,192},{8,200},{1,193},{9,201},{2,194},{10,202},{3,195},{11,203},... | collective-permute-start | bytes 884744 | tf_op jit(solution)/shard_map/ppermute | solution.py:615
  41.6 0.7 copy-start.8
  43.6 13.9 %collective-permute-start.5 = (bf16[32,1024]{1,0:T(8,128)(2,1)S(1)}, bf16[32,1024]{1,0:T(8,128)(2,1)S(1)}, u32[]{:S(2)}, u32[]{:S(2)}) collective-permute-start(bf16[32,1024]{1,0:T(8,128)(2,1)S(1)} %block.1.block_ref), channel_id=1, source_target_pairs={{0,56},{8,0},{16,8},{24,16},{32,24},{40,32},{48,40},{56,48},{64,12... | collective-permute-start | bytes 196616 | tf_op jit(solution)/shard_map/ppermute | solution.py:613
  43.6 15.1 %collective-permute-start.4 = (bf16[32,1024]{1,0:T(8,128)(2,1)S(1)}, bf16[32,1024]{1,0:T(8,128)(2,1)S(1)}, u32[]{:S(2)}, u32[]{:S(2)}) collective-permute-start(bf16[32,1024]{1,0:T(8,128)(2,1)S(1)} %block.1.block_ref), channel_id=1, source_target_pairs={{0,8},{8,16},{16,24},{24,32},{32,40},{40,48},{48,56},{56,0},{64,72... | collective-permute-start | bytes 196616 | tf_op jit(solution)/shard_map/ppermute | solution.py:612
  45.1 13.8 %collective-permute-start.8 = (bf16[32,1024]{1,0:T(8,128)(2,1)S(1)}, bf16[32,1024]{1,0:T(8,128)(2,1)S(1)}, u32[]{:S(2)}, u32[]{:S(2)}) collective-permute-start(bf16[32,1024]{1,0:T(8,128)(2,1)S(1)} %block.1.block_ref), channel_id=1, source_target_pairs={{0,32},{8,40},{16,48},{24,56},{32,0},{40,8},{48,16},{56,24},{64,96... | collective-permute-start | bytes 196616 | tf_op jit(solution)/shard_map/ppermute | solution.py:614
  48.7 24.3 %collective-permute-start.15 = (bf16[384,512]{1,0:T(8,128)(2,1)}, bf16[384,512]{1,0:T(8,128)(2,1)S(1)}, u32[]{:S(2)}, u32[]{:S(2)}) collective-permute-start(bf16[384,512]{1,0:T(8,128)(2,1)} %get-tuple-element.490), channel_id=1, source_target_pairs={{0,2},{1,3},{8,10},{9,11},{16,18},{17,19},{24,26},{25,27},{32,34},... | collective-permute-start | bytes 1179656 | tf_op jit(solution)/shard_map/ppermute | solution.py:617
  51.9 22.5 %collective-permute-start.16 = (bf16[384,512]{1,0:T(8,128)(2,1)}, bf16[384,512]{1,0:T(8,128)(2,1)S(1)}, u32[]{:S(2)}, u32[]{:S(2)}) collective-permute-start(bf16[384,512]{1,0:T(8,128)(2,1)} %get-tuple-element.491), channel_id=1, source_target_pairs={{0,4},{1,5},{8,12},{9,13},{16,20},{17,21},{24,28},{25,29},{32,36},... | collective-permute-start | bytes 1179656 | tf_op jit(solution)/shard_map/ppermute | solution.py:617
  54.1 1.0 copy-start.4
  55.0 0.9 copy-start.6
  57.5 16.9 %collective-permute-start.17 = (bf16[384,512]{1,0:T(8,128)(2,1)}, bf16[384,512]{1,0:T(8,128)(2,1)S(1)}, u32[]{:S(2)}, u32[]{:S(2)}) collective-permute-start(bf16[384,512]{1,0:T(8,128)(2,1)} %get-tuple-element.492), channel_id=1, source_target_pairs={{0,6},{1,7},{8,14},{9,15},{16,22},{17,23},{24,30},{25,31},{32,38},... | collective-permute-start | bytes 1179656 | tf_op jit(solution)/shard_map/ppermute | solution.py:617
  58.8 6.1 %collective-permute-start.6 = (bf16[64,1024]{1,0:T(8,128)(2,1)S(1)}, bf16[64,1024]{1,0:T(8,128)(2,1)S(1)}, u32[]{:S(2)}, u32[]{:S(2)}) collective-permute-start(bf16[64,1024]{1,0:T(8,128)(2,1)S(1)} %get-tuple-element.477), channel_id=1, source_target_pairs={{0,16},{8,24},{16,32},{24,40},{32,48},{40,56},{48,0},{56,8},{64,80... | collective-permute-start | bytes 393224 | tf_op jit(solution)/shard_map/ppermute | solution.py:634
  58.9 11.4 %collective-permute-start.3 = (bf16[128,1024]{1,0:T(8,128)(2,1)S(1)}, bf16[128,1024]{1,0:T(8,128)(2,1)S(1)}, u32[]{:S(2)}, u32[]{:S(2)}) collective-permute-start(bf16[128,1024]{1,0:T(8,128)(2,1)S(1)} %get-tuple-element.476), channel_id=1, source_target_pairs={{0,32},{8,40},{64,96},{72,104},{128,160},{136,168},{192,224},{200,... | collective-permute-start | bytes 786440 | tf_op jit(solution)/shard_map/ppermute | solution.py:628
  65.0 4.8 %collective-permute-start.7 = (bf16[64,1024]{1,0:T(8,128)(2,1)S(1)}, bf16[64,1024]{1,0:T(8,128)(2,1)S(1)}, u32[]{:S(2)}, u32[]{:S(2)}) collective-permute-start(bf16[64,1024]{1,0:T(8,128)(2,1)S(1)} %get-tuple-element.478), channel_id=1, source_target_pairs={{0,48},{8,56},{16,0},{24,8},{32,16},{40,24},{48,32},{56,40},{64,11... | collective-permute-start | bytes 393224 | tf_op jit(solution)/shard_map/ppermute | solution.py:635
  70.9 27.1 %collective-permute-start.12 = (bf16[256,1024]{1,0:T(8,128)(2,1)S(1)}, bf16[256,1024]{1,0:T(8,128)(2,1)S(1)}, u32[]{:S(2)}, u32[]{:S(2)}) collective-permute-start(bf16[256,1024]{1,0:T(8,128)(2,1)S(1)} %get-tuple-element.482.y0_ref), channel_id=1, source_target_pairs={{0,192},{8,200},{16,208},{24,216},{32,224},{40,232},{48,240},{56,2... | collective-permute-start | bytes 1572872 | tf_op jit(solution)/shard_map/ppermute | solution.py:652
  72.5 25.4 %collective-permute-start.11 = (bf16[256,1024]{1,0:T(8,128)(2,1)S(1)}, bf16[256,1024]{1,0:T(8,128)(2,1)S(1)}, u32[]{:S(2)}, u32[]{:S(2)}) collective-permute-start(bf16[256,1024]{1,0:T(8,128)(2,1)S(1)} %get-tuple-element.482.y0_ref), channel_id=1, source_target_pairs={{0,64},{8,72},{16,80},{24,88},{32,96},{40,104},{48,112},{56,120},{... | collective-permute-start | bytes 1572872 | tf_op jit(solution)/shard_map/ppermute | solution.py:651
  73.1 3.5 %collective-permute-start.9 = (bf16[64,1024]{1,0:T(8,128)(2,1)S(1)}, bf16[64,1024]{1,0:T(8,128)(2,1)S(1)}, u32[]{:S(2)}, u32[]{:S(2)}) collective-permute-start(bf16[64,1024]{1,0:T(8,128)(2,1)S(1)} %get-tuple-element.485), channel_id=1, source_target_pairs={{0,16},{8,24},{32,48},{40,56},{64,80},{72,88},{96,112},{104,120},{... | collective-permute-start | bytes 393224 | tf_op jit(solution)/shard_map/ppermute | solution.py:675
  75.0 22.9 %collective-permute-start.19 = (bf16[384,512]{1,0:T(8,128)(2,1)S(1)}, bf16[384,512]{1,0:T(8,128)(2,1)S(1)}, u32[]{:S(2)}, u32[]{:S(2)}) collective-permute-start(bf16[384,512]{1,0:T(8,128)(2,1)S(1)} %choose.1.mine_ref), channel_id=1, source_target_pairs={{2,0},{3,1},{4,2},{5,3},{6,4},{7,5},{0,6},{1,7},{10,8},{11,9},{12,... | collective-permute-start | bytes 1179656 | tf_op jit(solution)/shard_map/ppermute | solution.py:659
  75.1 22.8 %collective-permute-start.18 = (bf16[384,512]{1,0:T(8,128)(2,1)S(1)}, bf16[384,512]{1,0:T(8,128)(2,1)S(1)}, u32[]{:S(2)}, u32[]{:S(2)}) collective-permute-start(bf16[384,512]{1,0:T(8,128)(2,1)S(1)} %choose.1.mine_ref), channel_id=1, source_target_pairs={{0,2},{1,3},{2,4},{3,5},{4,6},{5,7},{6,0},{7,1},{8,10},{9,11},{10,... | collective-permute-start | bytes 1179656 | tf_op jit(solution)/shard_map/ppermute | solution.py:658
  76.5 6.1 %collective-permute-start.13 = (bf16[128,512]{1,0:T(8,128)(2,1)S(1)}, bf16[128,512]{1,0:T(8,128)(2,1)S(1)}, u32[]{:S(2)}, u32[]{:S(2)}) collective-permute-start(bf16[128,512]{1,0:T(8,128)(2,1)S(1)} %get-tuple-element.488.own_ref), channel_id=1, source_target_pairs={{0,4},{1,5},{8,12},{9,13},{16,20},{17,21},{24,28},{25,29},{32,36},... | collective-permute-start | bytes 393224 | tf_op jit(solution)/shard_map/ppermute | solution.py:661
  82.7 12.0 %collective-permute-start.10 = (bf16[32,1024]{1,0:T(8,128)(2,1)S(1)}, bf16[32,1024]{1,0:T(8,128)(2,1)S(1)}, u32[]{:S(2)}, u32[]{:S(2)}) collective-permute-start(bf16[32,1024]{1,0:T(8,128)(2,1)S(1)} %get-tuple-element.487), channel_id=1, source_target_pairs={{0,8},{8,16},{16,24},{24,32},{32,40},{40,48},{48,56},{56,0},{64,72... | collective-permute-start | bytes 196616 | tf_op jit(solution)/shard_map/ppermute | solution.py:684
  94.7 3.2 %collective-permute-start.14 = (bf16[128,512]{1,0:T(8,128)(2,1)S(1)}, bf16[128,512]{1,0:T(8,128)(2,1)S(1)}, u32[]{:S(2)}, u32[]{:S(2)}) collective-permute-start(bf16[128,512]{1,0:T(8,128)(2,1)S(1)} %pass.1.even_ref), channel_id=1, source_target_pairs={{0,2},{1,3},{4,6},{5,7},{8,10},{9,11},{12,14},{13,15},{16,18},{17,... | collective-permute-start | bytes 393224 | tf_op jit(solution)/shard_map/ppermute | solution.py:666
  97.9 12.4 %collective-permute-start.20 = (bf16[384,512]{1,0:T(8,128)(2,1)S(1)}, bf16[384,512]{1,0:T(8,128)(2,1)S(1)}, u32[]{:S(2)}, u32[]{:S(2)}) collective-permute-start(bf16[384,512]{1,0:T(8,128)(2,1)S(1)} %choose.1.mine_ref), channel_id=1, source_target_pairs={{0,4},{1,5},{2,6},{3,7},{4,0},{5,1},{6,2},{7,3},{8,12},{9,13},{10,... | collective-permute-start | bytes 1179656 | tf_op jit(solution)/shard_map/ppermute | solution.py:686
  101.5 8.8 %collective-permute-start.22 = (bf16[128,1024]{1,0:T(8,128)(2,1)S(1)}, bf16[128,1024]{1,0:T(8,128)(2,1)S(1)}, u32[]{:S(2)}, u32[]{:S(2)}) collective-permute-start(bf16[128,1024]{1,0:T(8,128)(2,1)S(1)} %slice.131), channel_id=1, source_target_pairs={{0,64},{8,72},{16,80},{24,88},{32,96},{40,104},{48,112},{56,120},{... | collective-permute-start | bytes 786440 | tf_op jit(solution)/shard_map/ppermute | solution.py:690
  101.6 8.8 %collective-permute-start.23 = (bf16[128,1024]{1,0:T(8,128)(2,1)S(1)}, bf16[128,1024]{1,0:T(8,128)(2,1)S(1)}, u32[]{:S(2)}, u32[]{:S(2)}) collective-permute-start(bf16[128,1024]{1,0:T(8,128)(2,1)S(1)} %slice.132), channel_id=1, source_target_pairs={{0,192},{8,200},{16,208},{24,216},{32,224},{40,232},{48,240},{56,2... | collective-permute-start | bytes 786440 | tf_op jit(solution)/shard_map/ppermute | solution.py:691
  105.8 4.2 %collective-permute-start.21 = (bf16[128,512]{1,0:T(8,128)(2,1)S(1)}, bf16[128,512]{1,0:T(8,128)(2,1)S(1)}, u32[]{:S(2)}, u32[]{:S(2)}) collective-permute-start(bf16[128,512]{1,0:T(8,128)(2,1)S(1)} %extra.1.own_ref), channel_id=1, source_target_pairs={{0,64},{8,72},{16,80},{24,88},{32,96},{40,104},{48,112},{56,120},{... | collective-permute-start | bytes 393224 | tf_op jit(solution)/shard_map/ppermute | solution.py:695
  106.5 3.8 %collective-permute-start.24 = (bf16[64,512]{1,0:T(8,128)(2,1)S(1)}, bf16[64,512]{1,0:T(8,128)(2,1)S(1)}, u32[]{:S(2)}, u32[]{:S(2)}) collective-permute-start(bf16[64,512]{1,0:T(8,128)(2,1)S(1)} %get-tuple-element.502.own_ref), channel_id=1, source_target_pairs={{0,4},{1,5},{8,12},{9,13},{16,20},{17,21},{24,28},{25,29},{32,36},... | collective-permute-start | bytes 196616 | tf_op jit(solution)/shard_map/ppermute | solution.py:704
  111.0 18.4 %collective-permute-start.25 = (bf16[1536,512]{1,0:T(8,128)(2,1)S(1)}, bf16[1536,512]{1,0:T(8,128)(2,1)S(1)}, u32[]{:S(2)}, u32[]{:S(2)}) collective-permute-start(bf16[1536,512]{1,0:T(8,128)(2,1)S(1)} %part.1.part_ref), channel_id=1, source_target_pairs={{0,1},{1,0},{2,3},{3,2},{4,5},{5,4},{6,7},{7,6},{8,9},{9,8},{10,11... | collective-permute-start | bytes 4718600 | tf_op jit(solution)/shard_map/ppermute | solution.py:728
  117.8 9.4 %collective-permute-start.26 = (bf16[256,512]{1,0:T(8,128)(2,1)S(1)}, bf16[256,512]{1,0:T(8,128)(2,1)S(1)}, u32[]{:S(2)}, u32[]{:S(2)}) collective-permute-start(bf16[256,512]{1,0:T(8,128)(2,1)S(1)} %two.1.near_ref), channel_id=1, source_target_pairs={{0,128},{8,136},{16,144},{24,152},{32,160},{40,168},{48,176},{56,1... | collective-permute-start | bytes 786440 | tf_op jit(solution)/shard_map/ppermute | solution.py:713
  121.0 6.2 %collective-permute-start.27 = (bf16[64,512]{1,0:T(8,128)(2,1)S(1)}, bf16[64,512]{1,0:T(8,128)(2,1)S(1)}, u32[]{:S(2)}, u32[]{:S(2)}) collective-permute-start(bf16[64,512]{1,0:T(8,128)(2,1)S(1)} %pass2.1.even_ref), channel_id=1, source_target_pairs={{0,2},{1,3},{4,6},{5,7},{8,10},{9,11},{12,14},{13,15},{16,18},{17,... | collective-permute-start | bytes 196616 | tf_op jit(solution)/shard_map/ppermute | solution.py:717
  124.5 4.2 %copy-start.1 = (bf16[2,512,512]{2,1,0:T(8,128)(2,1)S(1)}, bf16[2,512,512]{2,1,0:T(8,128)(2,1)}, u32[]{:S(2)}) copy-start(bf16[2,512,512]{2,1,0:T(8,128)(2,1)} %copy-done) | copy-start | bytes 3145732
  126.2 3.2 %copy-start.11 = (bf16[2,512,512]{2,1,0:T(8,128)(2,1)S(1)}, bf16[2,512,512]{2,1,0:T(8,128)(2,1)}, u32[]{:S(2)}) copy-start(bf16[2,512,512]{2,1,0:T(8,128)(2,1)} %upper_ref.3) | copy-start | bytes 3145732
  127.7 4.2 %collective-permute-start.28 = (bf16[576,512]{1,0:T(8,128)(2,1)S(1)}, bf16[576,512]{1,0:T(8,128)(2,1)S(1)}, u32[]{:S(2)}, u32[]{:S(2)}) collective-permute-start(bf16[576,512]{1,0:T(8,128)(2,1)S(1)} %cross.1.cross_ref), channel_id=1, source_target_pairs={{0,1},{1,0},{2,3},{3,2},{4,5},{5,4},{6,7},{7,6},{8,9},{9,8},{10,11... | collective-permute-start | bytes 1769480 | tf_op jit(solution)/shard_map/ppermute | solution.py:767

commit v10 on v8

--- a/solution.py
+++ b/solution.py
@@ -570,8 +570,8 @@
         functools.partial(deal_kernel, panel),
         "deal",
         [
-            shape((N_HOMES * PAIR_ROWS, local_cols)),
-            shape((2 * per_home, 1), i32),
+            pltpu.HBM((N_HOMES * PAIR_ROWS, local_cols), jnp.bfloat16),
+            pltpu.HBM((2 * per_home, 1), i32),
             shape((2, panel), i32),
             shape((1, panel), i32),
         ],

time: 150 us -> 150 us (level)
    unnamed x27 -> x23, local copies, waits for them, and re-layouts: 9.07 us -> 7.73 us
  transfers between devices with their start and end apart: 30 -> 30, of which waited for: 7 -> 6; matrix products, arithmetic and copies ran while one was open for 1% -> 1% of each run, Pallas kernels for 11% -> 11%
where the time goes in v10:
time: 150 us; the launch traced here: 149 us
  starting transfers between devices  71.3 us (48%)
  Pallas kernels  31.5 us (21%)
  waiting for transfers between devices  19 us (13%)
  between operations  13.8 us (9%)
  local copies, waits for them, and re-layouts  12.7 us (8%)
    pallas_call x16, Pallas kernels, local_kernel(): pl.pallas_call(body, grid=(1,), in_specs=[smem() for _ in scalars] + [who...  16.4 us
    all_to_all x1, starting transfers between devices, per_device(): dealt = lax.all_to_all(picks, 'prow', 0, 0, tiled=True)  12.2 us
    pallas_call x1, Pallas kernels, per_device(): pl.pallas_call(functools.partial(finish_kernel, panel), grid=(steps + 1,)...  10.2 us
    ppermute x3, starting transfers between devices, per_device(): got = [lax.ppermute(own[k], 'pcol', move_x([(0, k)])) for k in range(1, NX)]  9.19 us
    unnamed x23, local copies, waits for them, and re-layouts  7.73 us
    ppermute x1, starting transfers between devices, per_device(): other = lax.ppermute(part, 'pcol', SWAP)  7.58 us
    ppermute x3, starting transfers between devices, per_device(): lax.ppermute(leaving[s], 'prow', shift_y(s, [0], [0, 1]))  7.39 us
    ppermute x1, waiting for transfers between devices, per_device(): opposite = lax.ppermute(block, 'prow', shift_z(4))  5.46 us
  transfers between devices with their start and end apart: 30, of which 6 were waited for; matrix products, arithmetic and copies ran while one was open for 1% of the time, Pallas kernels for 11%

profile of v10, /device:TPU:1, one launch (start us, length us, event | category | flops | bytes accessed | tf_op | source)
XLA Modules:
  0.0 149.2 jit_solution(8286920109737220289)
XLA Ops:
  6.5 2.7 %copy.11 = bf16[192,8,2,512]{3,1,2,0:T(8,128)(2,1)S(1)} copy(bf16[192,8,2,512]{3,2,1,0:T(2,128)(2,1)} %bitcast.74) | data formatting | bytes 6291456
  9.4 3.7 %deal.1 = (bf16[256,1024]{1,0:T(8,128)(2,1)}, s32[32,1]{1,0:T(8,128)}, s32[2,512]{1,0:T(2,128)S(1)}, s32[1,512]{1,0:T(1,128)S(1)}) custom-call(s32[2]{0:T(128)S(1)} %pad_add_fusion.pos_ref, s32[2,512]{1,0:T(2,128)S(1)} %copy-done.11, bf16[1536,1024]{1,0:T(8,128)(2,1)S(1)} %bitcast.69), custom_call_target="tpu_custom_call" | custom-call | tf_op jit(solution)/shard_map/deal/pallas_call | solution.py:543
  13.0 12.2 %all-to-all-start = ((bf16[32,8,1024]{2,1,0:T(8,128)(2,1)}), bf16[32,8,1024]{2,1,0:T(8,128)(2,1)}, u32[]{:S(2)}, u32[]{:S(2)}) async-start(bf16[32,8,1024]{2,1,0:T(8,128)(2,1)} %bitcast.81), calls=%async_computation | async-start | bytes 1048576 | tf_op jit(solution)/shard_map/all_to_all | solution.py:583
  25.2 1.1 fusion.28
  26.3 5.1 %collective-permute-start.8 = (bf16[384,512]{1,0:T(8,128)(2,1)}, bf16[384,512]{1,0:T(8,128)(2,1)}, u32[]{:S(2)}, u32[]{:S(2)}) collective-permute-start(bf16[384,512]{1,0:T(8,128)(2,1)} %get-tuple-element.566), channel_id=1, source_target_pairs={{0,6},{1,7},{8,14},{9,15},{16,22},{17,23},{24,30},{25,31},{32,38},... | collective-permute-start | bytes 1179656 | tf_op jit(solution)/shard_map/ppermute | solution.py:587
  31.4 2.0 %collective-permute-start.7 = (bf16[384,512]{1,0:T(8,128)(2,1)}, bf16[384,512]{1,0:T(8,128)(2,1)}, u32[]{:S(2)}, u32[]{:S(2)}) collective-permute-start(bf16[384,512]{1,0:T(8,128)(2,1)} %get-tuple-element.567), channel_id=1, source_target_pairs={{0,4},{1,5},{8,12},{9,13},{16,20},{17,21},{24,28},{25,29},{32,36},... | collective-permute-start | bytes 1179656 | tf_op jit(solution)/shard_map/ppermute | solution.py:587
  33.5 2.0 %collective-permute-start.6 = (bf16[384,512]{1,0:T(8,128)(2,1)}, bf16[384,512]{1,0:T(8,128)(2,1)}, u32[]{:S(2)}, u32[]{:S(2)}) collective-permute-start(bf16[384,512]{1,0:T(8,128)(2,1)} %get-tuple-element.568), channel_id=1, source_target_pairs={{0,2},{1,3},{8,10},{9,11},{16,18},{17,19},{24,26},{25,27},{32,34},... | collective-permute-start | bytes 1179656 | tf_op jit(solution)/shard_map/ppermute | solution.py:587
  35.5 4.0 %leave.1 = (bf16[144,1024]{1,0:T(8,128)(2,1)S(1)}, bf16[144,1024]{1,0:T(8,128)(2,1)}, bf16[144,1024]{1,0:T(8,128)(2,1)}, bf16[144,1024]{1,0:T(8,128)(2,1)}, s32[...) custom-call(s32[2]{0:T(128)S(1)} %pad_add_fusion.pos_ref, ...), custom_call_target="tpu_custom_call" | custom-call | tf_op jit(solution)/shard_map/leave/pallas_call | solution.py:543
  39.6 1.0 copy-done
  40.5 0.7 copy-done.2
  41.2 0.7 copy-done.4
  41.9 0.7 copy-done.6
  42.6 1.3 block.1.block_ref
  43.9 2.4 %collective-permute-start.5 = (bf16[32,1024]{1,0:T(8,128)(2,1)S(1)}, bf16[32,1024]{1,0:T(8,128)(2,1)S(1)}, u32[]{:S(2)}, u32[]{:S(2)}) collective-permute-start(bf16[32,1024]{1,0:T(8,128)(2,1)S(1)} %block.1.block_ref), channel_id=1, source_target_pairs={{0,56},{8,0},{16,8},{24,16},{32,24},{40,32},{48,40},{56,48},{64,12... | collective-permute-start | bytes 196616 | tf_op jit(solution)/shard_map/ppermute | solution.py:617
  46.4 3.1 %collective-permute-start = (bf16[144,1024]{1,0:T(8,128)(2,1)}, bf16[144,1024]{1,0:T(8,128)(2,1)S(1)}, u32[]{:S(2)}, u32[]{:S(2)}) collective-permute-start(bf16[144,1024]{1,0:T(8,128)(2,1)} %get-tuple-element.468), channel_id=1, source_target_pairs={{0,64},{8,72},{1,65},{9,73},{2,66},{10,74},{3,67},{11,75},{4,68},{... | collective-permute-start | bytes 884744 | tf_op jit(solution)/shard_map/ppermute | solution.py:619
  49.5 2.2 %collective-permute-start.1 = (bf16[144,1024]{1,0:T(8,128)(2,1)}, bf16[144,1024]{1,0:T(8,128)(2,1)S(1)}, u32[]{:S(2)}, u32[]{:S(2)}) collective-permute-start(bf16[144,1024]{1,0:T(8,128)(2,1)} %get-tuple-element.469), channel_id=1, source_target_pairs={{0,128},{8,136},{1,129},{9,137},{2,130},{10,138},{3,131},{11,139},... | collective-permute-start | bytes 884744 | tf_op jit(solution)/shard_map/ppermute | solution.py:619
  51.7 1.3 choose.1.mine_ref
  53.1 1.5 collective-permute-start.12
  54.6 2.1 %collective-permute-start.2 = (bf16[144,1024]{1,0:T(8,128)(2,1)}, bf16[144,1024]{1,0:T(8,128)(2,1)S(1)}, u32[]{:S(2)}, u32[]{:S(2)}) collective-permute-start(bf16[144,1024]{1,0:T(8,128)(2,1)} %get-tuple-element.470), channel_id=1, source_target_pairs={{0,192},{8,200},{1,193},{9,201},{2,194},{10,202},{3,195},{11,203},... | collective-permute-start | bytes 884744 | tf_op jit(solution)/shard_map/ppermute | solution.py:619
  56.8 3.8 %collective-permute-done.1.two_ref = bf16[144,1024]{1,0:T(8,128)(2,1)S(1)} collective-permute-done((bf16[144,1024]{1,0:T(8,128)(2,1)}, bf16[144,1024]{1,0:T(8,128)(2,1)S(1)}, u32[]{:S(2)}, u32[]{:S(2)}) %collective-permute-start.1) | collective-permute-done | bytes 294944 | tf_op jit(solution)/shard_map/ppermute | solution.py:619
  60.6 1.0 copy-done.3
  61.6 0.9 copy-done.5
  62.5 0.9 spread.1
  63.4 5.5 %collective-permute-done.11.opposite_ref = bf16[32,1024]{1,0:T(8,128)(2,1)S(1)} collective-permute-done((bf16[32,1024]{1,0:T(8,128)(2,1)S(1)}, bf16[32,1024]{1,0:T(8,128)(2,1)S(1)}, u32[]{:S(2)}, u32[]{:S(2)}) %collective-permute-start.11) | collective-permute-done | bytes 65568 | tf_op jit(solution)/shard_map/ppermute | solution.py:618
  68.9 0.6 line.1
  69.5 3.6 %collective-permute-start.17 = (bf16[256,1024]{1,0:T(8,128)(2,1)S(1)}, bf16[256,1024]{1,0:T(8,128)(2,1)S(1)}, u32[]{:S(2)}, u32[]{:S(2)}) collective-permute-start(bf16[256,1024]{1,0:T(8,128)(2,1)S(1)} %get-tuple-element.481.y0_ref), channel_id=1, source_target_pairs={{0,192},{8,200},{16,208},{24,216},{32,224},{40,232},{48,240},{56,2... | collective-permute-start | bytes 1572872 | tf_op jit(solution)/shard_map/ppermute | solution.py:660
  73.1 2.8 %collective-permute-start.3 = (bf16[128,1024]{1,0:T(8,128)(2,1)S(1)}, bf16[128,1024]{1,0:T(8,128)(2,1)S(1)}, u32[]{:S(2)}, u32[]{:S(2)}) collective-permute-start(bf16[128,1024]{1,0:T(8,128)(2,1)S(1)} %get-tuple-element.472), channel_id=1, source_target_pairs={{0,32},{8,40},{64,96},{72,104},{128,160},{136,168},{192,224},{200,... | collective-permute-start | bytes 786440 | tf_op jit(solution)/shard_map/ppermute | solution.py:630
  75.8 1.8 %collective-permute-start.20 = (bf16[384,512]{1,0:T(8,128)(2,1)S(1)}, bf16[384,512]{1,0:T(8,128)(2,1)S(1)}, u32[]{:S(2)}, u32[]{:S(2)}) collective-permute-start(bf16[384,512]{1,0:T(8,128)(2,1)S(1)} %choose.1.mine_ref), channel_id=1, source_target_pairs={{0,4},{1,5},{2,6},{3,7},{4,0},{5,1},{6,2},{7,3},{8,12},{9,13},{10,... | collective-permute-start | bytes 1179656 | tf_op jit(solution)/shard_map/ppermute | solution.py:685
  77.6 3.2 %collective-permute-start.18 = (bf16[128,512]{1,0:T(8,128)(2,1)S(1)}, bf16[128,512]{1,0:T(8,128)(2,1)S(1)}, u32[]{:S(2)}, u32[]{:S(2)}) collective-permute-start(bf16[128,512]{1,0:T(8,128)(2,1)S(1)} %get-tuple-element.487.own_ref), channel_id=1, source_target_pairs={{0,4},{1,5},{8,12},{9,13},{16,20},{17,21},{24,28},{25,29},{32,36},... | collective-permute-start | bytes 393224 | tf_op jit(solution)/shard_map/ppermute | solution.py:661
  81.4 1.3 collective-permute-start.14
  82.7 2.7 %collective-permute-done.18.came_ref = bf16[128,512]{1,0:T(8,128)(2,1)S(1)} collective-permute-done((bf16[128,512]{1,0:T(8,128)(2,1)S(1)}, bf16[128,512]{1,0:T(8,128)(2,1)S(1)}, u32[]{:S(2)}, u32[]{:S(2)}) %collective-permute-start.18) | collective-permute-done | bytes 131104 | tf_op jit(solution)/shard_map/ppermute | solution.py:661
  85.9 1.3 collective-permute-start.19
  88.0 4.3 %collective-permute-done.15.came_ref = bf16[32,1024]{1,0:T(8,128)(2,1)S(1)} collective-permute-done((bf16[32,1024]{1,0:T(8,128)(2,1)S(1)}, bf16[32,1024]{1,0:T(8,128)(2,1)S(1)}, u32[]{:S(2)}, u32[]{:S(2)}) %collective-permute-start.15) | collective-permute-done | bytes 65568 | tf_op jit(solution)/shard_map/ppermute | solution.py:684
  92.2 0.7 part.1.part_ref
  92.9 7.6 %collective-permute-start.21 = (bf16[1536,512]{1,0:T(8,128)(2,1)S(1)}, bf16[1536,512]{1,0:T(8,128)(2,1)S(1)}, u32[]{:S(2)}, u32[]{:S(2)}) collective-permute-start(bf16[1536,512]{1,0:T(8,128)(2,1)S(1)} %part.1.part_ref), channel_id=1, source_target_pairs={{0,1},{1,0},{2,3},{3,2},{4,5},{5,4},{6,7},{7,6},{8,9},{9,8},{10,11... | collective-permute-start | bytes 4718600 | tf_op jit(solution)/shard_map/ppermute | solution.py:728
  100.6 3.0 %collective-permute-start.24 = (bf16[128,1024]{1,0:T(8,128)(2,1)S(1)}, bf16[128,1024]{1,0:T(8,128)(2,1)S(1)}, u32[]{:S(2)}, u32[]{:S(2)}) collective-permute-start(bf16[128,1024]{1,0:T(8,128)(2,1)S(1)} %slice.132), channel_id=1, source_target_pairs={{0,192},{8,200},{16,208},{24,216},{32,224},{40,232},{48,240},{56,2... | collective-permute-start | bytes 786440 | tf_op jit(solution)/shard_map/ppermute | solution.py:691
  104.9 4.8 %collective-permute-start.25 = (bf16[64,512]{1,0:T(8,128)(2,1)S(1)}, bf16[64,512]{1,0:T(8,128)(2,1)S(1)}, u32[]{:S(2)}, u32[]{:S(2)}) collective-permute-start(bf16[64,512]{1,0:T(8,128)(2,1)S(1)} %get-tuple-element.495.own_ref), channel_id=1, source_target_pairs={{0,4},{1,5},{8,12},{9,13},{16,20},{17,21},{24,28},{25,29},{32,36},... | collective-permute-start | bytes 196616 | tf_op jit(solution)/shard_map/ppermute | solution.py:704
  109.6 1.8 %collective-permute-done.22.came_ref = bf16[128,512]{1,0:T(8,128)(2,1)S(1)} collective-permute-done((bf16[128,512]{1,0:T(8,128)(2,1)S(1)}, bf16[128,512]{1,0:T(8,128)(2,1)S(1)}, u32[]{:S(2)}, u32[]{:S(2)}) %collective-permute-start.22) | collective-permute-done | bytes 131104 | tf_op jit(solution)/shard_map/ppermute | solution.py:695
  111.5 3.8 %collective-permute-start.26 = (bf16[256,512]{1,0:T(8,128)(2,1)S(1)}, bf16[256,512]{1,0:T(8,128)(2,1)S(1)}, u32[]{:S(2)}, u32[]{:S(2)}) collective-permute-start(bf16[256,512]{1,0:T(8,128)(2,1)S(1)} %two.1.near_ref), channel_id=1, source_target_pairs={{0,128},{8,136},{16,144},{24,152},{32,160},{40,168},{48,176},{56,1... | collective-permute-start | bytes 786440 | tf_op jit(solution)/shard_map/ppermute | solution.py:713
  115.8 3.3 %collective-permute-start.27 = (bf16[64,512]{1,0:T(8,128)(2,1)S(1)}, bf16[64,512]{1,0:T(8,128)(2,1)S(1)}, u32[]{:S(2)}, u32[]{:S(2)}) collective-permute-start(bf16[64,512]{1,0:T(8,128)(2,1)S(1)} %pass2.1.even_ref), channel_id=1, source_target_pairs={{0,2},{1,3},{4,6},{5,7},{8,10},{9,11},{12,14},{13,15},{16,18},{17,... | collective-permute-start | bytes 196616 | tf_op jit(solution)/shard_map/ppermute | solution.py:717
  119.1 1.7 %settle.1.rows_ref = bf16[1536,1024]{1,0:T(8,128)(2,1)S(1)} custom-call(bf16[1536,1024]{1,0:T(8,128)(2,1)S(1)} %bitcast.72, s32[1,64]{1,0:T(1,128)S(1)} %get-tuple-element.461.land_ref, bf16[64,1024]{1,0:T(8,128)(2,1)S(1)} %get-tuple-element.492.gone_ref), custom_call_target="tpu_custom_call" | custom-call | tf_op jit(solution)/shard_map/settle/pallas_call | solution.py:735
  120.9 2.5 %factor.1.factor_ref = bf16[1536,512]{1,0:T(8,128)(2,1)S(1)} custom-call(s32[2]{0:T(128)S(1)} %pad_add_fusion.pos_ref, bf16[1536,512]{1,0:T(8,128)(2,1)S(1)} %part.1.part_ref, bf16[1536,512]{1,0:T(8,128)(2,1)S(1)} %collective-permute-done.21.other_ref, bf16[2,512,512]{2,1,0:T(8,128)(2,1)S(1)} %copy-done.9), custom_call_target="tpu_custom_call" | custom-call | tf_op jit(solution)/shard_map/factor/pallas_call | solution.py:745
  124.0 1.8 %collective-permute-start.28 = (bf16[576,512]{1,0:T(8,128)(2,1)S(1)}, bf16[576,512]{1,0:T(8,128)(2,1)S(1)}, u32[]{:S(2)}, u32[]{:S(2)}) collective-permute-start(bf16[576,512]{1,0:T(8,128)(2,1)S(1)} %cross.1.cross_ref), channel_id=1, source_target_pairs={{0,1},{1,0},{2,3},{3,2},{4,5},{5,4},{6,7},{7,6},{8,9},{9,8},{10,11... | collective-permute-start | bytes 1769480 | tf_op jit(solution)/shard_map/ppermute | solution.py:767
  125.8 0.7 first.1
  126.5 0.9 collective-permute-done.28.cross_other_ref
  127.4 10.2 %finish.1 = bf16[1536,1024]{1,0:T(8,128)(2,1)S(1)} custom-call(s32[2]{0:T(128)S(1)} %pad_add_fusion.pos_ref, bf16[1536,1024]{1,0:T(8,128)(2,1)S(1)} %settle.1.rows_ref, bf16[1536,512]{1,0:T(8,128)(2,1)S(1)} %part.1.part_ref, bf16[1536,512]{1,0:T(8,128)(2,1)S(1)} %collective-permute-done.21.other_ref, bf16[1536,512]{1,0:T(8,128)(2,1)S(1)} %factor.1.factor_ref, ...), custom_call_target="tpu_custom_call" | custom-call | tf_op jit(solution)/shard_map/finish/pallas_call | solution.py:783
  137.6 3.9 %reshape.435 = bf16[3,512,2,512]{3,2,1,0:T(2,128)(2,1)} reshape(bf16[1536,1024]{1,0:T(8,128)(2,1)S(1)} %finish.1) | data formatting | bytes 6291456 | tf_op jit(solution)/shard_map/reshape | solution.py:814
  141.6 0.8 while.26
  (61 shorter events, 4.8 us)
Async XLA Ops:
  6.5 2.8 %copy-start.11 = (s32[2,512]{1,0:T(2,128)S(1)}, s32[2,512]{1,0:T(2,128)}, u32[]{:S(2)}) copy-start(s32[2,512]{1,0:T(2,128)} %across_ref.3) | copy-start | bytes 12292
  13.0 28.9 %all-to-all-start = ((bf16[32,8,1024]{2,1,0:T(8,128)(2,1)}), bf16[32,8,1024]{2,1,0:T(8,128)(2,1)}, u32[]{:S(2)}, u32[]{:S(2)}) async-start(bf16[32,8,1024]{2,1,0:T(8,128)(2,1)} %bitcast.81), calls=%async_computation | async-start | bytes 1048576 | tf_op jit(solution)/shard_map/all_to_all | solution.py:583
  25.2 10.3 %copy-start.10 = (bf16[2,512,512]{2,1,0:T(8,128)(2,1)S(1)}, bf16[2,512,512]{2,1,0:T(8,128)(2,1)}, u32[]{:S(2)}) copy-start(bf16[2,512,512]{2,1,0:T(8,128)(2,1)} %lower_ref.1) | copy-start | bytes 3145732
  26.3 20.0 %collective-permute-start.8 = (bf16[384,512]{1,0:T(8,128)(2,1)}, bf16[384,512]{1,0:T(8,128)(2,1)}, u32[]{:S(2)}, u32[]{:S(2)}) collective-permute-start(bf16[384,512]{1,0:T(8,128)(2,1)} %get-tuple-element.566), channel_id=1, source_target_pairs={{0,6},{1,7},{8,14},{9,15},{16,22},{17,23},{24,30},{25,31},{32,38},... | collective-permute-start | bytes 1179656 | tf_op jit(solution)/shard_map/ppermute | solution.py:587
  31.4 18.0 %collective-permute-start.7 = (bf16[384,512]{1,0:T(8,128)(2,1)}, bf16[384,512]{1,0:T(8,128)(2,1)}, u32[]{:S(2)}, u32[]{:S(2)}) collective-permute-start(bf16[384,512]{1,0:T(8,128)(2,1)} %get-tuple-element.567), channel_id=1, source_target_pairs={{0,4},{1,5},{8,12},{9,13},{16,20},{17,21},{24,28},{25,29},{32,36},... | collective-permute-start | bytes 1179656 | tf_op jit(solution)/shard_map/ppermute | solution.py:587
  33.5 18.2 %collective-permute-start.6 = (bf16[384,512]{1,0:T(8,128)(2,1)}, bf16[384,512]{1,0:T(8,128)(2,1)}, u32[]{:S(2)}, u32[]{:S(2)}) collective-permute-start(bf16[384,512]{1,0:T(8,128)(2,1)} %get-tuple-element.568), channel_id=1, source_target_pairs={{0,2},{1,3},{8,10},{9,11},{16,18},{17,19},{24,26},{25,27},{32,34},... | collective-permute-start | bytes 1179656 | tf_op jit(solution)/shard_map/ppermute | solution.py:587
  39.5 1.0 copy-start
  40.5 0.7 copy-start.2
  41.2 0.7 copy-start.4
  41.9 0.7 copy-start.6
  43.9 9.1 %collective-permute-start.5 = (bf16[32,1024]{1,0:T(8,128)(2,1)S(1)}, bf16[32,1024]{1,0:T(8,128)(2,1)S(1)}, u32[]{:S(2)}, u32[]{:S(2)}) collective-permute-start(bf16[32,1024]{1,0:T(8,128)(2,1)S(1)} %block.1.block_ref), channel_id=1, source_target_pairs={{0,56},{8,0},{16,8},{24,16},{32,24},{40,32},{48,40},{56,48},{64,12... | collective-permute-start | bytes 196616 | tf_op jit(solution)/shard_map/ppermute | solution.py:617
  46.3 6.7 %collective-permute-start.4 = (bf16[32,1024]{1,0:T(8,128)(2,1)S(1)}, bf16[32,1024]{1,0:T(8,128)(2,1)S(1)}, u32[]{:S(2)}, u32[]{:S(2)}) collective-permute-start(bf16[32,1024]{1,0:T(8,128)(2,1)S(1)} %block.1.block_ref), channel_id=1, source_target_pairs={{0,8},{8,16},{16,24},{24,32},{32,40},{40,48},{48,56},{56,0},{64,72... | collective-permute-start | bytes 196616 | tf_op jit(solution)/shard_map/ppermute | solution.py:616
  46.4 10.3 %collective-permute-start = (bf16[144,1024]{1,0:T(8,128)(2,1)}, bf16[144,1024]{1,0:T(8,128)(2,1)S(1)}, u32[]{:S(2)}, u32[]{:S(2)}) collective-permute-start(bf16[144,1024]{1,0:T(8,128)(2,1)} %get-tuple-element.468), channel_id=1, source_target_pairs={{0,64},{8,72},{1,65},{9,73},{2,66},{10,74},{3,67},{11,75},{4,68},{... | collective-permute-start | bytes 884744 | tf_op jit(solution)/shard_map/ppermute | solution.py:619
  49.5 11.1 %collective-permute-start.1 = (bf16[144,1024]{1,0:T(8,128)(2,1)}, bf16[144,1024]{1,0:T(8,128)(2,1)S(1)}, u32[]{:S(2)}, u32[]{:S(2)}) collective-permute-start(bf16[144,1024]{1,0:T(8,128)(2,1)} %get-tuple-element.469), channel_id=1, source_target_pairs={{0,128},{8,136},{1,129},{9,137},{2,130},{10,138},{3,131},{11,139},... | collective-permute-start | bytes 884744 | tf_op jit(solution)/shard_map/ppermute | solution.py:619
  53.0 15.8 %collective-permute-start.13 = (bf16[384,512]{1,0:T(8,128)(2,1)S(1)}, bf16[384,512]{1,0:T(8,128)(2,1)S(1)}, u32[]{:S(2)}, u32[]{:S(2)}) collective-permute-start(bf16[384,512]{1,0:T(8,128)(2,1)S(1)} %choose.1.mine_ref), channel_id=1, source_target_pairs={{2,0},{3,1},{4,2},{5,3},{6,4},{7,5},{0,6},{1,7},{10,8},{11,9},{12,... | collective-permute-start | bytes 1179656 | tf_op jit(solution)/shard_map/ppermute | solution.py:642
  53.1 15.7 %collective-permute-start.12 = (bf16[384,512]{1,0:T(8,128)(2,1)S(1)}, bf16[384,512]{1,0:T(8,128)(2,1)S(1)}, u32[]{:S(2)}, u32[]{:S(2)}) collective-permute-start(bf16[384,512]{1,0:T(8,128)(2,1)S(1)} %choose.1.mine_ref), channel_id=1, source_target_pairs={{0,2},{1,3},{2,4},{3,5},{4,6},{5,7},{6,0},{7,1},{8,10},{9,11},{10,... | collective-permute-start | bytes 1179656 | tf_op jit(solution)/shard_map/ppermute | solution.py:641
  54.6 6.0 %collective-permute-start.2 = (bf16[144,1024]{1,0:T(8,128)(2,1)}, bf16[144,1024]{1,0:T(8,128)(2,1)S(1)}, u32[]{:S(2)}, u32[]{:S(2)}) collective-permute-start(bf16[144,1024]{1,0:T(8,128)(2,1)} %get-tuple-element.470), channel_id=1, source_target_pairs={{0,192},{8,200},{1,193},{9,201},{2,194},{10,202},{3,195},{11,203},... | collective-permute-start | bytes 884744 | tf_op jit(solution)/shard_map/ppermute | solution.py:619
  56.7 12.2 %collective-permute-start.10 = (bf16[64,1024]{1,0:T(8,128)(2,1)S(1)}, bf16[64,1024]{1,0:T(8,128)(2,1)S(1)}, u32[]{:S(2)}, u32[]{:S(2)}) collective-permute-start(bf16[64,1024]{1,0:T(8,128)(2,1)S(1)} %get-tuple-element.476), channel_id=1, source_target_pairs={{0,48},{8,56},{16,0},{24,8},{32,16},{40,24},{48,32},{56,40},{64,11... | collective-permute-start | bytes 393224 | tf_op jit(solution)/shard_map/ppermute | solution.py:638
  60.6 8.3 %collective-permute-start.9 = (bf16[64,1024]{1,0:T(8,128)(2,1)S(1)}, bf16[64,1024]{1,0:T(8,128)(2,1)S(1)}, u32[]{:S(2)}, u32[]{:S(2)}) collective-permute-start(bf16[64,1024]{1,0:T(8,128)(2,1)S(1)} %get-tuple-element.475), channel_id=1, source_target_pairs={{0,16},{8,24},{16,32},{24,40},{32,48},{40,56},{48,0},{56,8},{64,80... | collective-permute-start | bytes 393224 | tf_op jit(solution)/shard_map/ppermute | solution.py:637
  60.6 8.2 %collective-permute-start.11 = (bf16[32,1024]{1,0:T(8,128)(2,1)S(1)}, bf16[32,1024]{1,0:T(8,128)(2,1)S(1)}, u32[]{:S(2)}, u32[]{:S(2)}) collective-permute-start(bf16[32,1024]{1,0:T(8,128)(2,1)S(1)} %block.1.block_ref), channel_id=1, source_target_pairs={{0,32},{8,40},{16,48},{24,56},{32,0},{40,8},{48,16},{56,24},{64,96... | collective-permute-start | bytes 196616 | tf_op jit(solution)/shard_map/ppermute | solution.py:618
  60.6 1.0 copy-start.3
  61.6 0.9 copy-start.5
  69.5 22.8 %collective-permute-start.17 = (bf16[256,1024]{1,0:T(8,128)(2,1)S(1)}, bf16[256,1024]{1,0:T(8,128)(2,1)S(1)}, u32[]{:S(2)}, u32[]{:S(2)}) collective-permute-start(bf16[256,1024]{1,0:T(8,128)(2,1)S(1)} %get-tuple-element.481.y0_ref), channel_id=1, source_target_pairs={{0,192},{8,200},{16,208},{24,216},{32,224},{40,232},{48,240},{56,2... | collective-permute-start | bytes 1572872 | tf_op jit(solution)/shard_map/ppermute | solution.py:660
  73.1 19.2 %collective-permute-start.16 = (bf16[256,1024]{1,0:T(8,128)(2,1)S(1)}, bf16[256,1024]{1,0:T(8,128)(2,1)S(1)}, u32[]{:S(2)}, u32[]{:S(2)}) collective-permute-start(bf16[256,1024]{1,0:T(8,128)(2,1)S(1)} %get-tuple-element.481.y0_ref), channel_id=1, source_target_pairs={{0,64},{8,72},{16,80},{24,88},{32,96},{40,104},{48,112},{56,120},{... | collective-permute-start | bytes 1572872 | tf_op jit(solution)/shard_map/ppermute | solution.py:659
  73.1 7.7 %collective-permute-start.3 = (bf16[128,1024]{1,0:T(8,128)(2,1)S(1)}, bf16[128,1024]{1,0:T(8,128)(2,1)S(1)}, u32[]{:S(2)}, u32[]{:S(2)}) collective-permute-start(bf16[128,1024]{1,0:T(8,128)(2,1)S(1)} %get-tuple-element.472), channel_id=1, source_target_pairs={{0,32},{8,40},{64,96},{72,104},{128,160},{136,168},{192,224},{200,... | collective-permute-start | bytes 786440 | tf_op jit(solution)/shard_map/ppermute | solution.py:630
  75.8 16.4 %collective-permute-start.20 = (bf16[384,512]{1,0:T(8,128)(2,1)S(1)}, bf16[384,512]{1,0:T(8,128)(2,1)S(1)}, u32[]{:S(2)}, u32[]{:S(2)}) collective-permute-start(bf16[384,512]{1,0:T(8,128)(2,1)S(1)} %choose.1.mine_ref), channel_id=1, source_target_pairs={{0,4},{1,5},{2,6},{3,7},{4,0},{5,1},{6,2},{7,3},{8,12},{9,13},{10,... | collective-permute-start | bytes 1179656 | tf_op jit(solution)/shard_map/ppermute | solution.py:685
  77.6 7.8 %collective-permute-start.18 = (bf16[128,512]{1,0:T(8,128)(2,1)S(1)}, bf16[128,512]{1,0:T(8,128)(2,1)S(1)}, u32[]{:S(2)}, u32[]{:S(2)}) collective-permute-start(bf16[128,512]{1,0:T(8,128)(2,1)S(1)} %get-tuple-element.487.own_ref), channel_id=1, source_target_pairs={{0,4},{1,5},{8,12},{9,13},{16,20},{17,21},{24,28},{25,29},{32,36},... | collective-permute-start | bytes 393224 | tf_op jit(solution)/shard_map/ppermute | solution.py:661
  81.4 5.8 %collective-permute-start.14 = (bf16[64,1024]{1,0:T(8,128)(2,1)S(1)}, bf16[64,1024]{1,0:T(8,128)(2,1)S(1)}, u32[]{:S(2)}, u32[]{:S(2)}) collective-permute-start(bf16[64,1024]{1,0:T(8,128)(2,1)S(1)} %get-tuple-element.484), channel_id=1, source_target_pairs={{0,16},{8,24},{32,48},{40,56},{64,80},{72,88},{96,112},{104,120},{... | collective-permute-start | bytes 393224 | tf_op jit(solution)/shard_map/ppermute | solution.py:675
  85.9 6.3 %collective-permute-start.19 = (bf16[128,512]{1,0:T(8,128)(2,1)S(1)}, bf16[128,512]{1,0:T(8,128)(2,1)S(1)}, u32[]{:S(2)}, u32[]{:S(2)}) collective-permute-start(bf16[128,512]{1,0:T(8,128)(2,1)S(1)} %pass.1.even_ref), channel_id=1, source_target_pairs={{0,2},{1,3},{4,6},{5,7},{8,10},{9,11},{12,14},{13,15},{16,18},{17,... | collective-permute-start | bytes 393224 | tf_op jit(solution)/shard_map/ppermute | solution.py:666
  87.8 4.4 %collective-permute-start.15 = (bf16[32,1024]{1,0:T(8,128)(2,1)S(1)}, bf16[32,1024]{1,0:T(8,128)(2,1)S(1)}, u32[]{:S(2)}, u32[]{:S(2)}) collective-permute-start(bf16[32,1024]{1,0:T(8,128)(2,1)S(1)} %get-tuple-element.486), channel_id=1, source_target_pairs={{0,8},{8,16},{16,24},{24,32},{32,40},{40,48},{48,56},{56,0},{64,72... | collective-permute-start | bytes 196616 | tf_op jit(solution)/shard_map/ppermute | solution.py:684
  92.9 28.0 %collective-permute-start.21 = (bf16[1536,512]{1,0:T(8,128)(2,1)S(1)}, bf16[1536,512]{1,0:T(8,128)(2,1)S(1)}, u32[]{:S(2)}, u32[]{:S(2)}) collective-permute-start(bf16[1536,512]{1,0:T(8,128)(2,1)S(1)} %part.1.part_ref), channel_id=1, source_target_pairs={{0,1},{1,0},{2,3},{3,2},{4,5},{5,4},{6,7},{7,6},{8,9},{9,8},{10,11... | collective-permute-start | bytes 4718600 | tf_op jit(solution)/shard_map/ppermute | solution.py:728
  100.5 10.9 %collective-permute-start.23 = (bf16[128,1024]{1,0:T(8,128)(2,1)S(1)}, bf16[128,1024]{1,0:T(8,128)(2,1)S(1)}, u32[]{:S(2)}, u32[]{:S(2)}) collective-permute-start(bf16[128,1024]{1,0:T(8,128)(2,1)S(1)} %slice.131), channel_id=1, source_target_pairs={{0,64},{8,72},{16,80},{24,88},{32,96},{40,104},{48,112},{56,120},{... | collective-permute-start | bytes 786440 | tf_op jit(solution)/shard_map/ppermute | solution.py:690
  100.6 10.8 %collective-permute-start.24 = (bf16[128,1024]{1,0:T(8,128)(2,1)S(1)}, bf16[128,1024]{1,0:T(8,128)(2,1)S(1)}, u32[]{:S(2)}, u32[]{:S(2)}) collective-permute-start(bf16[128,1024]{1,0:T(8,128)(2,1)S(1)} %slice.132), channel_id=1, source_target_pairs={{0,192},{8,200},{16,208},{24,216},{32,224},{40,232},{48,240},{56,2... | collective-permute-start | bytes 786440 | tf_op jit(solution)/shard_map/ppermute | solution.py:691
  104.2 7.2 %collective-permute-start.22 = (bf16[128,512]{1,0:T(8,128)(2,1)S(1)}, bf16[128,512]{1,0:T(8,128)(2,1)S(1)}, u32[]{:S(2)}, u32[]{:S(2)}) collective-permute-start(bf16[128,512]{1,0:T(8,128)(2,1)S(1)} %extra.1.own_ref), channel_id=1, source_target_pairs={{0,64},{8,72},{16,80},{24,88},{32,96},{40,104},{48,112},{56,120},{... | collective-permute-start | bytes 393224 | tf_op jit(solution)/shard_map/ppermute | solution.py:695
  104.9 6.6 %collective-permute-start.25 = (bf16[64,512]{1,0:T(8,128)(2,1)S(1)}, bf16[64,512]{1,0:T(8,128)(2,1)S(1)}, u32[]{:S(2)}, u32[]{:S(2)}) collective-permute-start(bf16[64,512]{1,0:T(8,128)(2,1)S(1)} %get-tuple-element.495.own_ref), channel_id=1, source_target_pairs={{0,4},{1,5},{8,12},{9,13},{16,20},{17,21},{24,28},{25,29},{32,36},... | collective-permute-start | bytes 196616 | tf_op jit(solution)/shard_map/ppermute | solution.py:704
  111.5 11.9 %collective-permute-start.26 = (bf16[256,512]{1,0:T(8,128)(2,1)S(1)}, bf16[256,512]{1,0:T(8,128)(2,1)S(1)}, u32[]{:S(2)}, u32[]{:S(2)}) collective-permute-start(bf16[256,512]{1,0:T(8,128)(2,1)S(1)} %two.1.near_ref), channel_id=1, source_target_pairs={{0,128},{8,136},{16,144},{24,152},{32,160},{40,168},{48,176},{56,1... | collective-permute-start | bytes 786440 | tf_op jit(solution)/shard_map/ppermute | solution.py:713
  115.8 7.6 %collective-permute-start.27 = (bf16[64,512]{1,0:T(8,128)(2,1)S(1)}, bf16[64,512]{1,0:T(8,128)(2,1)S(1)}, u32[]{:S(2)}, u32[]{:S(2)}) collective-permute-start(bf16[64,512]{1,0:T(8,128)(2,1)S(1)} %pass2.1.even_ref), channel_id=1, source_target_pairs={{0,2},{1,3},{4,6},{5,7},{8,10},{9,11},{12,14},{13,15},{16,18},{17,... | collective-permute-start | bytes 196616 | tf_op jit(solution)/shard_map/ppermute | solution.py:717
  119.1 1.8 %copy-start.9 = (bf16[2,512,512]{2,1,0:T(8,128)(2,1)S(1)}, bf16[2,512,512]{2,1,0:T(8,128)(2,1)}, u32[]{:S(2)}) copy-start(bf16[2,512,512]{2,1,0:T(8,128)(2,1)} %upper_ref.3) | copy-start | bytes 3145732
  120.9 4.9 %copy-start.1 = (bf16[2,512,512]{2,1,0:T(8,128)(2,1)S(1)}, bf16[2,512,512]{2,1,0:T(8,128)(2,1)}, u32[]{:S(2)}) copy-start(bf16[2,512,512]{2,1,0:T(8,128)(2,1)} %copy-done) | copy-start | bytes 3145732
  124.0 3.4 %collective-permute-start.28 = (bf16[576,512]{1,0:T(8,128)(2,1)S(1)}, bf16[576,512]{1,0:T(8,128)(2,1)S(1)}, u32[]{:S(2)}, u32[]{:S(2)}) collective-permute-start(bf16[576,512]{1,0:T(8,128)(2,1)S(1)} %cross.1.cross_ref), channel_id=1, source_target_pairs={{0,1},{1,0},{2,3},{3,2},{4,5},{5,4},{6,7},{7,6},{8,9},{9,8},{10,11... | collective-permute-start | bytes 1769480 | tf_op jit(solution)/shard_map/ppermute | solution.py:767
  137.6 3.9 %copy-start.12 = (s32[2,512]{1,0:T(2,128)S(1)}, s32[2,512]{1,0:T(2,128)}, u32[]{:S(2)}) copy-start(s32[2,512]{1,0:T(2,128)} %across_ref.3) | copy-start | bytes 12292
